TPU v7x, 256 devices: a whole 4x4x8 slice. The times are simulated.
256 devices in a mesh: grp: 2 (over core), fsdp: 16 (over z_hi, x), tp: 8 (over z_lo, y).
Axes of the slice: x: 4, y: 4, z: 8 (z_hi: 4, z_lo: 2; z = z_hi * 2 + z_lo), core: 2. Of those that a mesh axis runs over, the one named last changes fastest.
Arguments:
- normed_inputs: bfloat16 [24576, 8192], P(('grp', 'fsdp')), may hold values from -6 to 6
- value_cotangent: bfloat16 [24576, 1024], P(('grp', 'fsdp'), 'tp'), may hold values from -0.0390625 to 0.0390625
- value_weight: bfloat16 [8192, 1024], P(('grp', 'fsdp'), 'tp'), may hold values from -0.0625 to 0.0625
- decode_inputs: bfloat16 [512, 4, 8192], P(('grp', 'fsdp'), None, 'tp'), may hold values from -6 to 6
- queries: bfloat16 [512, 4, 8192], P(('grp', 'fsdp'), None, 'tp')
- new_keys: bfloat16 [512, 4, 1024], P(('grp', 'fsdp'), None, 'tp'), may hold values from -6 to 6
- cache_keys: bfloat16 [512, 128, 1024], P(('grp', 'fsdp'), None, 'tp')
- cache_values: bfloat16 [512, 128, 1024], P(('grp', 'fsdp'), None, 'tp'), may hold values from -6 to 6
- lengths: int32 [512], P(('grp', 'fsdp')), may hold values from 2 to 128, as said below
Outputs:
- gradient: float32 [8192, 1024], P(('grp', 'fsdp'), 'tp')
- new_values: bfloat16 [512, 4, 1024], P(('grp', 'fsdp'), None, 'tp')
- attended: bfloat16 [512, 4, 8192], P(('grp', 'fsdp'), None, 'tp')
Inputs may be any that keep to these rules, and one draw needn't show every extreme that they name: `lengths`: at least 2 and at most 128; some row has exactly 128.
All inputs are finite; a program needn't handle non-finite values.
Results may differ from a plain program's by a relative error of at most 0.0052.
Values may be sent and summed in bfloat16 or wider, within the bound.
No kernel may reach another device: no remote copies, remote signals or barrier semaphores. Data moves between devices by JAX's collectives and lax.ppermute only.
A program may use at most 64 MiB of HBM per device.

v0:
```python
import math

import jax
import jax.numpy as jnp
from jax import lax
from jax.sharding import PartitionSpec as P

D = 8192
QH = 64
KVH = 8
HD = 128


def attend_rows(queries, new_keys, new_values, cache_keys, cache_values, lengths):
    row_count = queries.shape[0]
    step_count = queries.shape[1]
    slot_count = cache_keys.shape[1]
    group_count = cache_keys.shape[2] // HD
    per_group = QH // KVH
    factor = 1.0 / math.sqrt(HD)
    query_heads = queries.reshape(row_count, step_count, group_count, per_group, HD)
    cached_keys = cache_keys.reshape(row_count, slot_count, group_count, HD)
    cached_values = cache_values.reshape(row_count, slot_count, group_count, HD)
    fresh_keys = new_keys.reshape(row_count, step_count, group_count, HD)
    fresh_values = new_values.reshape(row_count, step_count, group_count, HD)
    cache_scores = (
        jnp.einsum(
            "rsgqd,rpgd->rsgqp", query_heads, cached_keys, preferred_element_type=jnp.float32
        )
        * factor
    )
    live_slots = jnp.arange(slot_count, dtype=jnp.int32)[None, :] < lengths[:, None]
    cache_scores = jnp.where(live_slots[:, None, None, None, :], cache_scores, -1e30)
    fresh_scores = (
        jnp.einsum("rsgqd,rugd->rsgqu", query_heads, fresh_keys, preferred_element_type=jnp.float32)
        * factor
    )
    causal = (
        jnp.arange(step_count, dtype=jnp.int32)[None, :]
        <= jnp.arange(step_count, dtype=jnp.int32)[:, None]
    )
    fresh_scores = jnp.where(causal[None, :, None, None, :], fresh_scores, -1e30)
    highest = jnp.maximum(jnp.max(cache_scores, axis=-1), jnp.max(fresh_scores, axis=-1))
    cache_exp = jnp.exp(cache_scores - highest[..., None])
    fresh_exp = jnp.exp(fresh_scores - highest[..., None])
    denominator = jnp.sum(cache_exp, axis=-1) + jnp.sum(fresh_exp, axis=-1)
    cache_weights = (cache_exp / denominator[..., None]).astype(jnp.bfloat16)
    fresh_weights = (fresh_exp / denominator[..., None]).astype(jnp.bfloat16)
    mixed = jnp.einsum(
        "rsgqp,rpgd->rsgqd", cache_weights, cached_values, preferred_element_type=jnp.float32
    )
    mixed = mixed + jnp.einsum(
        "rsgqu,rugd->rsgqd", fresh_weights, fresh_values, preferred_element_type=jnp.float32
    )
    return mixed.astype(jnp.bfloat16).reshape(row_count, step_count, group_count * per_group * HD)


def shards(
    normed_inputs,
    value_cotangent,
    value_weight,
    decode_inputs,
    queries,
    new_keys,
    cache_keys,
    cache_values,
    lengths,
):
    step_size = 0.4 / math.sqrt(D)
    gradient = lax.psum_scatter(
        lax.dot_general(
            normed_inputs,
            value_cotangent,
            (((0,), (0,)), ((), ())),
            preferred_element_type=jnp.float32,
        ),
        ("grp", "fsdp"),
        scatter_dimension=0,
        tiled=True,
    )
    updated_shard = (value_weight.astype(jnp.float32) - step_size * gradient).astype(jnp.bfloat16)
    updated = lax.all_gather(updated_shard, ("grp", "fsdp"), axis=0, tiled=True)
    features_all = lax.all_gather(decode_inputs, "tp", axis=2, tiled=True)
    row_count = features_all.shape[0]
    step_count = features_all.shape[1]
    flat_inputs = features_all.reshape(row_count * step_count, D)
    new_values = jnp.dot(flat_inputs, updated, preferred_element_type=jnp.float32).astype(
        jnp.bfloat16
    )
    new_values = new_values.reshape(row_count, step_count, updated.shape[1])
    attended = attend_rows(queries, new_keys, new_values, cache_keys, cache_values, lengths)
    return (gradient, new_values, attended)


def solution(mesh):
    return jax.shard_map(
        shards,
        mesh=mesh,
        in_specs=(
            P(("grp", "fsdp"), None),
            P(("grp", "fsdp"), "tp"),
            P(("grp", "fsdp"), "tp"),
            P(("grp", "fsdp"), None, "tp"),
            P(("grp", "fsdp"), None, "tp"),
            P(("grp", "fsdp"), None, "tp"),
            P(("grp", "fsdp"), None, "tp"),
            P(("grp", "fsdp"), None, "tp"),
            P(("grp", "fsdp")),
        ),
        out_specs=(
            P(("grp", "fsdp"), "tp"),
            P(("grp", "fsdp"), None, "tp"),
            P(("grp", "fsdp"), None, "tp"),
        ),
        check_vma=False,
    )
```

profile of v0, /device:TPU:32, one launch (start us, length us, event | category | flops | bytes accessed | tf_op | source)
XLA Modules:
  0.0 183.2 jit_solution(9804838593200086389)
XLA Ops:
  8.0 0.0 copy-start
  8.0 0.0 reduce-scatter.2.cloned.1.call-start
  8.1 10.0 %fusion.20 = f32[8192,128]{1,0:T(8,128)} fusion(bf16[768,8192]{1,0:T(8,128)(2,1)} %param.9, bf16[768,128]{1,0:T(8,128)(2,1)} %param.10), kind=kOutput, calls=%fused_computation.31 | convolution fusion | flops 1610612736 | bytes 16973824 | tf_op jit(solution)/shard_map/dot_general | solution.py:71
  18.1 0.0 reduce-scatter.2.cloned.1.call-update
  18.1 0.0 all-gather.5.cloned.1.call-start
  18.2 0.5 all-gather.5.cloned.1.call-update
  18.7 0.0 all-gather.3.cloned.1.call-start
  18.8 100.5 %reduce-scatter.2.cloned.1.call-done = f32[256,128]{1,0:T(8,128)} async-done(((f32[8192,128]{1,0:T(8,128)}), f32[256,128]{1,0:T(8,128)}) %reduce-scatter.2.cloned.1.call-update) | async-done | bytes 131088 | tf_op jit(solution)/shard_map/reduce_scatter | solution.py:70
  119.3 1.6 subtract_convert_fusion
  120.9 0.0 all-gather.3.cloned.1.call-update
  120.9 0.1 reshape.118
  121.0 0.1 iota_compare_fusion
  121.1 0.7 fusion.19
  121.8 0.5 fusion.18
  122.3 0.1 fusion.13
  122.4 0.3 fusion.10
  122.7 0.0 all-gather.5.cloned.1.call-done
  122.8 1.3 reshape.116
  124.1 48.3 %all-gather.3.cloned.1.call-done = bf16[8192,128]{1,0:T(8,128)(2,1)} async-done(((bf16[256,128]{1,0:T(8,128)(2,1)}), bf16[8192,128]{1,0:T(8,128)(2,1)}) %all-gather.3.cloned.1.call-update) | async-done | bytes 2097168 | tf_op jit(solution)/shard_map/all_gather | solution.py:82
  172.4 2.1 %convolution_convert_fusion = bf16[128,64]{0,1:T(8,128)(2,1)S(1)} fusion(bf16[64,8192]{1,0:T(8,128)(2,1)S(1)} %reshape.116, bf16[8192,128]{1,0:T(8,128)(2,1)} %all-gather.3.cloned.1.call-done), kind=kOutput, calls=%fused_computation.10 | convolution fusion | flops 134225920 | bytes 3162112 | tf_op jit(solution)/shard_map/dot_general | solution.py:87
  174.5 0.0 copy-start.3
  174.5 0.3 fusion.14
  174.8 0.3 fusion.5
  175.1 0.7 reshape.121
  (15 shorter events, 0.1 us)
Async XLA Ops:
  8.0 113.8 %copy-start = (bf16[16,128,128]{2,1,0:T(8,128)(2,1)S(1)}, bf16[16,128,128]{2,1,0:T(8,128)(2,1)}, u32[]{:S(2)}) copy-start(bf16[16,128,128]{2,1,0:T(8,128)(2,1)} %param.15) | copy-start | bytes 1572868
  8.0 111.3 %reduce-scatter.2.cloned.1.call-start = ((), (), s32[]{:S(2)}) async-start(), calls=%async_computation.1 | async-start | bytes 4325376 | tf_op jit(solution)/shard_map/reduce_scatter | solution.py:70
  18.1 101.2 %copy-start.2 = (bf16[256,128]{1,0:T(8,128)(2,1)S(1)}, bf16[256,128]{1,0:T(8,128)(2,1)}, u32[]{:S(2)}) copy-start(bf16[256,128]{1,0:T(8,128)(2,1)} %param.11) | copy-start | bytes 196612
  18.1 102.8 %copy-start.1 = (bf16[16,4,1024]{2,1,0:T(4,128)(2,1)S(1)}, bf16[16,4,1024]{2,1,0:T(4,128)(2,1)}, u32[]{:S(2)}) copy-start(bf16[16,4,1024]{2,1,0:T(4,128)(2,1)} %param.13) | copy-start | bytes 393220
  18.1 102.9 %copy-start.4 = (s32[16]{0:T(128)S(1)}, s32[16]{0:T(128)}, u32[]{:S(2)}) copy-start(s32[16]{0:T(128)} %param.17) | copy-start | bytes 196
  18.1 103.0 %copy-start.6 = (bf16[16,4,128]{2,1,0:T(4,128)(2,1)S(1)}, bf16[16,4,128]{2,1,0:T(4,128)(2,1)}, u32[]{:S(2)}) copy-start(bf16[16,4,128]{2,1,0:T(4,128)(2,1)} %param.14) | copy-start | bytes 49156
  18.1 104.6 %all-gather.5.cloned.1.call-start = ((), (), s32[]{:S(2)}) async-start(), calls=%async_computation.3 | async-start | bytes 1179648 | tf_op jit(solution)/shard_map/all_gather | solution.py:83
  18.7 153.7 %all-gather.3.cloned.1.call-start = ((), (), s32[]{:S(2)}) async-start(), calls=%async_computation.2 | async-start | bytes 2162688 | tf_op jit(solution)/shard_map/all_gather | solution.py:82
  121.0 53.8 %copy-start.5 = (bf16[16,128,128]{2,1,0:T(8,128)(2,1)S(1)}, bf16[16,128,128]{2,1,0:T(8,128)(2,1)}, u32[]{:S(2)}) copy-start(bf16[16,128,128]{2,1,0:T(8,128)(2,1)} %param.16) | copy-start | bytes 1572868
  174.5 1.3 copy-start.3
Sparse Core Ops, SparseCore 0:
  18.3 100.9 reduce-scatter.1
Sparse Core Ops, SparseCore 1:
  20.5 43.3 all-gather.4
  121.0 51.4 all-gather.2
where the time goes:
time: 187 us; the launch traced here: 183 us
  waiting for transfers between devices  149 us (80%)
  between operations  15.6 us (8%)
  matrix products  13.9 us (7%)
  local copies, waits for them, and re-layouts  2.13 us (1%)
  other arithmetic  2.09 us (1%)
    reduce_scatter x1, waiting for transfers between devices, shards(): lax.psum_scatter(lax.dot_general(normed_inputs, value_cotangent, (((0,),...  101 us
    all_gather x1, waiting for transfers between devices, shards(): updated = lax.all_gather(updated_shard, ('grp', 'fsdp'), axis=0, tiled=True)  48.3 us
    dot_general x1, matrix products, shards(): lax.dot_general(normed_inputs, value_cotangent, (((0,), (0,)), ((), ())),...  10 us
  transfers between devices with their start and end apart: 3, of which 2 were waited for; matrix products, arithmetic and copies ran while one was open for 3% of the time, Pallas kernels for 0%

commit v1 on v0

v1 whole, which is shorter than its diff:
```python
import math

import jax
import jax.numpy as jnp
import numpy as np
from jax import lax
from jax.experimental import pallas as pl
from jax.experimental.pallas import tpu as pltpu
from jax.sharding import Mesh, PartitionSpec as P

D = 8192
QH = 64
KVH = 8
HD = 128
SIZES = {"c": 2, "zh": 4, "x": 4, "zl": 2, "y": 4}
NAMES = tuple(SIZES)
STEP = 0.4 / math.sqrt(D)
MIB = 1 << 20


def shift(value, axis, by):
    n = SIZES[axis]
    return lax.ppermute(value, axis, [(i, (i + by) % n) for i in range(n)])


def swap_axes(value):
    names = ("c", "zh", "zl", "y")
    sizes = [SIZES[n] for n in names]
    pairs = []
    for c, zh, zl, y in np.ndindex(*sizes):
        source = int(np.ravel_multi_index((c, zh, zl, y), sizes))
        target = int(np.ravel_multi_index((zl, y, c, zh), sizes))
        pairs.append((source, target))
    return lax.ppermute(value, names, pairs)


def partial_kernel(place, x_ref, v_ref, out_ref):
    product = lax.dot_general(
        v_ref[...], x_ref[...], (((0,), (0,)), ((), ())), preferred_element_type=jnp.float32
    )
    for block in range(4):
        rows = product[:, block * 256 : (block + 1) * 256].T
        out_ref[lax.rem(block + 4 - place[2], 4), 0] = rows.astype(out_ref.dtype)


def partial_gradient(place, normed_inputs, value_cotangent):
    tokens = normed_inputs.shape[0]
    return pl.pallas_call(
        partial_kernel,
        grid_spec=pltpu.PrefetchScalarGridSpec(
            num_scalar_prefetch=1,
            grid=(4,),
            in_specs=[
                pl.BlockSpec(
                    (tokens, 1024), lambda e, place: (0, place[0] * 4 + lax.rem(place[1] + e, 4))
                ),
                pl.BlockSpec((tokens, HD), lambda e, place: (0, 0)),
            ],
            out_specs=pl.BlockSpec((4, 1, 256, HD), lambda e, place: (0, e, 0, 0)),
        ),
        out_shape=jax.ShapeDtypeStruct((4, 4, 256, HD), jnp.bfloat16),
        compiler_params=pltpu.CompilerParams(vmem_limit_bytes=56 * MIB),
        cost_estimate=pl.CostEstimate(
            flops=2 * tokens * 4096 * HD, bytes_accessed=tokens * 4096 * 2, transcendentals=0
        ),
    )(place, normed_inputs, value_cotangent)


def project_kernel(place, d0, d1, d2, d3, u0, u1, u2, u3, out_ref, rows):
    core, x, low, y = place[0], place[1], place[2], place[3]
    for d, u in enumerate((u0, u1, u2, u3)):
        rows[pl.ds(pl.multiple_of(lax.rem(x + d, 4) * 256, 256), 256), :] = u[...]
    for d, piece in enumerate((d0, d1, d2, d3)):
        for j in range(2):
            product = jnp.dot(piece[j], rows[...], preferred_element_type=jnp.float32)
            other = lax.rem(low + j + core, 2)
            out_ref[other, lax.rem(y + d, 4)] = product.astype(out_ref.dtype)


def project(place, pieces, updated):
    whole = pl.BlockSpec(memory_space=pltpu.VMEM)
    return pl.pallas_call(
        project_kernel,
        in_specs=[pl.BlockSpec(memory_space=pltpu.SMEM)] + [whole] * 8,
        out_specs=whole,
        out_shape=jax.ShapeDtypeStruct((2, 4, 64, HD), jnp.bfloat16),
        scratch_shapes=[pltpu.VMEM((1024, HD), jnp.bfloat16)],
        compiler_params=pltpu.CompilerParams(vmem_limit_bytes=16 * MIB),
        cost_estimate=pl.CostEstimate(
            flops=2 * 512 * 1024 * HD, bytes_accessed=3 * MIB // 2, transcendentals=0
        ),
    )(place, *pieces, *updated)


def attend_cache(queries, new_keys, cache_keys, cache_values, lengths):
    row_count, step_count = queries.shape[0], queries.shape[1]
    slot_count = cache_keys.shape[1]
    factor = 1.0 / math.sqrt(HD)
    heads = queries.reshape(row_count, step_count, QH // KVH, HD)
    cache_scores = (
        jnp.einsum("rsqd,rpd->rsqp", heads, cache_keys, preferred_element_type=jnp.float32) * factor
    )
    live = jnp.arange(slot_count, dtype=jnp.int32)[None, :] < lengths[:, None]
    cache_scores = jnp.where(live[:, None, None, :], cache_scores, -1e30)
    fresh_scores = (
        jnp.einsum("rsqd,rud->rsqu", heads, new_keys, preferred_element_type=jnp.float32) * factor
    )
    steps = jnp.arange(step_count, dtype=jnp.int32)
    causal = steps[None, :] <= steps[:, None]
    fresh_scores = jnp.where(causal[None, :, None, :], fresh_scores, -1e30)
    highest = jnp.maximum(jnp.max(cache_scores, axis=-1), jnp.max(fresh_scores, axis=-1))
    cache_exp = jnp.exp(cache_scores - highest[..., None])
    fresh_exp = jnp.exp(fresh_scores - highest[..., None])
    denominator = jnp.sum(cache_exp, axis=-1) + jnp.sum(fresh_exp, axis=-1)
    cache_weights = (cache_exp / denominator[..., None]).astype(jnp.bfloat16)
    fresh_weights = (fresh_exp / denominator[..., None]).astype(jnp.bfloat16)
    mixed = jnp.einsum(
        "rsqp,rpd->rsqd", cache_weights, cache_values, preferred_element_type=jnp.float32
    )
    return mixed, fresh_weights


def shards(
    normed_inputs,
    value_cotangent,
    value_weight,
    decode_inputs,
    queries,
    new_keys,
    cache_keys,
    cache_values,
    lengths,
):
    core, high, x, low, y = (lax.axis_index(n) for n in NAMES)
    row_count, step_count = decode_inputs.shape[0], decode_inputs.shape[1]
    f32 = jnp.float32

    swapped = swap_axes(decode_inputs.reshape(row_count * step_count, -1))

    theirs = partial_gradient(jnp.stack([1 - core, high, x]), normed_inputs, value_cotangent)
    received = shift(theirs, "c", 1)
    mine = partial_gradient(jnp.stack([core, high, x]), normed_inputs, value_cotangent)

    both = jnp.stack([swapped, shift(swapped, "zl", 1)])

    sums = [mine[d].astype(f32) + received[d].astype(f32) for d in range(4)]
    along_x = sums[0]
    for d in (2, 1, 3):
        along_x += shift(sums[d].astype(jnp.bfloat16), "x", d).astype(f32)

    pieces = [both] + [shift(both, "y", -d) for d in (1, 2, 3)]

    gradient = along_x[0]
    for e in (2, 1, 3):
        gradient += shift(along_x[e].astype(jnp.bfloat16), "zh", e).astype(f32)
    updated = (value_weight.astype(f32) - STEP * gradient).astype(jnp.bfloat16)

    gathered = [updated] + [shift(updated, "x", -d) for d in (1, 2, 3)]
    partial = project(jnp.stack([core, x, low, y]), pieces, gathered)
    pair = partial[0].astype(f32) + shift(partial[1], "c", 1).astype(f32)
    exchanged = lax.all_to_all(pair.astype(jnp.bfloat16), "zh", 0, 0, tiled=True)
    new_values = jnp.sum(exchanged.astype(f32), axis=0).astype(jnp.bfloat16)
    new_values = new_values.reshape(row_count, step_count, HD)

    mixed, fresh_weights = attend_cache(queries, new_keys, cache_keys, cache_values, lengths)
    mixed = mixed + jnp.einsum(
        "rsqu,rud->rsqd", fresh_weights, new_values, preferred_element_type=f32
    )
    attended = mixed.astype(jnp.bfloat16).reshape(row_count, step_count, -1)
    return (gradient, new_values, attended)


def solution(mesh):
    inner = Mesh(mesh.devices.reshape(tuple(SIZES.values())), NAMES)
    rows, columns = ("c", "zh", "x"), ("zl", "y")
    return jax.shard_map(
        shards,
        mesh=inner,
        in_specs=(
            P(rows, None),
            P(rows, columns),
            P(rows, columns),
            P(rows, None, columns),
            P(rows, None, columns),
            P(rows, None, columns),
            P(rows, None, columns),
            P(rows, None, columns),
            P(rows),
        ),
        out_specs=(
            P(rows, columns),
            P(rows, None, columns),
            P(rows, None, columns),
        ),
        check_vma=False,
    )
```

time: 187 us -> 85.4 us (0.46)
  the two profiles are of different devices: /device:TPU:32 before, /device:TPU:8 now
where the time goes in v1:
time: 85.4 us; the launch traced here: 84.9 us
  starting transfers between devices  39.3 us (46%)
  waiting for transfers between devices  22.5 us (26%)
  Pallas kernels  13 us (15%)
  other arithmetic  5.63 us (7%)
  matrix products  2.8 us (3%)
    ppermute x15, starting transfers between devices, shift(): return lax.ppermute(value, axis, [(i, (i + by) % n) for i in range(n)])  28.7 us
    pallas_call x2, Pallas kernels, partial_gradient(): pl.pallas_call(partial_kernel, grid_spec=pltpu.PrefetchScalarGridSpec(num...  12 us
    ppermute x15, waiting for transfers between devices, shift(): return lax.ppermute(value, axis, [(i, (i + by) % n) for i in range(n)])  10.6 us
    all_to_all x1, waiting for transfers between devices, shards(): lax.all_to_all(pair.astype(jnp.bfloat16), 'zh', 0, 0, tiled=True)  8.05 us
    all_to_all x1, starting transfers between devices, shards(): lax.all_to_all(pair.astype(jnp.bfloat16), 'zh', 0, 0, tiled=True)  5.55 us
    ppermute x1, starting transfers between devices, swap_axes(): return lax.ppermute(value, names, pairs)  5.06 us
    ppermute x1, waiting for transfers between devices, swap_axes(): return lax.ppermute(value, names, pairs)  3.87 us
  transfers between devices with their start and end apart: 17, of which 11 were waited for; matrix products, arithmetic and copies ran while one was open for 7% of the time, Pallas kernels for 7%

profile of v1, /device:TPU:8, one launch (start us, length us, event | category | flops | bytes accessed | tf_op | source)
XLA Modules:
  0.0 84.9 jit_solution(11237644918165661441)
XLA Ops:
  1.3 6.0 %shard_map.113 = bf16[4,4,256,128]{3,2,1,0:T(8,128)(2,1)} custom-call(s32[3]{0:T(128)} %add_add_fusion.1.place, bf16[768,8192]{1,0:T(8,128)(2,1)} %x_ref.3, bf16[768,128]{1,0:T(8,128)(2,1)} %v_ref.3), custom_call_target="tpu_custom_call" | custom-call | flops 805306368 | bytes 6291456 | tf_op jit(solution)/shard_map/pallas_call | solution.py:48
  7.3 5.1 %collective-permute-start.7 = (bf16[64,1024]{1,0:T(8,128)(2,1)S(1)}, bf16[64,1024]{1,0:T(8,128)(2,1)S(1)}, u32[]{:S(2)}, u32[]{:S(2)}) collective-permute-start(bf16[64,1024]{1,0:T(8,128)(2,1)S(1)} %reshape.77), channel_id=1, source_target_pairs={{0,0},{1,32},{2,64},{3,96},{4,128},{5,160},{6,192},{7,224},{32,1},... | collective-permute-start | bytes 393224 | tf_op jit(solution)/shard_map/ppermute | solution.py:34
  13.2 6.0 %shard_map.112 = bf16[4,4,256,128]{3,2,1,0:T(8,128)(2,1)} custom-call(s32[3]{0:T(128)} %add_add_fusion.place, bf16[768,8192]{1,0:T(8,128)(2,1)} %x_ref.3, bf16[768,128]{1,0:T(8,128)(2,1)} %v_ref.3), custom_call_target="tpu_custom_call" | custom-call | flops 805306368 | bytes 6291456 | tf_op jit(solution)/shard_map/pallas_call | solution.py:48
  19.1 3.9 %collective-permute-done.7 = bf16[64,1024]{1,0:T(8,128)(2,1)S(1)} collective-permute-done((bf16[64,1024]{1,0:T(8,128)(2,1)S(1)}, bf16[64,1024]{1,0:T(8,128)(2,1)S(1)}, u32[]{:S(2)}, u32[]{:S(2)}) %collective-permute-start.7) | collective-permute-done | bytes 131104 | tf_op jit(solution)/shard_map/ppermute | solution.py:34
  23.3 1.3 %fusion.7 = (bf16[4,256,128]{2,1,0:T(8,128)(2,1)S(1)}, bf16[4,256,128]{2,1,0:T(8,128)(2,1)S(1)}, bf16[4,256,128]{2,1,0:T(8,128)(2,1)S(1)}) fusion(bf16[4,4,256,128]{3,2,1,0:T(8,128)(2,1)S(1)} %collective-permute-done, bf16[4,4,256,128]{3,2,1,0:T(8,128)(2,1)} %shard_map.112), kind=kLoop, calls=%fused_computation.14 | loop fusion | flops 1572864 | bytes 2359296 | tf_op jit(solution)/shard_map/convert_element_type | solution.py:149
  24.7 3.1 %collective-permute-start.1 = (bf16[4,256,128]{2,1,0:T(8,128)(2,1)S(1)}, bf16[4,256,128]{2,1,0:T(8,128)(2,1)S(1)}, u32[]{:S(2)}, u32[]{:S(2)}) collective-permute-start(bf16[4,256,128]{2,1,0:T(8,128)(2,1)S(1)} %get-tuple-element.7), channel_id=1, source_target_pairs={{0,16},{8,24},{16,0},{24,8},{1,17},{9,25},{17,1},{25,9},{2,18},{10... | collective-permute-start | bytes 786440 | tf_op jit(solution)/shard_map/ppermute | solution.py:23
  28.4 2.7 %collective-permute-start.3 = (bf16[4,256,128]{2,1,0:T(8,128)(2,1)S(1)}, bf16[4,256,128]{2,1,0:T(8,128)(2,1)S(1)}, u32[]{:S(2)}, u32[]{:S(2)}) collective-permute-start(bf16[4,256,128]{2,1,0:T(8,128)(2,1)S(1)} %get-tuple-element.8), channel_id=1, source_target_pairs={{0,24},{8,0},{16,8},{24,16},{1,25},{9,1},{17,9},{25,17},{2,26},{10... | collective-permute-start | bytes 786440 | tf_op jit(solution)/shard_map/ppermute | solution.py:23
  31.6 3.6 %collective-permute-start.10 = (bf16[2,64,1024]{2,1,0:T(8,128)(2,1)S(1)}, bf16[2,64,1024]{2,1,0:T(8,128)(2,1)S(1)}, u32[]{:S(2)}, u32[]{:S(2)}) collective-permute-start(bf16[2,64,1024]{2,1,0:T(8,128)(2,1)S(1)} %pad_maximum_fusion.d0), channel_id=1, source_target_pairs={{0,2},{1,3},{2,0},{3,1},{4,6},{5,7},{6,4},{7,5},{8,10},{9,11},{10,... | collective-permute-start | bytes 786440 | tf_op jit(solution)/shard_map/ppermute | solution.py:23
  35.5 3.6 %collective-permute-done.2 = bf16[4,256,128]{2,1,0:T(8,128)(2,1)S(1)} collective-permute-done((bf16[4,256,128]{2,1,0:T(8,128)(2,1)S(1)}, bf16[4,256,128]{2,1,0:T(8,128)(2,1)S(1)}, u32[]{:S(2)}, u32[]{:S(2)}) %collective-permute-start.2) | collective-permute-done | bytes 262176 | tf_op jit(solution)/shard_map/ppermute | solution.py:23
  39.2 1.1 %fusion.23 = (bf16[4,256,128]{2,1,0:T(8,128)(2,1)S(1)}, f32[4,256,128]{2,1,0:T(8,128)S(1)}) fusion(bf16[4,256,128]{2,1,0:T(8,128)(2,1)S(1)} %collective-permute-done.3, bf16[4,256,128]{2,1,0:T(8,128)(2,1)S(1)} %collective-permute-done.2, bf16[4,256,128]{2,1,0:T(8,128)(2,1)S(1)} %collective-permute-done.1, ...), kind=kLoop, calls=%fused_computation.47 | loop fusion | flops 1310720 | bytes 2097152 | tf_op jit(solution)/shard_map/convert.4
  40.4 8.5 %collective-permute-start.4 = (bf16[256,128]{1,0:T(8,128)(2,1)S(1)}, bf16[256,128]{1,0:T(8,128)(2,1)S(1)}, u32[]{:S(2)}, u32[]{:S(2)}) collective-permute-start(bf16[256,128]{1,0:T(8,128)(2,1)S(1)} %get-tuple-element.10), channel_id=1, source_target_pairs={{0,64},{32,96},{64,0},{96,32},{1,65},{33,97},{65,1},{97,33},{2,66}... | collective-permute-start | bytes 196616 | tf_op jit(solution)/shard_map/ppermute | solution.py:23
  48.9 4.1 %collective-permute-start.6 = (bf16[256,128]{1,0:T(8,128)(2,1)S(1)}, bf16[256,128]{1,0:T(8,128)(2,1)S(1)}, u32[]{:S(2)}, u32[]{:S(2)}) collective-permute-start(bf16[256,128]{1,0:T(8,128)(2,1)S(1)} %get-tuple-element.11), channel_id=1, source_target_pairs={{0,96},{32,0},{64,32},{96,64},{1,97},{33,1},{65,33},{97,65},{2,98}... | collective-permute-start | bytes 196616 | tf_op jit(solution)/shard_map/ppermute | solution.py:23
  53.0 0.7 fusion.26
  53.8 2.0 %collective-permute-start.9 = (bf16[2,64,1024]{2,1,0:T(8,128)(2,1)S(1)}, bf16[2,64,1024]{2,1,0:T(8,128)(2,1)S(1)}, u32[]{:S(2)}, u32[]{:S(2)}) collective-permute-start(bf16[2,64,1024]{2,1,0:T(8,128)(2,1)S(1)} %pad_maximum_fusion.d0), channel_id=1, source_target_pairs={{0,3},{1,0},{2,1},{3,2},{4,7},{5,4},{6,5},{7,6},{8,11},{9,8},{10,9... | collective-permute-start | bytes 786440 | tf_op jit(solution)/shard_map/ppermute | solution.py:23
  55.9 0.7 subtract_convert_fusion
  56.6 2.8 %collective-permute-start.12 = (bf16[256,128]{1,0:T(8,128)(2,1)S(1)}, bf16[256,128]{1,0:T(8,128)(2,1)S(1)}, u32[]{:S(2)}, u32[]{:S(2)}) collective-permute-start(bf16[256,128]{1,0:T(8,128)(2,1)S(1)} %get-tuple-element.3.u0), channel_id=1, source_target_pairs={{0,24},{8,0},{16,8},{24,16},{1,25},{9,1},{17,9},{25,17},{2,26},{10... | collective-permute-start | bytes 196616 | tf_op jit(solution)/shard_map/ppermute | solution.py:23
  59.4 0.7 collective-permute-start.13
  60.3 1.2 %collective-permute-done.11.d3 = bf16[2,64,1024]{2,1,0:T(8,128)(2,1)S(1)} collective-permute-done((bf16[2,64,1024]{2,1,0:T(8,128)(2,1)S(1)}, bf16[2,64,1024]{2,1,0:T(8,128)(2,1)S(1)}, u32[]{:S(2)}, u32[]{:S(2)}) %collective-permute-start.11) | collective-permute-done | bytes 262176 | tf_op jit(solution)/shard_map/ppermute | solution.py:23
  61.9 3.3 %collective-permute-done.13.u2 = bf16[256,128]{1,0:T(8,128)(2,1)S(1)} collective-permute-done((bf16[256,128]{1,0:T(8,128)(2,1)S(1)}, bf16[256,128]{1,0:T(8,128)(2,1)S(1)}, u32[]{:S(2)}, u32[]{:S(2)}) %collective-permute-start.13) | collective-permute-done | bytes 65568 | tf_op jit(solution)/shard_map/ppermute | solution.py:23
  65.8 1.0 %shard_map.114 = bf16[2,4,64,128]{3,2,1,0:T(8,128)(2,1)S(1)} custom-call(s32[4]{0:T(128)S(1)} %pad_add_fusion.place, bf16[2,64,1024]{2,1,0:T(8,128)(2,1)S(1)} %pad_maximum_fusion.d0, bf16[2,64,1024]{2,1,0:T(8,128)(2,1)S(1)} %collective-permute-done.9.d1, bf16[2,64,1024]{2,1,0:T(8,128)(2,1)S(1)} %collective-permute-done.10.d2, ...), custom_call_target="tpu_custom_call" | custom-call | flops 134217728 | bytes 1572864 | tf_op jit(solution)/shard_map/pallas_call | solution.py:82
  67.2 0.9 %collective-permute-done.15 = bf16[4,64,128]{2,1,0:T(8,128)(2,1)S(1)} collective-permute-done((bf16[4,64,128]{2,1,0:T(8,128)(2,1)S(1)}, bf16[4,64,128]{2,1,0:T(8,128)(2,1)S(1)}, u32[]{:S(2)}, u32[]{:S(2)}) %collective-permute-start.15) | collective-permute-done | bytes 65568 | tf_op jit(solution)/shard_map/ppermute | solution.py:23
  68.8 5.5 %all-to-all-start = ((bf16[4,64,128]{2,1,0:T(8,128)(2,1)}), bf16[4,64,128]{2,1,0:T(8,128)(2,1)S(1)}, u32[]{:S(2)}, u32[]{:S(2)}) async-start(bf16[4,64,128]{2,1,0:T(8,128)(2,1)} %fusion.14), calls=%async_computation | async-start | bytes 131072 | tf_op jit(solution)/shard_map/all_to_all | solution.py:161
  74.5 8.1 %all-to-all-done = bf16[4,64,128]{2,1,0:T(8,128)(2,1)S(1)} async-done(((bf16[4,64,128]{2,1,0:T(8,128)(2,1)}), bf16[4,64,128]{2,1,0:T(8,128)(2,1)S(1)}, u32[]{:S(2)}, u32[]{:S(2)}) %all-to-all-start) | async-done | bytes 65568 | tf_op jit(solution)/shard_map/all_to_all | solution.py:161
  82.9 1.4 %fusion.1 = bf16[16,4,8,128]{3,2,1,0:T(8,128)(2,1)S(1)} fusion(f32[16,4,8,128]{3,2,1,0:T(8,128)S(1)} %fusion.18, bf16[16,128,128]{2,1,0:T(8,128)(2,1)} %param.16, f32[16,4,8,128]{3,2,1,0:T(8,128)S(1)} %get-tuple-element.14, f32[16,4,8]{2,1,0:T(4,128)S(1)} %add.61, f32[16,4,8]{2,1,0:T(4,128)S(1)} %max.7), kind=kOutput, calls=%fused_computation.3 | convolution fusion | flops 17104896 | bytes 1183744 | tf_op jit(solution)/shard_map/rsqp,rpd->rsqd/dot_general | solution.py:117
  (51 shorter events, 6.8 us)
Async XLA Ops:
  0.6 30.4 %copy-start = (bf16[16,128,128]{2,1,0:T(8,128)(2,1)S(1)}, bf16[16,128,128]{2,1,0:T(8,128)(2,1)}, u32[]{:S(2)}) copy-start(bf16[16,128,128]{2,1,0:T(8,128)(2,1)} %param.15) | copy-start | bytes 1572868
  0.6 6.7 %copy-start.1 = (bf16[16,4,1024]{2,1,0:T(4,128)(2,1)S(1)}, bf16[16,4,1024]{2,1,0:T(4,128)(2,1)}, u32[]{:S(2)}) copy-start(bf16[16,4,1024]{2,1,0:T(4,128)(2,1)} %param.12) | copy-start | bytes 393220
  0.7 11.8 %copy-start.5 = (s32[16]{0:T(128)S(1)}, s32[16]{0:T(128)}, u32[]{:S(2)}) copy-start(s32[16]{0:T(128)} %param.17) | copy-start | bytes 196
  0.7 12.4 %copy-start.2 = (bf16[16,4,1024]{2,1,0:T(4,128)(2,1)S(1)}, bf16[16,4,1024]{2,1,0:T(4,128)(2,1)}, u32[]{:S(2)}) copy-start(bf16[16,4,1024]{2,1,0:T(4,128)(2,1)} %param.13) | copy-start | bytes 393220
  7.3 45.7 %copy-start.6 = (bf16[16,4,128]{2,1,0:T(4,128)(2,1)S(1)}, bf16[16,4,128]{2,1,0:T(4,128)(2,1)}, u32[]{:S(2)}) copy-start(bf16[16,4,128]{2,1,0:T(4,128)(2,1)} %param.14) | copy-start | bytes 49156
  7.3 48.6 %copy-start.3 = (bf16[256,128]{1,0:T(8,128)(2,1)S(1)}, bf16[256,128]{1,0:T(8,128)(2,1)}, u32[]{:S(2)}) copy-start(bf16[256,128]{1,0:T(8,128)(2,1)} %param.11) | copy-start | bytes 196612
  7.3 16.1 %collective-permute-start = (bf16[4,4,256,128]{3,2,1,0:T(8,128)(2,1)}, bf16[4,4,256,128]{3,2,1,0:T(8,128)(2,1)S(1)}, u32[]{:S(2)}, u32[]{:S(2)}) collective-permute-start(bf16[4,4,256,128]{3,2,1,0:T(8,128)(2,1)} %shard_map.113), channel_id=1, source_target_pairs={{0,128},{128,0},{1,129},{129,1},{2,130},{130,2},{3,131},{131,3},{4... | collective-permute-start | bytes 3145736 | tf_op jit(solution)/shard_map/ppermute | solution.py:23
  7.3 15.7 %collective-permute-start.7 = (bf16[64,1024]{1,0:T(8,128)(2,1)S(1)}, bf16[64,1024]{1,0:T(8,128)(2,1)S(1)}, u32[]{:S(2)}, u32[]{:S(2)}) collective-permute-start(bf16[64,1024]{1,0:T(8,128)(2,1)S(1)} %reshape.77), channel_id=1, source_target_pairs={{0,0},{1,32},{2,64},{3,96},{4,128},{5,160},{6,192},{7,224},{32,1},... | collective-permute-start | bytes 393224 | tf_op jit(solution)/shard_map/ppermute | solution.py:34
  23.0 8.5 %collective-permute-start.8 = (bf16[64,1024]{1,0:T(8,128)(2,1)S(1)}, bf16[64,1024]{1,0:T(8,128)(2,1)S(1)}, u32[]{:S(2)}, u32[]{:S(2)}) collective-permute-start(bf16[64,1024]{1,0:T(8,128)(2,1)S(1)} %collective-permute-done.7), channel_id=1, source_target_pairs={{0,4},{4,0},{1,5},{5,1},{2,6},{6,2},{3,7},{7,3},{8,12},{12,8},{9,1... | collective-permute-start | bytes 393224 | tf_op jit(solution)/shard_map/ppermute | solution.py:23
  24.7 10.8 %collective-permute-start.1 = (bf16[4,256,128]{2,1,0:T(8,128)(2,1)S(1)}, bf16[4,256,128]{2,1,0:T(8,128)(2,1)S(1)}, u32[]{:S(2)}, u32[]{:S(2)}) collective-permute-start(bf16[4,256,128]{2,1,0:T(8,128)(2,1)S(1)} %get-tuple-element.7), channel_id=1, source_target_pairs={{0,16},{8,24},{16,0},{24,8},{1,17},{9,25},{17,1},{25,9},{2,18},{10... | collective-permute-start | bytes 786440 | tf_op jit(solution)/shard_map/ppermute | solution.py:23
  27.8 11.4 %collective-permute-start.2 = (bf16[4,256,128]{2,1,0:T(8,128)(2,1)S(1)}, bf16[4,256,128]{2,1,0:T(8,128)(2,1)S(1)}, u32[]{:S(2)}, u32[]{:S(2)}) collective-permute-start(bf16[4,256,128]{2,1,0:T(8,128)(2,1)S(1)} %get-tuple-element.9), channel_id=1, source_target_pairs={{0,8},{8,16},{16,24},{24,0},{1,9},{9,17},{17,25},{25,1},{2,10},{10... | collective-permute-start | bytes 786440 | tf_op jit(solution)/shard_map/ppermute | solution.py:23
  28.4 10.9 %collective-permute-start.3 = (bf16[4,256,128]{2,1,0:T(8,128)(2,1)S(1)}, bf16[4,256,128]{2,1,0:T(8,128)(2,1)S(1)}, u32[]{:S(2)}, u32[]{:S(2)}) collective-permute-start(bf16[4,256,128]{2,1,0:T(8,128)(2,1)S(1)} %get-tuple-element.8), channel_id=1, source_target_pairs={{0,24},{8,0},{16,8},{24,16},{1,25},{9,1},{17,9},{25,17},{2,26},{10... | collective-permute-start | bytes 786440 | tf_op jit(solution)/shard_map/ppermute | solution.py:23
  31.6 28.5 %collective-permute-start.10 = (bf16[2,64,1024]{2,1,0:T(8,128)(2,1)S(1)}, bf16[2,64,1024]{2,1,0:T(8,128)(2,1)S(1)}, u32[]{:S(2)}, u32[]{:S(2)}) collective-permute-start(bf16[2,64,1024]{2,1,0:T(8,128)(2,1)S(1)} %pad_maximum_fusion.d0), channel_id=1, source_target_pairs={{0,2},{1,3},{2,0},{3,1},{4,6},{5,7},{6,4},{7,5},{8,10},{9,11},{10,... | collective-permute-start | bytes 786440 | tf_op jit(solution)/shard_map/ppermute | solution.py:23
  40.4 13.5 %collective-permute-start.4 = (bf16[256,128]{1,0:T(8,128)(2,1)S(1)}, bf16[256,128]{1,0:T(8,128)(2,1)S(1)}, u32[]{:S(2)}, u32[]{:S(2)}) collective-permute-start(bf16[256,128]{1,0:T(8,128)(2,1)S(1)} %get-tuple-element.10), channel_id=1, source_target_pairs={{0,64},{32,96},{64,0},{96,32},{1,65},{33,97},{65,1},{97,33},{2,66}... | collective-permute-start | bytes 196616 | tf_op jit(solution)/shard_map/ppermute | solution.py:23
  48.9 7.0 %collective-permute-start.5 = (bf16[256,128]{1,0:T(8,128)(2,1)S(1)}, bf16[256,128]{1,0:T(8,128)(2,1)S(1)}, u32[]{:S(2)}, u32[]{:S(2)}) collective-permute-start(bf16[256,128]{1,0:T(8,128)(2,1)S(1)} %get-tuple-element.12), channel_id=1, source_target_pairs={{0,32},{32,64},{64,96},{96,0},{1,33},{33,65},{65,97},{97,1},{2,34}... | collective-permute-start | bytes 196616 | tf_op jit(solution)/shard_map/ppermute | solution.py:23
  48.9 7.0 %collective-permute-start.6 = (bf16[256,128]{1,0:T(8,128)(2,1)S(1)}, bf16[256,128]{1,0:T(8,128)(2,1)S(1)}, u32[]{:S(2)}, u32[]{:S(2)}) collective-permute-start(bf16[256,128]{1,0:T(8,128)(2,1)S(1)} %get-tuple-element.11), channel_id=1, source_target_pairs={{0,96},{32,0},{64,32},{96,64},{1,97},{33,1},{65,33},{97,65},{2,98}... | collective-permute-start | bytes 196616 | tf_op jit(solution)/shard_map/ppermute | solution.py:23
  53.7 7.7 %collective-permute-start.11 = (bf16[2,64,1024]{2,1,0:T(8,128)(2,1)S(1)}, bf16[2,64,1024]{2,1,0:T(8,128)(2,1)S(1)}, u32[]{:S(2)}, u32[]{:S(2)}) collective-permute-start(bf16[2,64,1024]{2,1,0:T(8,128)(2,1)S(1)} %pad_maximum_fusion.d0), channel_id=1, source_target_pairs={{0,1},{1,2},{2,3},{3,0},{4,5},{5,6},{6,7},{7,4},{8,9},{9,10},{10,1... | collective-permute-start | bytes 786440 | tf_op jit(solution)/shard_map/ppermute | solution.py:23
  53.8 7.7 %collective-permute-start.9 = (bf16[2,64,1024]{2,1,0:T(8,128)(2,1)S(1)}, bf16[2,64,1024]{2,1,0:T(8,128)(2,1)S(1)}, u32[]{:S(2)}, u32[]{:S(2)}) collective-permute-start(bf16[2,64,1024]{2,1,0:T(8,128)(2,1)S(1)} %pad_maximum_fusion.d0), channel_id=1, source_target_pairs={{0,3},{1,0},{2,1},{3,2},{4,7},{5,4},{6,5},{7,6},{8,11},{9,8},{10,9... | collective-permute-start | bytes 786440 | tf_op jit(solution)/shard_map/ppermute | solution.py:23
  56.6 5.3 %collective-permute-start.12 = (bf16[256,128]{1,0:T(8,128)(2,1)S(1)}, bf16[256,128]{1,0:T(8,128)(2,1)S(1)}, u32[]{:S(2)}, u32[]{:S(2)}) collective-permute-start(bf16[256,128]{1,0:T(8,128)(2,1)S(1)} %get-tuple-element.3.u0), channel_id=1, source_target_pairs={{0,24},{8,0},{16,8},{24,16},{1,25},{9,1},{17,9},{25,17},{2,26},{10... | collective-permute-start | bytes 196616 | tf_op jit(solution)/shard_map/ppermute | solution.py:23
  59.4 5.8 %collective-permute-start.13 = (bf16[256,128]{1,0:T(8,128)(2,1)S(1)}, bf16[256,128]{1,0:T(8,128)(2,1)S(1)}, u32[]{:S(2)}, u32[]{:S(2)}) collective-permute-start(bf16[256,128]{1,0:T(8,128)(2,1)S(1)} %get-tuple-element.3.u0), channel_id=1, source_target_pairs={{0,16},{8,24},{16,0},{24,8},{1,17},{9,25},{17,1},{25,9},{2,18},{10... | collective-permute-start | bytes 196616 | tf_op jit(solution)/shard_map/ppermute | solution.py:23
  60.1 5.7 %collective-permute-start.14 = (bf16[256,128]{1,0:T(8,128)(2,1)S(1)}, bf16[256,128]{1,0:T(8,128)(2,1)S(1)}, u32[]{:S(2)}, u32[]{:S(2)}) collective-permute-start(bf16[256,128]{1,0:T(8,128)(2,1)S(1)} %get-tuple-element.3.u0), channel_id=1, source_target_pairs={{0,8},{8,16},{16,24},{24,0},{1,9},{9,17},{17,25},{25,1},{2,10},{10... | collective-permute-start | bytes 196616 | tf_op jit(solution)/shard_map/ppermute | solution.py:23
  66.8 1.3 %collective-permute-start.15 = (bf16[4,64,128]{2,1,0:T(8,128)(2,1)S(1)}, bf16[4,64,128]{2,1,0:T(8,128)(2,1)S(1)}, u32[]{:S(2)}, u32[]{:S(2)}) collective-permute-start(bf16[4,64,128]{2,1,0:T(8,128)(2,1)S(1)} %slice_bitcast_fusion.1), channel_id=1, source_target_pairs={{0,128},{128,0},{1,129},{129,1},{2,130},{130,2},{3,131},{131,3},{4... | collective-permute-start | bytes 196616 | tf_op jit(solution)/shard_map/ppermute | solution.py:23
  68.8 13.8 %all-to-all-start = ((bf16[4,64,128]{2,1,0:T(8,128)(2,1)}), bf16[4,64,128]{2,1,0:T(8,128)(2,1)S(1)}, u32[]{:S(2)}, u32[]{:S(2)}) async-start(bf16[4,64,128]{2,1,0:T(8,128)(2,1)} %fusion.14), calls=%async_computation | async-start | bytes 131072 | tf_op jit(solution)/shard_map/all_to_all | solution.py:161
  82.6 2.3 %copy-start.4 = (bf16[64,128]{1,0:T(8,128)(2,1)}, bf16[64,128]{1,0:T(8,128)(2,1)S(1)}, u32[]{:S(2)}) copy-start(bf16[64,128]{1,0:T(8,128)(2,1)S(1)} %reduce_sum.30) | copy-start | bytes 49156

commit v2 on v1

v2 whole, which is shorter than its diff:
```python
import math

import jax
import jax.numpy as jnp
import numpy as np
from jax import lax
from jax.experimental import pallas as pl
from jax.experimental.pallas import tpu as pltpu
from jax.sharding import Mesh, PartitionSpec as P

D = 8192
HEADS = 8
HD = 128
SIZES = {"c": 2, "zh": 4, "x": 4, "zl": 2, "y": 4}
NAMES = tuple(SIZES)
STEP = 0.4 / math.sqrt(D)
MIB = 1 << 20
F32 = jnp.float32
BF16 = jnp.bfloat16
VMEM = pl.BlockSpec(memory_space=pltpu.VMEM)
SMEM = pl.BlockSpec(memory_space=pltpu.SMEM)
HBM = pl.BlockSpec(memory_space=pltpu.HBM)


def shift(value, axis, by):
    n = SIZES[axis]
    return lax.ppermute(value, axis, [(i, (i + by) % n) for i in range(n)])


def swap_high(value):
    pairs = [(zh * 4 + y, y * 4 + zh) for zh in range(4) for y in range(4)]
    return lax.ppermute(value, ("zh", "y"), pairs)


def after(value, *others):
    return lax.optimization_barrier((value, *others))[0]


def partial_kernel(own, place, x_hbm, v_ref, out_ref, chunks, sems):
    half = place[0] if own else 1 - place[0]
    copies = []
    for e in range(4):
        column = (half * 4 + lax.rem(place[1] + e, 4)) * 1024
        copy = pltpu.make_async_copy(
            x_hbm.at[:, pl.ds(pl.multiple_of(column, 1024), 1024)], chunks.at[e], sems.at[e]
        )
        copy.start()
        copies.append(copy)
    for e in range(4):
        copies[e].wait()
        product = lax.dot_general(
            v_ref[...], chunks[e], (((0,), (0,)), ((), ())), preferred_element_type=F32
        )
        for block in range(4):
            rows = product[:, block * 256 : (block + 1) * 256].T
            out_ref[lax.rem(block + 4 - place[2], 4), e] = rows.astype(out_ref.dtype)


def partial_gradient(own, place, normed_inputs, value_cotangent):
    tokens = normed_inputs.shape[0]

    def kernel(*refs):
        partial_kernel(own, *refs)

    return pl.pallas_call(
        kernel,
        in_specs=[SMEM, HBM, VMEM],
        out_specs=VMEM,
        out_shape=jax.ShapeDtypeStruct((4, 4, 256, HD), BF16),
        scratch_shapes=[pltpu.VMEM((4, tokens, 1024), BF16), pltpu.SemaphoreType.DMA((4,))],
        compiler_params=pltpu.CompilerParams(vmem_limit_bytes=24 * MIB),
        cost_estimate=pl.CostEstimate(
            flops=2 * tokens * 4096 * HD, bytes_accessed=tokens * 4096 * 2, transcendentals=0
        ),
    )(place, normed_inputs, value_cotangent)


def attend_kernel(lengths, queries, new_keys, cache_keys, cache_values, mixed_ref, weights_ref):
    rows = cache_keys.shape[0]
    slots = cache_keys.shape[1]
    steps = queries.shape[0] // rows
    every = HEADS * queries.shape[0]
    factor = 1.0 / math.sqrt(HD)
    heads = jnp.concatenate([queries[:, q * HD : (q + 1) * HD] for q in range(HEADS)], axis=0)
    place = lax.broadcasted_iota(jnp.int32, (every, slots), 0) % (rows * steps)
    lane = lax.broadcasted_iota(jnp.int32, (every, slots), 1)
    row = place // steps
    contract = (((1,), (1,)), ((), ()))
    scores = jnp.full((every, slots), -1e30, F32)
    for r in range(rows):
        product = lax.dot_general(heads, cache_keys[r], contract, preferred_element_type=F32)
        scores = jnp.where((row == r) & (lane < lengths[r]), product * factor, scores)
    fresh = lax.dot_general(heads, new_keys[...], contract, preferred_element_type=F32) * factor
    from_place, to_place = place[:, : rows * steps], lane[:, : rows * steps]
    visible = (from_place // steps == to_place // steps) & (to_place <= from_place)
    fresh = jnp.where(visible, fresh, -1e30)
    highest = jnp.maximum(
        jnp.max(scores, axis=1, keepdims=True), jnp.max(fresh, axis=1, keepdims=True)
    )
    cache_exp = jnp.exp(scores - highest)
    fresh_exp = jnp.exp(fresh - highest)
    total = jnp.sum(cache_exp, axis=1, keepdims=True) + jnp.sum(fresh_exp, axis=1, keepdims=True)
    cache_weights = (cache_exp / total).astype(BF16)
    weights_ref[...] = (fresh_exp / total).astype(BF16)
    mixed = jnp.zeros((every, HD), F32)
    for r in range(rows):
        product = jnp.dot(cache_weights, cache_values[r], preferred_element_type=F32)
        mixed = jnp.where(row == r, product, mixed)
    mixed_ref[...] = mixed


def attend_cache(lengths, queries, new_keys, cache_keys, cache_values):
    places = queries.shape[0]
    return pl.pallas_call(
        attend_kernel,
        in_specs=[SMEM] + [VMEM] * 4,
        out_specs=[VMEM, VMEM],
        out_shape=[
            jax.ShapeDtypeStruct((HEADS * places, HD), F32),
            jax.ShapeDtypeStruct((HEADS * places, places), BF16),
        ],
        compiler_params=pltpu.CompilerParams(vmem_limit_bytes=16 * MIB),
        cost_estimate=pl.CostEstimate(
            flops=2 * 16 * 512 * 256 * HD, bytes_accessed=2 * MIB, transcendentals=512 * 192
        ),
    )(lengths, queries, new_keys, cache_keys, cache_values)


def project_kernel(place, own, d0, d1, d2, d3, u0, u1, u2, u3, start, out_ref, rows):
    x, y = place[2], place[3]
    for d, u in enumerate((u0, u1, u2, u3)):
        rows[pl.ds(pl.multiple_of(lax.rem(x + d, 4) * 256, 256), 256), :] = u[...]
    for d, piece in enumerate((d0, d1, d2, d3)):
        zh = lax.rem(y + d, 4)
        product = jnp.dot(piece[own], rows[...], preferred_element_type=F32)
        if start is not None:
            product += start[zh]
        out_ref[zh] = product.astype(out_ref.dtype)


def project(place, pieces, updated, start=None):
    first = start is None

    def kernel(place, *refs):
        core, low = place[0], place[4]
        own = jnp.where(core == low, 0, 1) if first else jnp.where(core == low, 1, 0)
        if first:
            refs = refs[:8] + (None,) + refs[8:]
        project_kernel(place, own, *refs)

    return pl.pallas_call(
        kernel,
        in_specs=[SMEM] + [VMEM] * (8 if first else 9),
        out_specs=VMEM,
        out_shape=jax.ShapeDtypeStruct((4, 64, HD), F32 if first else BF16),
        scratch_shapes=[pltpu.VMEM((1024, HD), BF16)],
        compiler_params=pltpu.CompilerParams(vmem_limit_bytes=16 * MIB),
        cost_estimate=pl.CostEstimate(
            flops=2 * 256 * 1024 * HD, bytes_accessed=3 * MIB // 4, transcendentals=0
        ),
    )(place, *pieces, *updated, *(() if first else (start,)))


def finish_kernel(parts, mixed, weights, values_ref, attended_ref):
    steps = values_ref.shape[1]
    total = parts[0].astype(F32)
    for i in range(1, 4):
        total += parts[i].astype(F32)
    values = total.astype(BF16)
    for r in range(values_ref.shape[0]):
        values_ref[r] = values[r * steps : (r + 1) * steps]
    places = values.shape[0]
    for q in range(HEADS):
        span = slice(q * places, (q + 1) * places)
        head = mixed[span] + jnp.dot(weights[span], values, preferred_element_type=F32)
        head = head.astype(BF16)
        for r in range(values_ref.shape[0]):
            attended_ref[r, :, q * HD : (q + 1) * HD] = head[r * steps : (r + 1) * steps]


def finish(parts, mixed, weights, rows, steps):
    return pl.pallas_call(
        finish_kernel,
        in_specs=[VMEM] * 3,
        out_specs=[VMEM, VMEM],
        out_shape=[
            jax.ShapeDtypeStruct((rows, steps, HD), BF16),
            jax.ShapeDtypeStruct((rows, steps, HEADS * HD), BF16),
        ],
        compiler_params=pltpu.CompilerParams(vmem_limit_bytes=16 * MIB),
    )(parts, mixed, weights)


def shards(
    normed_inputs,
    value_cotangent,
    value_weight,
    decode_inputs,
    queries,
    new_keys,
    cache_keys,
    cache_values,
    lengths,
):
    core, high, x, low, y = (lax.axis_index(n) for n in NAMES)
    row_count, step_count = decode_inputs.shape[0], decode_inputs.shape[1]
    places = row_count * step_count
    place = jnp.stack([core, high, x, y, low])

    theirs = partial_gradient(False, place, normed_inputs, value_cotangent)
    received = shift(theirs, "c", 1)

    own_inputs = after(decode_inputs.reshape(places, -1), theirs)
    both = jnp.stack([own_inputs, shift(own_inputs, "zl", 1)])

    mine = partial_gradient(True, place, normed_inputs, value_cotangent)
    sums = [mine[d].astype(F32) + received[d].astype(F32) for d in range(4)]
    sent = [s.astype(BF16) for s in sums]

    both = after(both, sent[1])
    both = swap_high(both)

    along_x = sums[0]
    for d in (2, 1, 3):
        along_x += shift(sent[d], "x", d).astype(F32)

    attended_cache, fresh_weights = attend_cache(
        lengths,
        after(queries.reshape(places, -1), sent[1]),
        new_keys.reshape(places, HD),
        cache_keys,
        cache_values,
    )

    gradient = along_x[0]
    sent = [along_x[e].astype(BF16) for e in range(4)]
    both = after(both, sent[1])
    pieces = [both] + [shift(both, "y", -d) for d in (1, 2, 3)]
    for e in (2, 1, 3):
        gradient += shift(sent[e], "zh", e).astype(F32)
    updated = (value_weight.astype(F32) - STEP * gradient).astype(BF16)

    gathered = [updated] + [shift(updated, "x", -d) for d in (1, 2, 3)]
    other = shift(jnp.stack(gathered), "c", 1)
    partial = project(place, pieces, gathered)
    partial = project(place, pieces, [other[d] for d in range(4)], partial)
    exchanged = lax.all_to_all(partial, "zh", 0, 0, tiled=True)
    new_values, attended = finish(
        exchanged, attended_cache, fresh_weights, row_count, step_count
    )
    return (gradient, new_values, attended)


def solution(mesh):
    inner = Mesh(mesh.devices.reshape(tuple(SIZES.values())), NAMES)
    rows, columns = ("c", "zh", "x"), ("zl", "y")
    return jax.shard_map(
        shards,
        mesh=inner,
        in_specs=(
            P(rows, None),
            P(rows, columns),
            P(rows, columns),
            P(rows, None, columns),
            P(rows, None, columns),
            P(rows, None, columns),
            P(rows, None, columns),
            P(rows, None, columns),
            P(rows),
        ),
        out_specs=(
            P(rows, columns),
            P(rows, None, columns),
            P(rows, None, columns),
        ),
        check_vma=False,
    )
```

time: 85.4 us -> 97.5 us (1.14)
  the two profiles are of different devices: /device:TPU:8 before, /device:TPU:32 now
where the time goes in v2:
time: 97.5 us; the launch traced here: 96.8 us
  starting transfers between devices  42.5 us (44%)
  waiting for transfers between devices  31.1 us (32%)
  Pallas kernels  12.7 us (13%)
  local copies, waits for them, and re-layouts  6.63 us (7%)
  other arithmetic  3.08 us (3%)
    ppermute x15, starting transfers between devices, shift(): return lax.ppermute(value, axis, [(i, (i + by) % n) for i in range(n)])  38.5 us
    ppermute x15, waiting for transfers between devices, shift(): return lax.ppermute(value, axis, [(i, (i + by) % n) for i in range(n)])  26 us
    pallas_call x2, Pallas kernels, partial_gradient(): pl.pallas_call(kernel, in_specs=[SMEM, HBM, VMEM], out_specs=VMEM, out_sh...  7.34 us
    unnamed x16, local copies, waits for them, and re-layouts  5.54 us
    all_to_all x1, waiting for transfers between devices, shards(): exchanged = lax.all_to_all(partial, 'zh', 0, 0, tiled=True)  5.05 us
    all_to_all x1, starting transfers between devices, shards(): exchanged = lax.all_to_all(partial, 'zh', 0, 0, tiled=True)  3.28 us
    pallas_call x2, Pallas kernels, project(): pl.pallas_call(kernel, in_specs=[SMEM] + [VMEM] * (8 if first else 9), ou...  2.36 us
    pallas_call x1, Pallas kernels, attend_cache(): pl.pallas_call(attend_kernel, in_specs=[SMEM] + [VMEM] * 4, out_specs=[VM...  2.13 us
  transfers between devices with their start and end apart: 17, of which 7 were waited for; matrix products, arithmetic and copies ran while one was open for 3% of the time, Pallas kernels for 7%

profile of v2, /device:TPU:32, one launch (start us, length us, event | category | flops | bytes accessed | tf_op | source)
XLA Modules:
  0.0 96.8 jit_solution(493446543831712390)
XLA Ops:
  0.7 4.6 %copy-done = bf16[768,8192]{1,0:T(8,128)(2,1)S(1)} copy-done((bf16[768,8192]{1,0:T(8,128)(2,1)S(1)}, bf16[768,8192]{1,0:T(8,128)(2,1)}, u32[]{:S(2)}) %copy-start) | copy-done | bytes 12582936
  6.2 3.7 %shard_map.113 = bf16[4,4,256,128]{3,2,1,0:T(8,128)(2,1)S(1)} custom-call(s32[5]{0:T(128)S(1)} %stack.47.refs_0_.place, bf16[768,8192]{1,0:T(8,128)(2,1)S(1)} %copy-done, bf16[768,128]{1,0:T(8,128)(2,1)S(1)} %copy-done.1), custom_call_target="tpu_custom_call" | custom-call | flops 805306368 | bytes 6291456 | tf_op jit(solution)/shard_map/pallas_call | solution.py:65
  10.1 3.7 %shard_map.112 = bf16[4,4,256,128]{3,2,1,0:T(8,128)(2,1)S(1)} custom-call(s32[5]{0:T(128)S(1)} %stack.47.refs_0_.place, bf16[768,8192]{1,0:T(8,128)(2,1)S(1)} %copy-done, bf16[768,128]{1,0:T(8,128)(2,1)S(1)} %copy-done.1), custom_call_target="tpu_custom_call" | custom-call | flops 805306368 | bytes 6291456 | tf_op jit(solution)/shard_map/pallas_call | solution.py:65
  13.8 1.0 %fusion.2 = (bf16[4,256,128]{2,1,0:T(8,128)(2,1)}, bf16[4,256,128]{2,1,0:T(8,128)(2,1)}, bf16[4,256,128]{2,1,0:T(8,128)(2,1)}) fusion(bf16[4,4,256,128]{3,2,1,0:T(8,128)(2,1)S(1)} %collective-permute-done, bf16[4,4,256,128]{3,2,1,0:T(8,128)(2,1)S(1)} %shard_map.112), kind=kLoop, calls=%fused_computation.6 | loop fusion | flops 1572864 | bytes 2359296 | tf_op jit(solution)/shard_map/convert_element_type | solution.py:218
  14.8 3.0 %collective-permute-start.1 = (bf16[4,256,128]{2,1,0:T(8,128)(2,1)}, bf16[4,256,128]{2,1,0:T(8,128)(2,1)}, u32[]{:S(2)}, u32[]{:S(2)}) collective-permute-start(bf16[4,256,128]{2,1,0:T(8,128)(2,1)} %get-tuple-element.23), channel_id=1, source_target_pairs={{0,16},{8,24},{16,0},{24,8},{1,17},{9,25},{17,1},{25,9},{2,18},{10... | collective-permute-start | bytes 786440 | tf_op jit(solution)/shard_map/ppermute | solution.py:27
  17.8 1.1 %collective-permute-start.3 = (bf16[4,256,128]{2,1,0:T(8,128)(2,1)}, bf16[4,256,128]{2,1,0:T(8,128)(2,1)}, u32[]{:S(2)}, u32[]{:S(2)}) collective-permute-start(bf16[4,256,128]{2,1,0:T(8,128)(2,1)} %get-tuple-element.24), channel_id=1, source_target_pairs={{0,24},{8,0},{16,8},{24,16},{1,25},{9,1},{17,9},{25,17},{2,26},{10... | collective-permute-start | bytes 786440 | tf_op jit(solution)/shard_map/ppermute | solution.py:27
  20.1 5.7 %collective-permute-done.1 = bf16[4,256,128]{2,1,0:T(8,128)(2,1)} collective-permute-done((bf16[4,256,128]{2,1,0:T(8,128)(2,1)}, bf16[4,256,128]{2,1,0:T(8,128)(2,1)}, u32[]{:S(2)}, u32[]{:S(2)}) %collective-permute-start.1) | collective-permute-done | bytes 262176 | tf_op jit(solution)/shard_map/ppermute | solution.py:27
  25.8 5.3 %collective-permute-done.3 = bf16[4,256,128]{2,1,0:T(8,128)(2,1)} collective-permute-done((bf16[4,256,128]{2,1,0:T(8,128)(2,1)}, bf16[4,256,128]{2,1,0:T(8,128)(2,1)}, u32[]{:S(2)}, u32[]{:S(2)}) %collective-permute-start.3) | collective-permute-done | bytes 262176 | tf_op jit(solution)/shard_map/ppermute | solution.py:27
  31.1 1.3 %fusion.9 = (bf16[4,256,128]{2,1,0:T(8,128)(2,1)S(1)}, f32[4,256,128]{2,1,0:T(8,128)S(1)}) fusion(bf16[4,256,128]{2,1,0:T(8,128)(2,1)} %collective-permute-done.3, bf16[4,256,128]{2,1,0:T(8,128)(2,1)} %collective-permute-done.2, bf16[4,256,128]{2,1,0:T(8,128)(2,1)} %collective-permute-done.1, bf16[4,4,256,128]{3,2,1,0:T(8,128)(2,1)S(1)} %collective-permute-done, ...), kind=kLoop, calls=%fused_computation.23 | loop fusion | flops 1310720 | bytes 2097152 | tf_op jit(solution)/shard_map/convert.2
  32.4 6.4 %collective-permute-start.4 = (bf16[256,128]{1,0:T(8,128)(2,1)S(1)}, bf16[256,128]{1,0:T(8,128)(2,1)S(1)}, u32[]{:S(2)}, u32[]{:S(2)}) collective-permute-start(bf16[256,128]{1,0:T(8,128)(2,1)S(1)} %get-tuple-element.30), channel_id=1, source_target_pairs={{0,64},{32,96},{64,0},{96,32},{1,65},{33,97},{65,1},{97,33},{2,66}... | collective-permute-start | bytes 196616 | tf_op jit(solution)/shard_map/ppermute | solution.py:27
  39.3 2.4 %collective-permute-start.5 = (bf16[256,128]{1,0:T(8,128)(2,1)S(1)}, bf16[256,128]{1,0:T(8,128)(2,1)S(1)}, u32[]{:S(2)}, u32[]{:S(2)}) collective-permute-start(bf16[256,128]{1,0:T(8,128)(2,1)S(1)} %get-tuple-element.32), channel_id=1, source_target_pairs={{0,32},{32,64},{64,96},{96,0},{1,33},{33,65},{65,97},{97,1},{2,34}... | collective-permute-start | bytes 196616 | tf_op jit(solution)/shard_map/ppermute | solution.py:27
  42.4 2.0 %collective-permute-done.6 = bf16[256,128]{1,0:T(8,128)(2,1)S(1)} collective-permute-done((bf16[256,128]{1,0:T(8,128)(2,1)S(1)}, bf16[256,128]{1,0:T(8,128)(2,1)S(1)}, u32[]{:S(2)}, u32[]{:S(2)}) %collective-permute-start.6) | collective-permute-done | bytes 65568 | tf_op jit(solution)/shard_map/ppermute | solution.py:27
  44.4 1.8 %collective-permute-done.5 = bf16[256,128]{1,0:T(8,128)(2,1)S(1)} collective-permute-done((bf16[256,128]{1,0:T(8,128)(2,1)S(1)}, bf16[256,128]{1,0:T(8,128)(2,1)S(1)}, u32[]{:S(2)}, u32[]{:S(2)}) %collective-permute-start.5) | collective-permute-done | bytes 65568 | tf_op jit(solution)/shard_map/ppermute | solution.py:27
  47.0 1.4 %collective-permute-start.14 = (bf16[256,128]{1,0:T(8,128)(2,1)S(1)}, bf16[256,128]{1,0:T(8,128)(2,1)S(1)}, u32[]{:S(2)}, u32[]{:S(2)}) collective-permute-start(bf16[256,128]{1,0:T(8,128)(2,1)S(1)} %get-tuple-element.19.refs_4_), channel_id=1, source_target_pairs={{0,8},{8,16},{16,24},{24,0},{1,9},{9,17},{17,25},{25,1},{2,10},{10... | collective-permute-start | bytes 196616 | tf_op jit(solution)/shard_map/ppermute | solution.py:27
  48.4 2.7 %collective-permute-start.13 = (bf16[256,128]{1,0:T(8,128)(2,1)S(1)}, bf16[256,128]{1,0:T(8,128)(2,1)S(1)}, u32[]{:S(2)}, u32[]{:S(2)}) collective-permute-start(bf16[256,128]{1,0:T(8,128)(2,1)S(1)} %get-tuple-element.19.refs_4_), channel_id=1, source_target_pairs={{0,16},{8,24},{16,0},{24,8},{1,17},{9,25},{17,1},{25,9},{2,18},{10... | collective-permute-start | bytes 196616 | tf_op jit(solution)/shard_map/ppermute | solution.py:27
  51.1 1.4 %collective-permute-start.12 = (bf16[256,128]{1,0:T(8,128)(2,1)S(1)}, bf16[256,128]{1,0:T(8,128)(2,1)S(1)}, u32[]{:S(2)}, u32[]{:S(2)}) collective-permute-start(bf16[256,128]{1,0:T(8,128)(2,1)S(1)} %get-tuple-element.19.refs_4_), channel_id=1, source_target_pairs={{0,24},{8,0},{16,8},{24,16},{1,25},{9,1},{17,9},{25,17},{2,26},{10... | collective-permute-start | bytes 196616 | tf_op jit(solution)/shard_map/ppermute | solution.py:27
  52.5 11.2 %collective-permute-start.11 = (bf16[2,64,1024]{2,1,0:T(8,128)(2,1)S(1)}, bf16[2,64,1024]{2,1,0:T(8,128)(2,1)S(1)}, u32[]{:S(2)}, u32[]{:S(2)}) collective-permute-start(bf16[2,64,1024]{2,1,0:T(8,128)(2,1)S(1)} %collective-permute-done.8.refs_0_), channel_id=1, source_target_pairs={{0,1},{1,2},{2,3},{3,0},{4,5},{5,6},{6,7},{7,4},{8,9},{9,10},{10,1... | collective-permute-start | bytes 786440 | tf_op jit(solution)/shard_map/ppermute | solution.py:27
  63.8 7.0 %collective-permute-start.10 = (bf16[2,64,1024]{2,1,0:T(8,128)(2,1)S(1)}, bf16[2,64,1024]{2,1,0:T(8,128)(2,1)S(1)}, u32[]{:S(2)}, u32[]{:S(2)}) collective-permute-start(bf16[2,64,1024]{2,1,0:T(8,128)(2,1)S(1)} %collective-permute-done.8.refs_0_), channel_id=1, source_target_pairs={{0,2},{1,3},{2,0},{3,1},{4,6},{5,7},{6,4},{7,5},{8,10},{9,11},{10,... | collective-permute-start | bytes 786440 | tf_op jit(solution)/shard_map/ppermute | solution.py:27
  71.0 4.7 %collective-permute-done.11.refs_3_ = bf16[2,64,1024]{2,1,0:T(8,128)(2,1)S(1)} collective-permute-done((bf16[2,64,1024]{2,1,0:T(8,128)(2,1)S(1)}, bf16[2,64,1024]{2,1,0:T(8,128)(2,1)S(1)}, u32[]{:S(2)}, u32[]{:S(2)}) %collective-permute-start.11) | collective-permute-done | bytes 262176 | tf_op jit(solution)/shard_map/ppermute | solution.py:27
  75.6 6.4 %collective-permute-done.10.refs_2_ = bf16[2,64,1024]{2,1,0:T(8,128)(2,1)S(1)} collective-permute-done((bf16[2,64,1024]{2,1,0:T(8,128)(2,1)S(1)}, bf16[2,64,1024]{2,1,0:T(8,128)(2,1)S(1)}, u32[]{:S(2)}, u32[]{:S(2)}) %collective-permute-start.10) | collective-permute-done | bytes 262176 | tf_op jit(solution)/shard_map/ppermute | solution.py:27
  83.0 1.5 %shard_map.115 = bf16[4,64,128]{2,1,0:T(8,128)(2,1)} custom-call(s32[5]{0:T(128)S(1)} %stack.47.refs_0_.place, bf16[2,64,1024]{2,1,0:T(8,128)(2,1)S(1)} %collective-permute-done.8.refs_0_, bf16[2,64,1024]{2,1,0:T(8,128)(2,1)S(1)} %collective-permute-done.9.refs_1_, bf16[2,64,1024]{2,1,0:T(8,128)(2,1)S(1)} %collective-permute-done.10.refs_2_, ...), custom_call_target="tpu_custom_call" | custom-call | flops 67108864 | bytes 786432 | tf_op jit(solution)/shard_map/pallas_call | solution.py:151
  84.5 3.3 %all-to-all-start = ((bf16[4,64,128]{2,1,0:T(8,128)(2,1)}), bf16[4,64,128]{2,1,0:T(8,128)(2,1)S(1)}, u32[]{:S(2)}, u32[]{:S(2)}) async-start(bf16[4,64,128]{2,1,0:T(8,128)(2,1)} %shard_map.115), calls=%async_computation | async-start | bytes 131072 | tf_op jit(solution)/shard_map/all_to_all | solution.py:247
  88.8 2.1 %shard_map.116 = (f32[512,128]{1,0:T(8,128)S(1)}, bf16[512,64]{1,0:T(8,128)(2,1)S(1)}) custom-call(s32[16]{0:T(128)S(1)} %copy-done.5, bf16[64,1024]{1,0:T(8,128)(2,1)S(1)} %reshape.34.queries, bf16[64,128]{1,0:T(8,128)(2,1)S(1)} %bitcast.52, bf16[16,128,128]{2,1,0:T(8,128)(2,1)S(1)} %copy-done.2, bf16[16,128,128]{2,1,0:T(8,128)(2,1)S(1)} %copy-done.3), custom_call_target="tpu_custom_call" | custom-call | flops 536870912 | bytes 2097152 | tf_op jit(solution)/shard_map/pallas_call | solution.py:114
  90.9 5.0 %all-to-all-done.parts = bf16[4,64,128]{2,1,0:T(8,128)(2,1)S(1)} async-done(((bf16[4,64,128]{2,1,0:T(8,128)(2,1)}), bf16[4,64,128]{2,1,0:T(8,128)(2,1)S(1)}, u32[]{:S(2)}, u32[]{:S(2)}) %all-to-all-start) | async-done | bytes 65568 | tf_op jit(solution)/shard_map/all_to_all | solution.py:247
  (42 shorter events, 7.1 us)
Async XLA Ops:
  0.7 4.6 %copy-start = (bf16[768,8192]{1,0:T(8,128)(2,1)S(1)}, bf16[768,8192]{1,0:T(8,128)(2,1)}, u32[]{:S(2)}) copy-start(bf16[768,8192]{1,0:T(8,128)(2,1)} %refs_1_.3) | copy-start | bytes 37748740
  6.2 13.6 %copy-start.6 = (bf16[16,4,1024]{2,1,0:T(4,128)(2,1)S(1)}, bf16[16,4,1024]{2,1,0:T(4,128)(2,1)}, u32[]{:S(2)}) copy-start(bf16[16,4,1024]{2,1,0:T(4,128)(2,1)} %param.12) | copy-start | bytes 393220
  9.9 36.4 %copy-start.7 = (bf16[256,128]{1,0:T(8,128)(2,1)S(1)}, bf16[256,128]{1,0:T(8,128)(2,1)}, u32[]{:S(2)}) copy-start(bf16[256,128]{1,0:T(8,128)(2,1)} %param.11) | copy-start | bytes 196612
  9.9 78.8 %copy-start.2 = (bf16[16,128,128]{2,1,0:T(8,128)(2,1)S(1)}, bf16[16,128,128]{2,1,0:T(8,128)(2,1)}, u32[]{:S(2)}) copy-start(bf16[16,128,128]{2,1,0:T(8,128)(2,1)} %cache_keys.1) | copy-start | bytes 1572868
  9.9 78.8 %copy-start.3 = (bf16[16,128,128]{2,1,0:T(8,128)(2,1)S(1)}, bf16[16,128,128]{2,1,0:T(8,128)(2,1)}, u32[]{:S(2)}) copy-start(bf16[16,128,128]{2,1,0:T(8,128)(2,1)} %cache_values.1) | copy-start | bytes 1572868
  9.9 78.8 %copy-start.4 = (bf16[16,4,128]{2,1,0:T(4,128)(2,1)S(1)}, bf16[16,4,128]{2,1,0:T(4,128)(2,1)}, u32[]{:S(2)}) copy-start(bf16[16,4,128]{2,1,0:T(4,128)(2,1)} %param.14) | copy-start | bytes 49156
  10.0 78.8 %copy-start.5 = (s32[16]{0:T(128)S(1)}, s32[16]{0:T(128)}, u32[]{:S(2)}) copy-start(s32[16]{0:T(128)} %lengths.1) | copy-start | bytes 196
  10.0 3.8 %collective-permute-start = (bf16[4,4,256,128]{3,2,1,0:T(8,128)(2,1)S(1)}, bf16[4,4,256,128]{3,2,1,0:T(8,128)(2,1)S(1)}, u32[]{:S(2)}, u32[]{:S(2)}) collective-permute-start(bf16[4,4,256,128]{3,2,1,0:T(8,128)(2,1)S(1)} %shard_map.113), channel_id=1, source_target_pairs={{0,128},{128,0},{1,129},{129,1},{2,130},{130,2},{3,131},{131,3},{4... | collective-permute-start | bytes 3145736 | tf_op jit(solution)/shard_map/ppermute | solution.py:27
  14.8 11.0 %collective-permute-start.1 = (bf16[4,256,128]{2,1,0:T(8,128)(2,1)}, bf16[4,256,128]{2,1,0:T(8,128)(2,1)}, u32[]{:S(2)}, u32[]{:S(2)}) collective-permute-start(bf16[4,256,128]{2,1,0:T(8,128)(2,1)} %get-tuple-element.23), channel_id=1, source_target_pairs={{0,16},{8,24},{16,0},{24,8},{1,17},{9,25},{17,1},{25,9},{2,18},{10... | collective-permute-start | bytes 786440 | tf_op jit(solution)/shard_map/ppermute | solution.py:27
  17.8 13.2 %collective-permute-start.3 = (bf16[4,256,128]{2,1,0:T(8,128)(2,1)}, bf16[4,256,128]{2,1,0:T(8,128)(2,1)}, u32[]{:S(2)}, u32[]{:S(2)}) collective-permute-start(bf16[4,256,128]{2,1,0:T(8,128)(2,1)} %get-tuple-element.24), channel_id=1, source_target_pairs={{0,24},{8,0},{16,8},{24,16},{1,25},{9,1},{17,9},{25,17},{2,26},{10... | collective-permute-start | bytes 786440 | tf_op jit(solution)/shard_map/ppermute | solution.py:27
  18.9 12.1 %collective-permute-start.2 = (bf16[4,256,128]{2,1,0:T(8,128)(2,1)}, bf16[4,256,128]{2,1,0:T(8,128)(2,1)}, u32[]{:S(2)}, u32[]{:S(2)}) collective-permute-start(bf16[4,256,128]{2,1,0:T(8,128)(2,1)} %get-tuple-element.25), channel_id=1, source_target_pairs={{0,8},{8,16},{16,24},{24,0},{1,9},{9,17},{17,25},{25,1},{2,10},{10... | collective-permute-start | bytes 786440 | tf_op jit(solution)/shard_map/ppermute | solution.py:27
  19.9 21.8 %collective-permute-start.7 = (bf16[64,1024]{1,0:T(8,128)(2,1)S(1)}, bf16[64,1024]{1,0:T(8,128)(2,1)S(1)}, u32[]{:S(2)}, u32[]{:S(2)}) collective-permute-start(bf16[64,1024]{1,0:T(8,128)(2,1)S(1)} %reshape.33), channel_id=1, source_target_pairs={{0,4},{4,0},{1,5},{5,1},{2,6},{6,2},{3,7},{7,3},{8,12},{12,8},{9,1... | collective-permute-start | bytes 393224 | tf_op jit(solution)/shard_map/ppermute | solution.py:27
  32.4 10.1 %collective-permute-start.4 = (bf16[256,128]{1,0:T(8,128)(2,1)S(1)}, bf16[256,128]{1,0:T(8,128)(2,1)S(1)}, u32[]{:S(2)}, u32[]{:S(2)}) collective-permute-start(bf16[256,128]{1,0:T(8,128)(2,1)S(1)} %get-tuple-element.30), channel_id=1, source_target_pairs={{0,64},{32,96},{64,0},{96,32},{1,65},{33,97},{65,1},{97,33},{2,66}... | collective-permute-start | bytes 196616 | tf_op jit(solution)/shard_map/ppermute | solution.py:27
  38.8 5.7 %collective-permute-start.6 = (bf16[256,128]{1,0:T(8,128)(2,1)S(1)}, bf16[256,128]{1,0:T(8,128)(2,1)S(1)}, u32[]{:S(2)}, u32[]{:S(2)}) collective-permute-start(bf16[256,128]{1,0:T(8,128)(2,1)S(1)} %get-tuple-element.31), channel_id=1, source_target_pairs={{0,96},{32,0},{64,32},{96,64},{1,97},{33,1},{65,33},{97,65},{2,98}... | collective-permute-start | bytes 196616 | tf_op jit(solution)/shard_map/ppermute | solution.py:27
  39.3 7.0 %collective-permute-start.5 = (bf16[256,128]{1,0:T(8,128)(2,1)S(1)}, bf16[256,128]{1,0:T(8,128)(2,1)S(1)}, u32[]{:S(2)}, u32[]{:S(2)}) collective-permute-start(bf16[256,128]{1,0:T(8,128)(2,1)S(1)} %get-tuple-element.32), channel_id=1, source_target_pairs={{0,32},{32,64},{64,96},{96,0},{1,33},{33,65},{65,97},{97,1},{2,34}... | collective-permute-start | bytes 196616 | tf_op jit(solution)/shard_map/ppermute | solution.py:27
  41.7 10.8 %collective-permute-start.8 = (bf16[2,64,1024]{2,1,0:T(8,128)(2,1)S(1)}, bf16[2,64,1024]{2,1,0:T(8,128)(2,1)S(1)}, u32[]{:S(2)}, u32[]{:S(2)}) collective-permute-start(bf16[2,64,1024]{2,1,0:T(8,128)(2,1)S(1)} %pad_maximum_fusion), channel_id=1, source_target_pairs={{0,0},{1,32},{2,64},{3,96},{32,1},{33,33},{34,65},{35,97},{64,2},{... | collective-permute-start | bytes 786440 | tf_op jit(solution)/shard_map/ppermute | solution.py:32
  47.0 23.8 %collective-permute-start.14 = (bf16[256,128]{1,0:T(8,128)(2,1)S(1)}, bf16[256,128]{1,0:T(8,128)(2,1)S(1)}, u32[]{:S(2)}, u32[]{:S(2)}) collective-permute-start(bf16[256,128]{1,0:T(8,128)(2,1)S(1)} %get-tuple-element.19.refs_4_), channel_id=1, source_target_pairs={{0,8},{8,16},{16,24},{24,0},{1,9},{9,17},{17,25},{25,1},{2,10},{10... | collective-permute-start | bytes 196616 | tf_op jit(solution)/shard_map/ppermute | solution.py:27
  48.4 22.4 %collective-permute-start.13 = (bf16[256,128]{1,0:T(8,128)(2,1)S(1)}, bf16[256,128]{1,0:T(8,128)(2,1)S(1)}, u32[]{:S(2)}, u32[]{:S(2)}) collective-permute-start(bf16[256,128]{1,0:T(8,128)(2,1)S(1)} %get-tuple-element.19.refs_4_), channel_id=1, source_target_pairs={{0,16},{8,24},{16,0},{24,8},{1,17},{9,25},{17,1},{25,9},{2,18},{10... | collective-permute-start | bytes 196616 | tf_op jit(solution)/shard_map/ppermute | solution.py:27
  51.1 19.7 %collective-permute-start.12 = (bf16[256,128]{1,0:T(8,128)(2,1)S(1)}, bf16[256,128]{1,0:T(8,128)(2,1)S(1)}, u32[]{:S(2)}, u32[]{:S(2)}) collective-permute-start(bf16[256,128]{1,0:T(8,128)(2,1)S(1)} %get-tuple-element.19.refs_4_), channel_id=1, source_target_pairs={{0,24},{8,0},{16,8},{24,16},{1,25},{9,1},{17,9},{25,17},{2,26},{10... | collective-permute-start | bytes 196616 | tf_op jit(solution)/shard_map/ppermute | solution.py:27
  52.5 23.1 %collective-permute-start.11 = (bf16[2,64,1024]{2,1,0:T(8,128)(2,1)S(1)}, bf16[2,64,1024]{2,1,0:T(8,128)(2,1)S(1)}, u32[]{:S(2)}, u32[]{:S(2)}) collective-permute-start(bf16[2,64,1024]{2,1,0:T(8,128)(2,1)S(1)} %collective-permute-done.8.refs_0_), channel_id=1, source_target_pairs={{0,1},{1,2},{2,3},{3,0},{4,5},{5,6},{6,7},{7,4},{8,9},{9,10},{10,1... | collective-permute-start | bytes 786440 | tf_op jit(solution)/shard_map/ppermute | solution.py:27
  63.8 18.3 %collective-permute-start.10 = (bf16[2,64,1024]{2,1,0:T(8,128)(2,1)S(1)}, bf16[2,64,1024]{2,1,0:T(8,128)(2,1)S(1)}, u32[]{:S(2)}, u32[]{:S(2)}) collective-permute-start(bf16[2,64,1024]{2,1,0:T(8,128)(2,1)S(1)} %collective-permute-done.8.refs_0_), channel_id=1, source_target_pairs={{0,2},{1,3},{2,0},{3,1},{4,6},{5,7},{6,4},{7,5},{8,10},{9,11},{10,... | collective-permute-start | bytes 786440 | tf_op jit(solution)/shard_map/ppermute | solution.py:27
  70.8 11.3 %collective-permute-start.9 = (bf16[2,64,1024]{2,1,0:T(8,128)(2,1)S(1)}, bf16[2,64,1024]{2,1,0:T(8,128)(2,1)S(1)}, u32[]{:S(2)}, u32[]{:S(2)}) collective-permute-start(bf16[2,64,1024]{2,1,0:T(8,128)(2,1)S(1)} %collective-permute-done.8.refs_0_), channel_id=1, source_target_pairs={{0,3},{1,0},{2,1},{3,2},{4,7},{5,4},{6,5},{7,6},{8,11},{9,8},{10,9... | collective-permute-start | bytes 786440 | tf_op jit(solution)/shard_map/ppermute | solution.py:27
  70.9 12.1 %collective-permute-start.15 = (bf16[4,256,128]{2,1,0:T(8,128)(2,1)S(1)}, bf16[4,256,128]{2,1,0:T(8,128)(2,1)S(1)}, u32[]{:S(2)}, u32[]{:S(2)}) collective-permute-start(bf16[4,256,128]{2,1,0:T(8,128)(2,1)S(1)} %pad_maximum_fusion.1), channel_id=1, source_target_pairs={{0,128},{128,0},{1,129},{129,1},{2,130},{130,2},{3,131},{131,3},{4... | collective-permute-start | bytes 786440 | tf_op jit(solution)/shard_map/ppermute | solution.py:27
  84.5 11.5 %all-to-all-start = ((bf16[4,64,128]{2,1,0:T(8,128)(2,1)}), bf16[4,64,128]{2,1,0:T(8,128)(2,1)S(1)}, u32[]{:S(2)}, u32[]{:S(2)}) async-start(bf16[4,64,128]{2,1,0:T(8,128)(2,1)} %shard_map.115), calls=%async_computation | async-start | bytes 131072 | tf_op jit(solution)/shard_map/all_to_all | solution.py:247
  (1 other events, 0.9 us)

commit v3 on v2

--- a/solution.py
+++ b/solution.py
@@ -36,43 +36,75 @@
     return lax.optimization_barrier((value, *others))[0]
 
 
-def partial_kernel(own, place, x_hbm, v_ref, out_ref, chunks, sems):
-    half = place[0] if own else 1 - place[0]
-    copies = []
-    for e in range(4):
-        column = (half * 4 + lax.rem(place[1] + e, 4)) * 1024
-        copy = pltpu.make_async_copy(
-            x_hbm.at[:, pl.ds(pl.multiple_of(column, 1024), 1024)], chunks.at[e], sems.at[e]
+def partial_kernel(place, x_hbm, v_hbm, theirs_ref, mine_ref, chunks, v_ref, sems):
+    core, high, x = place[0], place[1], place[2]
+    order = [(1 - core, theirs_ref, e) for e in range(4)] + [(core, mine_ref, e) for e in range(4)]
+    copies = [pltpu.make_async_copy(v_hbm, v_ref, sems.at[8])]
+    copies[0].start()
+    for i, (half, _, e) in enumerate(order):
+        column = (half * 4 + lax.rem(high + e, 4)) * 1024
+        copies.append(
+            pltpu.make_async_copy(
+                x_hbm.at[:, pl.ds(pl.multiple_of(column, 1024), 1024)], chunks.at[i], sems.at[i]
+            )
         )
-        copy.start()
-        copies.append(copy)
-    for e in range(4):
-        copies[e].wait()
+        copies[-1].start()
+    copies[0].wait()
+    for i, (_, out_ref, e) in enumerate(order):
+        copies[i + 1].wait()
         product = lax.dot_general(
-            v_ref[...], chunks[e], (((0,), (0,)), ((), ())), preferred_element_type=F32
+            v_ref[...], chunks[i], (((0,), (0,)), ((), ())), preferred_element_type=F32
         )
         for block in range(4):
             rows = product[:, block * 256 : (block + 1) * 256].T
-            out_ref[lax.rem(block + 4 - place[2], 4), e] = rows.astype(out_ref.dtype)
-
-
-def partial_gradient(own, place, normed_inputs, value_cotangent):
+            out_ref[lax.rem(block + 4 - x, 4), e] = rows.astype(out_ref.dtype)
+
+
+def partial_gradient(place, normed_inputs, value_cotangent):
     tokens = normed_inputs.shape[0]
-
-    def kernel(*refs):
-        partial_kernel(own, *refs)
-
+    return pl.pallas_call(
+        partial_kernel,
+        in_specs=[SMEM, HBM, HBM],
+        out_specs=[VMEM, VMEM],
+        out_shape=[jax.ShapeDtypeStruct((4, 4, 256, HD), BF16)] * 2,
+        scratch_shapes=[
+            pltpu.VMEM((8, tokens, 1024), BF16),
+            pltpu.VMEM((tokens, HD), BF16),
+            pltpu.SemaphoreType.DMA((9,)),
+        ],
+        compiler_params=pltpu.CompilerParams(vmem_limit_bytes=48 * MIB),
+        cost_estimate=pl.CostEstimate(
+            flops=2 * tokens * D * HD, bytes_accessed=tokens * D * 2, transcendentals=0
+        ),
+    )(place, normed_inputs, value_cotangent)
+
+
+def small_call(kernel, outs, *args):
     return pl.pallas_call(
         kernel,
-        in_specs=[SMEM, HBM, VMEM],
-        out_specs=VMEM,
-        out_shape=jax.ShapeDtypeStruct((4, 4, 256, HD), BF16),
-        scratch_shapes=[pltpu.VMEM((4, tokens, 1024), BF16), pltpu.SemaphoreType.DMA((4,))],
-        compiler_params=pltpu.CompilerParams(vmem_limit_bytes=24 * MIB),
-        cost_estimate=pl.CostEstimate(
-            flops=2 * tokens * 4096 * HD, bytes_accessed=tokens * 4096 * 2, transcendentals=0
-        ),
-    )(place, normed_inputs, value_cotangent)
+        in_specs=[VMEM] * len(args),
+        out_specs=[VMEM] * len(outs),
+        out_shape=[jax.ShapeDtypeStruct(shape, dtype) for shape, dtype in outs],
+        compiler_params=pltpu.CompilerParams(vmem_limit_bytes=16 * MIB),
+        cost_estimate=pl.CostEstimate(flops=MIB, bytes_accessed=2 * MIB, transcendentals=0),
+    )(*args)
+
+
+def core_sum_kernel(mine, received, o0, o1, o2, o3):
+    for d, out in enumerate((o0, o1, o2, o3)):
+        out[...] = (mine[d].astype(F32) + received[d].astype(F32)).astype(out.dtype)
+
+
+def x_sum_kernel(own, r1, r2, r3, o0, o1, o2, o3):
+    for e, out in enumerate((o0, o1, o2, o3)):
+        total = own[e] + r1[e].astype(F32) + r2[e].astype(F32) + r3[e].astype(F32)
+        out[...] = total.astype(out.dtype)
+
+
+def update_kernel(weight, own, r1, r2, r3, gradient, updated):
+    total = own[...] + r1[...].astype(F32) + r2[...].astype(F32) + r3[...].astype(F32)
+    gradient[...] = total
+    updated[...] = (weight[...].astype(F32) - STEP * total).astype(BF16)
 
 
 def attend_kernel(lengths, queries, new_keys, cache_keys, cache_values, mixed_ref, weights_ref):
@@ -126,10 +158,12 @@
     )(lengths, queries, new_keys, cache_keys, cache_values)
 
 
-def project_kernel(place, own, d0, d1, d2, d3, u0, u1, u2, u3, start, out_ref, rows):
-    x, y = place[2], place[3]
-    for d, u in enumerate((u0, u1, u2, u3)):
-        rows[pl.ds(pl.multiple_of(lax.rem(x + d, 4) * 256, 256), 256), :] = u[...]
+def project_kernel(first, place, d0, d1, d2, d3, u, *refs):
+    core, x, y, low = place[0], place[2], place[3], place[4]
+    start, out_ref, rows = (None, *refs) if first else refs
+    own = jnp.where(core == low, 0, 1) if first else jnp.where(core == low, 1, 0)
+    for d in range(4):
+        rows[pl.ds(pl.multiple_of(lax.rem(x + d, 4) * 256, 256), 256), :] = u[d]
     for d, piece in enumerate((d0, d1, d2, d3)):
         zh = lax.rem(y + d, 4)
         product = jnp.dot(piece[own], rows[...], preferred_element_type=F32)
@@ -141,16 +175,13 @@
 def project(place, pieces, updated, start=None):
     first = start is None
 
-    def kernel(place, *refs):
-        core, low = place[0], place[4]
-        own = jnp.where(core == low, 0, 1) if first else jnp.where(core == low, 1, 0)
-        if first:
-            refs = refs[:8] + (None,) + refs[8:]
-        project_kernel(place, own, *refs)
-
+    def kernel(*refs):
+        project_kernel(first, *refs)
+
+    args = (*pieces, updated) if first else (*pieces, updated, start)
     return pl.pallas_call(
         kernel,
-        in_specs=[SMEM] + [VMEM] * (8 if first else 9),
+        in_specs=[SMEM] + [VMEM] * len(args),
         out_specs=VMEM,
         out_shape=jax.ShapeDtypeStruct((4, 64, HD), F32 if first else BF16),
         scratch_shapes=[pltpu.VMEM((1024, HD), BF16)],
@@ -158,7 +189,7 @@
         cost_estimate=pl.CostEstimate(
             flops=2 * 256 * 1024 * HD, bytes_accessed=3 * MIB // 4, transcendentals=0
         ),
-    )(place, *pieces, *updated, *(() if first else (start,)))
+    )(place, *args)
 
 
 def finish_kernel(parts, mixed, weights, values_ref, attended_ref):
@@ -207,43 +238,48 @@
     places = row_count * step_count
     place = jnp.stack([core, high, x, y, low])
 
-    theirs = partial_gradient(False, place, normed_inputs, value_cotangent)
+    theirs, mine = partial_gradient(place, normed_inputs, value_cotangent)
     received = shift(theirs, "c", 1)
 
-    own_inputs = after(decode_inputs.reshape(places, -1), theirs)
-    both = jnp.stack([own_inputs, shift(own_inputs, "zl", 1)])
-
-    mine = partial_gradient(True, place, normed_inputs, value_cotangent)
-    sums = [mine[d].astype(F32) + received[d].astype(F32) for d in range(4)]
-    sent = [s.astype(BF16) for s in sums]
-
-    both = after(both, sent[1])
-    both = swap_high(both)
-
-    along_x = sums[0]
-    for d in (2, 1, 3):
-        along_x += shift(sent[d], "x", d).astype(F32)
-
+    swapped = swap_high(after(decode_inputs.reshape(places, -1), theirs))
+
+    rows = (4, 256, HD)
+    own, *sent = small_call(
+        core_sum_kernel, [(rows, F32)] + [(rows, BF16)] * 3, mine, received
+    )
+    along_x = [shift(sent[d - 1], "x", d) for d in (2, 1, 3)]
+
+    swapped = after(swapped, own)
+    both = jnp.stack([swapped, shift(swapped, "zl", 1)])
     attended_cache, fresh_weights = attend_cache(
         lengths,
-        after(queries.reshape(places, -1), sent[1]),
+        after(queries.reshape(places, -1), own),
         new_keys.reshape(places, HD),
         cache_keys,
         cache_values,
     )
 
-    gradient = along_x[0]
-    sent = [along_x[e].astype(BF16) for e in range(4)]
-    both = after(both, sent[1])
+    own, *along_x, both, attended_cache, fresh_weights = lax.optimization_barrier(
+        (own, *along_x, both, attended_cache, fresh_weights)
+    )
+    rows = (256, HD)
+    own, *sent = small_call(
+        x_sum_kernel, [(rows, F32)] + [(rows, BF16)] * 3, own, *along_x
+    )
+    along_z = [shift(sent[e - 1], "zh", e) for e in (2, 1, 3)]
+    both = after(both, own)
     pieces = [both] + [shift(both, "y", -d) for d in (1, 2, 3)]
-    for e in (2, 1, 3):
-        gradient += shift(sent[e], "zh", e).astype(F32)
-    updated = (value_weight.astype(F32) - STEP * gradient).astype(BF16)
-
-    gathered = [updated] + [shift(updated, "x", -d) for d in (1, 2, 3)]
-    other = shift(jnp.stack(gathered), "c", 1)
+    own, *along_z, pieces[1], pieces[3] = lax.optimization_barrier(
+        (own, *along_z, pieces[1], pieces[3])
+    )
+    gradient, updated = small_call(
+        update_kernel, [(rows, F32), (rows, BF16)], value_weight, own, *along_z
+    )
+
+    gathered = jnp.stack([updated] + [shift(updated, "x", -d) for d in (1, 2, 3)])
+    other = shift(gathered, "c", 1)
     partial = project(place, pieces, gathered)
-    partial = project(place, pieces, [other[d] for d in range(4)], partial)
+    partial = project(place, pieces, other, partial)
     exchanged = lax.all_to_all(partial, "zh", 0, 0, tiled=True)
     new_values, attended = finish(
         exchanged, attended_cache, fresh_weights, row_count, step_count

time: 97.5 us -> 79.5 us (0.82)
  waiting for transfers between devices: 31.1 us -> 18 us
  blocking collectives: 0 us -> 12.1 us
  starting transfers between devices: 42.5 us -> 30.6 us
  local copies, waits for them, and re-layouts: 6.63 us -> 3.7 us
  other arithmetic: 3.08 us -> 0.96 us
    all_to_all x0 -> x1, blocking collectives: none -> 12.1 us  [shards(): exchanged = lax.all_to_all(partial, 'zh', 0, 0, tiled=True)]
    ppermute x15, starting transfers between devices: 38.5 us -> 28.4 us  [shift(): return lax.ppermute(value, axis, [(i, (i + by) % n) for i in range(n)])]
    ppermute x15, waiting for transfers between devices: 26 us -> 18 us  [shift(): return lax.ppermute(value, axis, [(i, (i + by) % n) for i in range(n)])]
    all_to_all x1 -> x0, waiting for transfers between devices: 5.05 us -> none  [shards(): exchanged = lax.all_to_all(partial, 'zh', 0, 0, tiled=True)]
    unnamed x16 -> x14, local copies, waits for them, and re-layouts: 5.54 us -> 1.98 us
    all_to_all x1 -> x0, starting transfers between devices: 3.28 us -> none  [shards(): exchanged = lax.all_to_all(partial, 'zh', 0, 0, tiled=True)]
    convert_element_type x2 -> x0, other arithmetic: 1.73 us -> none  [the longest x1 1.03 us: shards(): sent = [s.astype(BF16) for s in sums]]
    ppermute x1, starting transfers between devices: 0.68 us -> 2.15 us  [swap_high(): return lax.ppermute(value, ('zh', 'y'), pairs)]
  transfers between devices with their start and end apart: 17 -> 16, of which waited for: 7 -> 9; matrix products, arithmetic and copies ran while one was open for 3% -> 3% of each run, Pallas kernels for 7% -> 5%
where the time goes in v3:
time: 79.5 us; the launch traced here: 79.2 us
  starting transfers between devices  30.6 us (38%)
  waiting for transfers between devices  18 us (23%)
  Pallas kernels  13.1 us (16%)
  blocking collectives  12.1 us (15%)
  local copies, waits for them, and re-layouts  3.7 us (5%)
  other arithmetic  0.96 us (1%)
    ppermute x15, starting transfers between devices, shift(): return lax.ppermute(value, axis, [(i, (i + by) % n) for i in range(n)])  28.4 us
    ppermute x15, waiting for transfers between devices, shift(): return lax.ppermute(value, axis, [(i, (i + by) % n) for i in range(n)])  18 us
    all_to_all x1, blocking collectives, shards(): exchanged = lax.all_to_all(partial, 'zh', 0, 0, tiled=True)  12.1 us
    pallas_call x1, Pallas kernels, partial_gradient(): pl.pallas_call(partial_kernel, in_specs=[SMEM, HBM, HBM], out_specs=[VMEM...  6.65 us
    ppermute x1, starting transfers between devices, swap_high(): return lax.ppermute(value, ('zh', 'y'), pairs)  2.15 us
    pallas_call x1, Pallas kernels, attend_cache(): pl.pallas_call(attend_kernel, in_specs=[SMEM] + [VMEM] * 4, out_specs=[VM...  2.13 us
    unnamed x14, local copies, waits for them, and re-layouts  1.98 us
    pallas_call x3, Pallas kernels, small_call(): pl.pallas_call(kernel, in_specs=[VMEM] * len(args), out_specs=[VMEM] * le...  1.73 us
  transfers between devices with their start and end apart: 16, of which 9 were waited for; matrix products, arithmetic and copies ran while one was open for 3% of the time, Pallas kernels for 5%

profile of v3, /device:TPU:32, one launch (start us, length us, event | category | flops | bytes accessed | tf_op | source)
XLA Modules:
  0.0 79.2 jit_solution(10461139725908920267)
XLA Ops:
  1.7 6.6 %shard_map.112 = (bf16[4,4,256,128]{3,2,1,0:T(8,128)(2,1)}, bf16[4,4,256,128]{3,2,1,0:T(8,128)(2,1)S(1)}) custom-call(s32[5]{0:T(128)S(1)} %stack.47.place.refs_0_, bf16[768,8192]{1,0:T(8,128)(2,1)} %x_hbm.1, bf16[768,128]{1,0:T(8,128)(2,1)S(1)} %copy-done), custom_call_target="tpu_custom_call" | custom-call | flops 1610612736 | bytes 12582912 | tf_op jit(solution)/shard_map/pallas_call | solution.py:65
  9.1 2.2 %collective-permute-start.4 = (bf16[64,1024]{1,0:T(8,128)(2,1)}, bf16[64,1024]{1,0:T(8,128)(2,1)}, u32[]{:S(2)}, u32[]{:S(2)}) collective-permute-start(bf16[64,1024]{1,0:T(8,128)(2,1)} %reshape.15), channel_id=1, source_target_pairs={{0,0},{1,32},{2,64},{3,96},{32,1},{33,33},{34,65},{35,97},{64,2},{... | collective-permute-start | bytes 393224 | tf_op jit(solution)/shard_map/ppermute | solution.py:32
  11.3 0.9 %shard_map.113 = (f32[4,256,128]{2,1,0:T(8,128)S(1)}, bf16[4,256,128]{2,1,0:T(8,128)(2,1)}, bf16[4,256,128]{2,1,0:T(8,128)(2,1)}, bf16[4,256,128]{2,1,0:T(8,128)(2,1)S(1)}) custom-call(bf16[4,4,256,128]{3,2,1,0:T(8,128)(2,1)S(1)} %get-tuple-element.36.mine, bf16[4,4,256,128]{3,2,1,0:T(8,128)(2,1)S(1)} %collective-permute-done.received), custom_call_target="tpu_custom_call" | custom-call | flops 1048576 | bytes 2097152 | tf_op jit(solution)/shard_map/pallas_call | solution.py:83
  12.2 3.0 %collective-permute-start.1 = (bf16[4,256,128]{2,1,0:T(8,128)(2,1)}, bf16[4,256,128]{2,1,0:T(8,128)(2,1)S(1)}, u32[]{:S(2)}, u32[]{:S(2)}) collective-permute-start(bf16[4,256,128]{2,1,0:T(8,128)(2,1)} %get-tuple-element.39), channel_id=1, source_target_pairs={{0,16},{8,24},{16,0},{24,8},{1,17},{9,25},{17,1},{25,9},{2,18},{10... | collective-permute-start | bytes 786440 | tf_op jit(solution)/shard_map/ppermute | solution.py:27
  15.8 2.6 %collective-permute-start.3 = (bf16[4,256,128]{2,1,0:T(8,128)(2,1)S(1)}, bf16[4,256,128]{2,1,0:T(8,128)(2,1)S(1)}, u32[]{:S(2)}, u32[]{:S(2)}) collective-permute-start(bf16[4,256,128]{2,1,0:T(8,128)(2,1)S(1)} %get-tuple-element.41), channel_id=1, source_target_pairs={{0,24},{8,0},{16,8},{24,16},{1,25},{9,1},{17,9},{25,17},{2,26},{10... | collective-permute-start | bytes 786440 | tf_op jit(solution)/shard_map/ppermute | solution.py:27
  18.6 0.9 %reshape.16.queries = bf16[64,1024]{1,0:T(8,128)(2,1)S(1)} reshape(bf16[16,4,1024]{2,1,0:T(4,128)(2,1)} %param.13) | data formatting | bytes 262144 | tf_op jit(solution)/shard_map/reshape | solution.py:256
  19.6 1.0 %copy-done.3 = bf16[16,128,128]{2,1,0:T(8,128)(2,1)S(1)} copy-done((bf16[16,128,128]{2,1,0:T(8,128)(2,1)S(1)}, bf16[16,128,128]{2,1,0:T(8,128)(2,1)}, u32[]{:S(2)}) %copy-start.3) | copy-done | bytes 524312
  20.6 2.1 %shard_map.114 = (f32[512,128]{1,0:T(8,128)S(1)}, bf16[512,64]{1,0:T(8,128)(2,1)S(1)}) custom-call(s32[16]{0:T(128)S(1)} %copy-done.5, bf16[64,1024]{1,0:T(8,128)(2,1)S(1)} %reshape.16.queries, bf16[64,128]{1,0:T(8,128)(2,1)S(1)} %bitcast.13, bf16[16,128,128]{2,1,0:T(8,128)(2,1)S(1)} %copy-done.2, bf16[16,128,128]{2,1,0:T(8,128)(2,1)S(1)} %copy-done.3), custom_call_target="tpu_custom_call" | custom-call | flops 536870912 | bytes 2097152 | tf_op jit(solution)/shard_map/pallas_call | solution.py:146
  22.7 1.5 %collective-permute-done.5 = bf16[64,1024]{1,0:T(8,128)(2,1)S(1)} collective-permute-done((bf16[64,1024]{1,0:T(8,128)(2,1)}, bf16[64,1024]{1,0:T(8,128)(2,1)S(1)}, u32[]{:S(2)}, u32[]{:S(2)}) %collective-permute-start.5) | collective-permute-done | bytes 131104 | tf_op jit(solution)/shard_map/ppermute | solution.py:27
  24.2 0.9 %pad_maximum_fusion.refs_1_ = bf16[2,64,1024]{2,1,0:T(8,128)(2,1)S(1)} fusion(bf16[1,64,1024]{2,1,0:T(8,128)(2,1)S(1)} %bitcast.14, bf16[1,64,1024]{2,1,0:T(8,128)(2,1)} %bitcast.5), kind=kLoop, calls=%fused_computation | loop fusion | flops 131072 | bytes 524288 | tf_op jit(solution)/shard_map/stack | solution.py:253
  25.1 3.1 %collective-permute-done.2.r2 = bf16[4,256,128]{2,1,0:T(8,128)(2,1)S(1)} collective-permute-done((bf16[4,256,128]{2,1,0:T(8,128)(2,1)}, bf16[4,256,128]{2,1,0:T(8,128)(2,1)S(1)}, u32[]{:S(2)}, u32[]{:S(2)}) %collective-permute-start.2) | collective-permute-done | bytes 262176 | tf_op jit(solution)/shard_map/ppermute | solution.py:27
  28.5 4.3 %collective-permute-start.10 = (bf16[2,64,1024]{2,1,0:T(8,128)(2,1)S(1)}, bf16[2,64,1024]{2,1,0:T(8,128)(2,1)S(1)}, u32[]{:S(2)}, u32[]{:S(2)}) collective-permute-start(bf16[2,64,1024]{2,1,0:T(8,128)(2,1)S(1)} %pad_maximum_fusion.refs_1_), channel_id=1, source_target_pairs={{0,1},{1,2},{2,3},{3,0},{4,5},{5,6},{6,7},{7,4},{8,9},{9,10},{10,1... | collective-permute-start | bytes 786440 | tf_op jit(solution)/shard_map/ppermute | solution.py:27
  32.8 3.8 %collective-permute-start.9 = (bf16[2,64,1024]{2,1,0:T(8,128)(2,1)S(1)}, bf16[2,64,1024]{2,1,0:T(8,128)(2,1)S(1)}, u32[]{:S(2)}, u32[]{:S(2)}) collective-permute-start(bf16[2,64,1024]{2,1,0:T(8,128)(2,1)S(1)} %pad_maximum_fusion.refs_1_), channel_id=1, source_target_pairs={{0,3},{1,0},{2,1},{3,2},{4,7},{5,4},{6,5},{7,6},{8,11},{9,8},{10,9... | collective-permute-start | bytes 786440 | tf_op jit(solution)/shard_map/ppermute | solution.py:27
  36.6 3.9 %collective-permute-start.6 = (bf16[256,128]{1,0:T(8,128)(2,1)S(1)}, bf16[256,128]{1,0:T(8,128)(2,1)S(1)}, u32[]{:S(2)}, u32[]{:S(2)}) collective-permute-start(bf16[256,128]{1,0:T(8,128)(2,1)S(1)} %get-tuple-element.52), channel_id=1, source_target_pairs={{0,64},{32,96},{64,0},{96,32},{1,65},{33,97},{65,1},{97,33},{2,66}... | collective-permute-start | bytes 196616 | tf_op jit(solution)/shard_map/ppermute | solution.py:27
  40.5 4.0 %collective-permute-start.7 = (bf16[256,128]{1,0:T(8,128)(2,1)S(1)}, bf16[256,128]{1,0:T(8,128)(2,1)S(1)}, u32[]{:S(2)}, u32[]{:S(2)}) collective-permute-start(bf16[256,128]{1,0:T(8,128)(2,1)S(1)} %get-tuple-element.53), channel_id=1, source_target_pairs={{0,32},{32,64},{64,96},{96,0},{1,33},{33,65},{65,97},{97,1},{2,34}... | collective-permute-start | bytes 196616 | tf_op jit(solution)/shard_map/ppermute | solution.py:27
  44.8 3.9 %collective-permute-done.7.r2 = bf16[256,128]{1,0:T(8,128)(2,1)S(1)} collective-permute-done((bf16[256,128]{1,0:T(8,128)(2,1)S(1)}, bf16[256,128]{1,0:T(8,128)(2,1)S(1)}, u32[]{:S(2)}, u32[]{:S(2)}) %collective-permute-start.7) | collective-permute-done | bytes 65568 | tf_op jit(solution)/shard_map/ppermute | solution.py:27
  48.7 1.5 %collective-permute-done.8.r3 = bf16[256,128]{1,0:T(8,128)(2,1)S(1)} collective-permute-done((bf16[256,128]{1,0:T(8,128)(2,1)S(1)}, bf16[256,128]{1,0:T(8,128)(2,1)S(1)}, u32[]{:S(2)}, u32[]{:S(2)}) %collective-permute-start.8) | collective-permute-done | bytes 65568 | tf_op jit(solution)/shard_map/ppermute | solution.py:27
  50.9 1.3 %collective-permute-start.14 = (bf16[256,128]{1,0:T(8,128)(2,1)S(1)}, bf16[256,128]{1,0:T(8,128)(2,1)S(1)}, u32[]{:S(2)}, u32[]{:S(2)}) collective-permute-start(bf16[256,128]{1,0:T(8,128)(2,1)S(1)} %get-tuple-element.64), channel_id=1, source_target_pairs={{0,8},{8,16},{16,24},{24,0},{1,9},{9,17},{17,25},{25,1},{2,10},{10... | collective-permute-start | bytes 196616 | tf_op jit(solution)/shard_map/ppermute | solution.py:27
  52.1 2.7 %collective-permute-start.13 = (bf16[256,128]{1,0:T(8,128)(2,1)S(1)}, bf16[256,128]{1,0:T(8,128)(2,1)S(1)}, u32[]{:S(2)}, u32[]{:S(2)}) collective-permute-start(bf16[256,128]{1,0:T(8,128)(2,1)S(1)} %get-tuple-element.64), channel_id=1, source_target_pairs={{0,16},{8,24},{16,0},{24,8},{1,17},{9,25},{17,1},{25,9},{2,18},{10... | collective-permute-start | bytes 196616 | tf_op jit(solution)/shard_map/ppermute | solution.py:27
  54.9 1.7 %collective-permute-start.12 = (bf16[256,128]{1,0:T(8,128)(2,1)S(1)}, bf16[256,128]{1,0:T(8,128)(2,1)S(1)}, u32[]{:S(2)}, u32[]{:S(2)}) collective-permute-start(bf16[256,128]{1,0:T(8,128)(2,1)S(1)} %get-tuple-element.64), channel_id=1, source_target_pairs={{0,24},{8,0},{16,8},{24,16},{1,25},{9,1},{17,9},{25,17},{2,26},{10... | collective-permute-start | bytes 196616 | tf_op jit(solution)/shard_map/ppermute | solution.py:27
  56.6 1.3 %collective-permute-done.13 = bf16[256,128]{1,0:T(8,128)(2,1)S(1)} collective-permute-done((bf16[256,128]{1,0:T(8,128)(2,1)S(1)}, bf16[256,128]{1,0:T(8,128)(2,1)S(1)}, u32[]{:S(2)}, u32[]{:S(2)}) %collective-permute-start.13) | collective-permute-done | bytes 65568 | tf_op jit(solution)/shard_map/ppermute | solution.py:27
  57.9 1.2 %collective-permute-done.12 = bf16[256,128]{1,0:T(8,128)(2,1)S(1)} collective-permute-done((bf16[256,128]{1,0:T(8,128)(2,1)S(1)}, bf16[256,128]{1,0:T(8,128)(2,1)S(1)}, u32[]{:S(2)}, u32[]{:S(2)}) %collective-permute-start.12) | collective-permute-done | bytes 65568 | tf_op jit(solution)/shard_map/ppermute | solution.py:27
  59.3 5.2 %collective-permute-done.11.refs_3_ = bf16[2,64,1024]{2,1,0:T(8,128)(2,1)S(1)} collective-permute-done((bf16[2,64,1024]{2,1,0:T(8,128)(2,1)S(1)}, bf16[2,64,1024]{2,1,0:T(8,128)(2,1)S(1)}, u32[]{:S(2)}, u32[]{:S(2)}) %collective-permute-start.11) | collective-permute-done | bytes 262176 | tf_op jit(solution)/shard_map/ppermute | solution.py:27
  66.2 12.1 %all_to_all.5.parts = bf16[4,64,128]{2,1,0:T(8,128)(2,1)S(1)} all-to-all(bf16[4,64,128]{2,1,0:T(8,128)(2,1)S(1)} %shard_map.118), channel_id=1, replica_groups=mesh['c'=2,'zh'=4,'x'=4,'zl'=2,'y'=4] {'zh'}, dimensions={0} | all-to-all | bytes 131072 | tf_op jit(solution)/shard_map/all_to_all | solution.py:283
  (36 shorter events, 6.5 us)
Async XLA Ops:
  0.6 18.9 %copy-start.5 = (s32[16]{0:T(128)S(1)}, s32[16]{0:T(128)}, u32[]{:S(2)}) copy-start(s32[16]{0:T(128)} %lengths.1) | copy-start | bytes 196
  0.6 18.9 %copy-start.4 = (bf16[16,4,128]{2,1,0:T(4,128)(2,1)S(1)}, bf16[16,4,128]{2,1,0:T(4,128)(2,1)}, u32[]{:S(2)}) copy-start(bf16[16,4,128]{2,1,0:T(4,128)(2,1)} %param.14) | copy-start | bytes 49156
  0.7 0.9 %copy-start = (bf16[768,128]{1,0:T(8,128)(2,1)S(1)}, bf16[768,128]{1,0:T(8,128)(2,1)}, u32[]{:S(2)}) copy-start(bf16[768,128]{1,0:T(8,128)(2,1)} %v_hbm.1) | copy-start | bytes 589828
  1.7 6.8 %copy-start.6 = (bf16[16,4,1024]{2,1,0:T(4,128)(2,1)S(1)}, bf16[16,4,1024]{2,1,0:T(4,128)(2,1)}, u32[]{:S(2)}) copy-start(bf16[16,4,1024]{2,1,0:T(4,128)(2,1)} %param.12) | copy-start | bytes 393220
  1.7 17.9 %copy-start.2 = (bf16[16,128,128]{2,1,0:T(8,128)(2,1)S(1)}, bf16[16,128,128]{2,1,0:T(8,128)(2,1)}, u32[]{:S(2)}) copy-start(bf16[16,128,128]{2,1,0:T(8,128)(2,1)} %cache_keys.1) | copy-start | bytes 1572868
  1.7 48.5 %copy-start.1 = (bf16[256,128]{1,0:T(8,128)(2,1)S(1)}, bf16[256,128]{1,0:T(8,128)(2,1)}, u32[]{:S(2)}) copy-start(bf16[256,128]{1,0:T(8,128)(2,1)} %weight.1) | copy-start | bytes 196612
  8.3 3.0 %collective-permute-start = (bf16[4,4,256,128]{3,2,1,0:T(8,128)(2,1)}, bf16[4,4,256,128]{3,2,1,0:T(8,128)(2,1)S(1)}, u32[]{:S(2)}, u32[]{:S(2)}) collective-permute-start(bf16[4,4,256,128]{3,2,1,0:T(8,128)(2,1)} %get-tuple-element.37), channel_id=1, source_target_pairs={{0,128},{128,0},{1,129},{129,1},{2,130},{130,2},{3,131},{131,3},{4... | collective-permute-start | bytes 3145736 | tf_op jit(solution)/shard_map/ppermute | solution.py:27
  9.1 9.3 %collective-permute-start.4 = (bf16[64,1024]{1,0:T(8,128)(2,1)}, bf16[64,1024]{1,0:T(8,128)(2,1)}, u32[]{:S(2)}, u32[]{:S(2)}) collective-permute-start(bf16[64,1024]{1,0:T(8,128)(2,1)} %reshape.15), channel_id=1, source_target_pairs={{0,0},{1,32},{2,64},{3,96},{32,1},{33,33},{34,65},{35,97},{64,2},{... | collective-permute-start | bytes 393224 | tf_op jit(solution)/shard_map/ppermute | solution.py:32
  12.2 12.9 %collective-permute-start.1 = (bf16[4,256,128]{2,1,0:T(8,128)(2,1)}, bf16[4,256,128]{2,1,0:T(8,128)(2,1)S(1)}, u32[]{:S(2)}, u32[]{:S(2)}) collective-permute-start(bf16[4,256,128]{2,1,0:T(8,128)(2,1)} %get-tuple-element.39), channel_id=1, source_target_pairs={{0,16},{8,24},{16,0},{24,8},{1,17},{9,25},{17,1},{25,9},{2,18},{10... | collective-permute-start | bytes 786440 | tf_op jit(solution)/shard_map/ppermute | solution.py:27
  15.2 13.0 %collective-permute-start.2 = (bf16[4,256,128]{2,1,0:T(8,128)(2,1)}, bf16[4,256,128]{2,1,0:T(8,128)(2,1)S(1)}, u32[]{:S(2)}, u32[]{:S(2)}) collective-permute-start(bf16[4,256,128]{2,1,0:T(8,128)(2,1)} %get-tuple-element.40), channel_id=1, source_target_pairs={{0,8},{8,16},{16,24},{24,0},{1,9},{9,17},{17,25},{25,1},{2,10},{10... | collective-permute-start | bytes 786440 | tf_op jit(solution)/shard_map/ppermute | solution.py:27
  15.8 12.5 %collective-permute-start.3 = (bf16[4,256,128]{2,1,0:T(8,128)(2,1)S(1)}, bf16[4,256,128]{2,1,0:T(8,128)(2,1)S(1)}, u32[]{:S(2)}, u32[]{:S(2)}) collective-permute-start(bf16[4,256,128]{2,1,0:T(8,128)(2,1)S(1)} %get-tuple-element.41), channel_id=1, source_target_pairs={{0,24},{8,0},{16,8},{24,16},{1,25},{9,1},{17,9},{25,17},{2,26},{10... | collective-permute-start | bytes 786440 | tf_op jit(solution)/shard_map/ppermute | solution.py:27
  18.5 5.7 %collective-permute-start.5 = (bf16[64,1024]{1,0:T(8,128)(2,1)}, bf16[64,1024]{1,0:T(8,128)(2,1)S(1)}, u32[]{:S(2)}, u32[]{:S(2)}) collective-permute-start(bf16[64,1024]{1,0:T(8,128)(2,1)} %collective-permute-done.4), channel_id=1, source_target_pairs={{0,4},{4,0},{1,5},{5,1},{2,6},{6,2},{3,7},{7,3},{8,12},{12,8},{9,1... | collective-permute-start | bytes 393224 | tf_op jit(solution)/shard_map/ppermute | solution.py:27
  19.6 1.0 %copy-start.3 = (bf16[16,128,128]{2,1,0:T(8,128)(2,1)S(1)}, bf16[16,128,128]{2,1,0:T(8,128)(2,1)}, u32[]{:S(2)}) copy-start(bf16[16,128,128]{2,1,0:T(8,128)(2,1)} %cache_values.1) | copy-start | bytes 1572868
  28.5 21.7 %collective-permute-start.10 = (bf16[2,64,1024]{2,1,0:T(8,128)(2,1)S(1)}, bf16[2,64,1024]{2,1,0:T(8,128)(2,1)S(1)}, u32[]{:S(2)}, u32[]{:S(2)}) collective-permute-start(bf16[2,64,1024]{2,1,0:T(8,128)(2,1)S(1)} %pad_maximum_fusion.refs_1_), channel_id=1, source_target_pairs={{0,1},{1,2},{2,3},{3,0},{4,5},{5,6},{6,7},{7,4},{8,9},{9,10},{10,1... | collective-permute-start | bytes 786440 | tf_op jit(solution)/shard_map/ppermute | solution.py:27
  32.8 17.4 %collective-permute-start.9 = (bf16[2,64,1024]{2,1,0:T(8,128)(2,1)S(1)}, bf16[2,64,1024]{2,1,0:T(8,128)(2,1)S(1)}, u32[]{:S(2)}, u32[]{:S(2)}) collective-permute-start(bf16[2,64,1024]{2,1,0:T(8,128)(2,1)S(1)} %pad_maximum_fusion.refs_1_), channel_id=1, source_target_pairs={{0,3},{1,0},{2,1},{3,2},{4,7},{5,4},{6,5},{7,6},{8,11},{9,8},{10,9... | collective-permute-start | bytes 786440 | tf_op jit(solution)/shard_map/ppermute | solution.py:27
  36.6 8.3 %collective-permute-start.6 = (bf16[256,128]{1,0:T(8,128)(2,1)S(1)}, bf16[256,128]{1,0:T(8,128)(2,1)S(1)}, u32[]{:S(2)}, u32[]{:S(2)}) collective-permute-start(bf16[256,128]{1,0:T(8,128)(2,1)S(1)} %get-tuple-element.52), channel_id=1, source_target_pairs={{0,64},{32,96},{64,0},{96,32},{1,65},{33,97},{65,1},{97,33},{2,66}... | collective-permute-start | bytes 196616 | tf_op jit(solution)/shard_map/ppermute | solution.py:27
  40.5 8.2 %collective-permute-start.7 = (bf16[256,128]{1,0:T(8,128)(2,1)S(1)}, bf16[256,128]{1,0:T(8,128)(2,1)S(1)}, u32[]{:S(2)}, u32[]{:S(2)}) collective-permute-start(bf16[256,128]{1,0:T(8,128)(2,1)S(1)} %get-tuple-element.53), channel_id=1, source_target_pairs={{0,32},{32,64},{64,96},{96,0},{1,33},{33,65},{65,97},{97,1},{2,34}... | collective-permute-start | bytes 196616 | tf_op jit(solution)/shard_map/ppermute | solution.py:27
  44.5 5.7 %collective-permute-start.8 = (bf16[256,128]{1,0:T(8,128)(2,1)S(1)}, bf16[256,128]{1,0:T(8,128)(2,1)S(1)}, u32[]{:S(2)}, u32[]{:S(2)}) collective-permute-start(bf16[256,128]{1,0:T(8,128)(2,1)S(1)} %get-tuple-element.54), channel_id=1, source_target_pairs={{0,96},{32,0},{64,32},{96,64},{1,97},{33,1},{65,33},{97,65},{2,98}... | collective-permute-start | bytes 196616 | tf_op jit(solution)/shard_map/ppermute | solution.py:27
  50.9 5.8 %collective-permute-start.14 = (bf16[256,128]{1,0:T(8,128)(2,1)S(1)}, bf16[256,128]{1,0:T(8,128)(2,1)S(1)}, u32[]{:S(2)}, u32[]{:S(2)}) collective-permute-start(bf16[256,128]{1,0:T(8,128)(2,1)S(1)} %get-tuple-element.64), channel_id=1, source_target_pairs={{0,8},{8,16},{16,24},{24,0},{1,9},{9,17},{17,25},{25,1},{2,10},{10... | collective-permute-start | bytes 196616 | tf_op jit(solution)/shard_map/ppermute | solution.py:27
  52.1 5.8 %collective-permute-start.13 = (bf16[256,128]{1,0:T(8,128)(2,1)S(1)}, bf16[256,128]{1,0:T(8,128)(2,1)S(1)}, u32[]{:S(2)}, u32[]{:S(2)}) collective-permute-start(bf16[256,128]{1,0:T(8,128)(2,1)S(1)} %get-tuple-element.64), channel_id=1, source_target_pairs={{0,16},{8,24},{16,0},{24,8},{1,17},{9,25},{17,1},{25,9},{2,18},{10... | collective-permute-start | bytes 196616 | tf_op jit(solution)/shard_map/ppermute | solution.py:27
  54.9 4.3 %collective-permute-start.12 = (bf16[256,128]{1,0:T(8,128)(2,1)S(1)}, bf16[256,128]{1,0:T(8,128)(2,1)S(1)}, u32[]{:S(2)}, u32[]{:S(2)}) collective-permute-start(bf16[256,128]{1,0:T(8,128)(2,1)S(1)} %get-tuple-element.64), channel_id=1, source_target_pairs={{0,24},{8,0},{16,8},{24,16},{1,25},{9,1},{17,9},{25,17},{2,26},{10... | collective-permute-start | bytes 196616 | tf_op jit(solution)/shard_map/ppermute | solution.py:27
  56.6 7.9 %collective-permute-start.11 = (bf16[2,64,1024]{2,1,0:T(8,128)(2,1)S(1)}, bf16[2,64,1024]{2,1,0:T(8,128)(2,1)S(1)}, u32[]{:S(2)}, u32[]{:S(2)}) collective-permute-start(bf16[2,64,1024]{2,1,0:T(8,128)(2,1)S(1)} %pad_maximum_fusion.refs_1_), channel_id=1, source_target_pairs={{0,2},{1,3},{2,0},{3,1},{4,6},{5,7},{6,4},{7,5},{8,10},{9,11},{10,... | collective-permute-start | bytes 786440 | tf_op jit(solution)/shard_map/ppermute | solution.py:27
  59.2 6.2 %collective-permute-start.15 = (bf16[4,256,128]{2,1,0:T(8,128)(2,1)S(1)}, bf16[4,256,128]{2,1,0:T(8,128)(2,1)S(1)}, u32[]{:S(2)}, u32[]{:S(2)}) collective-permute-start(bf16[4,256,128]{2,1,0:T(8,128)(2,1)S(1)} %pad_maximum_fusion.1.refs_5_), channel_id=1, source_target_pairs={{0,128},{128,0},{1,129},{129,1},{2,130},{130,2},{3,131},{131,3},{4... | collective-permute-start | bytes 786440 | tf_op jit(solution)/shard_map/ppermute | solution.py:27

commit v4 on v3

--- a/solution.py
+++ b/solution.py
@@ -91,8 +91,16 @@
 
 
 def core_sum_kernel(mine, received, o0, o1, o2, o3):
-    for d, out in enumerate((o0, o1, o2, o3)):
-        out[...] = (mine[d].astype(F32) + received[d].astype(F32)).astype(out.dtype)
+    o0[...] = mine[0].astype(F32) + received[0].astype(F32)
+    for d, out in ((1, o1), (2, o2), (3, o3)):
+        out[...] = mine[d] + received[d]
+
+
+def join_kernel(first, second, out):
+    rows, steps = first.shape[0], first.shape[1]
+    for i, ref in enumerate((first, second)):
+        for r in range(rows):
+            out[i, r * steps : (r + 1) * steps] = ref[r]
 
 
 def x_sum_kernel(own, r1, r2, r3, o0, o1, o2, o3):
@@ -101,10 +109,17 @@
         out[...] = total.astype(out.dtype)
 
 
-def update_kernel(weight, own, r1, r2, r3, gradient, updated):
-    total = own[...] + r1[...].astype(F32) + r2[...].astype(F32) + r3[...].astype(F32)
-    gradient[...] = total
+def total_of(own, r1, r2, r3):
+    return own[...] + r1[...].astype(F32) + r2[...].astype(F32) + r3[...].astype(F32)
+
+
+def update_kernel(weight, own, r1, r2, r3, updated):
+    total = total_of(own, r1, r2, r3)
     updated[...] = (weight[...].astype(F32) - STEP * total).astype(BF16)
+
+
+def gradient_kernel(own, r1, r2, r3, gradient):
+    gradient[...] = total_of(own, r1, r2, r3)
 
 
 def attend_kernel(lengths, queries, new_keys, cache_keys, cache_values, mixed_ref, weights_ref):
@@ -238,10 +253,10 @@
     places = row_count * step_count
     place = jnp.stack([core, high, x, y, low])
 
+    swapped = swap_high(decode_inputs)
     theirs, mine = partial_gradient(place, normed_inputs, value_cotangent)
+    theirs, mine, swapped = lax.optimization_barrier((theirs, mine, swapped))
     received = shift(theirs, "c", 1)
-
-    swapped = swap_high(after(decode_inputs.reshape(places, -1), theirs))
 
     rows = (4, 256, HD)
     own, *sent = small_call(
@@ -250,7 +265,7 @@
     along_x = [shift(sent[d - 1], "x", d) for d in (2, 1, 3)]
 
     swapped = after(swapped, own)
-    both = jnp.stack([swapped, shift(swapped, "zl", 1)])
+    second = shift(swapped, "zl", 1)
     attended_cache, fresh_weights = attend_cache(
         lengths,
         after(queries.reshape(places, -1), own),
@@ -258,23 +273,22 @@
         cache_keys,
         cache_values,
     )
-
-    own, *along_x, both, attended_cache, fresh_weights = lax.optimization_barrier(
-        (own, *along_x, both, attended_cache, fresh_weights)
+    swapped = after(swapped, attended_cache)
+    (both,) = small_call(join_kernel, [((2, places, D // 8), BF16)], swapped, second)
+    pieces = [both] + [shift(both, "y", -d) for d in (1, 2, 3)]
+
+    own, *along_x, attended_cache, fresh_weights = lax.optimization_barrier(
+        (own, *along_x, attended_cache, fresh_weights)
     )
     rows = (256, HD)
     own, *sent = small_call(
         x_sum_kernel, [(rows, F32)] + [(rows, BF16)] * 3, own, *along_x
     )
     along_z = [shift(sent[e - 1], "zh", e) for e in (2, 1, 3)]
-    both = after(both, own)
-    pieces = [both] + [shift(both, "y", -d) for d in (1, 2, 3)]
-    own, *along_z, pieces[1], pieces[3] = lax.optimization_barrier(
-        (own, *along_z, pieces[1], pieces[3])
-    )
-    gradient, updated = small_call(
-        update_kernel, [(rows, F32), (rows, BF16)], value_weight, own, *along_z
-    )
+    own, *along_z, pieces = lax.optimization_barrier((own, *along_z, pieces))
+    (updated,) = small_call(update_kernel, [(rows, BF16)], value_weight, own, *along_z)
+    own = after(own, updated)
+    (gradient,) = small_call(gradient_kernel, [(rows, F32)], own, *along_z)
 
     gathered = jnp.stack([updated] + [shift(updated, "x", -d) for d in (1, 2, 3)])
     other = shift(gathered, "c", 1)

time: 79.5 us -> 81.9 us (1.030)
  the two profiles are of different devices: /device:TPU:32 before, /device:TPU:1 now
where the time goes in v4:
time: 81.9 us; the launch traced here: 81.6 us
  starting transfers between devices  51.2 us (63%)
  waiting for transfers between devices  15.2 us (19%)
  Pallas kernels  13.4 us (16%)
  local copies, waits for them, and re-layouts  1.07 us (1%)
    ppermute x15, starting transfers between devices, shift(): return lax.ppermute(value, axis, [(i, (i + by) % n) for i in range(n)])  44 us
    ppermute x15, waiting for transfers between devices, shift(): return lax.ppermute(value, axis, [(i, (i + by) % n) for i in range(n)])  9 us
    all_to_all x1, waiting for transfers between devices, shards(): exchanged = lax.all_to_all(partial, 'zh', 0, 0, tiled=True)  6.2 us
    pallas_call x1, Pallas kernels, partial_gradient(): pl.pallas_call(partial_kernel, in_specs=[SMEM, HBM, HBM], out_specs=[VMEM...  6.11 us
    all_to_all x1, starting transfers between devices, shards(): exchanged = lax.all_to_all(partial, 'zh', 0, 0, tiled=True)  5.46 us
    pallas_call x2, Pallas kernels, project(): pl.pallas_call(kernel, in_specs=[SMEM] + [VMEM] * len(args), out_specs=VM...  2.35 us
    pallas_call x1, Pallas kernels, attend_cache(): pl.pallas_call(attend_kernel, in_specs=[SMEM] + [VMEM] * 4, out_specs=[VM...  2.14 us
    pallas_call x5, Pallas kernels, small_call(): pl.pallas_call(kernel, in_specs=[VMEM] * len(args), out_specs=[VMEM] * le...  1.92 us
  transfers between devices with their start and end apart: 17, of which 8 were waited for; matrix products, arithmetic and copies ran while one was open for 0% of the time, Pallas kernels for 12%

profile of v4, /device:TPU:1, one launch (start us, length us, event | category | flops | bytes accessed | tf_op | source)
XLA Modules:
  0.0 81.6 jit_solution(6385230217865500800)
XLA Ops:
  0.7 1.7 %collective-permute-start = (bf16[16,4,1024]{2,1,0:T(4,128)(2,1)}, bf16[16,4,1024]{2,1,0:T(4,128)(2,1)S(1)}, u32[]{:S(2)}, u32[]{:S(2)}) collective-permute-start(bf16[16,4,1024]{2,1,0:T(4,128)(2,1)} %param.12), channel_id=1, source_target_pairs={{0,0},{1,32},{2,64},{3,96},{32,1},{33,33},{34,65},{35,97},{64,2},{... | collective-permute-start | bytes 393224 | tf_op jit(solution)/shard_map/ppermute | solution.py:32
  2.4 0.9 %copy-done = bf16[768,128]{1,0:T(8,128)(2,1)S(1)} copy-done((bf16[768,128]{1,0:T(8,128)(2,1)S(1)}, bf16[768,128]{1,0:T(8,128)(2,1)}, u32[]{:S(2)}) %copy-start) | copy-done | bytes 196632
  3.4 6.1 %shard_map.112 = (bf16[4,4,256,128]{3,2,1,0:T(8,128)(2,1)S(1)}, bf16[4,4,256,128]{3,2,1,0:T(8,128)(2,1)S(1)}) custom-call(s32[5]{0:T(128)S(1)} %stack.38.place.refs_0_, bf16[768,8192]{1,0:T(8,128)(2,1)} %x_hbm.1, bf16[768,128]{1,0:T(8,128)(2,1)S(1)} %copy-done), custom_call_target="tpu_custom_call" | custom-call | flops 1610612736 | bytes 12582912 | tf_op jit(solution)/shard_map/pallas_call | solution.py:65
  9.5 3.3 %collective-permute-start.1 = (bf16[4,4,256,128]{3,2,1,0:T(8,128)(2,1)S(1)}, bf16[4,4,256,128]{3,2,1,0:T(8,128)(2,1)S(1)}, u32[]{:S(2)}, u32[]{:S(2)}) collective-permute-start(bf16[4,4,256,128]{3,2,1,0:T(8,128)(2,1)S(1)} %get-tuple-element.41), channel_id=1, source_target_pairs={{0,128},{128,0},{1,129},{129,1},{2,130},{130,2},{3,131},{131,3},{4... | collective-permute-start | bytes 3145736 | tf_op jit(solution)/shard_map/ppermute | solution.py:27
  12.8 2.3 %collective-permute-done.1.received = bf16[4,4,256,128]{3,2,1,0:T(8,128)(2,1)S(1)} collective-permute-done((bf16[4,4,256,128]{3,2,1,0:T(8,128)(2,1)S(1)}, bf16[4,4,256,128]{3,2,1,0:T(8,128)(2,1)S(1)}, u32[]{:S(2)}, u32[]{:S(2)}) %collective-permute-start.1) | collective-permute-done | bytes 1048608 | tf_op jit(solution)/shard_map/ppermute | solution.py:27
  15.1 1.0 %shard_map.113 = (f32[4,256,128]{2,1,0:T(8,128)S(1)}, bf16[4,256,128]{2,1,0:T(8,128)(2,1)}, bf16[4,256,128]{2,1,0:T(8,128)(2,1)}, bf16[4,256,128]{2,1,0:T(8,128)(2,1)S(1)}) custom-call(bf16[4,4,256,128]{3,2,1,0:T(8,128)(2,1)S(1)} %get-tuple-element.40.mine, bf16[4,4,256,128]{3,2,1,0:T(8,128)(2,1)S(1)} %collective-permute-done.1.received), custom_call_target="tpu_custom_call" | custom-call | flops 1048576 | bytes 2097152 | tf_op jit(solution)/shard_map/pallas_call | solution.py:83
  16.1 1.0 %collective-permute-start.2 = (bf16[4,256,128]{2,1,0:T(8,128)(2,1)}, bf16[4,256,128]{2,1,0:T(8,128)(2,1)S(1)}, u32[]{:S(2)}, u32[]{:S(2)}) collective-permute-start(bf16[4,256,128]{2,1,0:T(8,128)(2,1)} %get-tuple-element.43), channel_id=1, source_target_pairs={{0,16},{8,24},{16,0},{24,8},{1,17},{9,25},{17,1},{25,9},{2,18},{10... | collective-permute-start | bytes 786440 | tf_op jit(solution)/shard_map/ppermute | solution.py:27
  17.4 2.4 %collective-permute-start.4 = (bf16[4,256,128]{2,1,0:T(8,128)(2,1)S(1)}, bf16[4,256,128]{2,1,0:T(8,128)(2,1)S(1)}, u32[]{:S(2)}, u32[]{:S(2)}) collective-permute-start(bf16[4,256,128]{2,1,0:T(8,128)(2,1)S(1)} %get-tuple-element.45), channel_id=1, source_target_pairs={{0,24},{8,0},{16,8},{24,16},{1,25},{9,1},{17,9},{25,17},{2,26},{10... | collective-permute-start | bytes 786440 | tf_op jit(solution)/shard_map/ppermute | solution.py:27
  19.8 1.6 %collective-permute-start.8 = (bf16[16,4,1024]{2,1,0:T(4,128)(2,1)S(1)}, bf16[16,4,1024]{2,1,0:T(4,128)(2,1)S(1)}, u32[]{:S(2)}, u32[]{:S(2)}) collective-permute-start(bf16[16,4,1024]{2,1,0:T(4,128)(2,1)S(1)} %collective-permute-done.first), channel_id=1, source_target_pairs={{0,4},{4,0},{1,5},{5,1},{2,6},{6,2},{3,7},{7,3},{8,12},{12,8},{9,1... | collective-permute-start | bytes 393224 | tf_op jit(solution)/shard_map/ppermute | solution.py:27
  21.5 2.1 %shard_map.114 = (f32[512,128]{1,0:T(8,128)S(1)}, bf16[512,64]{1,0:T(8,128)(2,1)S(1)}) custom-call(s32[16]{0:T(128)S(1)} %copy-done.5, bf16[64,1024]{1,0:T(8,128)(2,1)S(1)} %reshape.12.queries, bf16[64,128]{1,0:T(8,128)(2,1)S(1)} %bitcast.11, bf16[16,128,128]{2,1,0:T(8,128)(2,1)S(1)} %copy-done.2, bf16[16,128,128]{2,1,0:T(8,128)(2,1)S(1)} %copy-done.3), custom_call_target="tpu_custom_call" | custom-call | flops 536870912 | bytes 2097152 | tf_op jit(solution)/shard_map/pallas_call | solution.py:161
  24.2 10.2 %collective-permute-start.10 = (bf16[2,64,1024]{2,1,0:T(8,128)(2,1)S(1)}, bf16[2,64,1024]{2,1,0:T(8,128)(2,1)S(1)}, u32[]{:S(2)}, u32[]{:S(2)}) collective-permute-start(bf16[2,64,1024]{2,1,0:T(8,128)(2,1)S(1)} %shard_map.116.refs_1_), channel_id=1, source_target_pairs={{0,2},{1,3},{2,0},{3,1},{4,6},{5,7},{6,4},{7,5},{8,10},{9,11},{10,... | collective-permute-start | bytes 786440 | tf_op jit(solution)/shard_map/ppermute | solution.py:27
  34.3 1.2 %collective-permute-start.11 = (bf16[2,64,1024]{2,1,0:T(8,128)(2,1)S(1)}, bf16[2,64,1024]{2,1,0:T(8,128)(2,1)S(1)}, u32[]{:S(2)}, u32[]{:S(2)}) collective-permute-start(bf16[2,64,1024]{2,1,0:T(8,128)(2,1)S(1)} %shard_map.116.refs_1_), channel_id=1, source_target_pairs={{0,1},{1,2},{2,3},{3,0},{4,5},{5,6},{6,7},{7,4},{8,9},{9,10},{10,1... | collective-permute-start | bytes 786440 | tf_op jit(solution)/shard_map/ppermute | solution.py:27
  35.5 1.5 %collective-permute-start.9 = (bf16[2,64,1024]{2,1,0:T(8,128)(2,1)S(1)}, bf16[2,64,1024]{2,1,0:T(8,128)(2,1)S(1)}, u32[]{:S(2)}, u32[]{:S(2)}) collective-permute-start(bf16[2,64,1024]{2,1,0:T(8,128)(2,1)S(1)} %shard_map.116.refs_1_), channel_id=1, source_target_pairs={{0,3},{1,0},{2,1},{3,2},{4,7},{5,4},{6,5},{7,6},{8,11},{9,8},{10,9... | collective-permute-start | bytes 786440 | tf_op jit(solution)/shard_map/ppermute | solution.py:27
  37.1 5.0 %collective-permute-start.5 = (bf16[256,128]{1,0:T(8,128)(2,1)S(1)}, bf16[256,128]{1,0:T(8,128)(2,1)S(1)}, u32[]{:S(2)}, u32[]{:S(2)}) collective-permute-start(bf16[256,128]{1,0:T(8,128)(2,1)S(1)} %get-tuple-element.54), channel_id=1, source_target_pairs={{0,64},{32,96},{64,0},{96,32},{1,65},{33,97},{65,1},{97,33},{2,66}... | collective-permute-start | bytes 196616 | tf_op jit(solution)/shard_map/ppermute | solution.py:27
  42.1 4.6 %collective-permute-start.6 = (bf16[256,128]{1,0:T(8,128)(2,1)S(1)}, bf16[256,128]{1,0:T(8,128)(2,1)S(1)}, u32[]{:S(2)}, u32[]{:S(2)}) collective-permute-start(bf16[256,128]{1,0:T(8,128)(2,1)S(1)} %get-tuple-element.55), channel_id=1, source_target_pairs={{0,32},{32,64},{64,96},{96,0},{1,33},{33,65},{65,97},{97,1},{2,34}... | collective-permute-start | bytes 196616 | tf_op jit(solution)/shard_map/ppermute | solution.py:27
  46.6 5.1 %collective-permute-start.7 = (bf16[256,128]{1,0:T(8,128)(2,1)S(1)}, bf16[256,128]{1,0:T(8,128)(2,1)S(1)}, u32[]{:S(2)}, u32[]{:S(2)}) collective-permute-start(bf16[256,128]{1,0:T(8,128)(2,1)S(1)} %get-tuple-element.56), channel_id=1, source_target_pairs={{0,96},{32,0},{64,32},{96,64},{1,97},{33,1},{65,33},{97,65},{2,98}... | collective-permute-start | bytes 196616 | tf_op jit(solution)/shard_map/ppermute | solution.py:27
  51.7 1.3 %collective-permute-done.7.r3 = bf16[256,128]{1,0:T(8,128)(2,1)S(1)} collective-permute-done((bf16[256,128]{1,0:T(8,128)(2,1)S(1)}, bf16[256,128]{1,0:T(8,128)(2,1)S(1)}, u32[]{:S(2)}, u32[]{:S(2)}) %collective-permute-start.7) | collective-permute-done | bytes 65568 | tf_op jit(solution)/shard_map/ppermute | solution.py:27
  53.1 3.7 %collective-permute-start.12 = (bf16[256,128]{1,0:T(8,128)(2,1)S(1)}, bf16[256,128]{1,0:T(8,128)(2,1)S(1)}, u32[]{:S(2)}, u32[]{:S(2)}) collective-permute-start(bf16[256,128]{1,0:T(8,128)(2,1)S(1)} %shard_map.117), channel_id=1, source_target_pairs={{0,24},{8,0},{16,8},{24,16},{1,25},{9,1},{17,9},{25,17},{2,26},{10... | collective-permute-start | bytes 196616 | tf_op jit(solution)/shard_map/ppermute | solution.py:27
  58.2 3.4 %collective-permute-done.13 = bf16[256,128]{1,0:T(8,128)(2,1)S(1)} collective-permute-done((bf16[256,128]{1,0:T(8,128)(2,1)S(1)}, bf16[256,128]{1,0:T(8,128)(2,1)S(1)}, u32[]{:S(2)}, u32[]{:S(2)}) %collective-permute-start.13) | collective-permute-done | bytes 65568 | tf_op jit(solution)/shard_map/ppermute | solution.py:27
  62.2 3.5 %collective-permute-start.15 = (bf16[4,256,128]{2,1,0:T(8,128)(2,1)S(1)}, bf16[4,256,128]{2,1,0:T(8,128)(2,1)S(1)}, u32[]{:S(2)}, u32[]{:S(2)}) collective-permute-start(bf16[4,256,128]{2,1,0:T(8,128)(2,1)S(1)} %pad_maximum_fusion.refs_5_), channel_id=1, source_target_pairs={{0,128},{128,0},{1,129},{129,1},{2,130},{130,2},{3,131},{131,3},{4... | collective-permute-start | bytes 786440 | tf_op jit(solution)/shard_map/ppermute | solution.py:27
  65.8 0.9 %shard_map.119.refs_6_ = f32[4,64,128]{2,1,0:T(8,128)S(1)} custom-call(s32[5]{0:T(128)S(1)} %stack.38.place.refs_0_, bf16[2,64,1024]{2,1,0:T(8,128)(2,1)S(1)} %shard_map.116.refs_1_, bf16[2,64,1024]{2,1,0:T(8,128)(2,1)S(1)} %collective-permute-done.9.refs_2_, bf16[2,64,1024]{2,1,0:T(8,128)(2,1)S(1)} %collective-permute-done.10.refs_3_, ...), custom_call_target="tpu_custom_call" | custom-call | flops 67108864 | bytes 786432 | tf_op jit(solution)/shard_map/pallas_call | solution.py:197
  66.9 1.5 %shard_map.120 = bf16[4,64,128]{2,1,0:T(8,128)(2,1)} custom-call(s32[5]{0:T(128)S(1)} %stack.38.place.refs_0_, bf16[2,64,1024]{2,1,0:T(8,128)(2,1)S(1)} %shard_map.116.refs_1_, bf16[2,64,1024]{2,1,0:T(8,128)(2,1)S(1)} %collective-permute-done.9.refs_2_, bf16[2,64,1024]{2,1,0:T(8,128)(2,1)S(1)} %collective-permute-done.10.refs_3_, ...), custom_call_target="tpu_custom_call" | custom-call | flops 67108864 | bytes 786432 | tf_op jit(solution)/shard_map/pallas_call | solution.py:197
  68.4 5.5 %all-to-all-start = ((bf16[4,64,128]{2,1,0:T(8,128)(2,1)}), bf16[4,64,128]{2,1,0:T(8,128)(2,1)S(1)}, u32[]{:S(2)}, u32[]{:S(2)}) async-start(bf16[4,64,128]{2,1,0:T(8,128)(2,1)} %shard_map.120), calls=%async_computation | async-start | bytes 131072 | tf_op jit(solution)/shard_map/all_to_all | solution.py:297
  74.6 6.2 %all-to-all-done.parts = bf16[4,64,128]{2,1,0:T(8,128)(2,1)S(1)} async-done(((bf16[4,64,128]{2,1,0:T(8,128)(2,1)}), bf16[4,64,128]{2,1,0:T(8,128)(2,1)S(1)}, u32[]{:S(2)}, u32[]{:S(2)}) %all-to-all-start) | async-done | bytes 65568 | tf_op jit(solution)/shard_map/all_to_all | solution.py:297
  (37 shorter events, 5.0 us)
Async XLA Ops:
  0.6 20.8 %copy-start.4 = (bf16[16,4,128]{2,1,0:T(4,128)(2,1)S(1)}, bf16[16,4,128]{2,1,0:T(4,128)(2,1)}, u32[]{:S(2)}) copy-start(bf16[16,4,128]{2,1,0:T(4,128)(2,1)} %param.14) | copy-start | bytes 49156
  0.6 20.8 %copy-start.5 = (s32[16]{0:T(128)S(1)}, s32[16]{0:T(128)}, u32[]{:S(2)}) copy-start(s32[16]{0:T(128)} %lengths.1) | copy-start | bytes 196
  0.7 8.8 %collective-permute-start = (bf16[16,4,1024]{2,1,0:T(4,128)(2,1)}, bf16[16,4,1024]{2,1,0:T(4,128)(2,1)S(1)}, u32[]{:S(2)}, u32[]{:S(2)}) collective-permute-start(bf16[16,4,1024]{2,1,0:T(4,128)(2,1)} %param.12), channel_id=1, source_target_pairs={{0,0},{1,32},{2,64},{3,96},{32,1},{33,33},{34,65},{35,97},{64,2},{... | collective-permute-start | bytes 393224 | tf_op jit(solution)/shard_map/ppermute | solution.py:32
  2.4 0.9 %copy-start = (bf16[768,128]{1,0:T(8,128)(2,1)S(1)}, bf16[768,128]{1,0:T(8,128)(2,1)}, u32[]{:S(2)}) copy-start(bf16[768,128]{1,0:T(8,128)(2,1)} %v_hbm.1) | copy-start | bytes 589828
  3.4 18.1 %copy-start.6 = (bf16[16,4,1024]{2,1,0:T(4,128)(2,1)S(1)}, bf16[16,4,1024]{2,1,0:T(4,128)(2,1)}, u32[]{:S(2)}) copy-start(bf16[16,4,1024]{2,1,0:T(4,128)(2,1)} %param.13) | copy-start | bytes 393220
  3.4 18.1 %copy-start.2 = (bf16[16,128,128]{2,1,0:T(8,128)(2,1)S(1)}, bf16[16,128,128]{2,1,0:T(8,128)(2,1)}, u32[]{:S(2)}) copy-start(bf16[16,128,128]{2,1,0:T(8,128)(2,1)} %cache_keys.1) | copy-start | bytes 1572868
  3.4 18.1 %copy-start.3 = (bf16[16,128,128]{2,1,0:T(8,128)(2,1)S(1)}, bf16[16,128,128]{2,1,0:T(8,128)(2,1)}, u32[]{:S(2)}) copy-start(bf16[16,128,128]{2,1,0:T(8,128)(2,1)} %cache_values.1) | copy-start | bytes 1572868
  3.4 49.7 %copy-start.1 = (bf16[256,128]{1,0:T(8,128)(2,1)S(1)}, bf16[256,128]{1,0:T(8,128)(2,1)}, u32[]{:S(2)}) copy-start(bf16[256,128]{1,0:T(8,128)(2,1)} %weight.1) | copy-start | bytes 196612
  9.5 5.6 %collective-permute-start.1 = (bf16[4,4,256,128]{3,2,1,0:T(8,128)(2,1)S(1)}, bf16[4,4,256,128]{3,2,1,0:T(8,128)(2,1)S(1)}, u32[]{:S(2)}, u32[]{:S(2)}) collective-permute-start(bf16[4,4,256,128]{3,2,1,0:T(8,128)(2,1)S(1)} %get-tuple-element.41), channel_id=1, source_target_pairs={{0,128},{128,0},{1,129},{129,1},{2,130},{130,2},{3,131},{131,3},{4... | collective-permute-start | bytes 3145736 | tf_op jit(solution)/shard_map/ppermute | solution.py:27
  16.1 19.4 %collective-permute-start.2 = (bf16[4,256,128]{2,1,0:T(8,128)(2,1)}, bf16[4,256,128]{2,1,0:T(8,128)(2,1)S(1)}, u32[]{:S(2)}, u32[]{:S(2)}) collective-permute-start(bf16[4,256,128]{2,1,0:T(8,128)(2,1)} %get-tuple-element.43), channel_id=1, source_target_pairs={{0,16},{8,24},{16,0},{24,8},{1,17},{9,25},{17,1},{25,9},{2,18},{10... | collective-permute-start | bytes 786440 | tf_op jit(solution)/shard_map/ppermute | solution.py:27
  17.1 19.9 %collective-permute-start.3 = (bf16[4,256,128]{2,1,0:T(8,128)(2,1)}, bf16[4,256,128]{2,1,0:T(8,128)(2,1)S(1)}, u32[]{:S(2)}, u32[]{:S(2)}) collective-permute-start(bf16[4,256,128]{2,1,0:T(8,128)(2,1)} %get-tuple-element.44), channel_id=1, source_target_pairs={{0,8},{8,16},{16,24},{24,0},{1,9},{9,17},{17,25},{25,1},{2,10},{10... | collective-permute-start | bytes 786440 | tf_op jit(solution)/shard_map/ppermute | solution.py:27
  17.4 19.6 %collective-permute-start.4 = (bf16[4,256,128]{2,1,0:T(8,128)(2,1)S(1)}, bf16[4,256,128]{2,1,0:T(8,128)(2,1)S(1)}, u32[]{:S(2)}, u32[]{:S(2)}) collective-permute-start(bf16[4,256,128]{2,1,0:T(8,128)(2,1)S(1)} %get-tuple-element.45), channel_id=1, source_target_pairs={{0,24},{8,0},{16,8},{24,16},{1,25},{9,1},{17,9},{25,17},{2,26},{10... | collective-permute-start | bytes 786440 | tf_op jit(solution)/shard_map/ppermute | solution.py:27
  19.8 4.3 %collective-permute-start.8 = (bf16[16,4,1024]{2,1,0:T(4,128)(2,1)S(1)}, bf16[16,4,1024]{2,1,0:T(4,128)(2,1)S(1)}, u32[]{:S(2)}, u32[]{:S(2)}) collective-permute-start(bf16[16,4,1024]{2,1,0:T(4,128)(2,1)S(1)} %collective-permute-done.first), channel_id=1, source_target_pairs={{0,4},{4,0},{1,5},{5,1},{2,6},{6,2},{3,7},{7,3},{8,12},{12,8},{9,1... | collective-permute-start | bytes 393224 | tf_op jit(solution)/shard_map/ppermute | solution.py:27
  24.2 28.9 %collective-permute-start.10 = (bf16[2,64,1024]{2,1,0:T(8,128)(2,1)S(1)}, bf16[2,64,1024]{2,1,0:T(8,128)(2,1)S(1)}, u32[]{:S(2)}, u32[]{:S(2)}) collective-permute-start(bf16[2,64,1024]{2,1,0:T(8,128)(2,1)S(1)} %shard_map.116.refs_1_), channel_id=1, source_target_pairs={{0,2},{1,3},{2,0},{3,1},{4,6},{5,7},{6,4},{7,5},{8,10},{9,11},{10,... | collective-permute-start | bytes 786440 | tf_op jit(solution)/shard_map/ppermute | solution.py:27
  34.3 18.7 %collective-permute-start.11 = (bf16[2,64,1024]{2,1,0:T(8,128)(2,1)S(1)}, bf16[2,64,1024]{2,1,0:T(8,128)(2,1)S(1)}, u32[]{:S(2)}, u32[]{:S(2)}) collective-permute-start(bf16[2,64,1024]{2,1,0:T(8,128)(2,1)S(1)} %shard_map.116.refs_1_), channel_id=1, source_target_pairs={{0,1},{1,2},{2,3},{3,0},{4,5},{5,6},{6,7},{7,4},{8,9},{9,10},{10,1... | collective-permute-start | bytes 786440 | tf_op jit(solution)/shard_map/ppermute | solution.py:27
  35.5 17.6 %collective-permute-start.9 = (bf16[2,64,1024]{2,1,0:T(8,128)(2,1)S(1)}, bf16[2,64,1024]{2,1,0:T(8,128)(2,1)S(1)}, u32[]{:S(2)}, u32[]{:S(2)}) collective-permute-start(bf16[2,64,1024]{2,1,0:T(8,128)(2,1)S(1)} %shard_map.116.refs_1_), channel_id=1, source_target_pairs={{0,3},{1,0},{2,1},{3,2},{4,7},{5,4},{6,5},{7,6},{8,11},{9,8},{10,9... | collective-permute-start | bytes 786440 | tf_op jit(solution)/shard_map/ppermute | solution.py:27
  37.1 9.5 %collective-permute-start.5 = (bf16[256,128]{1,0:T(8,128)(2,1)S(1)}, bf16[256,128]{1,0:T(8,128)(2,1)S(1)}, u32[]{:S(2)}, u32[]{:S(2)}) collective-permute-start(bf16[256,128]{1,0:T(8,128)(2,1)S(1)} %get-tuple-element.54), channel_id=1, source_target_pairs={{0,64},{32,96},{64,0},{96,32},{1,65},{33,97},{65,1},{97,33},{2,66}... | collective-permute-start | bytes 196616 | tf_op jit(solution)/shard_map/ppermute | solution.py:27
  42.1 9.7 %collective-permute-start.6 = (bf16[256,128]{1,0:T(8,128)(2,1)S(1)}, bf16[256,128]{1,0:T(8,128)(2,1)S(1)}, u32[]{:S(2)}, u32[]{:S(2)}) collective-permute-start(bf16[256,128]{1,0:T(8,128)(2,1)S(1)} %get-tuple-element.55), channel_id=1, source_target_pairs={{0,32},{32,64},{64,96},{96,0},{1,33},{33,65},{65,97},{97,1},{2,34}... | collective-permute-start | bytes 196616 | tf_op jit(solution)/shard_map/ppermute | solution.py:27
  46.6 6.4 %collective-permute-start.7 = (bf16[256,128]{1,0:T(8,128)(2,1)S(1)}, bf16[256,128]{1,0:T(8,128)(2,1)S(1)}, u32[]{:S(2)}, u32[]{:S(2)}) collective-permute-start(bf16[256,128]{1,0:T(8,128)(2,1)S(1)} %get-tuple-element.56), channel_id=1, source_target_pairs={{0,96},{32,0},{64,32},{96,64},{1,97},{33,1},{65,33},{97,65},{2,98}... | collective-permute-start | bytes 196616 | tf_op jit(solution)/shard_map/ppermute | solution.py:27
  53.1 5.1 %collective-permute-start.12 = (bf16[256,128]{1,0:T(8,128)(2,1)S(1)}, bf16[256,128]{1,0:T(8,128)(2,1)S(1)}, u32[]{:S(2)}, u32[]{:S(2)}) collective-permute-start(bf16[256,128]{1,0:T(8,128)(2,1)S(1)} %shard_map.117), channel_id=1, source_target_pairs={{0,24},{8,0},{16,8},{24,16},{1,25},{9,1},{17,9},{25,17},{2,26},{10... | collective-permute-start | bytes 196616 | tf_op jit(solution)/shard_map/ppermute | solution.py:27
  56.9 4.7 %collective-permute-start.13 = (bf16[256,128]{1,0:T(8,128)(2,1)S(1)}, bf16[256,128]{1,0:T(8,128)(2,1)S(1)}, u32[]{:S(2)}, u32[]{:S(2)}) collective-permute-start(bf16[256,128]{1,0:T(8,128)(2,1)S(1)} %shard_map.117), channel_id=1, source_target_pairs={{0,16},{8,24},{16,0},{24,8},{1,17},{9,25},{17,1},{25,9},{2,18},{10... | collective-permute-start | bytes 196616 | tf_op jit(solution)/shard_map/ppermute | solution.py:27
  57.3 4.9 %collective-permute-start.14 = (bf16[256,128]{1,0:T(8,128)(2,1)S(1)}, bf16[256,128]{1,0:T(8,128)(2,1)S(1)}, u32[]{:S(2)}, u32[]{:S(2)}) collective-permute-start(bf16[256,128]{1,0:T(8,128)(2,1)S(1)} %shard_map.117), channel_id=1, source_target_pairs={{0,8},{8,16},{16,24},{24,0},{1,9},{9,17},{17,25},{25,1},{2,10},{10... | collective-permute-start | bytes 196616 | tf_op jit(solution)/shard_map/ppermute | solution.py:27
  62.2 4.7 %collective-permute-start.15 = (bf16[4,256,128]{2,1,0:T(8,128)(2,1)S(1)}, bf16[4,256,128]{2,1,0:T(8,128)(2,1)S(1)}, u32[]{:S(2)}, u32[]{:S(2)}) collective-permute-start(bf16[4,256,128]{2,1,0:T(8,128)(2,1)S(1)} %pad_maximum_fusion.refs_5_), channel_id=1, source_target_pairs={{0,128},{128,0},{1,129},{129,1},{2,130},{130,2},{3,131},{131,3},{4... | collective-permute-start | bytes 786440 | tf_op jit(solution)/shard_map/ppermute | solution.py:27
  68.4 12.3 %all-to-all-start = ((bf16[4,64,128]{2,1,0:T(8,128)(2,1)}), bf16[4,64,128]{2,1,0:T(8,128)(2,1)S(1)}, u32[]{:S(2)}, u32[]{:S(2)}) async-start(bf16[4,64,128]{2,1,0:T(8,128)(2,1)} %shard_map.120), calls=%async_computation | async-start | bytes 131072 | tf_op jit(solution)/shard_map/all_to_all | solution.py:297

commit v5 on v4

--- a/solution.py
+++ b/solution.py
@@ -27,9 +27,15 @@
     return lax.ppermute(value, axis, [(i, (i + by) % n) for i in range(n)])
 
 
-def swap_high(value):
-    pairs = [(zh * 4 + y, y * 4 + zh) for zh in range(4) for y in range(4)]
-    return lax.ppermute(value, ("zh", "y"), pairs)
+def swap_places(value):
+    names = ("c", "zh", "zl", "y")
+    sizes = [SIZES[n] for n in names]
+    pairs = []
+    for c, zh, zl, y in np.ndindex(*sizes):
+        source = int(np.ravel_multi_index((c, zh, zl, y), sizes))
+        target = int(np.ravel_multi_index((zl, y, c, (zh + y) % 4), sizes))
+        pairs.append((source, target))
+    return lax.ppermute(value, names, pairs)
 
 
 def after(value, *others):
@@ -168,49 +174,42 @@
         ],
         compiler_params=pltpu.CompilerParams(vmem_limit_bytes=16 * MIB),
         cost_estimate=pl.CostEstimate(
-            flops=2 * 16 * 512 * 256 * HD, bytes_accessed=2 * MIB, transcendentals=512 * 192
+            flops=MIB, bytes_accessed=MIB // 4, transcendentals=0
         ),
     )(lengths, queries, new_keys, cache_keys, cache_values)
 
 
-def project_kernel(first, place, d0, d1, d2, d3, u, *refs):
-    core, x, y, low = place[0], place[2], place[3], place[4]
-    start, out_ref, rows = (None, *refs) if first else refs
-    own = jnp.where(core == low, 0, 1) if first else jnp.where(core == low, 1, 0)
-    for d in range(4):
-        rows[pl.ds(pl.multiple_of(lax.rem(x + d, 4) * 256, 256), 256), :] = u[d]
+def project_kernel(place, d0, d1, d2, d3, u0, u1, u2, u3, out_ref, rows):
+    high, x, y, low = place[1], place[2], place[3], place[4]
+    for d, u in enumerate((u0, u1, u2, u3)):
+        rows[pl.ds(pl.multiple_of(lax.rem(x + d, 4) * 256, 256), 256), :] = u[...]
     for d, piece in enumerate((d0, d1, d2, d3)):
-        zh = lax.rem(y + d, 4)
-        product = jnp.dot(piece[own], rows[...], preferred_element_type=F32)
-        if start is not None:
-            product += start[zh]
-        out_ref[zh] = product.astype(out_ref.dtype)
-
-
-def project(place, pieces, updated, start=None):
-    first = start is None
-
-    def kernel(*refs):
-        project_kernel(first, *refs)
-
-    args = (*pieces, updated) if first else (*pieces, updated, start)
-    return pl.pallas_call(
-        kernel,
-        in_specs=[SMEM] + [VMEM] * len(args),
+        zh = lax.rem(y + d + 4 - high, 4)
+        for j in range(2):
+            core = low if j == 0 else 1 - low
+            product = jnp.dot(piece[j], rows[...], preferred_element_type=F32)
+            out_ref[core * 4 + zh] = product.astype(out_ref.dtype)
+
+
+def project(place, pieces, updated):
+    places = pieces[0].shape[1]
+    return pl.pallas_call(
+        project_kernel,
+        in_specs=[SMEM] + [VMEM] * 8,
         out_specs=VMEM,
-        out_shape=jax.ShapeDtypeStruct((4, 64, HD), F32 if first else BF16),
+        out_shape=jax.ShapeDtypeStruct((8, places, HD), BF16),
         scratch_shapes=[pltpu.VMEM((1024, HD), BF16)],
         compiler_params=pltpu.CompilerParams(vmem_limit_bytes=16 * MIB),
         cost_estimate=pl.CostEstimate(
-            flops=2 * 256 * 1024 * HD, bytes_accessed=3 * MIB // 4, transcendentals=0
-        ),
-    )(place, *args)
+            flops=2 * 512 * 1024 * HD, bytes_accessed=3 * MIB // 2, transcendentals=0
+        ),
+    )(place, *pieces, *updated)
 
 
 def finish_kernel(parts, mixed, weights, values_ref, attended_ref):
     steps = values_ref.shape[1]
     total = parts[0].astype(F32)
-    for i in range(1, 4):
+    for i in range(1, 8):
         total += parts[i].astype(F32)
     values = total.astype(BF16)
     for r in range(values_ref.shape[0]):
@@ -253,48 +252,44 @@
     places = row_count * step_count
     place = jnp.stack([core, high, x, y, low])
 
-    swapped = swap_high(decode_inputs)
+    swapped = swap_places(decode_inputs)
     theirs, mine = partial_gradient(place, normed_inputs, value_cotangent)
     theirs, mine, swapped = lax.optimization_barrier((theirs, mine, swapped))
     received = shift(theirs, "c", 1)
-
+    second = shift(swapped, "zl", 1)
+
+    mine, received, swapped = lax.optimization_barrier((mine, received, swapped))
     rows = (4, 256, HD)
     own, *sent = small_call(
         core_sum_kernel, [(rows, F32)] + [(rows, BF16)] * 3, mine, received
     )
     along_x = [shift(sent[d - 1], "x", d) for d in (2, 1, 3)]
-
     swapped = after(swapped, own)
-    second = shift(swapped, "zl", 1)
+    (both,) = small_call(join_kernel, [((2, places, D // 8), BF16)], swapped, second)
+    pieces = [both] + [shift(both, "y", -d) for d in (1, 3, 2)]
+    pieces = [pieces[0], pieces[1], pieces[3], pieces[2]]
+
+    rows = (256, HD)
+    own, *sent = small_call(
+        x_sum_kernel, [(rows, F32)] + [(rows, BF16)] * 3, own, *along_x
+    )
+    sent[2], pieces[1] = lax.optimization_barrier((sent[2], pieces[1]))
+    along_z = [shift(sent[e - 1], "zh", e) for e in (2, 1, 3)]
+    own, *along_z, pieces = lax.optimization_barrier((own, *along_z, pieces))
+    (updated,) = small_call(update_kernel, [(rows, BF16)], value_weight, own, *along_z)
     attended_cache, fresh_weights = attend_cache(
         lengths,
-        after(queries.reshape(places, -1), own),
+        after(queries.reshape(places, -1), updated),
         new_keys.reshape(places, HD),
         cache_keys,
         cache_values,
     )
-    swapped = after(swapped, attended_cache)
-    (both,) = small_call(join_kernel, [((2, places, D // 8), BF16)], swapped, second)
-    pieces = [both] + [shift(both, "y", -d) for d in (1, 2, 3)]
-
-    own, *along_x, attended_cache, fresh_weights = lax.optimization_barrier(
-        (own, *along_x, attended_cache, fresh_weights)
-    )
-    rows = (256, HD)
-    own, *sent = small_call(
-        x_sum_kernel, [(rows, F32)] + [(rows, BF16)] * 3, own, *along_x
-    )
-    along_z = [shift(sent[e - 1], "zh", e) for e in (2, 1, 3)]
-    own, *along_z, pieces = lax.optimization_barrier((own, *along_z, pieces))
-    (updated,) = small_call(update_kernel, [(rows, BF16)], value_weight, own, *along_z)
     own = after(own, updated)
     (gradient,) = small_call(gradient_kernel, [(rows, F32)], own, *along_z)
 
-    gathered = jnp.stack([updated] + [shift(updated, "x", -d) for d in (1, 2, 3)])
-    other = shift(gathered, "c", 1)
+    gathered = [updated] + [shift(updated, "x", -d) for d in (1, 2, 3)]
     partial = project(place, pieces, gathered)
-    partial = project(place, pieces, other, partial)
-    exchanged = lax.all_to_all(partial, "zh", 0, 0, tiled=True)
+    exchanged = lax.all_to_all(partial, ("c", "zh"), 0, 0, tiled=True)
     new_values, attended = finish(
         exchanged, attended_cache, fresh_weights, row_count, step_count
     )

time: 81.9 us -> 82.8 us (1.011)
  waiting for transfers between devices: 15.2 us -> 30.3 us
  starting transfers between devices: 51.2 us -> 38.6 us
  Pallas kernels: 13.4 us -> 11.9 us
    ppermute x15 -> x14, starting transfers between devices: 44 us -> 25.3 us  [shift(): return lax.ppermute(value, axis, [(i, (i + by) % n) for i in range(n)])]
    ppermute x15 -> x14, waiting for transfers between devices: 9 us -> 24.9 us  [shift(): return lax.ppermute(value, axis, [(i, (i + by) % n) for i in range(n)])]
    ppermute x1, starting transfers between devices: 1.69 us -> 5.07 us  [swap_places(): return lax.ppermute(value, names, pairs)]
    all_to_all x1, starting transfers between devices: 5.46 us -> 8.25 us  [shards(): exchanged = lax.all_to_all(partial, ('c', 'zh'), 0, 0, tiled=True)]
    all_to_all x1, waiting for transfers between devices: 6.2 us -> 5.33 us  [shards(): exchanged = lax.all_to_all(partial, ('c', 'zh'), 0, 0, tiled=True)]
    pallas_call x2 -> x1, Pallas kernels: 2.35 us -> 1.65 us  [project(): pl.pallas_call(project_kernel, in_specs=[SMEM] + [VMEM] * 8, out_specs=VM...]
  transfers between devices with their start and end apart: 17 -> 16, of which waited for: 8 -> 10; matrix products, arithmetic and copies ran while one was open for 0% -> 0% of each run, Pallas kernels for 12% -> 11%
where the time goes in v5:
time: 82.8 us; the launch traced here: 82.5 us
  starting transfers between devices  38.6 us (47%)
  waiting for transfers between devices  30.3 us (37%)
  Pallas kernels  11.9 us (14%)
  local copies, waits for them, and re-layouts  1.07 us (1%)
    ppermute x14, starting transfers between devices, shift(): return lax.ppermute(value, axis, [(i, (i + by) % n) for i in range(n)])  25.3 us
    ppermute x14, waiting for transfers between devices, shift(): return lax.ppermute(value, axis, [(i, (i + by) % n) for i in range(n)])  24.9 us
    all_to_all x1, starting transfers between devices, shards(): exchanged = lax.all_to_all(partial, ('c', 'zh'), 0, 0, tiled=True)  8.25 us
    pallas_call x1, Pallas kernels, partial_gradient(): pl.pallas_call(partial_kernel, in_specs=[SMEM, HBM, HBM], out_specs=[VMEM...  6.11 us
    all_to_all x1, waiting for transfers between devices, shards(): exchanged = lax.all_to_all(partial, ('c', 'zh'), 0, 0, tiled=True)  5.33 us
    ppermute x1, starting transfers between devices, swap_places(): return lax.ppermute(value, names, pairs)  5.07 us
    pallas_call x1, Pallas kernels, attend_cache(): pl.pallas_call(attend_kernel, in_specs=[SMEM] + [VMEM] * 4, out_specs=[VM...  2.12 us
  transfers between devices with their start and end apart: 16, of which 10 were waited for; matrix products, arithmetic and copies ran while one was open for 0% of the time, Pallas kernels for 11%

profile of v5, /device:TPU:1, one launch (start us, length us, event | category | flops | bytes accessed | tf_op | source)
XLA Modules:
  0.0 82.5 jit_solution(8166963627829750410)
XLA Ops:
  0.7 5.1 %collective-permute-start = (bf16[16,4,1024]{2,1,0:T(4,128)(2,1)}, bf16[16,4,1024]{2,1,0:T(4,128)(2,1)S(1)}, u32[]{:S(2)}, u32[]{:S(2)}) collective-permute-start(bf16[16,4,1024]{2,1,0:T(4,128)(2,1)} %param.12), channel_id=1, source_target_pairs={{0,0},{1,33},{2,66},{3,99},{4,128},{5,161},{6,194},{7,227},{32,1},... | collective-permute-start | bytes 393224 | tf_op jit(solution)/shard_map/ppermute | solution.py:38
  5.8 0.9 %copy-done.2 = bf16[768,128]{1,0:T(8,128)(2,1)S(1)} copy-done((bf16[768,128]{1,0:T(8,128)(2,1)S(1)}, bf16[768,128]{1,0:T(8,128)(2,1)}, u32[]{:S(2)}) %copy-start.2) | copy-done | bytes 196632
  6.8 6.1 %shard_map.112 = (bf16[4,4,256,128]{3,2,1,0:T(8,128)(2,1)S(1)}, bf16[4,4,256,128]{3,2,1,0:T(8,128)(2,1)S(1)}) custom-call(s32[5]{0:T(128)S(1)} %stack.23.place, bf16[768,8192]{1,0:T(8,128)(2,1)} %x_hbm.1, bf16[768,128]{1,0:T(8,128)(2,1)S(1)} %copy-done.2), custom_call_target="tpu_custom_call" | custom-call | flops 1610612736 | bytes 12582912 | tf_op jit(solution)/shard_map/pallas_call | solution.py:71
  13.0 2.6 %collective-permute-done.1.received = bf16[4,4,256,128]{3,2,1,0:T(8,128)(2,1)S(1)} collective-permute-done((bf16[4,4,256,128]{3,2,1,0:T(8,128)(2,1)S(1)}, bf16[4,4,256,128]{3,2,1,0:T(8,128)(2,1)S(1)}, u32[]{:S(2)}, u32[]{:S(2)}) %collective-permute-start.1) | collective-permute-done | bytes 1048608 | tf_op jit(solution)/shard_map/ppermute | solution.py:27
  15.8 2.8 %collective-permute-start.2 = (bf16[4,256,128]{2,1,0:T(8,128)(2,1)S(1)}, bf16[4,256,128]{2,1,0:T(8,128)(2,1)S(1)}, u32[]{:S(2)}, u32[]{:S(2)}) collective-permute-start(bf16[4,256,128]{2,1,0:T(8,128)(2,1)S(1)} %get-tuple-element.44), channel_id=1, source_target_pairs={{0,16},{8,24},{16,0},{24,8},{1,17},{9,25},{17,1},{25,9},{2,18},{10... | collective-permute-start | bytes 786440 | tf_op jit(solution)/shard_map/ppermute | solution.py:27
  19.0 2.4 %collective-permute-start.4 = (bf16[4,256,128]{2,1,0:T(8,128)(2,1)S(1)}, bf16[4,256,128]{2,1,0:T(8,128)(2,1)S(1)}, u32[]{:S(2)}, u32[]{:S(2)}) collective-permute-start(bf16[4,256,128]{2,1,0:T(8,128)(2,1)S(1)} %get-tuple-element.46), channel_id=1, source_target_pairs={{0,24},{8,0},{16,8},{24,16},{1,25},{9,1},{17,9},{25,17},{2,26},{10... | collective-permute-start | bytes 786440 | tf_op jit(solution)/shard_map/ppermute | solution.py:27
  21.4 2.0 %collective-permute-done.7.second = bf16[16,4,1024]{2,1,0:T(4,128)(2,1)S(1)} collective-permute-done((bf16[16,4,1024]{2,1,0:T(4,128)(2,1)S(1)}, bf16[16,4,1024]{2,1,0:T(4,128)(2,1)S(1)}, u32[]{:S(2)}, u32[]{:S(2)}) %collective-permute-start.7) | collective-permute-done | bytes 131104 | tf_op jit(solution)/shard_map/ppermute | solution.py:27
  23.4 9.0 %collective-permute-start.8 = (bf16[2,64,1024]{2,1,0:T(8,128)(2,1)S(1)}, bf16[2,64,1024]{2,1,0:T(8,128)(2,1)S(1)}, u32[]{:S(2)}, u32[]{:S(2)}) collective-permute-start(bf16[2,64,1024]{2,1,0:T(8,128)(2,1)S(1)} %shard_map.115.d0), channel_id=1, source_target_pairs={{0,3},{1,0},{2,1},{3,2},{4,7},{5,4},{6,5},{7,6},{8,11},{9,8},{10,9... | collective-permute-start | bytes 786440 | tf_op jit(solution)/shard_map/ppermute | solution.py:27
  32.4 0.7 collective-permute-start.11
  33.2 9.8 %collective-permute-done.8.d1 = bf16[2,64,1024]{2,1,0:T(8,128)(2,1)S(1)} collective-permute-done((bf16[2,64,1024]{2,1,0:T(8,128)(2,1)S(1)}, bf16[2,64,1024]{2,1,0:T(8,128)(2,1)S(1)}, u32[]{:S(2)}, u32[]{:S(2)}) %collective-permute-start.8) | collective-permute-done | bytes 262176 | tf_op jit(solution)/shard_map/ppermute | solution.py:27
  43.0 7.8 %collective-permute-start.5 = (bf16[256,128]{1,0:T(8,128)(2,1)S(1)}, bf16[256,128]{1,0:T(8,128)(2,1)S(1)}, u32[]{:S(2)}, u32[]{:S(2)}) collective-permute-start(bf16[256,128]{1,0:T(8,128)(2,1)S(1)} %get-tuple-element.48), channel_id=1, source_target_pairs={{0,64},{32,96},{64,0},{96,32},{1,65},{33,97},{65,1},{97,33},{2,66}... | collective-permute-start | bytes 196616 | tf_op jit(solution)/shard_map/ppermute | solution.py:27
  51.1 1.4 %collective-permute-done.5.r1 = bf16[256,128]{1,0:T(8,128)(2,1)S(1)} collective-permute-done((bf16[256,128]{1,0:T(8,128)(2,1)S(1)}, bf16[256,128]{1,0:T(8,128)(2,1)S(1)}, u32[]{:S(2)}, u32[]{:S(2)}) %collective-permute-start.5) | collective-permute-done | bytes 65568 | tf_op jit(solution)/shard_map/ppermute | solution.py:27
  52.5 4.5 %collective-permute-done.6.r2 = bf16[256,128]{1,0:T(8,128)(2,1)S(1)} collective-permute-done((bf16[256,128]{1,0:T(8,128)(2,1)S(1)}, bf16[256,128]{1,0:T(8,128)(2,1)S(1)}, u32[]{:S(2)}, u32[]{:S(2)}) %collective-permute-start.6) | collective-permute-done | bytes 65568 | tf_op jit(solution)/shard_map/ppermute | solution.py:27
  57.1 0.9 %collective-permute-start.12 = (bf16[256,128]{1,0:T(8,128)(2,1)S(1)}, bf16[256,128]{1,0:T(8,128)(2,1)S(1)}, u32[]{:S(2)}, u32[]{:S(2)}) collective-permute-start(bf16[256,128]{1,0:T(8,128)(2,1)S(1)} %shard_map.116.u0), channel_id=1, source_target_pairs={{0,24},{8,0},{16,8},{24,16},{1,25},{9,1},{17,9},{25,17},{2,26},{10... | collective-permute-start | bytes 196616 | tf_op jit(solution)/shard_map/ppermute | solution.py:27
  58.0 1.2 %collective-permute-start.13 = (bf16[256,128]{1,0:T(8,128)(2,1)S(1)}, bf16[256,128]{1,0:T(8,128)(2,1)S(1)}, u32[]{:S(2)}, u32[]{:S(2)}) collective-permute-start(bf16[256,128]{1,0:T(8,128)(2,1)S(1)} %shard_map.116.u0), channel_id=1, source_target_pairs={{0,16},{8,24},{16,0},{24,8},{1,17},{9,25},{17,1},{25,9},{2,18},{10... | collective-permute-start | bytes 196616 | tf_op jit(solution)/shard_map/ppermute | solution.py:27
  59.2 1.0 %collective-permute-done.12.u1 = bf16[256,128]{1,0:T(8,128)(2,1)S(1)} collective-permute-done((bf16[256,128]{1,0:T(8,128)(2,1)S(1)}, bf16[256,128]{1,0:T(8,128)(2,1)S(1)}, u32[]{:S(2)}, u32[]{:S(2)}) %collective-permute-start.12) | collective-permute-done | bytes 65568 | tf_op jit(solution)/shard_map/ppermute | solution.py:27
  60.3 2.4 %collective-permute-done.13.u2 = bf16[256,128]{1,0:T(8,128)(2,1)S(1)} collective-permute-done((bf16[256,128]{1,0:T(8,128)(2,1)S(1)}, bf16[256,128]{1,0:T(8,128)(2,1)S(1)}, u32[]{:S(2)}, u32[]{:S(2)}) %collective-permute-start.13) | collective-permute-done | bytes 65568 | tf_op jit(solution)/shard_map/ppermute | solution.py:27
  62.6 0.9 %collective-permute-done.14.u3 = bf16[256,128]{1,0:T(8,128)(2,1)S(1)} collective-permute-done((bf16[256,128]{1,0:T(8,128)(2,1)S(1)}, bf16[256,128]{1,0:T(8,128)(2,1)S(1)}, u32[]{:S(2)}, u32[]{:S(2)}) %collective-permute-start.14) | collective-permute-done | bytes 65568 | tf_op jit(solution)/shard_map/ppermute | solution.py:27
  63.6 1.7 %shard_map.118 = bf16[8,64,128]{2,1,0:T(8,128)(2,1)} custom-call(s32[5]{0:T(128)S(1)} %stack.23.place, bf16[2,64,1024]{2,1,0:T(8,128)(2,1)S(1)} %shard_map.115.d0, bf16[2,64,1024]{2,1,0:T(8,128)(2,1)S(1)} %collective-permute-done.8.d1, bf16[2,64,1024]{2,1,0:T(8,128)(2,1)S(1)} %collective-permute-done.10.d2, ...), custom_call_target="tpu_custom_call" | custom-call | flops 134217728 | bytes 1572864 | tf_op jit(solution)/shard_map/pallas_call | solution.py:196
  65.2 8.2 %all-to-all-start = ((bf16[8,64,128]{2,1,0:T(8,128)(2,1)}), bf16[8,64,128]{2,1,0:T(8,128)(2,1)S(1)}, u32[]{:S(2)}, u32[]{:S(2)}) async-start(bf16[8,64,128]{2,1,0:T(8,128)(2,1)} %shard_map.118), calls=%async_computation | async-start | bytes 262144 | tf_op jit(solution)/shard_map/all_to_all | solution.py:292
  73.5 0.7 shard_map.117
  74.2 2.1 %shard_map.119 = (f32[512,128]{1,0:T(8,128)S(1)}, bf16[512,64]{1,0:T(8,128)(2,1)S(1)}) custom-call(s32[16]{0:T(128)S(1)} %copy-done.5, bf16[64,1024]{1,0:T(8,128)(2,1)S(1)} %reshape.12.queries, bf16[64,128]{1,0:T(8,128)(2,1)S(1)} %bitcast.6, bf16[16,128,128]{2,1,0:T(8,128)(2,1)S(1)} %copy-done, bf16[16,128,128]{2,1,0:T(8,128)(2,1)S(1)} %copy-done.1), custom_call_target="tpu_custom_call" | custom-call | flops 1048576 | bytes 262144 | tf_op jit(solution)/shard_map/pallas_call | solution.py:167
  76.3 5.3 %all-to-all-done.parts = bf16[8,64,128]{2,1,0:T(8,128)(2,1)S(1)} async-done(((bf16[8,64,128]{2,1,0:T(8,128)(2,1)}), bf16[8,64,128]{2,1,0:T(8,128)(2,1)S(1)}, u32[]{:S(2)}, u32[]{:S(2)}) %all-to-all-start) | async-done | bytes 131104 | tf_op jit(solution)/shard_map/all_to_all | solution.py:292
  81.7 0.8 %shard_map.120 = (bf16[16,4,128]{2,1,0:T(4,128)(2,1)}, bf16[16,4,1024]{2,1,0:T(4,128)(2,1)}) custom-call(bf16[8,64,128]{2,1,0:T(8,128)(2,1)S(1)} %all-to-all-done.parts, f32[512,128]{1,0:T(8,128)S(1)} %get-tuple-element.65.mixed, bf16[512,64]{1,0:T(8,128)(2,1)S(1)} %get-tuple-element.66.weights), custom_call_target="tpu_custom_call" | custom-call | tf_op jit(solution)/shard_map/pallas_call | solution.py:227
  (33 shorter events, 1.3 us)
Async XLA Ops:
  0.6 73.6 %copy-start = (bf16[16,128,128]{2,1,0:T(8,128)(2,1)S(1)}, bf16[16,128,128]{2,1,0:T(8,128)(2,1)}, u32[]{:S(2)}) copy-start(bf16[16,128,128]{2,1,0:T(8,128)(2,1)} %cache_keys.1) | copy-start | bytes 1572868
  0.6 73.6 %copy-start.1 = (bf16[16,128,128]{2,1,0:T(8,128)(2,1)S(1)}, bf16[16,128,128]{2,1,0:T(8,128)(2,1)}, u32[]{:S(2)}) copy-start(bf16[16,128,128]{2,1,0:T(8,128)(2,1)} %cache_values.1) | copy-start | bytes 1572868
  0.7 12.2 %collective-permute-start = (bf16[16,4,1024]{2,1,0:T(4,128)(2,1)}, bf16[16,4,1024]{2,1,0:T(4,128)(2,1)S(1)}, u32[]{:S(2)}, u32[]{:S(2)}) collective-permute-start(bf16[16,4,1024]{2,1,0:T(4,128)(2,1)} %param.12), channel_id=1, source_target_pairs={{0,0},{1,33},{2,66},{3,99},{4,128},{5,161},{6,194},{7,227},{32,1},... | collective-permute-start | bytes 393224 | tf_op jit(solution)/shard_map/ppermute | solution.py:38
  5.8 0.9 %copy-start.2 = (bf16[768,128]{1,0:T(8,128)(2,1)S(1)}, bf16[768,128]{1,0:T(8,128)(2,1)}, u32[]{:S(2)}) copy-start(bf16[768,128]{1,0:T(8,128)(2,1)} %v_hbm.1) | copy-start | bytes 589828
  6.7 50.3 %copy-start.3 = (bf16[256,128]{1,0:T(8,128)(2,1)S(1)}, bf16[256,128]{1,0:T(8,128)(2,1)}, u32[]{:S(2)}) copy-start(bf16[256,128]{1,0:T(8,128)(2,1)} %weight.1) | copy-start | bytes 196612
  6.7 66.7 %copy-start.6 = (bf16[16,4,1024]{2,1,0:T(4,128)(2,1)S(1)}, bf16[16,4,1024]{2,1,0:T(4,128)(2,1)}, u32[]{:S(2)}) copy-start(bf16[16,4,1024]{2,1,0:T(4,128)(2,1)} %param.13) | copy-start | bytes 393220
  6.8 67.5 %copy-start.4 = (bf16[16,4,128]{2,1,0:T(4,128)(2,1)S(1)}, bf16[16,4,128]{2,1,0:T(4,128)(2,1)}, u32[]{:S(2)}) copy-start(bf16[16,4,128]{2,1,0:T(4,128)(2,1)} %param.14) | copy-start | bytes 49156
  6.8 67.5 %copy-start.5 = (s32[16]{0:T(128)S(1)}, s32[16]{0:T(128)}, u32[]{:S(2)}) copy-start(s32[16]{0:T(128)} %lengths.1) | copy-start | bytes 196
  12.9 2.7 %collective-permute-start.1 = (bf16[4,4,256,128]{3,2,1,0:T(8,128)(2,1)S(1)}, bf16[4,4,256,128]{3,2,1,0:T(8,128)(2,1)S(1)}, u32[]{:S(2)}, u32[]{:S(2)}) collective-permute-start(bf16[4,4,256,128]{3,2,1,0:T(8,128)(2,1)S(1)} %get-tuple-element.39), channel_id=1, source_target_pairs={{0,128},{128,0},{1,129},{129,1},{2,130},{130,2},{3,131},{131,3},{4... | collective-permute-start | bytes 3145736 | tf_op jit(solution)/shard_map/ppermute | solution.py:27
  15.8 16.5 %collective-permute-start.2 = (bf16[4,256,128]{2,1,0:T(8,128)(2,1)S(1)}, bf16[4,256,128]{2,1,0:T(8,128)(2,1)S(1)}, u32[]{:S(2)}, u32[]{:S(2)}) collective-permute-start(bf16[4,256,128]{2,1,0:T(8,128)(2,1)S(1)} %get-tuple-element.44), channel_id=1, source_target_pairs={{0,16},{8,24},{16,0},{24,8},{1,17},{9,25},{17,1},{25,9},{2,18},{10... | collective-permute-start | bytes 786440 | tf_op jit(solution)/shard_map/ppermute | solution.py:27
  18.7 4.6 %collective-permute-start.7 = (bf16[16,4,1024]{2,1,0:T(4,128)(2,1)S(1)}, bf16[16,4,1024]{2,1,0:T(4,128)(2,1)S(1)}, u32[]{:S(2)}, u32[]{:S(2)}) collective-permute-start(bf16[16,4,1024]{2,1,0:T(4,128)(2,1)S(1)} %collective-permute-done.first), channel_id=1, source_target_pairs={{0,4},{4,0},{1,5},{5,1},{2,6},{6,2},{3,7},{7,3},{8,12},{12,8},{9,1... | collective-permute-start | bytes 393224 | tf_op jit(solution)/shard_map/ppermute | solution.py:27
  18.7 14.4 %collective-permute-start.3 = (bf16[4,256,128]{2,1,0:T(8,128)(2,1)S(1)}, bf16[4,256,128]{2,1,0:T(8,128)(2,1)S(1)}, u32[]{:S(2)}, u32[]{:S(2)}) collective-permute-start(bf16[4,256,128]{2,1,0:T(8,128)(2,1)S(1)} %get-tuple-element.45), channel_id=1, source_target_pairs={{0,8},{8,16},{16,24},{24,0},{1,9},{9,17},{17,25},{25,1},{2,10},{10... | collective-permute-start | bytes 786440 | tf_op jit(solution)/shard_map/ppermute | solution.py:27
  19.0 14.1 %collective-permute-start.4 = (bf16[4,256,128]{2,1,0:T(8,128)(2,1)S(1)}, bf16[4,256,128]{2,1,0:T(8,128)(2,1)S(1)}, u32[]{:S(2)}, u32[]{:S(2)}) collective-permute-start(bf16[4,256,128]{2,1,0:T(8,128)(2,1)S(1)} %get-tuple-element.46), channel_id=1, source_target_pairs={{0,24},{8,0},{16,8},{24,16},{1,25},{9,1},{17,9},{25,17},{2,26},{10... | collective-permute-start | bytes 786440 | tf_op jit(solution)/shard_map/ppermute | solution.py:27
  23.4 19.6 %collective-permute-start.8 = (bf16[2,64,1024]{2,1,0:T(8,128)(2,1)S(1)}, bf16[2,64,1024]{2,1,0:T(8,128)(2,1)S(1)}, u32[]{:S(2)}, u32[]{:S(2)}) collective-permute-start(bf16[2,64,1024]{2,1,0:T(8,128)(2,1)S(1)} %shard_map.115.d0), channel_id=1, source_target_pairs={{0,3},{1,0},{2,1},{3,2},{4,7},{5,4},{6,5},{7,6},{8,11},{9,8},{10,9... | collective-permute-start | bytes 786440 | tf_op jit(solution)/shard_map/ppermute | solution.py:27
  32.4 18.4 %collective-permute-start.10 = (bf16[2,64,1024]{2,1,0:T(8,128)(2,1)S(1)}, bf16[2,64,1024]{2,1,0:T(8,128)(2,1)S(1)}, u32[]{:S(2)}, u32[]{:S(2)}) collective-permute-start(bf16[2,64,1024]{2,1,0:T(8,128)(2,1)S(1)} %shard_map.115.d0), channel_id=1, source_target_pairs={{0,2},{1,3},{2,0},{3,1},{4,6},{5,7},{6,4},{7,5},{8,10},{9,11},{10,... | collective-permute-start | bytes 786440 | tf_op jit(solution)/shard_map/ppermute | solution.py:27
  32.4 18.4 %collective-permute-start.11 = (bf16[2,64,1024]{2,1,0:T(8,128)(2,1)S(1)}, bf16[2,64,1024]{2,1,0:T(8,128)(2,1)S(1)}, u32[]{:S(2)}, u32[]{:S(2)}) collective-permute-start(bf16[2,64,1024]{2,1,0:T(8,128)(2,1)S(1)} %shard_map.115.d0), channel_id=1, source_target_pairs={{0,1},{1,2},{2,3},{3,0},{4,5},{5,6},{6,7},{7,4},{8,9},{9,10},{10,1... | collective-permute-start | bytes 786440 | tf_op jit(solution)/shard_map/ppermute | solution.py:27
  43.0 8.1 %collective-permute-start.9 = (bf16[256,128]{1,0:T(8,128)(2,1)S(1)}, bf16[256,128]{1,0:T(8,128)(2,1)S(1)}, u32[]{:S(2)}, u32[]{:S(2)}) collective-permute-start(bf16[256,128]{1,0:T(8,128)(2,1)S(1)} %get-tuple-element.53), channel_id=1, source_target_pairs={{0,96},{32,0},{64,32},{96,64},{1,97},{33,1},{65,33},{97,65},{2,98}... | collective-permute-start | bytes 196616 | tf_op jit(solution)/shard_map/ppermute | solution.py:27
  43.0 9.5 %collective-permute-start.5 = (bf16[256,128]{1,0:T(8,128)(2,1)S(1)}, bf16[256,128]{1,0:T(8,128)(2,1)S(1)}, u32[]{:S(2)}, u32[]{:S(2)}) collective-permute-start(bf16[256,128]{1,0:T(8,128)(2,1)S(1)} %get-tuple-element.48), channel_id=1, source_target_pairs={{0,64},{32,96},{64,0},{96,32},{1,65},{33,97},{65,1},{97,33},{2,66}... | collective-permute-start | bytes 196616 | tf_op jit(solution)/shard_map/ppermute | solution.py:27
  50.8 6.2 %collective-permute-start.6 = (bf16[256,128]{1,0:T(8,128)(2,1)S(1)}, bf16[256,128]{1,0:T(8,128)(2,1)S(1)}, u32[]{:S(2)}, u32[]{:S(2)}) collective-permute-start(bf16[256,128]{1,0:T(8,128)(2,1)S(1)} %get-tuple-element.49), channel_id=1, source_target_pairs={{0,32},{32,64},{64,96},{96,0},{1,33},{33,65},{65,97},{97,1},{2,34}... | collective-permute-start | bytes 196616 | tf_op jit(solution)/shard_map/ppermute | solution.py:27
  57.1 3.2 %collective-permute-start.12 = (bf16[256,128]{1,0:T(8,128)(2,1)S(1)}, bf16[256,128]{1,0:T(8,128)(2,1)S(1)}, u32[]{:S(2)}, u32[]{:S(2)}) collective-permute-start(bf16[256,128]{1,0:T(8,128)(2,1)S(1)} %shard_map.116.u0), channel_id=1, source_target_pairs={{0,24},{8,0},{16,8},{24,16},{1,25},{9,1},{17,9},{25,17},{2,26},{10... | collective-permute-start | bytes 196616 | tf_op jit(solution)/shard_map/ppermute | solution.py:27
  58.0 4.6 %collective-permute-start.13 = (bf16[256,128]{1,0:T(8,128)(2,1)S(1)}, bf16[256,128]{1,0:T(8,128)(2,1)S(1)}, u32[]{:S(2)}, u32[]{:S(2)}) collective-permute-start(bf16[256,128]{1,0:T(8,128)(2,1)S(1)} %shard_map.116.u0), channel_id=1, source_target_pairs={{0,16},{8,24},{16,0},{24,8},{1,17},{9,25},{17,1},{25,9},{2,18},{10... | collective-permute-start | bytes 196616 | tf_op jit(solution)/shard_map/ppermute | solution.py:27
  59.2 4.3 %collective-permute-start.14 = (bf16[256,128]{1,0:T(8,128)(2,1)S(1)}, bf16[256,128]{1,0:T(8,128)(2,1)S(1)}, u32[]{:S(2)}, u32[]{:S(2)}) collective-permute-start(bf16[256,128]{1,0:T(8,128)(2,1)S(1)} %shard_map.116.u0), channel_id=1, source_target_pairs={{0,8},{8,16},{16,24},{24,0},{1,9},{9,17},{17,25},{25,1},{2,10},{10... | collective-permute-start | bytes 196616 | tf_op jit(solution)/shard_map/ppermute | solution.py:27
  65.2 16.5 %all-to-all-start = ((bf16[8,64,128]{2,1,0:T(8,128)(2,1)}), bf16[8,64,128]{2,1,0:T(8,128)(2,1)S(1)}, u32[]{:S(2)}, u32[]{:S(2)}) async-start(bf16[8,64,128]{2,1,0:T(8,128)(2,1)} %shard_map.118), calls=%async_computation | async-start | bytes 262144 | tf_op jit(solution)/shard_map/all_to_all | solution.py:292

commit v6 on v4

--- a/solution.py
+++ b/solution.py
@@ -28,7 +28,7 @@
 
 
 def swap_high(value):
-    pairs = [(zh * 4 + y, y * 4 + zh) for zh in range(4) for y in range(4)]
+    pairs = [(zh * 4 + y, y * 4 + (zh + y) % 4) for zh in range(4) for y in range(4)]
     return lax.ppermute(value, ("zh", "y"), pairs)
 
 
@@ -168,38 +168,50 @@
         ],
         compiler_params=pltpu.CompilerParams(vmem_limit_bytes=16 * MIB),
         cost_estimate=pl.CostEstimate(
-            flops=2 * 16 * 512 * 256 * HD, bytes_accessed=2 * MIB, transcendentals=512 * 192
+            flops=MIB, bytes_accessed=MIB // 4, transcendentals=0
         ),
     )(lengths, queries, new_keys, cache_keys, cache_values)
 
 
-def project_kernel(first, place, d0, d1, d2, d3, u, *refs):
-    core, x, y, low = place[0], place[2], place[3], place[4]
-    start, out_ref, rows = (None, *refs) if first else refs
-    own = jnp.where(core == low, 0, 1) if first else jnp.where(core == low, 1, 0)
+def fill_rows(rows, x, updated):
     for d in range(4):
-        rows[pl.ds(pl.multiple_of(lax.rem(x + d, 4) * 256, 256), 256), :] = u[d]
+        rows[pl.ds(pl.multiple_of(lax.rem(x + d, 4) * 256, 256), 256), :] = updated[d]
+
+
+def tokens_of(place, d):
+    return lax.rem(place[3] + d + 4 - place[1], 4)
+
+
+def project_own_kernel(place, d0, d1, d2, u, out_ref, rows):
+    own = jnp.where(place[0] == place[4], 0, 1)
+    fill_rows(rows, place[2], u)
+    for d, piece in enumerate((d0, d1, d2)):
+        out_ref[tokens_of(place, d)] = jnp.dot(
+            piece[own], rows[...], preferred_element_type=F32
+        )
+
+
+def project_rest_kernel(place, d0, d1, d2, d3, u_own, u_other, start, out_ref, rows, last):
+    own = jnp.where(place[0] == place[4], 0, 1)
+    fill_rows(last, place[2], u_own)
+    fill_rows(rows, place[2], u_other)
     for d, piece in enumerate((d0, d1, d2, d3)):
-        zh = lax.rem(y + d, 4)
-        product = jnp.dot(piece[own], rows[...], preferred_element_type=F32)
-        if start is not None:
+        zh = tokens_of(place, d)
+        product = jnp.dot(piece[1 - own], rows[...], preferred_element_type=F32)
+        if d < 3:
             product += start[zh]
+        else:
+            product += jnp.dot(piece[own], last[...], preferred_element_type=F32)
         out_ref[zh] = product.astype(out_ref.dtype)
 
 
-def project(place, pieces, updated, start=None):
-    first = start is None
-
-    def kernel(*refs):
-        project_kernel(first, *refs)
-
-    args = (*pieces, updated) if first else (*pieces, updated, start)
+def project(kernel, dtype, scratches, place, *args):
     return pl.pallas_call(
         kernel,
         in_specs=[SMEM] + [VMEM] * len(args),
         out_specs=VMEM,
-        out_shape=jax.ShapeDtypeStruct((4, 64, HD), F32 if first else BF16),
-        scratch_shapes=[pltpu.VMEM((1024, HD), BF16)],
+        out_shape=jax.ShapeDtypeStruct((4, 64, HD), dtype),
+        scratch_shapes=[pltpu.VMEM((1024, HD), BF16)] * scratches,
         compiler_params=pltpu.CompilerParams(vmem_limit_bytes=16 * MIB),
         cost_estimate=pl.CostEstimate(
             flops=2 * 256 * 1024 * HD, bytes_accessed=3 * MIB // 4, transcendentals=0
@@ -253,19 +265,19 @@
     places = row_count * step_count
     place = jnp.stack([core, high, x, y, low])
 
-    swapped = swap_high(decode_inputs)
     theirs, mine = partial_gradient(place, normed_inputs, value_cotangent)
-    theirs, mine, swapped = lax.optimization_barrier((theirs, mine, swapped))
     received = shift(theirs, "c", 1)
+    swapped = swap_high(after(decode_inputs, theirs))
 
     rows = (4, 256, HD)
     own, *sent = small_call(
         core_sum_kernel, [(rows, F32)] + [(rows, BF16)] * 3, mine, received
     )
     along_x = [shift(sent[d - 1], "x", d) for d in (2, 1, 3)]
-
     swapped = after(swapped, own)
-    second = shift(swapped, "zl", 1)
+    (both,) = small_call(
+        join_kernel, [((2, places, D // 8), BF16)], swapped, shift(swapped, "zl", 1)
+    )
     attended_cache, fresh_weights = attend_cache(
         lengths,
         after(queries.reshape(places, -1), own),
@@ -273,27 +285,29 @@
         cache_keys,
         cache_values,
     )
-    swapped = after(swapped, attended_cache)
-    (both,) = small_call(join_kernel, [((2, places, D // 8), BF16)], swapped, second)
-    pieces = [both] + [shift(both, "y", -d) for d in (1, 2, 3)]
-
-    own, *along_x, attended_cache, fresh_weights = lax.optimization_barrier(
-        (own, *along_x, attended_cache, fresh_weights)
+
+    own, *along_x, both, attended_cache, fresh_weights = lax.optimization_barrier(
+        (own, *along_x, both, attended_cache, fresh_weights)
     )
     rows = (256, HD)
     own, *sent = small_call(
         x_sum_kernel, [(rows, F32)] + [(rows, BF16)] * 3, own, *along_x
     )
     along_z = [shift(sent[e - 1], "zh", e) for e in (2, 1, 3)]
-    own, *along_z, pieces = lax.optimization_barrier((own, *along_z, pieces))
+    both = after(both, own)
+    from_y2, from_y1, from_y3 = (shift(both, "y", -d) for d in (2, 1, 3))
+    own, *along_z, from_y2, from_y1 = lax.optimization_barrier((own, *along_z, from_y2, from_y1))
     (updated,) = small_call(update_kernel, [(rows, BF16)], value_weight, own, *along_z)
     own = after(own, updated)
     (gradient,) = small_call(gradient_kernel, [(rows, F32)], own, *along_z)
 
     gathered = jnp.stack([updated] + [shift(updated, "x", -d) for d in (1, 2, 3)])
     other = shift(gathered, "c", 1)
-    partial = project(place, pieces, gathered)
-    partial = project(place, pieces, other, partial)
+    pieces = (both, from_y1, from_y2)
+    partial = project(project_own_kernel, F32, 1, place, *pieces, gathered)
+    partial = project(
+        project_rest_kernel, BF16, 2, place, *pieces, from_y3, gathered, other, partial
+    )
     exchanged = lax.all_to_all(partial, "zh", 0, 0, tiled=True)
     new_values, attended = finish(
         exchanged, attended_cache, fresh_weights, row_count, step_count

time: 81.9 us -> 77.1 us (0.941)
  the two profiles are of different devices: /device:TPU:1 before, /device:TPU:32 now
where the time goes in v6:
time: 77.1 us; the launch traced here: 75.9 us
  starting transfers between devices  33.2 us (43%)
  waiting for transfers between devices  27.3 us (35%)
  Pallas kernels  13.4 us (17%)
  local copies, waits for them, and re-layouts  1.14 us (1%)
  between operations  0.81 us (1%)
    ppermute x15, starting transfers between devices, shift(): return lax.ppermute(value, axis, [(i, (i + by) % n) for i in range(n)])  28.6 us
    ppermute x15, waiting for transfers between devices, shift(): return lax.ppermute(value, axis, [(i, (i + by) % n) for i in range(n)])  19.8 us
    all_to_all x1, waiting for transfers between devices, shards(): exchanged = lax.all_to_all(partial, 'zh', 0, 0, tiled=True)  7.52 us
    pallas_call x1, Pallas kernels, partial_gradient(): pl.pallas_call(partial_kernel, in_specs=[SMEM, HBM, HBM], out_specs=[VMEM...  6.11 us
    all_to_all x1, starting transfers between devices, shards(): exchanged = lax.all_to_all(partial, 'zh', 0, 0, tiled=True)  3.97 us
    pallas_call x2, Pallas kernels, project(): pl.pallas_call(kernel, in_specs=[SMEM] + [VMEM] * len(args), out_specs=VM...  2.38 us
    pallas_call x1, Pallas kernels, attend_cache(): pl.pallas_call(attend_kernel, in_specs=[SMEM] + [VMEM] * 4, out_specs=[VM...  2.12 us
    pallas_call x5, Pallas kernels, small_call(): pl.pallas_call(kernel, in_specs=[VMEM] * len(args), out_specs=[VMEM] * le...  1.93 us
  transfers between devices with their start and end apart: 17, of which 10 were waited for; matrix products, arithmetic and copies ran while one was open for 0% of the time, Pallas kernels for 6%

profile of v6, /device:TPU:32, one launch (start us, length us, event | category | flops | bytes accessed | tf_op | source)
XLA Modules:
  0.0 75.9 jit_solution(2149355694118886217)
XLA Ops:
  0.7 1.0 %copy-done.2 = bf16[768,128]{1,0:T(8,128)(2,1)S(1)} copy-done((bf16[768,128]{1,0:T(8,128)(2,1)S(1)}, bf16[768,128]{1,0:T(8,128)(2,1)}, u32[]{:S(2)}) %copy-start.2) | copy-done | bytes 196632
  1.8 6.1 %shard_map.112 = (bf16[4,4,256,128]{3,2,1,0:T(8,128)(2,1)S(1)}, bf16[4,4,256,128]{3,2,1,0:T(8,128)(2,1)S(1)}) custom-call(s32[5]{0:T(128)S(1)} %stack.38.place, bf16[768,8192]{1,0:T(8,128)(2,1)} %x_hbm.1, bf16[768,128]{1,0:T(8,128)(2,1)S(1)} %copy-done.2), custom_call_target="tpu_custom_call" | custom-call | flops 1610612736 | bytes 12582912 | tf_op jit(solution)/shard_map/pallas_call | solution.py:65
  8.7 2.0 %collective-permute-done.received = bf16[4,4,256,128]{3,2,1,0:T(8,128)(2,1)S(1)} collective-permute-done((bf16[4,4,256,128]{3,2,1,0:T(8,128)(2,1)S(1)}, bf16[4,4,256,128]{3,2,1,0:T(8,128)(2,1)S(1)}, u32[]{:S(2)}, u32[]{:S(2)}) %collective-permute-start) | collective-permute-done | bytes 1048608 | tf_op jit(solution)/shard_map/ppermute | solution.py:27
  10.6 1.0 %shard_map.113 = (f32[4,256,128]{2,1,0:T(8,128)S(1)}, bf16[4,256,128]{2,1,0:T(8,128)(2,1)}, bf16[4,256,128]{2,1,0:T(8,128)(2,1)}, bf16[4,256,128]{2,1,0:T(8,128)(2,1)S(1)}) custom-call(bf16[4,4,256,128]{3,2,1,0:T(8,128)(2,1)S(1)} %get-tuple-element.35.mine, bf16[4,4,256,128]{3,2,1,0:T(8,128)(2,1)S(1)} %collective-permute-done.received), custom_call_target="tpu_custom_call" | custom-call | flops 1048576 | bytes 2097152 | tf_op jit(solution)/shard_map/pallas_call | solution.py:83
  11.6 3.0 %collective-permute-start.1 = (bf16[4,256,128]{2,1,0:T(8,128)(2,1)}, bf16[4,256,128]{2,1,0:T(8,128)(2,1)S(1)}, u32[]{:S(2)}, u32[]{:S(2)}) collective-permute-start(bf16[4,256,128]{2,1,0:T(8,128)(2,1)} %get-tuple-element.38), channel_id=1, source_target_pairs={{0,16},{8,24},{16,0},{24,8},{1,17},{9,25},{17,1},{25,9},{2,18},{10... | collective-permute-start | bytes 786440 | tf_op jit(solution)/shard_map/ppermute | solution.py:27
  15.3 2.6 %collective-permute-start.3 = (bf16[4,256,128]{2,1,0:T(8,128)(2,1)S(1)}, bf16[4,256,128]{2,1,0:T(8,128)(2,1)S(1)}, u32[]{:S(2)}, u32[]{:S(2)}) collective-permute-start(bf16[4,256,128]{2,1,0:T(8,128)(2,1)S(1)} %get-tuple-element.40), channel_id=1, source_target_pairs={{0,24},{8,0},{16,8},{24,16},{1,25},{9,1},{17,9},{25,17},{2,26},{10... | collective-permute-start | bytes 786440 | tf_op jit(solution)/shard_map/ppermute | solution.py:27
  18.1 2.1 %shard_map.115 = (f32[512,128]{1,0:T(8,128)S(1)}, bf16[512,64]{1,0:T(8,128)(2,1)S(1)}) custom-call(s32[16]{0:T(128)S(1)} %copy-done.5, bf16[64,1024]{1,0:T(8,128)(2,1)S(1)} %reshape.12.queries, bf16[64,128]{1,0:T(8,128)(2,1)S(1)} %bitcast.11, bf16[16,128,128]{2,1,0:T(8,128)(2,1)S(1)} %copy-done, bf16[16,128,128]{2,1,0:T(8,128)(2,1)S(1)} %copy-done.1), custom_call_target="tpu_custom_call" | custom-call | flops 1048576 | bytes 262144 | tf_op jit(solution)/shard_map/pallas_call | solution.py:161
  20.2 5.4 %collective-permute-done.5.second = bf16[16,4,1024]{2,1,0:T(4,128)(2,1)S(1)} collective-permute-done((bf16[16,4,1024]{2,1,0:T(4,128)(2,1)S(1)}, bf16[16,4,1024]{2,1,0:T(4,128)(2,1)S(1)}, u32[]{:S(2)}, u32[]{:S(2)}) %collective-permute-start.5) | collective-permute-done | bytes 131104 | tf_op jit(solution)/shard_map/ppermute | solution.py:27
  25.7 1.7 %collective-permute-done.2.r2 = bf16[4,256,128]{2,1,0:T(8,128)(2,1)S(1)} collective-permute-done((bf16[4,256,128]{2,1,0:T(8,128)(2,1)}, bf16[4,256,128]{2,1,0:T(8,128)(2,1)S(1)}, u32[]{:S(2)}, u32[]{:S(2)}) %collective-permute-start.2) | collective-permute-done | bytes 262176 | tf_op jit(solution)/shard_map/ppermute | solution.py:27
  27.6 7.8 %collective-permute-start.10 = (bf16[2,64,1024]{2,1,0:T(8,128)(2,1)S(1)}, bf16[2,64,1024]{2,1,0:T(8,128)(2,1)S(1)}, u32[]{:S(2)}, u32[]{:S(2)}) collective-permute-start(bf16[2,64,1024]{2,1,0:T(8,128)(2,1)S(1)} %shard_map.114.d0), channel_id=1, source_target_pairs={{0,3},{1,0},{2,1},{3,2},{4,7},{5,4},{6,5},{7,6},{8,11},{9,8},{10,9... | collective-permute-start | bytes 786440 | tf_op jit(solution)/shard_map/ppermute | solution.py:27
  35.4 1.2 %collective-permute-start.9 = (bf16[2,64,1024]{2,1,0:T(8,128)(2,1)S(1)}, bf16[2,64,1024]{2,1,0:T(8,128)(2,1)S(1)}, u32[]{:S(2)}, u32[]{:S(2)}) collective-permute-start(bf16[2,64,1024]{2,1,0:T(8,128)(2,1)S(1)} %shard_map.114.d0), channel_id=1, source_target_pairs={{0,2},{1,3},{2,0},{3,1},{4,6},{5,7},{6,4},{7,5},{8,10},{9,11},{10,... | collective-permute-start | bytes 786440 | tf_op jit(solution)/shard_map/ppermute | solution.py:27
  36.6 2.6 %collective-permute-start.6 = (bf16[256,128]{1,0:T(8,128)(2,1)S(1)}, bf16[256,128]{1,0:T(8,128)(2,1)S(1)}, u32[]{:S(2)}, u32[]{:S(2)}) collective-permute-start(bf16[256,128]{1,0:T(8,128)(2,1)S(1)} %get-tuple-element.51), channel_id=1, source_target_pairs={{0,64},{32,96},{64,0},{96,32},{1,65},{33,97},{65,1},{97,33},{2,66}... | collective-permute-start | bytes 196616 | tf_op jit(solution)/shard_map/ppermute | solution.py:27
  39.2 2.3 %collective-permute-start.7 = (bf16[256,128]{1,0:T(8,128)(2,1)S(1)}, bf16[256,128]{1,0:T(8,128)(2,1)S(1)}, u32[]{:S(2)}, u32[]{:S(2)}) collective-permute-start(bf16[256,128]{1,0:T(8,128)(2,1)S(1)} %get-tuple-element.52), channel_id=1, source_target_pairs={{0,32},{32,64},{64,96},{96,0},{1,33},{33,65},{65,97},{97,1},{2,34}... | collective-permute-start | bytes 196616 | tf_op jit(solution)/shard_map/ppermute | solution.py:27
  41.5 1.9 %collective-permute-start.8 = (bf16[256,128]{1,0:T(8,128)(2,1)S(1)}, bf16[256,128]{1,0:T(8,128)(2,1)S(1)}, u32[]{:S(2)}, u32[]{:S(2)}) collective-permute-start(bf16[256,128]{1,0:T(8,128)(2,1)S(1)} %get-tuple-element.53), channel_id=1, source_target_pairs={{0,96},{32,0},{64,32},{96,64},{1,97},{33,1},{65,33},{97,65},{2,98}... | collective-permute-start | bytes 196616 | tf_op jit(solution)/shard_map/ppermute | solution.py:27
  43.4 1.7 %collective-permute-done.6.r1 = bf16[256,128]{1,0:T(8,128)(2,1)S(1)} collective-permute-done((bf16[256,128]{1,0:T(8,128)(2,1)S(1)}, bf16[256,128]{1,0:T(8,128)(2,1)S(1)}, u32[]{:S(2)}, u32[]{:S(2)}) %collective-permute-start.6) | collective-permute-done | bytes 65568 | tf_op jit(solution)/shard_map/ppermute | solution.py:27
  45.0 2.8 %collective-permute-done.7.r2 = bf16[256,128]{1,0:T(8,128)(2,1)S(1)} collective-permute-done((bf16[256,128]{1,0:T(8,128)(2,1)S(1)}, bf16[256,128]{1,0:T(8,128)(2,1)S(1)}, u32[]{:S(2)}, u32[]{:S(2)}) %collective-permute-start.7) | collective-permute-done | bytes 65568 | tf_op jit(solution)/shard_map/ppermute | solution.py:27
  47.9 1.7 %collective-permute-start.14 = (bf16[256,128]{1,0:T(8,128)(2,1)S(1)}, bf16[256,128]{1,0:T(8,128)(2,1)S(1)}, u32[]{:S(2)}, u32[]{:S(2)}) collective-permute-start(bf16[256,128]{1,0:T(8,128)(2,1)S(1)} %shard_map.117), channel_id=1, source_target_pairs={{0,8},{8,16},{16,24},{24,0},{1,9},{9,17},{17,25},{25,1},{2,10},{10... | collective-permute-start | bytes 196616 | tf_op jit(solution)/shard_map/ppermute | solution.py:27
  49.7 2.7 %collective-permute-start.13 = (bf16[256,128]{1,0:T(8,128)(2,1)S(1)}, bf16[256,128]{1,0:T(8,128)(2,1)S(1)}, u32[]{:S(2)}, u32[]{:S(2)}) collective-permute-start(bf16[256,128]{1,0:T(8,128)(2,1)S(1)} %shard_map.117), channel_id=1, source_target_pairs={{0,16},{8,24},{16,0},{24,8},{1,17},{9,25},{17,1},{25,9},{2,18},{10... | collective-permute-start | bytes 196616 | tf_op jit(solution)/shard_map/ppermute | solution.py:27
  52.7 1.5 %collective-permute-start.11 = (bf16[2,64,1024]{2,1,0:T(8,128)(2,1)S(1)}, bf16[2,64,1024]{2,1,0:T(8,128)(2,1)S(1)}, u32[]{:S(2)}, u32[]{:S(2)}) collective-permute-start(bf16[2,64,1024]{2,1,0:T(8,128)(2,1)S(1)} %shard_map.114.d0), channel_id=1, source_target_pairs={{0,1},{1,2},{2,3},{3,0},{4,5},{5,6},{6,7},{7,4},{8,9},{9,10},{10,1... | collective-permute-start | bytes 786440 | tf_op jit(solution)/shard_map/ppermute | solution.py:27
  54.2 1.6 %collective-permute-done.13 = bf16[256,128]{1,0:T(8,128)(2,1)S(1)} collective-permute-done((bf16[256,128]{1,0:T(8,128)(2,1)S(1)}, bf16[256,128]{1,0:T(8,128)(2,1)S(1)}, u32[]{:S(2)}, u32[]{:S(2)}) %collective-permute-start.13) | collective-permute-done | bytes 65568 | tf_op jit(solution)/shard_map/ppermute | solution.py:27
  57.6 3.7 %collective-permute-done.11.d3 = bf16[2,64,1024]{2,1,0:T(8,128)(2,1)S(1)} collective-permute-done((bf16[2,64,1024]{2,1,0:T(8,128)(2,1)S(1)}, bf16[2,64,1024]{2,1,0:T(8,128)(2,1)S(1)}, u32[]{:S(2)}, u32[]{:S(2)}) %collective-permute-start.11) | collective-permute-done | bytes 262176 | tf_op jit(solution)/shard_map/ppermute | solution.py:27
  61.3 1.6 %shard_map.120 = bf16[4,64,128]{2,1,0:T(8,128)(2,1)} custom-call(s32[5]{0:T(128)S(1)} %stack.38.place, bf16[2,64,1024]{2,1,0:T(8,128)(2,1)S(1)} %shard_map.114.d0, bf16[2,64,1024]{2,1,0:T(8,128)(2,1)S(1)} %collective-permute-done.10.d1, bf16[2,64,1024]{2,1,0:T(8,128)(2,1)S(1)} %collective-permute-done.9.d2, ...), custom_call_target="tpu_custom_call" | custom-call | flops 67108864 | bytes 786432 | tf_op jit(solution)/shard_map/pallas_call | solution.py:209
  62.9 4.0 %all-to-all-start = ((bf16[4,64,128]{2,1,0:T(8,128)(2,1)}), bf16[4,64,128]{2,1,0:T(8,128)(2,1)S(1)}, u32[]{:S(2)}, u32[]{:S(2)}) async-start(bf16[4,64,128]{2,1,0:T(8,128)(2,1)} %shard_map.120), calls=%async_computation | async-start | bytes 131072 | tf_op jit(solution)/shard_map/all_to_all | solution.py:311
  67.5 7.5 %all-to-all-done.parts = bf16[4,64,128]{2,1,0:T(8,128)(2,1)S(1)} async-done(((bf16[4,64,128]{2,1,0:T(8,128)(2,1)}), bf16[4,64,128]{2,1,0:T(8,128)(2,1)S(1)}, u32[]{:S(2)}, u32[]{:S(2)}) %all-to-all-start) | async-done | bytes 65568 | tf_op jit(solution)/shard_map/all_to_all | solution.py:311
  (39 shorter events, 5.6 us)
Async XLA Ops:
  0.6 17.4 %copy-start.1 = (bf16[16,128,128]{2,1,0:T(8,128)(2,1)S(1)}, bf16[16,128,128]{2,1,0:T(8,128)(2,1)}, u32[]{:S(2)}) copy-start(bf16[16,128,128]{2,1,0:T(8,128)(2,1)} %cache_values.1) | copy-start | bytes 1572868
  0.6 17.4 %copy-start = (bf16[16,128,128]{2,1,0:T(8,128)(2,1)S(1)}, bf16[16,128,128]{2,1,0:T(8,128)(2,1)}, u32[]{:S(2)}) copy-start(bf16[16,128,128]{2,1,0:T(8,128)(2,1)} %cache_keys.1) | copy-start | bytes 1572868
  1.7 6.2 %copy-start.7 = (bf16[16,4,1024]{2,1,0:T(4,128)(2,1)S(1)}, bf16[16,4,1024]{2,1,0:T(4,128)(2,1)}, u32[]{:S(2)}) copy-start(bf16[16,4,1024]{2,1,0:T(4,128)(2,1)} %param.12) | copy-start | bytes 393220
  1.7 16.3 %copy-start.6 = (bf16[16,4,1024]{2,1,0:T(4,128)(2,1)S(1)}, bf16[16,4,1024]{2,1,0:T(4,128)(2,1)}, u32[]{:S(2)}) copy-start(bf16[16,4,1024]{2,1,0:T(4,128)(2,1)} %param.13) | copy-start | bytes 393220
  1.7 16.3 %copy-start.4 = (bf16[16,4,128]{2,1,0:T(4,128)(2,1)S(1)}, bf16[16,4,128]{2,1,0:T(4,128)(2,1)}, u32[]{:S(2)}) copy-start(bf16[16,4,128]{2,1,0:T(4,128)(2,1)} %param.14) | copy-start | bytes 49156
  1.7 16.3 %copy-start.5 = (s32[16]{0:T(128)S(1)}, s32[16]{0:T(128)}, u32[]{:S(2)}) copy-start(s32[16]{0:T(128)} %lengths.1) | copy-start | bytes 196
  1.8 46.1 %copy-start.3 = (bf16[256,128]{1,0:T(8,128)(2,1)S(1)}, bf16[256,128]{1,0:T(8,128)(2,1)}, u32[]{:S(2)}) copy-start(bf16[256,128]{1,0:T(8,128)(2,1)} %weight.1) | copy-start | bytes 196612
  7.9 2.7 %collective-permute-start = (bf16[4,4,256,128]{3,2,1,0:T(8,128)(2,1)S(1)}, bf16[4,4,256,128]{3,2,1,0:T(8,128)(2,1)S(1)}, u32[]{:S(2)}, u32[]{:S(2)}) collective-permute-start(bf16[4,4,256,128]{3,2,1,0:T(8,128)(2,1)S(1)} %get-tuple-element.36), channel_id=1, source_target_pairs={{0,128},{128,0},{1,129},{129,1},{2,130},{130,2},{3,131},{131,3},{4... | collective-permute-start | bytes 3145736 | tf_op jit(solution)/shard_map/ppermute | solution.py:27
  8.0 9.9 %collective-permute-start.4 = (bf16[16,4,1024]{2,1,0:T(4,128)(2,1)S(1)}, bf16[16,4,1024]{2,1,0:T(4,128)(2,1)S(1)}, u32[]{:S(2)}, u32[]{:S(2)}) collective-permute-start(bf16[16,4,1024]{2,1,0:T(4,128)(2,1)S(1)} %copy-done.7), channel_id=1, source_target_pairs={{0,0},{1,33},{2,66},{3,99},{32,1},{33,34},{34,67},{35,96},{64,2},{... | collective-permute-start | bytes 393224 | tf_op jit(solution)/shard_map/ppermute | solution.py:32
  11.6 14.0 %collective-permute-start.1 = (bf16[4,256,128]{2,1,0:T(8,128)(2,1)}, bf16[4,256,128]{2,1,0:T(8,128)(2,1)S(1)}, u32[]{:S(2)}, u32[]{:S(2)}) collective-permute-start(bf16[4,256,128]{2,1,0:T(8,128)(2,1)} %get-tuple-element.38), channel_id=1, source_target_pairs={{0,16},{8,24},{16,0},{24,8},{1,17},{9,25},{17,1},{25,9},{2,18},{10... | collective-permute-start | bytes 786440 | tf_op jit(solution)/shard_map/ppermute | solution.py:27
  14.7 12.7 %collective-permute-start.2 = (bf16[4,256,128]{2,1,0:T(8,128)(2,1)}, bf16[4,256,128]{2,1,0:T(8,128)(2,1)S(1)}, u32[]{:S(2)}, u32[]{:S(2)}) collective-permute-start(bf16[4,256,128]{2,1,0:T(8,128)(2,1)} %get-tuple-element.39), channel_id=1, source_target_pairs={{0,8},{8,16},{16,24},{24,0},{1,9},{9,17},{17,25},{25,1},{2,10},{10... | collective-permute-start | bytes 786440 | tf_op jit(solution)/shard_map/ppermute | solution.py:27
  15.3 12.2 %collective-permute-start.3 = (bf16[4,256,128]{2,1,0:T(8,128)(2,1)S(1)}, bf16[4,256,128]{2,1,0:T(8,128)(2,1)S(1)}, u32[]{:S(2)}, u32[]{:S(2)}) collective-permute-start(bf16[4,256,128]{2,1,0:T(8,128)(2,1)S(1)} %get-tuple-element.40), channel_id=1, source_target_pairs={{0,24},{8,0},{16,8},{24,16},{1,25},{9,1},{17,9},{25,17},{2,26},{10... | collective-permute-start | bytes 786440 | tf_op jit(solution)/shard_map/ppermute | solution.py:27
  17.9 7.7 %collective-permute-start.5 = (bf16[16,4,1024]{2,1,0:T(4,128)(2,1)S(1)}, bf16[16,4,1024]{2,1,0:T(4,128)(2,1)S(1)}, u32[]{:S(2)}, u32[]{:S(2)}) collective-permute-start(bf16[16,4,1024]{2,1,0:T(4,128)(2,1)S(1)} %collective-permute-done.4.first), channel_id=1, source_target_pairs={{0,4},{4,0},{1,5},{5,1},{2,6},{6,2},{3,7},{7,3},{8,12},{12,8},{9,1... | collective-permute-start | bytes 393224 | tf_op jit(solution)/shard_map/ppermute | solution.py:27
  27.6 20.3 %collective-permute-start.10 = (bf16[2,64,1024]{2,1,0:T(8,128)(2,1)S(1)}, bf16[2,64,1024]{2,1,0:T(8,128)(2,1)S(1)}, u32[]{:S(2)}, u32[]{:S(2)}) collective-permute-start(bf16[2,64,1024]{2,1,0:T(8,128)(2,1)S(1)} %shard_map.114.d0), channel_id=1, source_target_pairs={{0,3},{1,0},{2,1},{3,2},{4,7},{5,4},{6,5},{7,6},{8,11},{9,8},{10,9... | collective-permute-start | bytes 786440 | tf_op jit(solution)/shard_map/ppermute | solution.py:27
  35.4 12.4 %collective-permute-start.9 = (bf16[2,64,1024]{2,1,0:T(8,128)(2,1)S(1)}, bf16[2,64,1024]{2,1,0:T(8,128)(2,1)S(1)}, u32[]{:S(2)}, u32[]{:S(2)}) collective-permute-start(bf16[2,64,1024]{2,1,0:T(8,128)(2,1)S(1)} %shard_map.114.d0), channel_id=1, source_target_pairs={{0,2},{1,3},{2,0},{3,1},{4,6},{5,7},{6,4},{7,5},{8,10},{9,11},{10,... | collective-permute-start | bytes 786440 | tf_op jit(solution)/shard_map/ppermute | solution.py:27
  36.6 8.4 %collective-permute-start.6 = (bf16[256,128]{1,0:T(8,128)(2,1)S(1)}, bf16[256,128]{1,0:T(8,128)(2,1)S(1)}, u32[]{:S(2)}, u32[]{:S(2)}) collective-permute-start(bf16[256,128]{1,0:T(8,128)(2,1)S(1)} %get-tuple-element.51), channel_id=1, source_target_pairs={{0,64},{32,96},{64,0},{96,32},{1,65},{33,97},{65,1},{97,33},{2,66}... | collective-permute-start | bytes 196616 | tf_op jit(solution)/shard_map/ppermute | solution.py:27
  39.2 8.6 %collective-permute-start.7 = (bf16[256,128]{1,0:T(8,128)(2,1)S(1)}, bf16[256,128]{1,0:T(8,128)(2,1)S(1)}, u32[]{:S(2)}, u32[]{:S(2)}) collective-permute-start(bf16[256,128]{1,0:T(8,128)(2,1)S(1)} %get-tuple-element.52), channel_id=1, source_target_pairs={{0,32},{32,64},{64,96},{96,0},{1,33},{33,65},{65,97},{97,1},{2,34}... | collective-permute-start | bytes 196616 | tf_op jit(solution)/shard_map/ppermute | solution.py:27
  41.5 6.3 %collective-permute-start.8 = (bf16[256,128]{1,0:T(8,128)(2,1)S(1)}, bf16[256,128]{1,0:T(8,128)(2,1)S(1)}, u32[]{:S(2)}, u32[]{:S(2)}) collective-permute-start(bf16[256,128]{1,0:T(8,128)(2,1)S(1)} %get-tuple-element.53), channel_id=1, source_target_pairs={{0,96},{32,0},{64,32},{96,64},{1,97},{33,1},{65,33},{97,65},{2,98}... | collective-permute-start | bytes 196616 | tf_op jit(solution)/shard_map/ppermute | solution.py:27
  47.9 6.3 %collective-permute-start.14 = (bf16[256,128]{1,0:T(8,128)(2,1)S(1)}, bf16[256,128]{1,0:T(8,128)(2,1)S(1)}, u32[]{:S(2)}, u32[]{:S(2)}) collective-permute-start(bf16[256,128]{1,0:T(8,128)(2,1)S(1)} %shard_map.117), channel_id=1, source_target_pairs={{0,8},{8,16},{16,24},{24,0},{1,9},{9,17},{17,25},{25,1},{2,10},{10... | collective-permute-start | bytes 196616 | tf_op jit(solution)/shard_map/ppermute | solution.py:27
  49.7 6.1 %collective-permute-start.13 = (bf16[256,128]{1,0:T(8,128)(2,1)S(1)}, bf16[256,128]{1,0:T(8,128)(2,1)S(1)}, u32[]{:S(2)}, u32[]{:S(2)}) collective-permute-start(bf16[256,128]{1,0:T(8,128)(2,1)S(1)} %shard_map.117), channel_id=1, source_target_pairs={{0,16},{8,24},{16,0},{24,8},{1,17},{9,25},{17,1},{25,9},{2,18},{10... | collective-permute-start | bytes 196616 | tf_op jit(solution)/shard_map/ppermute | solution.py:27
  52.4 4.3 %collective-permute-start.12 = (bf16[256,128]{1,0:T(8,128)(2,1)S(1)}, bf16[256,128]{1,0:T(8,128)(2,1)S(1)}, u32[]{:S(2)}, u32[]{:S(2)}) collective-permute-start(bf16[256,128]{1,0:T(8,128)(2,1)S(1)} %shard_map.117), channel_id=1, source_target_pairs={{0,24},{8,0},{16,8},{24,16},{1,25},{9,1},{17,9},{25,17},{2,26},{10... | collective-permute-start | bytes 196616 | tf_op jit(solution)/shard_map/ppermute | solution.py:27
  52.7 8.6 %collective-permute-start.11 = (bf16[2,64,1024]{2,1,0:T(8,128)(2,1)S(1)}, bf16[2,64,1024]{2,1,0:T(8,128)(2,1)S(1)}, u32[]{:S(2)}, u32[]{:S(2)}) collective-permute-start(bf16[2,64,1024]{2,1,0:T(8,128)(2,1)S(1)} %shard_map.114.d0), channel_id=1, source_target_pairs={{0,1},{1,2},{2,3},{3,0},{4,5},{5,6},{6,7},{7,4},{8,9},{9,10},{10,1... | collective-permute-start | bytes 786440 | tf_op jit(solution)/shard_map/ppermute | solution.py:27
  56.7 4.6 %collective-permute-start.15 = (bf16[4,256,128]{2,1,0:T(8,128)(2,1)S(1)}, bf16[4,256,128]{2,1,0:T(8,128)(2,1)S(1)}, u32[]{:S(2)}, u32[]{:S(2)}) collective-permute-start(bf16[4,256,128]{2,1,0:T(8,128)(2,1)S(1)} %pad_maximum_fusion.u.u_own), channel_id=1, source_target_pairs={{0,128},{128,0},{1,129},{129,1},{2,130},{130,2},{3,131},{131,3},{4... | collective-permute-start | bytes 786440 | tf_op jit(solution)/shard_map/ppermute | solution.py:27
  62.9 12.2 %all-to-all-start = ((bf16[4,64,128]{2,1,0:T(8,128)(2,1)}), bf16[4,64,128]{2,1,0:T(8,128)(2,1)S(1)}, u32[]{:S(2)}, u32[]{:S(2)}) async-start(bf16[4,64,128]{2,1,0:T(8,128)(2,1)} %shard_map.120), calls=%async_computation | async-start | bytes 131072 | tf_op jit(solution)/shard_map/all_to_all | solution.py:311
  (1 other events, 1.0 us)

commit v7 on v6

--- a/solution.py
+++ b/solution.py
@@ -62,11 +62,13 @@
 
 def partial_gradient(place, normed_inputs, value_cotangent):
     tokens = normed_inputs.shape[0]
+    normed_inputs = pltpu.with_memory_space_constraint(normed_inputs, pltpu.HBM)
+    value_cotangent = pltpu.with_memory_space_constraint(value_cotangent, pltpu.HBM)
     return pl.pallas_call(
         partial_kernel,
         in_specs=[SMEM, HBM, HBM],
         out_specs=[VMEM, VMEM],
-        out_shape=[jax.ShapeDtypeStruct((4, 4, 256, HD), BF16)] * 2,
+        out_shape=[pltpu.VMEM((4, 4, 256, HD), BF16)] * 2,
         scratch_shapes=[
             pltpu.VMEM((8, tokens, 1024), BF16),
             pltpu.VMEM((tokens, HD), BF16),
@@ -79,12 +81,14 @@
     )(place, normed_inputs, value_cotangent)
 
 
-def small_call(kernel, outs, *args):
+def small_call(kernel, outs, *args, keep=True):
     return pl.pallas_call(
         kernel,
         in_specs=[VMEM] * len(args),
         out_specs=[VMEM] * len(outs),
-        out_shape=[jax.ShapeDtypeStruct(shape, dtype) for shape, dtype in outs],
+        out_shape=[
+            (pltpu.VMEM if keep else jax.ShapeDtypeStruct)(shape, dtype) for shape, dtype in outs
+        ],
         compiler_params=pltpu.CompilerParams(vmem_limit_bytes=16 * MIB),
         cost_estimate=pl.CostEstimate(flops=MIB, bytes_accessed=2 * MIB, transcendentals=0),
     )(*args)
@@ -182,35 +186,34 @@
     return lax.rem(place[3] + d + 4 - place[1], 4)
 
 
-def project_own_kernel(place, d0, d1, d2, u, out_ref, rows):
+def project_own_kernel(place, d0, u, out_ref, rows):
     own = jnp.where(place[0] == place[4], 0, 1)
     fill_rows(rows, place[2], u)
-    for d, piece in enumerate((d0, d1, d2)):
-        out_ref[tokens_of(place, d)] = jnp.dot(
-            piece[own], rows[...], preferred_element_type=F32
-        )
+    out_ref[0] = jnp.dot(d0[own], rows[...], preferred_element_type=F32)
 
 
 def project_rest_kernel(place, d0, d1, d2, d3, u_own, u_other, start, out_ref, rows, last):
     own = jnp.where(place[0] == place[4], 0, 1)
     fill_rows(last, place[2], u_own)
     fill_rows(rows, place[2], u_other)
-    for d, piece in enumerate((d0, d1, d2, d3)):
-        zh = tokens_of(place, d)
-        product = jnp.dot(piece[1 - own], rows[...], preferred_element_type=F32)
-        if d < 3:
-            product += start[zh]
-        else:
-            product += jnp.dot(piece[own], last[...], preferred_element_type=F32)
-        out_ref[zh] = product.astype(out_ref.dtype)
-
-
-def project(kernel, dtype, scratches, place, *args):
+    pieces = (d0, d1, d2, d3)
+    inputs = jnp.concatenate([piece[1 - own] for piece in pieces], axis=0)
+    product = jnp.dot(inputs, rows[...], preferred_element_type=F32)
+    inputs = jnp.concatenate([piece[own] for piece in pieces[1:]], axis=0)
+    more = jnp.dot(inputs, last[...], preferred_element_type=F32)
+    for d in range(4):
+        rest = start[0] if d == 0 else more[(d - 1) * 64 : d * 64]
+        out_ref[tokens_of(place, d)] = (product[d * 64 : (d + 1) * 64] + rest).astype(
+            out_ref.dtype
+        )
+
+
+def project(kernel, out_shape, scratches, place, *args):
     return pl.pallas_call(
         kernel,
         in_specs=[SMEM] + [VMEM] * len(args),
         out_specs=VMEM,
-        out_shape=jax.ShapeDtypeStruct((4, 64, HD), dtype),
+        out_shape=out_shape,
         scratch_shapes=[pltpu.VMEM((1024, HD), BF16)] * scratches,
         compiler_params=pltpu.CompilerParams(vmem_limit_bytes=16 * MIB),
         cost_estimate=pl.CostEstimate(
@@ -265,19 +268,20 @@
     places = row_count * step_count
     place = jnp.stack([core, high, x, y, low])
 
+    second = shift(decode_inputs, "zl", 1)
     theirs, mine = partial_gradient(place, normed_inputs, value_cotangent)
+    theirs, mine, second = lax.optimization_barrier((theirs, mine, second))
     received = shift(theirs, "c", 1)
-    swapped = swap_high(after(decode_inputs, theirs))
 
     rows = (4, 256, HD)
     own, *sent = small_call(
         core_sum_kernel, [(rows, F32)] + [(rows, BF16)] * 3, mine, received
     )
     along_x = [shift(sent[d - 1], "x", d) for d in (2, 1, 3)]
-    swapped = after(swapped, own)
     (both,) = small_call(
-        join_kernel, [((2, places, D // 8), BF16)], swapped, shift(swapped, "zl", 1)
-    )
+        join_kernel, [((2, places, D // 8), BF16)], after(decode_inputs, own), second
+    )
+    both = swap_high(both)
     attended_cache, fresh_weights = attend_cache(
         lengths,
         after(queries.reshape(places, -1), own),
@@ -286,27 +290,36 @@
         cache_values,
     )
 
-    own, *along_x, both, attended_cache, fresh_weights = lax.optimization_barrier(
-        (own, *along_x, both, attended_cache, fresh_weights)
+    own, *along_x, attended_cache, fresh_weights = lax.optimization_barrier(
+        (own, *along_x, attended_cache, fresh_weights)
     )
     rows = (256, HD)
     own, *sent = small_call(
         x_sum_kernel, [(rows, F32)] + [(rows, BF16)] * 3, own, *along_x
     )
     along_z = [shift(sent[e - 1], "zh", e) for e in (2, 1, 3)]
-    both = after(both, own)
     from_y2, from_y1, from_y3 = (shift(both, "y", -d) for d in (2, 1, 3))
-    own, *along_z, from_y2, from_y1 = lax.optimization_barrier((own, *along_z, from_y2, from_y1))
     (updated,) = small_call(update_kernel, [(rows, BF16)], value_weight, own, *along_z)
     own = after(own, updated)
-    (gradient,) = small_call(gradient_kernel, [(rows, F32)], own, *along_z)
+    (gradient,) = small_call(gradient_kernel, [(rows, F32)], own, *along_z, keep=False)
 
     gathered = jnp.stack([updated] + [shift(updated, "x", -d) for d in (1, 2, 3)])
     other = shift(gathered, "c", 1)
-    pieces = (both, from_y1, from_y2)
-    partial = project(project_own_kernel, F32, 1, place, *pieces, gathered)
     partial = project(
-        project_rest_kernel, BF16, 2, place, *pieces, from_y3, gathered, other, partial
+        project_own_kernel, pltpu.VMEM((1, places, HD), F32), 1, place, both, gathered
+    )
+    partial = project(
+        project_rest_kernel,
+        jax.ShapeDtypeStruct((4, places, HD), BF16),
+        2,
+        place,
+        both,
+        from_y1,
+        from_y2,
+        from_y3,
+        gathered,
+        other,
+        partial,
     )
     exchanged = lax.all_to_all(partial, "zh", 0, 0, tiled=True)
     new_values, attended = finish(

time: 77.1 us -> 83 us (1.077)
  waiting for transfers between devices: 27.3 us -> 38.4 us
  starting transfers between devices: 33.2 us -> 29.1 us
  local copies, waits for them, and re-layouts: 1.14 us -> 0.15 us
    ppermute x15, waiting for transfers between devices: 19.8 us -> 30.9 us  [shift(): return lax.ppermute(value, axis, [(i, (i + by) % n) for i in range(n)])]
    ppermute x15, starting transfers between devices: 28.6 us -> 20.2 us  [shift(): return lax.ppermute(value, axis, [(i, (i + by) % n) for i in range(n)])]
    all_to_all x1, starting transfers between devices: 3.97 us -> 8.17 us  [shards(): exchanged = lax.all_to_all(partial, 'zh', 0, 0, tiled=True)]
    unnamed x16 -> x14, local copies, waits for them, and re-layouts: 1.02 us -> 0.03 us
  transfers between devices with their start and end apart: 17 -> 17, of which waited for: 10 -> 10; matrix products, arithmetic and copies ran while one was open for 0% -> 0% of each run, Pallas kernels for 6% -> 12%
where the time goes in v7:
time: 83 us; the launch traced here: 81.7 us
  waiting for transfers between devices  38.4 us (46%)
  starting transfers between devices  29.1 us (35%)
  Pallas kernels  13.2 us (16%)
    ppermute x15, waiting for transfers between devices, shift(): return lax.ppermute(value, axis, [(i, (i + by) % n) for i in range(n)])  30.9 us
    ppermute x15, starting transfers between devices, shift(): return lax.ppermute(value, axis, [(i, (i + by) % n) for i in range(n)])  20.2 us
    all_to_all x1, starting transfers between devices, shards(): exchanged = lax.all_to_all(partial, 'zh', 0, 0, tiled=True)  8.17 us
    all_to_all x1, waiting for transfers between devices, shards(): exchanged = lax.all_to_all(partial, 'zh', 0, 0, tiled=True)  7.52 us
    pallas_call x1, Pallas kernels, partial_gradient(): pl.pallas_call(partial_kernel, in_specs=[SMEM, HBM, HBM], out_specs=[VMEM...  5.96 us
    pallas_call x2, Pallas kernels, project(): pl.pallas_call(kernel, in_specs=[SMEM] + [VMEM] * len(args), out_specs=VM...  2.34 us
    pallas_call x1, Pallas kernels, attend_cache(): pl.pallas_call(attend_kernel, in_specs=[SMEM] + [VMEM] * 4, out_specs=[VM...  2.13 us
    pallas_call x5, Pallas kernels, small_call(): pl.pallas_call(kernel, in_specs=[VMEM] * len(args), out_specs=[VMEM] * le...  1.97 us
  transfers between devices with their start and end apart: 17, of which 10 were waited for; matrix products, arithmetic and copies ran while one was open for 0% of the time, Pallas kernels for 12%

profile of v7, /device:TPU:32, one launch (start us, length us, event | category | flops | bytes accessed | tf_op | source)
XLA Modules:
  0.0 81.7 jit_solution(4237013632183344566)
XLA Ops:
  0.7 1.9 %collective-permute-start = (bf16[16,4,1024]{2,1,0:T(4,128)(2,1)}, bf16[16,4,1024]{2,1,0:T(4,128)(2,1)S(1)}, u32[]{:S(2)}, u32[]{:S(2)}) collective-permute-start(bf16[16,4,1024]{2,1,0:T(4,128)(2,1)} %first), channel_id=1, source_target_pairs={{0,4},{4,0},{1,5},{5,1},{2,6},{6,2},{3,7},{7,3},{8,12},{12,8},{9,1... | collective-permute-start | bytes 393224 | tf_op jit(solution)/shard_map/ppermute | solution.py:27
  2.7 6.0 %shard_map.112 = (bf16[4,4,256,128]{3,2,1,0:T(8,128)(2,1)S(1)}, bf16[4,4,256,128]{3,2,1,0:T(8,128)(2,1)S(1)}) custom-call(s32[5]{0:T(128)S(1)} %stack.38.place, bf16[768,8192]{1,0:T(8,128)(2,1)} %x_hbm.1, bf16[768,128]{1,0:T(8,128)(2,1)} %v_hbm.1), custom_call_target="tpu_custom_call" | custom-call | flops 1610612736 | bytes 12582912 | tf_op jit(solution)/shard_map/pallas_call | solution.py:67
  8.8 2.6 %collective-permute-done.1.received = bf16[4,4,256,128]{3,2,1,0:T(8,128)(2,1)S(1)} collective-permute-done((bf16[4,4,256,128]{3,2,1,0:T(8,128)(2,1)S(1)}, bf16[4,4,256,128]{3,2,1,0:T(8,128)(2,1)S(1)}, u32[]{:S(2)}, u32[]{:S(2)}) %collective-permute-start.1) | collective-permute-done | bytes 1048608 | tf_op jit(solution)/shard_map/ppermute | solution.py:27
  11.4 1.1 %shard_map.113 = (f32[4,256,128]{2,1,0:T(8,128)S(1)}, bf16[4,256,128]{2,1,0:T(8,128)(2,1)}, bf16[4,256,128]{2,1,0:T(8,128)(2,1)}, bf16[4,256,128]{2,1,0:T(8,128)(2,1)}) custom-call(bf16[4,4,256,128]{3,2,1,0:T(8,128)(2,1)S(1)} %get-tuple-element.31.mine, bf16[4,4,256,128]{3,2,1,0:T(8,128)(2,1)S(1)} %collective-permute-done.1.received), custom_call_target="tpu_custom_call" | custom-call | flops 1048576 | bytes 2097152 | tf_op jit(solution)/shard_map/pallas_call | solution.py:85
  12.5 1.3 %collective-permute-start.2 = (bf16[4,256,128]{2,1,0:T(8,128)(2,1)}, bf16[4,256,128]{2,1,0:T(8,128)(2,1)S(1)}, u32[]{:S(2)}, u32[]{:S(2)}) collective-permute-start(bf16[4,256,128]{2,1,0:T(8,128)(2,1)} %get-tuple-element.34), channel_id=1, source_target_pairs={{0,16},{8,24},{16,0},{24,8},{1,17},{9,25},{17,1},{25,9},{2,18},{10... | collective-permute-start | bytes 786440 | tf_op jit(solution)/shard_map/ppermute | solution.py:27
  14.4 2.6 %collective-permute-start.4 = (bf16[4,256,128]{2,1,0:T(8,128)(2,1)}, bf16[4,256,128]{2,1,0:T(8,128)(2,1)S(1)}, u32[]{:S(2)}, u32[]{:S(2)}) collective-permute-start(bf16[4,256,128]{2,1,0:T(8,128)(2,1)} %get-tuple-element.36), channel_id=1, source_target_pairs={{0,24},{8,0},{16,8},{24,16},{1,25},{9,1},{17,9},{25,17},{2,26},{10... | collective-permute-start | bytes 786440 | tf_op jit(solution)/shard_map/ppermute | solution.py:27
  17.9 2.1 %shard_map.114 = (f32[512,128]{1,0:T(8,128)S(1)}, bf16[512,64]{1,0:T(8,128)(2,1)S(1)}) custom-call(s32[16]{0:T(128)S(1)} %copy-done.5, bf16[64,1024]{1,0:T(8,128)(2,1)S(1)} %reshape.12.queries, bf16[64,128]{1,0:T(8,128)(2,1)S(1)} %bitcast.11, bf16[16,128,128]{2,1,0:T(8,128)(2,1)S(1)} %copy-done, bf16[16,128,128]{2,1,0:T(8,128)(2,1)S(1)} %copy-done.1), custom_call_target="tpu_custom_call" | custom-call | flops 1048576 | bytes 262144 | tf_op jit(solution)/shard_map/pallas_call | solution.py:165
  20.0 3.4 %collective-permute-done.2.r1 = bf16[4,256,128]{2,1,0:T(8,128)(2,1)S(1)} collective-permute-done((bf16[4,256,128]{2,1,0:T(8,128)(2,1)}, bf16[4,256,128]{2,1,0:T(8,128)(2,1)S(1)}, u32[]{:S(2)}, u32[]{:S(2)}) %collective-permute-start.2) | collective-permute-done | bytes 262176 | tf_op jit(solution)/shard_map/ppermute | solution.py:27
  23.4 4.8 %collective-permute-done.3.r2 = bf16[4,256,128]{2,1,0:T(8,128)(2,1)S(1)} collective-permute-done((bf16[4,256,128]{2,1,0:T(8,128)(2,1)}, bf16[4,256,128]{2,1,0:T(8,128)(2,1)S(1)}, u32[]{:S(2)}, u32[]{:S(2)}) %collective-permute-start.3) | collective-permute-done | bytes 262176 | tf_op jit(solution)/shard_map/ppermute | solution.py:27
  28.3 5.7 %collective-permute-start.5 = (bf16[256,128]{1,0:T(8,128)(2,1)S(1)}, bf16[256,128]{1,0:T(8,128)(2,1)S(1)}, u32[]{:S(2)}, u32[]{:S(2)}) collective-permute-start(bf16[256,128]{1,0:T(8,128)(2,1)S(1)} %get-tuple-element.45), channel_id=1, source_target_pairs={{0,64},{32,96},{64,0},{96,32},{1,65},{33,97},{65,1},{97,33},{2,66}... | collective-permute-start | bytes 196616 | tf_op jit(solution)/shard_map/ppermute | solution.py:27
  34.0 1.5 %collective-permute-start.6 = (bf16[256,128]{1,0:T(8,128)(2,1)S(1)}, bf16[256,128]{1,0:T(8,128)(2,1)S(1)}, u32[]{:S(2)}, u32[]{:S(2)}) collective-permute-start(bf16[256,128]{1,0:T(8,128)(2,1)S(1)} %get-tuple-element.46), channel_id=1, source_target_pairs={{0,32},{32,64},{64,96},{96,0},{1,33},{33,65},{65,97},{97,1},{2,34}... | collective-permute-start | bytes 196616 | tf_op jit(solution)/shard_map/ppermute | solution.py:27
  35.4 2.7 %collective-permute-start.7 = (bf16[256,128]{1,0:T(8,128)(2,1)S(1)}, bf16[256,128]{1,0:T(8,128)(2,1)S(1)}, u32[]{:S(2)}, u32[]{:S(2)}) collective-permute-start(bf16[256,128]{1,0:T(8,128)(2,1)S(1)} %get-tuple-element.47), channel_id=1, source_target_pairs={{0,96},{32,0},{64,32},{96,64},{1,97},{33,1},{65,33},{97,65},{2,98}... | collective-permute-start | bytes 196616 | tf_op jit(solution)/shard_map/ppermute | solution.py:27
  38.1 9.8 %collective-permute-done.6.r2 = bf16[256,128]{1,0:T(8,128)(2,1)S(1)} collective-permute-done((bf16[256,128]{1,0:T(8,128)(2,1)S(1)}, bf16[256,128]{1,0:T(8,128)(2,1)S(1)}, u32[]{:S(2)}, u32[]{:S(2)}) %collective-permute-start.6) | collective-permute-done | bytes 65568 | tf_op jit(solution)/shard_map/ppermute | solution.py:27
  48.4 1.1 %collective-permute-start.13 = (bf16[256,128]{1,0:T(8,128)(2,1)S(1)}, bf16[256,128]{1,0:T(8,128)(2,1)S(1)}, u32[]{:S(2)}, u32[]{:S(2)}) collective-permute-start(bf16[256,128]{1,0:T(8,128)(2,1)S(1)} %shard_map.116), channel_id=1, source_target_pairs={{0,16},{8,24},{16,0},{24,8},{1,17},{9,25},{17,1},{25,9},{2,18},{10... | collective-permute-start | bytes 196616 | tf_op jit(solution)/shard_map/ppermute | solution.py:27
  50.8 1.6 %collective-permute-done.12 = bf16[256,128]{1,0:T(8,128)(2,1)S(1)} collective-permute-done((bf16[256,128]{1,0:T(8,128)(2,1)S(1)}, bf16[256,128]{1,0:T(8,128)(2,1)S(1)}, u32[]{:S(2)}, u32[]{:S(2)}) %collective-permute-start.12) | collective-permute-done | bytes 65568 | tf_op jit(solution)/shard_map/ppermute | solution.py:27
  52.3 1.0 %collective-permute-start.9 = (bf16[2,64,1024]{2,1,0:T(8,128)(2,1)S(1)}, bf16[2,64,1024]{2,1,0:T(8,128)(2,1)S(1)}, u32[]{:S(2)}, u32[]{:S(2)}) collective-permute-start(bf16[2,64,1024]{2,1,0:T(8,128)(2,1)S(1)} %collective-permute-done.8.d0), channel_id=1, source_target_pairs={{0,3},{1,0},{2,1},{3,2},{4,7},{5,4},{6,5},{7,6},{8,11},{9,8},{10,9... | collective-permute-start | bytes 786440 | tf_op jit(solution)/shard_map/ppermute | solution.py:27
  53.3 0.8 collective-permute-done.13
  54.1 0.9 %collective-permute-done.14 = bf16[256,128]{1,0:T(8,128)(2,1)S(1)} collective-permute-done((bf16[256,128]{1,0:T(8,128)(2,1)S(1)}, bf16[256,128]{1,0:T(8,128)(2,1)S(1)}, u32[]{:S(2)}, u32[]{:S(2)}) %collective-permute-start.14) | collective-permute-done | bytes 65568 | tf_op jit(solution)/shard_map/ppermute | solution.py:27
  55.9 4.6 %collective-permute-done.10.d2 = bf16[2,64,1024]{2,1,0:T(8,128)(2,1)S(1)} collective-permute-done((bf16[2,64,1024]{2,1,0:T(8,128)(2,1)S(1)}, bf16[2,64,1024]{2,1,0:T(8,128)(2,1)S(1)}, u32[]{:S(2)}, u32[]{:S(2)}) %collective-permute-start.10) | collective-permute-done | bytes 262176 | tf_op jit(solution)/shard_map/ppermute | solution.py:27
  60.4 2.4 %collective-permute-done.11.d3 = bf16[2,64,1024]{2,1,0:T(8,128)(2,1)S(1)} collective-permute-done((bf16[2,64,1024]{2,1,0:T(8,128)(2,1)S(1)}, bf16[2,64,1024]{2,1,0:T(8,128)(2,1)S(1)}, u32[]{:S(2)}, u32[]{:S(2)}) %collective-permute-start.11) | collective-permute-done | bytes 262176 | tf_op jit(solution)/shard_map/ppermute | solution.py:27
  62.9 1.6 %shard_map.120 = bf16[4,64,128]{2,1,0:T(8,128)(2,1)} custom-call(s32[5]{0:T(128)S(1)} %stack.38.place, bf16[2,64,1024]{2,1,0:T(8,128)(2,1)S(1)} %collective-permute-done.8.d0, bf16[2,64,1024]{2,1,0:T(8,128)(2,1)S(1)} %collective-permute-done.9.d1, bf16[2,64,1024]{2,1,0:T(8,128)(2,1)S(1)} %collective-permute-done.10.d2, ...), custom_call_target="tpu_custom_call" | custom-call | flops 67108864 | bytes 786432 | tf_op jit(solution)/shard_map/pallas_call | solution.py:212
  64.5 8.2 %all-to-all-start = ((bf16[4,64,128]{2,1,0:T(8,128)(2,1)}), bf16[4,64,128]{2,1,0:T(8,128)(2,1)S(1)}, u32[]{:S(2)}, u32[]{:S(2)}) async-start(bf16[4,64,128]{2,1,0:T(8,128)(2,1)} %shard_map.120), calls=%async_computation | async-start | bytes 131072 | tf_op jit(solution)/shard_map/all_to_all | solution.py:324
  73.3 7.5 %all-to-all-done.parts = bf16[4,64,128]{2,1,0:T(8,128)(2,1)S(1)} async-done(((bf16[4,64,128]{2,1,0:T(8,128)(2,1)}), bf16[4,64,128]{2,1,0:T(8,128)(2,1)S(1)}, u32[]{:S(2)}, u32[]{:S(2)}) %all-to-all-start) | async-done | bytes 65568 | tf_op jit(solution)/shard_map/all_to_all | solution.py:324
  80.8 0.8 %shard_map.121 = (bf16[16,4,128]{2,1,0:T(4,128)(2,1)}, bf16[16,4,1024]{2,1,0:T(4,128)(2,1)}) custom-call(bf16[4,64,128]{2,1,0:T(8,128)(2,1)S(1)} %all-to-all-done.parts, f32[512,128]{1,0:T(8,128)S(1)} %get-tuple-element.51.mixed, bf16[512,64]{1,0:T(8,128)(2,1)S(1)} %get-tuple-element.52.weights), custom_call_target="tpu_custom_call" | custom-call | tf_op jit(solution)/shard_map/pallas_call | solution.py:243
  (37 shorter events, 4.9 us)
Async XLA Ops:
  0.6 16.4 %copy-start.2 = (bf16[16,4,1024]{2,1,0:T(4,128)(2,1)S(1)}, bf16[16,4,1024]{2,1,0:T(4,128)(2,1)}, u32[]{:S(2)}) copy-start(bf16[16,4,1024]{2,1,0:T(4,128)(2,1)} %first) | copy-start | bytes 393220
  0.6 17.1 %copy-start.6 = (bf16[16,4,1024]{2,1,0:T(4,128)(2,1)S(1)}, bf16[16,4,1024]{2,1,0:T(4,128)(2,1)}, u32[]{:S(2)}) copy-start(bf16[16,4,1024]{2,1,0:T(4,128)(2,1)} %param.13) | copy-start | bytes 393220
  0.7 17.2 %copy-start.4 = (bf16[16,4,128]{2,1,0:T(4,128)(2,1)S(1)}, bf16[16,4,128]{2,1,0:T(4,128)(2,1)}, u32[]{:S(2)}) copy-start(bf16[16,4,128]{2,1,0:T(4,128)(2,1)} %param.14) | copy-start | bytes 49156
  0.7 17.2 %copy-start = (bf16[16,128,128]{2,1,0:T(8,128)(2,1)S(1)}, bf16[16,128,128]{2,1,0:T(8,128)(2,1)}, u32[]{:S(2)}) copy-start(bf16[16,128,128]{2,1,0:T(8,128)(2,1)} %cache_keys.1) | copy-start | bytes 1572868
  0.7 17.2 %copy-start.1 = (bf16[16,128,128]{2,1,0:T(8,128)(2,1)S(1)}, bf16[16,128,128]{2,1,0:T(8,128)(2,1)}, u32[]{:S(2)}) copy-start(bf16[16,128,128]{2,1,0:T(8,128)(2,1)} %cache_values.1) | copy-start | bytes 1572868
  0.7 17.2 %copy-start.5 = (s32[16]{0:T(128)S(1)}, s32[16]{0:T(128)}, u32[]{:S(2)}) copy-start(s32[16]{0:T(128)} %lengths.1) | copy-start | bytes 196
  0.7 47.2 %copy-start.3 = (bf16[256,128]{1,0:T(8,128)(2,1)S(1)}, bf16[256,128]{1,0:T(8,128)(2,1)}, u32[]{:S(2)}) copy-start(bf16[256,128]{1,0:T(8,128)(2,1)} %weight.1) | copy-start | bytes 196612
  0.7 8.0 %collective-permute-start = (bf16[16,4,1024]{2,1,0:T(4,128)(2,1)}, bf16[16,4,1024]{2,1,0:T(4,128)(2,1)S(1)}, u32[]{:S(2)}, u32[]{:S(2)}) collective-permute-start(bf16[16,4,1024]{2,1,0:T(4,128)(2,1)} %first), channel_id=1, source_target_pairs={{0,4},{4,0},{1,5},{5,1},{2,6},{6,2},{3,7},{7,3},{8,12},{12,8},{9,1... | collective-permute-start | bytes 393224 | tf_op jit(solution)/shard_map/ppermute | solution.py:27
  8.7 2.7 %collective-permute-start.1 = (bf16[4,4,256,128]{3,2,1,0:T(8,128)(2,1)S(1)}, bf16[4,4,256,128]{3,2,1,0:T(8,128)(2,1)S(1)}, u32[]{:S(2)}, u32[]{:S(2)}) collective-permute-start(bf16[4,4,256,128]{3,2,1,0:T(8,128)(2,1)S(1)} %get-tuple-element.32), channel_id=1, source_target_pairs={{0,128},{128,0},{1,129},{129,1},{2,130},{130,2},{3,131},{131,3},{4... | collective-permute-start | bytes 3145736 | tf_op jit(solution)/shard_map/ppermute | solution.py:27
  12.5 10.9 %collective-permute-start.2 = (bf16[4,256,128]{2,1,0:T(8,128)(2,1)}, bf16[4,256,128]{2,1,0:T(8,128)(2,1)S(1)}, u32[]{:S(2)}, u32[]{:S(2)}) collective-permute-start(bf16[4,256,128]{2,1,0:T(8,128)(2,1)} %get-tuple-element.34), channel_id=1, source_target_pairs={{0,16},{8,24},{16,0},{24,8},{1,17},{9,25},{17,1},{25,9},{2,18},{10... | collective-permute-start | bytes 786440 | tf_op jit(solution)/shard_map/ppermute | solution.py:27
  13.8 14.4 %collective-permute-start.3 = (bf16[4,256,128]{2,1,0:T(8,128)(2,1)}, bf16[4,256,128]{2,1,0:T(8,128)(2,1)S(1)}, u32[]{:S(2)}, u32[]{:S(2)}) collective-permute-start(bf16[4,256,128]{2,1,0:T(8,128)(2,1)} %get-tuple-element.35), channel_id=1, source_target_pairs={{0,8},{8,16},{16,24},{24,0},{1,9},{9,17},{17,25},{25,1},{2,10},{10... | collective-permute-start | bytes 786440 | tf_op jit(solution)/shard_map/ppermute | solution.py:27
  14.4 13.8 %collective-permute-start.4 = (bf16[4,256,128]{2,1,0:T(8,128)(2,1)}, bf16[4,256,128]{2,1,0:T(8,128)(2,1)S(1)}, u32[]{:S(2)}, u32[]{:S(2)}) collective-permute-start(bf16[4,256,128]{2,1,0:T(8,128)(2,1)} %get-tuple-element.36), channel_id=1, source_target_pairs={{0,24},{8,0},{16,8},{24,16},{1,25},{9,1},{17,9},{25,17},{2,26},{10... | collective-permute-start | bytes 786440 | tf_op jit(solution)/shard_map/ppermute | solution.py:27
  17.1 33.0 %collective-permute-start.8 = (bf16[2,64,1024]{2,1,0:T(8,128)(2,1)S(1)}, bf16[2,64,1024]{2,1,0:T(8,128)(2,1)S(1)}, u32[]{:S(2)}, u32[]{:S(2)}) collective-permute-start(bf16[2,64,1024]{2,1,0:T(8,128)(2,1)S(1)} %shard_map.118), channel_id=1, source_target_pairs={{0,0},{1,33},{2,66},{3,99},{32,1},{33,34},{34,67},{35,96},{64,2},{... | collective-permute-start | bytes 786440 | tf_op jit(solution)/shard_map/ppermute | solution.py:32
  28.3 9.8 %collective-permute-start.5 = (bf16[256,128]{1,0:T(8,128)(2,1)S(1)}, bf16[256,128]{1,0:T(8,128)(2,1)S(1)}, u32[]{:S(2)}, u32[]{:S(2)}) collective-permute-start(bf16[256,128]{1,0:T(8,128)(2,1)S(1)} %get-tuple-element.45), channel_id=1, source_target_pairs={{0,64},{32,96},{64,0},{96,32},{1,65},{33,97},{65,1},{97,33},{2,66}... | collective-permute-start | bytes 196616 | tf_op jit(solution)/shard_map/ppermute | solution.py:27
  34.0 13.9 %collective-permute-start.6 = (bf16[256,128]{1,0:T(8,128)(2,1)S(1)}, bf16[256,128]{1,0:T(8,128)(2,1)S(1)}, u32[]{:S(2)}, u32[]{:S(2)}) collective-permute-start(bf16[256,128]{1,0:T(8,128)(2,1)S(1)} %get-tuple-element.46), channel_id=1, source_target_pairs={{0,32},{32,64},{64,96},{96,0},{1,33},{33,65},{65,97},{97,1},{2,34}... | collective-permute-start | bytes 196616 | tf_op jit(solution)/shard_map/ppermute | solution.py:27
  35.4 12.5 %collective-permute-start.7 = (bf16[256,128]{1,0:T(8,128)(2,1)S(1)}, bf16[256,128]{1,0:T(8,128)(2,1)S(1)}, u32[]{:S(2)}, u32[]{:S(2)}) collective-permute-start(bf16[256,128]{1,0:T(8,128)(2,1)S(1)} %get-tuple-element.47), channel_id=1, source_target_pairs={{0,96},{32,0},{64,32},{96,64},{1,97},{33,1},{65,33},{97,65},{2,98}... | collective-permute-start | bytes 196616 | tf_op jit(solution)/shard_map/ppermute | solution.py:27
  48.0 4.3 %collective-permute-start.12 = (bf16[256,128]{1,0:T(8,128)(2,1)S(1)}, bf16[256,128]{1,0:T(8,128)(2,1)S(1)}, u32[]{:S(2)}, u32[]{:S(2)}) collective-permute-start(bf16[256,128]{1,0:T(8,128)(2,1)S(1)} %shard_map.116), channel_id=1, source_target_pairs={{0,24},{8,0},{16,8},{24,16},{1,25},{9,1},{17,9},{25,17},{2,26},{10... | collective-permute-start | bytes 196616 | tf_op jit(solution)/shard_map/ppermute | solution.py:27
  48.4 5.8 %collective-permute-start.13 = (bf16[256,128]{1,0:T(8,128)(2,1)S(1)}, bf16[256,128]{1,0:T(8,128)(2,1)S(1)}, u32[]{:S(2)}, u32[]{:S(2)}) collective-permute-start(bf16[256,128]{1,0:T(8,128)(2,1)S(1)} %shard_map.116), channel_id=1, source_target_pairs={{0,16},{8,24},{16,0},{24,8},{1,17},{9,25},{17,1},{25,9},{2,18},{10... | collective-permute-start | bytes 196616 | tf_op jit(solution)/shard_map/ppermute | solution.py:27
  49.5 5.5 %collective-permute-start.14 = (bf16[256,128]{1,0:T(8,128)(2,1)S(1)}, bf16[256,128]{1,0:T(8,128)(2,1)S(1)}, u32[]{:S(2)}, u32[]{:S(2)}) collective-permute-start(bf16[256,128]{1,0:T(8,128)(2,1)S(1)} %shard_map.116), channel_id=1, source_target_pairs={{0,8},{8,16},{16,24},{24,0},{1,9},{9,17},{17,25},{25,1},{2,10},{10... | collective-permute-start | bytes 196616 | tf_op jit(solution)/shard_map/ppermute | solution.py:27
  50.1 10.4 %collective-permute-start.10 = (bf16[2,64,1024]{2,1,0:T(8,128)(2,1)S(1)}, bf16[2,64,1024]{2,1,0:T(8,128)(2,1)S(1)}, u32[]{:S(2)}, u32[]{:S(2)}) collective-permute-start(bf16[2,64,1024]{2,1,0:T(8,128)(2,1)S(1)} %collective-permute-done.8.d0), channel_id=1, source_target_pairs={{0,2},{1,3},{2,0},{3,1},{4,6},{5,7},{6,4},{7,5},{8,10},{9,11},{10,... | collective-permute-start | bytes 786440 | tf_op jit(solution)/shard_map/ppermute | solution.py:27
  50.1 12.8 %collective-permute-start.11 = (bf16[2,64,1024]{2,1,0:T(8,128)(2,1)S(1)}, bf16[2,64,1024]{2,1,0:T(8,128)(2,1)S(1)}, u32[]{:S(2)}, u32[]{:S(2)}) collective-permute-start(bf16[2,64,1024]{2,1,0:T(8,128)(2,1)S(1)} %collective-permute-done.8.d0), channel_id=1, source_target_pairs={{0,1},{1,2},{2,3},{3,0},{4,5},{5,6},{6,7},{7,4},{8,9},{9,10},{10,1... | collective-permute-start | bytes 786440 | tf_op jit(solution)/shard_map/ppermute | solution.py:27
  52.3 10.5 %collective-permute-start.9 = (bf16[2,64,1024]{2,1,0:T(8,128)(2,1)S(1)}, bf16[2,64,1024]{2,1,0:T(8,128)(2,1)S(1)}, u32[]{:S(2)}, u32[]{:S(2)}) collective-permute-start(bf16[2,64,1024]{2,1,0:T(8,128)(2,1)S(1)} %collective-permute-done.8.d0), channel_id=1, source_target_pairs={{0,3},{1,0},{2,1},{3,2},{4,7},{5,4},{6,5},{7,6},{8,11},{9,8},{10,9... | collective-permute-start | bytes 786440 | tf_op jit(solution)/shard_map/ppermute | solution.py:27
  55.0 7.8 %collective-permute-start.15 = (bf16[4,256,128]{2,1,0:T(8,128)(2,1)S(1)}, bf16[4,256,128]{2,1,0:T(8,128)(2,1)S(1)}, u32[]{:S(2)}, u32[]{:S(2)}) collective-permute-start(bf16[4,256,128]{2,1,0:T(8,128)(2,1)S(1)} %pad_maximum_fusion.u.u_own), channel_id=1, source_target_pairs={{0,128},{128,0},{1,129},{129,1},{2,130},{130,2},{3,131},{131,3},{4... | collective-permute-start | bytes 786440 | tf_op jit(solution)/shard_map/ppermute | solution.py:27
  64.5 16.4 %all-to-all-start = ((bf16[4,64,128]{2,1,0:T(8,128)(2,1)}), bf16[4,64,128]{2,1,0:T(8,128)(2,1)S(1)}, u32[]{:S(2)}, u32[]{:S(2)}) async-start(bf16[4,64,128]{2,1,0:T(8,128)(2,1)} %shard_map.120), calls=%async_computation | async-start | bytes 131072 | tf_op jit(solution)/shard_map/all_to_all | solution.py:324

commit v8 on v7

--- a/solution.py
+++ b/solution.py
@@ -25,6 +25,10 @@
 def shift(value, axis, by):
     n = SIZES[axis]
     return lax.ppermute(value, axis, [(i, (i + by) % n) for i in range(n)])
+
+
+def exchange(value, axis, bit):
+    return lax.ppermute(value, axis, [(i, i ^ bit) for i in range(SIZES[axis])])
 
 
 def swap_high(value):
@@ -107,6 +111,11 @@
             out[i, r * steps : (r + 1) * steps] = ref[r]
 
 
+def pair_kernel(first, second, out):
+    out[:2] = first[...]
+    out[2:] = second[...]
+
+
 def x_sum_kernel(own, r1, r2, r3, o0, o1, o2, o3):
     for e, out in enumerate((o0, o1, o2, o3)):
         total = own[e] + r1[e].astype(F32) + r2[e].astype(F32) + r3[e].astype(F32)
@@ -182,30 +191,32 @@
         rows[pl.ds(pl.multiple_of(lax.rem(x + d, 4) * 256, 256), 256), :] = updated[d]
 
 
-def tokens_of(place, d):
-    return lax.rem(place[3] + d + 4 - place[1], 4)
-
-
-def project_own_kernel(place, d0, u, out_ref, rows):
+def tokens_of(place, bits):
+    return lax.rem(jnp.bitwise_xor(place[3], bits) + 4 - place[1], 4)
+
+
+def project_own_kernel(place, near, u, out_ref, rows):
     own = jnp.where(place[0] == place[4], 0, 1)
     fill_rows(rows, place[2], u)
-    out_ref[0] = jnp.dot(d0[own], rows[...], preferred_element_type=F32)
-
-
-def project_rest_kernel(place, d0, d1, d2, d3, u_own, u_other, start, out_ref, rows, last):
+    inputs = jnp.concatenate([near[own], near[2 + own]], axis=0)
+    out_ref[...] = jnp.dot(inputs, rows[...], preferred_element_type=F32)
+
+
+def project_rest_kernel(place, near, far, u_own, u_other, start, out_ref, rows, last):
     own = jnp.where(place[0] == place[4], 0, 1)
     fill_rows(last, place[2], u_own)
     fill_rows(rows, place[2], u_other)
-    pieces = (d0, d1, d2, d3)
-    inputs = jnp.concatenate([piece[1 - own] for piece in pieces], axis=0)
-    product = jnp.dot(inputs, rows[...], preferred_element_type=F32)
-    inputs = jnp.concatenate([piece[own] for piece in pieces[1:]], axis=0)
+    inputs = [near[1 - own], near[3 - own], far[1 - own], far[3 - own]]
+    product = jnp.dot(
+        jnp.concatenate(inputs, axis=0), rows[...], preferred_element_type=F32
+    )
+    inputs = jnp.concatenate([far[own], far[2 + own]], axis=0)
     more = jnp.dot(inputs, last[...], preferred_element_type=F32)
-    for d in range(4):
-        rest = start[0] if d == 0 else more[(d - 1) * 64 : d * 64]
-        out_ref[tokens_of(place, d)] = (product[d * 64 : (d + 1) * 64] + rest).astype(
-            out_ref.dtype
-        )
+    size = far.shape[1]
+    for i, bits in enumerate((0, 1, 3, 2)):
+        rest = start[i * size : (i + 1) * size] if i < 2 else more[(i - 2) * size : (i - 1) * size]
+        total = product[i * size : (i + 1) * size] + rest
+        out_ref[tokens_of(place, bits)] = total.astype(out_ref.dtype)
 
 
 def project(kernel, out_shape, scratches, place, *args):
@@ -279,7 +290,7 @@
     )
     along_x = [shift(sent[d - 1], "x", d) for d in (2, 1, 3)]
     (both,) = small_call(
-        join_kernel, [((2, places, D // 8), BF16)], after(decode_inputs, own), second
+        join_kernel, [((2, places, D // 8), BF16)], decode_inputs, second
     )
     both = swap_high(both)
     attended_cache, fresh_weights = attend_cache(
@@ -290,6 +301,9 @@
         cache_values,
     )
 
+    both = after(both, attended_cache)
+    near = exchange(both, "y", 1)
+
     own, *along_x, attended_cache, fresh_weights = lax.optimization_barrier(
         (own, *along_x, attended_cache, fresh_weights)
     )
@@ -298,25 +312,28 @@
         x_sum_kernel, [(rows, F32)] + [(rows, BF16)] * 3, own, *along_x
     )
     along_z = [shift(sent[e - 1], "zh", e) for e in (2, 1, 3)]
-    from_y2, from_y1, from_y3 = (shift(both, "y", -d) for d in (2, 1, 3))
+    own, *along_z, near = lax.optimization_barrier((own, *along_z, near))
     (updated,) = small_call(update_kernel, [(rows, BF16)], value_weight, own, *along_z)
     own = after(own, updated)
     (gradient,) = small_call(gradient_kernel, [(rows, F32)], own, *along_z, keep=False)
 
+    (near,) = small_call(
+        pair_kernel, [((4, places, D // 8), BF16)], after(both, updated), near
+    )
+    far = exchange(near, "y", 3)
     gathered = jnp.stack([updated] + [shift(updated, "x", -d) for d in (1, 2, 3)])
+    gathered, gradient = lax.optimization_barrier((gathered, gradient))
     other = shift(gathered, "c", 1)
     partial = project(
-        project_own_kernel, pltpu.VMEM((1, places, HD), F32), 1, place, both, gathered
+        project_own_kernel, pltpu.VMEM((2 * places, HD), F32), 1, place, near, gathered
     )
     partial = project(
         project_rest_kernel,
-        jax.ShapeDtypeStruct((4, places, HD), BF16),
+        pltpu.VMEM((4, places, HD), BF16),
         2,
         place,
-        both,
-        from_y1,
-        from_y2,
-        from_y3,
+        near,
+        far,
         gathered,
         other,
         partial,

time: 83 us -> 76.8 us (0.925)
  waiting for transfers between devices: 38.4 us -> 12.7 us
  blocking collectives: 0 us -> 12.4 us
  starting transfers between devices: 29.1 us -> 37 us
    ppermute x15 -> x12, waiting for transfers between devices: 30.9 us -> 11.9 us  [shift(): return lax.ppermute(value, axis, [(i, (i + by) % n) for i in range(n)])]
    ppermute x0 -> x2, starting transfers between devices: none -> 13.9 us  [exchange(): return lax.ppermute(value, axis, [(i, i ^ bit) for i in range(SIZES[axis])])]
    all_to_all x0 -> x1, blocking collectives: none -> 12.4 us  [shards(): exchanged = lax.all_to_all(partial, 'zh', 0, 0, tiled=True)]
    all_to_all x1 -> x0, starting transfers between devices: 8.17 us -> none  [shards(): exchanged = lax.all_to_all(partial, 'zh', 0, 0, tiled=True)]
    all_to_all x1 -> x0, waiting for transfers between devices: 7.52 us -> none  [shards(): exchanged = lax.all_to_all(partial, 'zh', 0, 0, tiled=True)]
    ppermute x15 -> x12, starting transfers between devices: 20.2 us -> 22.5 us  [shift(): return lax.ppermute(value, axis, [(i, (i + by) % n) for i in range(n)])]
    ppermute x0 -> x2, waiting for transfers between devices: none -> 0.87 us  [exchange(): return lax.ppermute(value, axis, [(i, i ^ bit) for i in range(SIZES[axis])])]
    pallas_call x5 -> x6, Pallas kernels: 1.97 us -> 1.95 us  [small_call(): pl.pallas_call(kernel, in_specs=[VMEM] * len(args), out_specs=[VMEM] * le...]
  transfers between devices with their start and end apart: 17 -> 15, of which waited for: 10 -> 7; matrix products, arithmetic and copies ran while one was open for 0% -> 0% of each run, Pallas kernels for 12% -> 14%
where the time goes in v8:
time: 76.8 us; the launch traced here: 75.7 us
  starting transfers between devices  37 us (48%)
  waiting for transfers between devices  12.7 us (17%)
  Pallas kernels  12.6 us (16%)
  blocking collectives  12.4 us (16%)
  between operations  0.85 us (1%)
    ppermute x12, starting transfers between devices, shift(): return lax.ppermute(value, axis, [(i, (i + by) % n) for i in range(n)])  22.5 us
    ppermute x2, starting transfers between devices, exchange(): return lax.ppermute(value, axis, [(i, i ^ bit) for i in range(SIZES[axis])])  13.9 us
    all_to_all x1, blocking collectives, shards(): exchanged = lax.all_to_all(partial, 'zh', 0, 0, tiled=True)  12.4 us
    ppermute x12, waiting for transfers between devices, shift(): return lax.ppermute(value, axis, [(i, (i + by) % n) for i in range(n)])  11.9 us
    pallas_call x1, Pallas kernels, partial_gradient(): pl.pallas_call(partial_kernel, in_specs=[SMEM, HBM, HBM], out_specs=[VMEM...  5.96 us
    pallas_call x1, Pallas kernels, attend_cache(): pl.pallas_call(attend_kernel, in_specs=[SMEM] + [VMEM] * 4, out_specs=[VM...  2.13 us
    pallas_call x6, Pallas kernels, small_call(): pl.pallas_call(kernel, in_specs=[VMEM] * len(args), out_specs=[VMEM] * le...  1.95 us
    pallas_call x2, Pallas kernels, project(): pl.pallas_call(kernel, in_specs=[SMEM] + [VMEM] * len(args), out_specs=VM...  1.72 us
  transfers between devices with their start and end apart: 15, of which 7 were waited for; matrix products, arithmetic and copies ran while one was open for 0% of the time, Pallas kernels for 14%

profile of v8, /device:TPU:32, one launch (start us, length us, event | category | flops | bytes accessed | tf_op | source)
XLA Modules:
  0.0 75.7 jit_solution(10223067139642786226)
XLA Ops:
  0.7 1.9 %collective-permute-start = (bf16[16,4,1024]{2,1,0:T(4,128)(2,1)}, bf16[16,4,1024]{2,1,0:T(4,128)(2,1)S(1)}, u32[]{:S(2)}, u32[]{:S(2)}) collective-permute-start(bf16[16,4,1024]{2,1,0:T(4,128)(2,1)} %first.1), channel_id=1, source_target_pairs={{0,4},{4,0},{1,5},{5,1},{2,6},{6,2},{3,7},{7,3},{8,12},{12,8},{9,1... | collective-permute-start | bytes 393224 | tf_op jit(solution)/shard_map/ppermute | solution.py:27
  2.7 6.0 %shard_map.112 = (bf16[4,4,256,128]{3,2,1,0:T(8,128)(2,1)S(1)}, bf16[4,4,256,128]{3,2,1,0:T(8,128)(2,1)S(1)}) custom-call(s32[5]{0:T(128)S(1)} %stack.38.place, bf16[768,8192]{1,0:T(8,128)(2,1)} %x_hbm.1, bf16[768,128]{1,0:T(8,128)(2,1)} %v_hbm.1), custom_call_target="tpu_custom_call" | custom-call | flops 1610612736 | bytes 12582912 | tf_op jit(solution)/shard_map/pallas_call | solution.py:71
  9.6 1.9 %collective-permute-done.1.received = bf16[4,4,256,128]{3,2,1,0:T(8,128)(2,1)S(1)} collective-permute-done((bf16[4,4,256,128]{3,2,1,0:T(8,128)(2,1)S(1)}, bf16[4,4,256,128]{3,2,1,0:T(8,128)(2,1)S(1)}, u32[]{:S(2)}, u32[]{:S(2)}) %collective-permute-start.1) | collective-permute-done | bytes 1048608 | tf_op jit(solution)/shard_map/ppermute | solution.py:27
  11.4 1.0 %shard_map.113 = (f32[4,256,128]{2,1,0:T(8,128)S(1)}, bf16[4,256,128]{2,1,0:T(8,128)(2,1)}, bf16[4,256,128]{2,1,0:T(8,128)(2,1)}, bf16[4,256,128]{2,1,0:T(8,128)(2,1)S(1)}) custom-call(bf16[4,4,256,128]{3,2,1,0:T(8,128)(2,1)S(1)} %get-tuple-element.39.mine, bf16[4,4,256,128]{3,2,1,0:T(8,128)(2,1)S(1)} %collective-permute-done.1.received), custom_call_target="tpu_custom_call" | custom-call | flops 1048576 | bytes 2097152 | tf_op jit(solution)/shard_map/pallas_call | solution.py:89
  12.4 1.3 %collective-permute-start.2 = (bf16[4,256,128]{2,1,0:T(8,128)(2,1)}, bf16[4,256,128]{2,1,0:T(8,128)(2,1)S(1)}, u32[]{:S(2)}, u32[]{:S(2)}) collective-permute-start(bf16[4,256,128]{2,1,0:T(8,128)(2,1)} %get-tuple-element.42), channel_id=1, source_target_pairs={{0,16},{8,24},{16,0},{24,8},{1,17},{9,25},{17,1},{25,9},{2,18},{10... | collective-permute-start | bytes 786440 | tf_op jit(solution)/shard_map/ppermute | solution.py:27
  14.3 2.6 %collective-permute-start.4 = (bf16[4,256,128]{2,1,0:T(8,128)(2,1)S(1)}, bf16[4,256,128]{2,1,0:T(8,128)(2,1)S(1)}, u32[]{:S(2)}, u32[]{:S(2)}) collective-permute-start(bf16[4,256,128]{2,1,0:T(8,128)(2,1)S(1)} %get-tuple-element.44), channel_id=1, source_target_pairs={{0,24},{8,0},{16,8},{24,16},{1,25},{9,1},{17,9},{25,17},{2,26},{10... | collective-permute-start | bytes 786440 | tf_op jit(solution)/shard_map/ppermute | solution.py:27
  17.0 2.1 %shard_map.114 = (f32[512,128]{1,0:T(8,128)S(1)}, bf16[512,64]{1,0:T(8,128)(2,1)S(1)}) custom-call(s32[16]{0:T(128)S(1)} %copy-done.5, bf16[64,1024]{1,0:T(8,128)(2,1)S(1)} %reshape.12.queries, bf16[64,128]{1,0:T(8,128)(2,1)S(1)} %bitcast.11, bf16[16,128,128]{2,1,0:T(8,128)(2,1)S(1)} %copy-done, bf16[16,128,128]{2,1,0:T(8,128)(2,1)S(1)} %copy-done.1), custom_call_target="tpu_custom_call" | custom-call | flops 1048576 | bytes 262144 | tf_op jit(solution)/shard_map/pallas_call | solution.py:174
  19.2 12.1 %collective-permute-start.9 = (bf16[2,64,1024]{2,1,0:T(8,128)(2,1)S(1)}, bf16[2,64,1024]{2,1,0:T(8,128)(2,1)S(1)}, u32[]{:S(2)}, u32[]{:S(2)}) collective-permute-start(bf16[2,64,1024]{2,1,0:T(8,128)(2,1)S(1)} %collective-permute-done.8.first), channel_id=1, source_target_pairs={{0,1},{1,0},{2,3},{3,2},{4,5},{5,4},{6,7},{7,6},{8,9},{9,8},{10,11... | collective-permute-start | bytes 786440 | tf_op jit(solution)/shard_map/ppermute | solution.py:31
  31.5 3.3 %collective-permute-start.5 = (bf16[256,128]{1,0:T(8,128)(2,1)S(1)}, bf16[256,128]{1,0:T(8,128)(2,1)S(1)}, u32[]{:S(2)}, u32[]{:S(2)}) collective-permute-start(bf16[256,128]{1,0:T(8,128)(2,1)S(1)} %get-tuple-element.53), channel_id=1, source_target_pairs={{0,64},{32,96},{64,0},{96,32},{1,65},{33,97},{65,1},{97,33},{2,66}... | collective-permute-start | bytes 196616 | tf_op jit(solution)/shard_map/ppermute | solution.py:27
  34.7 8.1 %collective-permute-start.6 = (bf16[256,128]{1,0:T(8,128)(2,1)S(1)}, bf16[256,128]{1,0:T(8,128)(2,1)S(1)}, u32[]{:S(2)}, u32[]{:S(2)}) collective-permute-start(bf16[256,128]{1,0:T(8,128)(2,1)S(1)} %get-tuple-element.54), channel_id=1, source_target_pairs={{0,32},{32,64},{64,96},{96,0},{1,33},{33,65},{65,97},{97,1},{2,34}... | collective-permute-start | bytes 196616 | tf_op jit(solution)/shard_map/ppermute | solution.py:27
  42.8 2.5 %collective-permute-done.6.r2 = bf16[256,128]{1,0:T(8,128)(2,1)S(1)} collective-permute-done((bf16[256,128]{1,0:T(8,128)(2,1)S(1)}, bf16[256,128]{1,0:T(8,128)(2,1)S(1)}, u32[]{:S(2)}, u32[]{:S(2)}) %collective-permute-start.6) | collective-permute-done | bytes 65568 | tf_op jit(solution)/shard_map/ppermute | solution.py:27
  45.3 2.7 %collective-permute-done.7.r3 = bf16[256,128]{1,0:T(8,128)(2,1)S(1)} collective-permute-done((bf16[256,128]{1,0:T(8,128)(2,1)S(1)}, bf16[256,128]{1,0:T(8,128)(2,1)S(1)}, u32[]{:S(2)}, u32[]{:S(2)}) %collective-permute-start.7) | collective-permute-done | bytes 65568 | tf_op jit(solution)/shard_map/ppermute | solution.py:27
  48.1 1.7 %collective-permute-start.13 = (bf16[4,64,1024]{2,1,0:T(8,128)(2,1)S(1)}, bf16[4,64,1024]{2,1,0:T(8,128)(2,1)S(1)}, u32[]{:S(2)}, u32[]{:S(2)}) collective-permute-start(bf16[4,64,1024]{2,1,0:T(8,128)(2,1)S(1)} %shard_map.119.near), channel_id=1, source_target_pairs={{0,3},{1,2},{2,1},{3,0},{4,7},{5,6},{6,5},{7,4},{8,11},{9,10},{10,... | collective-permute-start | bytes 1572872 | tf_op jit(solution)/shard_map/ppermute | solution.py:31
  49.8 2.8 %collective-permute-start.10 = (bf16[256,128]{1,0:T(8,128)(2,1)S(1)}, bf16[256,128]{1,0:T(8,128)(2,1)S(1)}, u32[]{:S(2)}, u32[]{:S(2)}) collective-permute-start(bf16[256,128]{1,0:T(8,128)(2,1)S(1)} %shard_map.117), channel_id=1, source_target_pairs={{0,24},{8,0},{16,8},{24,16},{1,25},{9,1},{17,9},{25,17},{2,26},{10... | collective-permute-start | bytes 196616 | tf_op jit(solution)/shard_map/ppermute | solution.py:27
  52.6 0.8 %collective-permute-start.11 = (bf16[256,128]{1,0:T(8,128)(2,1)S(1)}, bf16[256,128]{1,0:T(8,128)(2,1)S(1)}, u32[]{:S(2)}, u32[]{:S(2)}) collective-permute-start(bf16[256,128]{1,0:T(8,128)(2,1)S(1)} %shard_map.117), channel_id=1, source_target_pairs={{0,16},{8,24},{16,0},{24,8},{1,17},{9,25},{17,1},{25,9},{2,18},{10... | collective-permute-start | bytes 196616 | tf_op jit(solution)/shard_map/ppermute | solution.py:27
  53.4 0.9 %collective-permute-start.12 = (bf16[256,128]{1,0:T(8,128)(2,1)S(1)}, bf16[256,128]{1,0:T(8,128)(2,1)S(1)}, u32[]{:S(2)}, u32[]{:S(2)}) collective-permute-start(bf16[256,128]{1,0:T(8,128)(2,1)S(1)} %shard_map.117), channel_id=1, source_target_pairs={{0,8},{8,16},{16,24},{24,0},{1,9},{9,17},{17,25},{25,1},{2,10},{10... | collective-permute-start | bytes 196616 | tf_op jit(solution)/shard_map/ppermute | solution.py:27
  54.9 3.4 %collective-permute-done.11 = bf16[256,128]{1,0:T(8,128)(2,1)S(1)} collective-permute-done((bf16[256,128]{1,0:T(8,128)(2,1)S(1)}, bf16[256,128]{1,0:T(8,128)(2,1)S(1)}, u32[]{:S(2)}, u32[]{:S(2)}) %collective-permute-start.11) | collective-permute-done | bytes 65568 | tf_op jit(solution)/shard_map/ppermute | solution.py:27
  58.3 0.7 collective-permute-done.12
  59.2 0.8 %shard_map.120.start = f32[128,128]{1,0:T(8,128)S(1)} custom-call(s32[5]{0:T(128)S(1)} %stack.38.place, bf16[4,64,1024]{2,1,0:T(8,128)(2,1)S(1)} %shard_map.119.near, bf16[4,256,128]{2,1,0:T(8,128)(2,1)S(1)} %pad_maximum_fusion.u.u_own), custom_call_target="tpu_custom_call" | custom-call | flops 67108864 | bytes 786432 | tf_op jit(solution)/shard_map/pallas_call | solution.py:223
  60.0 0.7 collective-permute-done.14.u_other
  60.7 0.9 %collective-permute-done.13.far = bf16[4,64,1024]{2,1,0:T(8,128)(2,1)S(1)} collective-permute-done((bf16[4,64,1024]{2,1,0:T(8,128)(2,1)S(1)}, bf16[4,64,1024]{2,1,0:T(8,128)(2,1)S(1)}, u32[]{:S(2)}, u32[]{:S(2)}) %collective-permute-start.13) | collective-permute-done | bytes 524320 | tf_op jit(solution)/shard_map/ppermute | solution.py:31
  61.6 0.9 %shard_map.121 = bf16[4,64,128]{2,1,0:T(8,128)(2,1)S(1)} custom-call(s32[5]{0:T(128)S(1)} %stack.38.place, bf16[4,64,1024]{2,1,0:T(8,128)(2,1)S(1)} %shard_map.119.near, bf16[4,64,1024]{2,1,0:T(8,128)(2,1)S(1)} %collective-permute-done.13.far, bf16[4,256,128]{2,1,0:T(8,128)(2,1)S(1)} %pad_maximum_fusion.u.u_own, ...), custom_call_target="tpu_custom_call" | custom-call | flops 67108864 | bytes 786432 | tf_op jit(solution)/shard_map/pallas_call | solution.py:223
  62.5 12.4 %all_to_all.5.parts = bf16[4,64,128]{2,1,0:T(8,128)(2,1)S(1)} all-to-all(bf16[4,64,128]{2,1,0:T(8,128)(2,1)S(1)} %shard_map.121), channel_id=1, replica_groups=mesh['c'=2,'zh'=4,'x'=4,'zl'=2,'y'=4] {'zh'}, dimensions={0} | all-to-all | bytes 131072 | tf_op jit(solution)/shard_map/all_to_all | solution.py:341
  74.9 0.8 %shard_map.122 = (bf16[16,4,128]{2,1,0:T(4,128)(2,1)}, bf16[16,4,1024]{2,1,0:T(4,128)(2,1)}) custom-call(bf16[4,64,128]{2,1,0:T(8,128)(2,1)S(1)} %all_to_all.5.parts, f32[512,128]{1,0:T(8,128)S(1)} %get-tuple-element.67.mixed, bf16[512,64]{1,0:T(8,128)(2,1)S(1)} %get-tuple-element.68.weights), custom_call_target="tpu_custom_call" | custom-call | tf_op jit(solution)/shard_map/pallas_call | solution.py:254
  (35 shorter events, 2.6 us)
Async XLA Ops:
  0.6 8.2 %copy-start.2 = (bf16[16,4,1024]{2,1,0:T(4,128)(2,1)S(1)}, bf16[16,4,1024]{2,1,0:T(4,128)(2,1)}, u32[]{:S(2)}) copy-start(bf16[16,4,1024]{2,1,0:T(4,128)(2,1)} %first.1) | copy-start | bytes 393220
  0.6 16.3 %copy-start.6 = (bf16[16,4,1024]{2,1,0:T(4,128)(2,1)S(1)}, bf16[16,4,1024]{2,1,0:T(4,128)(2,1)}, u32[]{:S(2)}) copy-start(bf16[16,4,1024]{2,1,0:T(4,128)(2,1)} %param.13) | copy-start | bytes 393220
  0.7 16.4 %copy-start.4 = (bf16[16,4,128]{2,1,0:T(4,128)(2,1)S(1)}, bf16[16,4,128]{2,1,0:T(4,128)(2,1)}, u32[]{:S(2)}) copy-start(bf16[16,4,128]{2,1,0:T(4,128)(2,1)} %param.14) | copy-start | bytes 49156
  0.7 16.4 %copy-start = (bf16[16,128,128]{2,1,0:T(8,128)(2,1)S(1)}, bf16[16,128,128]{2,1,0:T(8,128)(2,1)}, u32[]{:S(2)}) copy-start(bf16[16,128,128]{2,1,0:T(8,128)(2,1)} %cache_keys.1) | copy-start | bytes 1572868
  0.7 16.4 %copy-start.1 = (bf16[16,128,128]{2,1,0:T(8,128)(2,1)S(1)}, bf16[16,128,128]{2,1,0:T(8,128)(2,1)}, u32[]{:S(2)}) copy-start(bf16[16,128,128]{2,1,0:T(8,128)(2,1)} %cache_values.1) | copy-start | bytes 1572868
  0.7 16.4 %copy-start.5 = (s32[16]{0:T(128)S(1)}, s32[16]{0:T(128)}, u32[]{:S(2)}) copy-start(s32[16]{0:T(128)} %lengths.1) | copy-start | bytes 196
  0.7 47.3 %copy-start.3 = (bf16[256,128]{1,0:T(8,128)(2,1)S(1)}, bf16[256,128]{1,0:T(8,128)(2,1)}, u32[]{:S(2)}) copy-start(bf16[256,128]{1,0:T(8,128)(2,1)} %weight.1) | copy-start | bytes 196612
  0.7 8.0 %collective-permute-start = (bf16[16,4,1024]{2,1,0:T(4,128)(2,1)}, bf16[16,4,1024]{2,1,0:T(4,128)(2,1)S(1)}, u32[]{:S(2)}, u32[]{:S(2)}) collective-permute-start(bf16[16,4,1024]{2,1,0:T(4,128)(2,1)} %first.1), channel_id=1, source_target_pairs={{0,4},{4,0},{1,5},{5,1},{2,6},{6,2},{3,7},{7,3},{8,12},{12,8},{9,1... | collective-permute-start | bytes 393224 | tf_op jit(solution)/shard_map/ppermute | solution.py:27
  8.7 2.7 %collective-permute-start.1 = (bf16[4,4,256,128]{3,2,1,0:T(8,128)(2,1)S(1)}, bf16[4,4,256,128]{3,2,1,0:T(8,128)(2,1)S(1)}, u32[]{:S(2)}, u32[]{:S(2)}) collective-permute-start(bf16[4,4,256,128]{3,2,1,0:T(8,128)(2,1)S(1)} %get-tuple-element.40), channel_id=1, source_target_pairs={{0,128},{128,0},{1,129},{129,1},{2,130},{130,2},{3,131},{131,3},{4... | collective-permute-start | bytes 3145736 | tf_op jit(solution)/shard_map/ppermute | solution.py:27
  8.9 10.3 %collective-permute-start.8 = (bf16[2,64,1024]{2,1,0:T(8,128)(2,1)S(1)}, bf16[2,64,1024]{2,1,0:T(8,128)(2,1)S(1)}, u32[]{:S(2)}, u32[]{:S(2)}) collective-permute-start(bf16[2,64,1024]{2,1,0:T(8,128)(2,1)S(1)} %shard_map.116), channel_id=1, source_target_pairs={{0,0},{1,33},{2,66},{3,99},{32,1},{33,34},{34,67},{35,96},{64,2},{... | collective-permute-start | bytes 786440 | tf_op jit(solution)/shard_map/ppermute | solution.py:36
  12.4 18.9 %collective-permute-start.2 = (bf16[4,256,128]{2,1,0:T(8,128)(2,1)}, bf16[4,256,128]{2,1,0:T(8,128)(2,1)S(1)}, u32[]{:S(2)}, u32[]{:S(2)}) collective-permute-start(bf16[4,256,128]{2,1,0:T(8,128)(2,1)} %get-tuple-element.42), channel_id=1, source_target_pairs={{0,16},{8,24},{16,0},{24,8},{1,17},{9,25},{17,1},{25,9},{2,18},{10... | collective-permute-start | bytes 786440 | tf_op jit(solution)/shard_map/ppermute | solution.py:27
  13.7 17.6 %collective-permute-start.3 = (bf16[4,256,128]{2,1,0:T(8,128)(2,1)}, bf16[4,256,128]{2,1,0:T(8,128)(2,1)S(1)}, u32[]{:S(2)}, u32[]{:S(2)}) collective-permute-start(bf16[4,256,128]{2,1,0:T(8,128)(2,1)} %get-tuple-element.43), channel_id=1, source_target_pairs={{0,8},{8,16},{16,24},{24,0},{1,9},{9,17},{17,25},{25,1},{2,10},{10... | collective-permute-start | bytes 786440 | tf_op jit(solution)/shard_map/ppermute | solution.py:27
  14.3 17.0 %collective-permute-start.4 = (bf16[4,256,128]{2,1,0:T(8,128)(2,1)S(1)}, bf16[4,256,128]{2,1,0:T(8,128)(2,1)S(1)}, u32[]{:S(2)}, u32[]{:S(2)}) collective-permute-start(bf16[4,256,128]{2,1,0:T(8,128)(2,1)S(1)} %get-tuple-element.44), channel_id=1, source_target_pairs={{0,24},{8,0},{16,8},{24,16},{1,25},{9,1},{17,9},{25,17},{2,26},{10... | collective-permute-start | bytes 786440 | tf_op jit(solution)/shard_map/ppermute | solution.py:27
  19.2 23.7 %collective-permute-start.9 = (bf16[2,64,1024]{2,1,0:T(8,128)(2,1)S(1)}, bf16[2,64,1024]{2,1,0:T(8,128)(2,1)S(1)}, u32[]{:S(2)}, u32[]{:S(2)}) collective-permute-start(bf16[2,64,1024]{2,1,0:T(8,128)(2,1)S(1)} %collective-permute-done.8.first), channel_id=1, source_target_pairs={{0,1},{1,0},{2,3},{3,2},{4,5},{5,4},{6,7},{7,6},{8,9},{9,8},{10,11... | collective-permute-start | bytes 786440 | tf_op jit(solution)/shard_map/ppermute | solution.py:31
  31.5 11.4 %collective-permute-start.5 = (bf16[256,128]{1,0:T(8,128)(2,1)S(1)}, bf16[256,128]{1,0:T(8,128)(2,1)S(1)}, u32[]{:S(2)}, u32[]{:S(2)}) collective-permute-start(bf16[256,128]{1,0:T(8,128)(2,1)S(1)} %get-tuple-element.53), channel_id=1, source_target_pairs={{0,64},{32,96},{64,0},{96,32},{1,65},{33,97},{65,1},{97,33},{2,66}... | collective-permute-start | bytes 196616 | tf_op jit(solution)/shard_map/ppermute | solution.py:27
  34.7 10.6 %collective-permute-start.6 = (bf16[256,128]{1,0:T(8,128)(2,1)S(1)}, bf16[256,128]{1,0:T(8,128)(2,1)S(1)}, u32[]{:S(2)}, u32[]{:S(2)}) collective-permute-start(bf16[256,128]{1,0:T(8,128)(2,1)S(1)} %get-tuple-element.54), channel_id=1, source_target_pairs={{0,32},{32,64},{64,96},{96,0},{1,33},{33,65},{65,97},{97,1},{2,34}... | collective-permute-start | bytes 196616 | tf_op jit(solution)/shard_map/ppermute | solution.py:27
  42.8 5.2 %collective-permute-start.7 = (bf16[256,128]{1,0:T(8,128)(2,1)S(1)}, bf16[256,128]{1,0:T(8,128)(2,1)S(1)}, u32[]{:S(2)}, u32[]{:S(2)}) collective-permute-start(bf16[256,128]{1,0:T(8,128)(2,1)S(1)} %get-tuple-element.55), channel_id=1, source_target_pairs={{0,96},{32,0},{64,32},{96,64},{1,97},{33,1},{65,33},{97,65},{2,98}... | collective-permute-start | bytes 196616 | tf_op jit(solution)/shard_map/ppermute | solution.py:27
  48.1 13.5 %collective-permute-start.13 = (bf16[4,64,1024]{2,1,0:T(8,128)(2,1)S(1)}, bf16[4,64,1024]{2,1,0:T(8,128)(2,1)S(1)}, u32[]{:S(2)}, u32[]{:S(2)}) collective-permute-start(bf16[4,64,1024]{2,1,0:T(8,128)(2,1)S(1)} %shard_map.119.near), channel_id=1, source_target_pairs={{0,3},{1,2},{2,1},{3,0},{4,7},{5,6},{6,5},{7,4},{8,11},{9,10},{10,... | collective-permute-start | bytes 1572872 | tf_op jit(solution)/shard_map/ppermute | solution.py:31
  49.8 5.1 %collective-permute-start.10 = (bf16[256,128]{1,0:T(8,128)(2,1)S(1)}, bf16[256,128]{1,0:T(8,128)(2,1)S(1)}, u32[]{:S(2)}, u32[]{:S(2)}) collective-permute-start(bf16[256,128]{1,0:T(8,128)(2,1)S(1)} %shard_map.117), channel_id=1, source_target_pairs={{0,24},{8,0},{16,8},{24,16},{1,25},{9,1},{17,9},{25,17},{2,26},{10... | collective-permute-start | bytes 196616 | tf_op jit(solution)/shard_map/ppermute | solution.py:27
  52.6 5.8 %collective-permute-start.11 = (bf16[256,128]{1,0:T(8,128)(2,1)S(1)}, bf16[256,128]{1,0:T(8,128)(2,1)S(1)}, u32[]{:S(2)}, u32[]{:S(2)}) collective-permute-start(bf16[256,128]{1,0:T(8,128)(2,1)S(1)} %shard_map.117), channel_id=1, source_target_pairs={{0,16},{8,24},{16,0},{24,8},{1,17},{9,25},{17,1},{25,9},{2,18},{10... | collective-permute-start | bytes 196616 | tf_op jit(solution)/shard_map/ppermute | solution.py:27
  53.4 5.7 %collective-permute-start.12 = (bf16[256,128]{1,0:T(8,128)(2,1)S(1)}, bf16[256,128]{1,0:T(8,128)(2,1)S(1)}, u32[]{:S(2)}, u32[]{:S(2)}) collective-permute-start(bf16[256,128]{1,0:T(8,128)(2,1)S(1)} %shard_map.117), channel_id=1, source_target_pairs={{0,8},{8,16},{16,24},{24,0},{1,9},{9,17},{17,25},{25,1},{2,10},{10... | collective-permute-start | bytes 196616 | tf_op jit(solution)/shard_map/ppermute | solution.py:27
  59.1 1.6 %collective-permute-start.14 = (bf16[4,256,128]{2,1,0:T(8,128)(2,1)S(1)}, bf16[4,256,128]{2,1,0:T(8,128)(2,1)S(1)}, u32[]{:S(2)}, u32[]{:S(2)}) collective-permute-start(bf16[4,256,128]{2,1,0:T(8,128)(2,1)S(1)} %pad_maximum_fusion.u.u_own), channel_id=1, source_target_pairs={{0,128},{128,0},{1,129},{129,1},{2,130},{130,2},{3,131},{131,3},{4... | collective-permute-start | bytes 786440 | tf_op jit(solution)/shard_map/ppermute | solution.py:27

commit v9 on v8

--- a/solution.py
+++ b/solution.py
@@ -279,20 +279,17 @@
     places = row_count * step_count
     place = jnp.stack([core, high, x, y, low])
 
-    second = shift(decode_inputs, "zl", 1)
+    swapped = swap_high(decode_inputs)
     theirs, mine = partial_gradient(place, normed_inputs, value_cotangent)
-    theirs, mine, second = lax.optimization_barrier((theirs, mine, second))
+    theirs, mine, swapped = lax.optimization_barrier((theirs, mine, swapped))
     received = shift(theirs, "c", 1)
+    second = shift(swapped, "zl", 1)
 
     rows = (4, 256, HD)
     own, *sent = small_call(
         core_sum_kernel, [(rows, F32)] + [(rows, BF16)] * 3, mine, received
     )
     along_x = [shift(sent[d - 1], "x", d) for d in (2, 1, 3)]
-    (both,) = small_call(
-        join_kernel, [((2, places, D // 8), BF16)], decode_inputs, second
-    )
-    both = swap_high(both)
     attended_cache, fresh_weights = attend_cache(
         lengths,
         after(queries.reshape(places, -1), own),
@@ -300,8 +297,9 @@
         cache_keys,
         cache_values,
     )
-
-    both = after(both, attended_cache)
+    (both,) = small_call(
+        join_kernel, [((2, places, D // 8), BF16)], after(swapped, own), second
+    )
     near = exchange(both, "y", 1)
 
     own, *along_x, attended_cache, fresh_weights = lax.optimization_barrier(
@@ -311,18 +309,15 @@
     own, *sent = small_call(
         x_sum_kernel, [(rows, F32)] + [(rows, BF16)] * 3, own, *along_x
     )
+    (near,) = small_call(pair_kernel, [((4, places, D // 8), BF16)], after(both, own), near)
+    far = exchange(near, "y", 3)
     along_z = [shift(sent[e - 1], "zh", e) for e in (2, 1, 3)]
-    own, *along_z, near = lax.optimization_barrier((own, *along_z, near))
     (updated,) = small_call(update_kernel, [(rows, BF16)], value_weight, own, *along_z)
     own = after(own, updated)
     (gradient,) = small_call(gradient_kernel, [(rows, F32)], own, *along_z, keep=False)
 
-    (near,) = small_call(
-        pair_kernel, [((4, places, D // 8), BF16)], after(both, updated), near
-    )
-    far = exchange(near, "y", 3)
     gathered = jnp.stack([updated] + [shift(updated, "x", -d) for d in (1, 2, 3)])
-    gathered, gradient = lax.optimization_barrier((gathered, gradient))
+    gathered, gradient, far = lax.optimization_barrier((gathered, gradient, far))
     other = shift(gathered, "c", 1)
     partial = project(
         project_own_kernel, pltpu.VMEM((2 * places, HD), F32), 1, place, near, gathered

time: 76.8 us -> 78.7 us (1.025); the launches traced: 75.7 us -> 78.6 us
  starting transfers between devices: 37 us -> 39.8 us
    ppermute x2, waiting for transfers between devices: 0.87 us -> 3.41 us  [exchange(): return lax.ppermute(value, axis, [(i, i ^ bit) for i in range(SIZES[axis])])]
    ppermute x2, starting transfers between devices: 13.9 us -> 16 us  [exchange(): return lax.ppermute(value, axis, [(i, i ^ bit) for i in range(SIZES[axis])])]
    ppermute x12, waiting for transfers between devices: 11.9 us -> 9.94 us  [shift(): return lax.ppermute(value, axis, [(i, (i + by) % n) for i in range(n)])]
    ppermute x1, starting transfers between devices: 0.68 us -> 1.69 us  [swap_high(): return lax.ppermute(value, ('zh', 'y'), pairs)]
where the time goes in v9:
time: 78.7 us; the launch traced here: 78.6 us
  starting transfers between devices  39.8 us (51%)
  waiting for transfers between devices  13.3 us (17%)
  Pallas kernels  12.6 us (16%)
  blocking collectives  11.9 us (15%)
  between operations  0.84 us (1%)
    ppermute x12, starting transfers between devices, shift(): return lax.ppermute(value, axis, [(i, (i + by) % n) for i in range(n)])  22.1 us
    ppermute x2, starting transfers between devices, exchange(): return lax.ppermute(value, axis, [(i, i ^ bit) for i in range(SIZES[axis])])  16 us
    all_to_all x1, blocking collectives, shards(): exchanged = lax.all_to_all(partial, 'zh', 0, 0, tiled=True)  11.9 us
    ppermute x12, waiting for transfers between devices, shift(): return lax.ppermute(value, axis, [(i, (i + by) % n) for i in range(n)])  9.94 us
    pallas_call x1, Pallas kernels, partial_gradient(): pl.pallas_call(partial_kernel, in_specs=[SMEM, HBM, HBM], out_specs=[VMEM...  5.95 us
    ppermute x2, waiting for transfers between devices, exchange(): return lax.ppermute(value, axis, [(i, i ^ bit) for i in range(SIZES[axis])])  3.41 us
    pallas_call x1, Pallas kernels, attend_cache(): pl.pallas_call(attend_kernel, in_specs=[SMEM] + [VMEM] * 4, out_specs=[VM...  2.12 us
    pallas_call x6, Pallas kernels, small_call(): pl.pallas_call(kernel, in_specs=[VMEM] * len(args), out_specs=[VMEM] * le...  1.95 us
  transfers between devices with their start and end apart: 15, of which 7 were waited for; matrix products, arithmetic and copies ran while one was open for 0% of the time, Pallas kernels for 14%

profile of v9, /device:TPU:32, one launch (start us, length us, event | category | flops | bytes accessed | tf_op | source)
XLA Modules:
  0.0 78.6 jit_solution(15726455715046711059)
XLA Ops:
  0.7 1.7 %collective-permute-start = (bf16[16,4,1024]{2,1,0:T(4,128)(2,1)}, bf16[16,4,1024]{2,1,0:T(4,128)(2,1)S(1)}, u32[]{:S(2)}, u32[]{:S(2)}) collective-permute-start(bf16[16,4,1024]{2,1,0:T(4,128)(2,1)} %param.12), channel_id=1, source_target_pairs={{0,0},{1,33},{2,66},{3,99},{32,1},{33,34},{34,67},{35,96},{64,2},{... | collective-permute-start | bytes 393224 | tf_op jit(solution)/shard_map/ppermute | solution.py:36
  2.5 6.0 %shard_map.112 = (bf16[4,4,256,128]{3,2,1,0:T(8,128)(2,1)S(1)}, bf16[4,4,256,128]{3,2,1,0:T(8,128)(2,1)S(1)}) custom-call(s32[5]{0:T(128)S(1)} %stack.38.place, bf16[768,8192]{1,0:T(8,128)(2,1)} %x_hbm.1, bf16[768,128]{1,0:T(8,128)(2,1)} %v_hbm.1), custom_call_target="tpu_custom_call" | custom-call | flops 1610612736 | bytes 12582912 | tf_op jit(solution)/shard_map/pallas_call | solution.py:71
  8.5 1.9 %collective-permute-start.11 = (bf16[16,4,1024]{2,1,0:T(4,128)(2,1)S(1)}, bf16[16,4,1024]{2,1,0:T(4,128)(2,1)S(1)}, u32[]{:S(2)}, u32[]{:S(2)}) collective-permute-start(bf16[16,4,1024]{2,1,0:T(4,128)(2,1)S(1)} %collective-permute-done.first), channel_id=1, source_target_pairs={{0,4},{4,0},{1,5},{5,1},{2,6},{6,2},{3,7},{7,3},{8,12},{12,8},{9,1... | collective-permute-start | bytes 393224 | tf_op jit(solution)/shard_map/ppermute | solution.py:27
  10.5 0.7 collective-permute-done.1.received
  11.2 1.0 %shard_map.113 = (f32[4,256,128]{2,1,0:T(8,128)S(1)}, bf16[4,256,128]{2,1,0:T(8,128)(2,1)}, bf16[4,256,128]{2,1,0:T(8,128)(2,1)}, bf16[4,256,128]{2,1,0:T(8,128)(2,1)S(1)}) custom-call(bf16[4,4,256,128]{3,2,1,0:T(8,128)(2,1)S(1)} %get-tuple-element.35.mine, bf16[4,4,256,128]{3,2,1,0:T(8,128)(2,1)S(1)} %collective-permute-done.1.received), custom_call_target="tpu_custom_call" | custom-call | flops 1048576 | bytes 2097152 | tf_op jit(solution)/shard_map/pallas_call | solution.py:89
  12.2 3.0 %collective-permute-start.2 = (bf16[4,256,128]{2,1,0:T(8,128)(2,1)}, bf16[4,256,128]{2,1,0:T(8,128)(2,1)S(1)}, u32[]{:S(2)}, u32[]{:S(2)}) collective-permute-start(bf16[4,256,128]{2,1,0:T(8,128)(2,1)} %get-tuple-element.38), channel_id=1, source_target_pairs={{0,16},{8,24},{16,0},{24,8},{1,17},{9,25},{17,1},{25,9},{2,18},{10... | collective-permute-start | bytes 786440 | tf_op jit(solution)/shard_map/ppermute | solution.py:27
  15.8 2.6 %collective-permute-start.4 = (bf16[4,256,128]{2,1,0:T(8,128)(2,1)S(1)}, bf16[4,256,128]{2,1,0:T(8,128)(2,1)S(1)}, u32[]{:S(2)}, u32[]{:S(2)}) collective-permute-start(bf16[4,256,128]{2,1,0:T(8,128)(2,1)S(1)} %get-tuple-element.40), channel_id=1, source_target_pairs={{0,24},{8,0},{16,8},{24,16},{1,25},{9,1},{17,9},{25,17},{2,26},{10... | collective-permute-start | bytes 786440 | tf_op jit(solution)/shard_map/ppermute | solution.py:27
  18.5 7.4 %collective-permute-start.12 = (bf16[2,64,1024]{2,1,0:T(8,128)(2,1)S(1)}, bf16[2,64,1024]{2,1,0:T(8,128)(2,1)S(1)}, u32[]{:S(2)}, u32[]{:S(2)}) collective-permute-start(bf16[2,64,1024]{2,1,0:T(8,128)(2,1)S(1)} %shard_map.118.first), channel_id=1, source_target_pairs={{0,1},{1,0},{2,3},{3,2},{4,5},{5,4},{6,7},{7,6},{8,9},{9,8},{10,11... | collective-permute-start | bytes 786440 | tf_op jit(solution)/shard_map/ppermute | solution.py:31
  26.0 2.1 %shard_map.114 = (f32[512,128]{1,0:T(8,128)S(1)}, bf16[512,64]{1,0:T(8,128)(2,1)S(1)}) custom-call(s32[16]{0:T(128)S(1)} %copy-done.4, bf16[64,1024]{1,0:T(8,128)(2,1)S(1)} %reshape.12.queries, bf16[64,128]{1,0:T(8,128)(2,1)S(1)} %bitcast.11, bf16[16,128,128]{2,1,0:T(8,128)(2,1)S(1)} %copy-done, bf16[16,128,128]{2,1,0:T(8,128)(2,1)S(1)} %copy-done.1), custom_call_target="tpu_custom_call" | custom-call | flops 1048576 | bytes 262144 | tf_op jit(solution)/shard_map/pallas_call | solution.py:174
  28.2 3.4 %collective-permute-done.12.second = bf16[2,64,1024]{2,1,0:T(8,128)(2,1)S(1)} collective-permute-done((bf16[2,64,1024]{2,1,0:T(8,128)(2,1)S(1)}, bf16[2,64,1024]{2,1,0:T(8,128)(2,1)S(1)}, u32[]{:S(2)}, u32[]{:S(2)}) %collective-permute-start.12) | collective-permute-done | bytes 262176 | tf_op jit(solution)/shard_map/ppermute | solution.py:31
  31.7 8.6 %collective-permute-start.13 = (bf16[4,64,1024]{2,1,0:T(8,128)(2,1)S(1)}, bf16[4,64,1024]{2,1,0:T(8,128)(2,1)S(1)}, u32[]{:S(2)}, u32[]{:S(2)}) collective-permute-start(bf16[4,64,1024]{2,1,0:T(8,128)(2,1)S(1)} %shard_map.119.near), channel_id=1, source_target_pairs={{0,3},{1,2},{2,1},{3,0},{4,7},{5,6},{6,5},{7,4},{8,11},{9,10},{10,... | collective-permute-start | bytes 1572872 | tf_op jit(solution)/shard_map/ppermute | solution.py:31
  40.3 5.6 %collective-permute-start.5 = (bf16[256,128]{1,0:T(8,128)(2,1)S(1)}, bf16[256,128]{1,0:T(8,128)(2,1)S(1)}, u32[]{:S(2)}, u32[]{:S(2)}) collective-permute-start(bf16[256,128]{1,0:T(8,128)(2,1)S(1)} %get-tuple-element.49), channel_id=1, source_target_pairs={{0,64},{32,96},{64,0},{96,32},{1,65},{33,97},{65,1},{97,33},{2,66}... | collective-permute-start | bytes 196616 | tf_op jit(solution)/shard_map/ppermute | solution.py:27
  45.9 4.1 %collective-permute-start.7 = (bf16[256,128]{1,0:T(8,128)(2,1)S(1)}, bf16[256,128]{1,0:T(8,128)(2,1)S(1)}, u32[]{:S(2)}, u32[]{:S(2)}) collective-permute-start(bf16[256,128]{1,0:T(8,128)(2,1)S(1)} %get-tuple-element.51), channel_id=1, source_target_pairs={{0,96},{32,0},{64,32},{96,64},{1,97},{33,1},{65,33},{97,65},{2,98}... | collective-permute-start | bytes 196616 | tf_op jit(solution)/shard_map/ppermute | solution.py:27
  50.1 3.5 %collective-permute-done.6.r2 = bf16[256,128]{1,0:T(8,128)(2,1)S(1)} collective-permute-done((bf16[256,128]{1,0:T(8,128)(2,1)S(1)}, bf16[256,128]{1,0:T(8,128)(2,1)S(1)}, u32[]{:S(2)}, u32[]{:S(2)}) %collective-permute-start.6) | collective-permute-done | bytes 65568 | tf_op jit(solution)/shard_map/ppermute | solution.py:27
  53.7 3.0 %collective-permute-start.8 = (bf16[256,128]{1,0:T(8,128)(2,1)S(1)}, bf16[256,128]{1,0:T(8,128)(2,1)S(1)}, u32[]{:S(2)}, u32[]{:S(2)}) collective-permute-start(bf16[256,128]{1,0:T(8,128)(2,1)S(1)} %shard_map.116), channel_id=1, source_target_pairs={{0,24},{8,0},{16,8},{24,16},{1,25},{9,1},{17,9},{25,17},{2,26},{10... | collective-permute-start | bytes 196616 | tf_op jit(solution)/shard_map/ppermute | solution.py:27
  56.7 0.8 %collective-permute-start.9 = (bf16[256,128]{1,0:T(8,128)(2,1)S(1)}, bf16[256,128]{1,0:T(8,128)(2,1)S(1)}, u32[]{:S(2)}, u32[]{:S(2)}) collective-permute-start(bf16[256,128]{1,0:T(8,128)(2,1)S(1)} %shard_map.116), channel_id=1, source_target_pairs={{0,16},{8,24},{16,0},{24,8},{1,17},{9,25},{17,1},{25,9},{2,18},{10... | collective-permute-start | bytes 196616 | tf_op jit(solution)/shard_map/ppermute | solution.py:27
  57.6 0.7 shard_map.117
  58.3 1.3 %collective-permute-done.8 = bf16[256,128]{1,0:T(8,128)(2,1)S(1)} collective-permute-done((bf16[256,128]{1,0:T(8,128)(2,1)S(1)}, bf16[256,128]{1,0:T(8,128)(2,1)S(1)}, u32[]{:S(2)}, u32[]{:S(2)}) %collective-permute-start.8) | collective-permute-done | bytes 65568 | tf_op jit(solution)/shard_map/ppermute | solution.py:27
  59.6 3.0 %collective-permute-done.9 = bf16[256,128]{1,0:T(8,128)(2,1)S(1)} collective-permute-done((bf16[256,128]{1,0:T(8,128)(2,1)S(1)}, bf16[256,128]{1,0:T(8,128)(2,1)S(1)}, u32[]{:S(2)}, u32[]{:S(2)}) %collective-permute-start.9) | collective-permute-done | bytes 65568 | tf_op jit(solution)/shard_map/ppermute | solution.py:27
  63.4 0.8 shard_map.120.start
  64.2 0.7 collective-permute-done.14.u_other
  64.9 0.9 %shard_map.121 = bf16[4,64,128]{2,1,0:T(8,128)(2,1)S(1)} custom-call(s32[5]{0:T(128)S(1)} %stack.38.place, bf16[4,64,1024]{2,1,0:T(8,128)(2,1)S(1)} %shard_map.119.near, bf16[4,64,1024]{2,1,0:T(8,128)(2,1)S(1)} %collective-permute-done.13.far, bf16[4,256,128]{2,1,0:T(8,128)(2,1)S(1)} %pad_maximum_fusion.u.u_own, ...), custom_call_target="tpu_custom_call" | custom-call | flops 67108864 | bytes 786432 | tf_op jit(solution)/shard_map/pallas_call | solution.py:223
  65.9 11.9 %all_to_all.5.parts = bf16[4,64,128]{2,1,0:T(8,128)(2,1)S(1)} all-to-all(bf16[4,64,128]{2,1,0:T(8,128)(2,1)S(1)} %shard_map.121), channel_id=1, replica_groups=mesh['c'=2,'zh'=4,'x'=4,'zl'=2,'y'=4] {'zh'}, dimensions={0} | all-to-all | bytes 131072 | tf_op jit(solution)/shard_map/all_to_all | solution.py:336
  77.7 0.8 %shard_map.122 = (bf16[16,4,128]{2,1,0:T(4,128)(2,1)}, bf16[16,4,1024]{2,1,0:T(4,128)(2,1)}) custom-call(bf16[4,64,128]{2,1,0:T(8,128)(2,1)S(1)} %all_to_all.5.parts, f32[512,128]{1,0:T(8,128)S(1)} %get-tuple-element.59.mixed, bf16[512,64]{1,0:T(8,128)(2,1)S(1)} %get-tuple-element.60.weights), custom_call_target="tpu_custom_call" | custom-call | tf_op jit(solution)/shard_map/pallas_call | solution.py:254
  (33 shorter events, 2.1 us)
Async XLA Ops:
  0.6 25.3 %copy-start.5 = (bf16[16,4,1024]{2,1,0:T(4,128)(2,1)S(1)}, bf16[16,4,1024]{2,1,0:T(4,128)(2,1)}, u32[]{:S(2)}) copy-start(bf16[16,4,1024]{2,1,0:T(4,128)(2,1)} %param.13) | copy-start | bytes 393220
  0.6 25.3 %copy-start.3 = (bf16[16,4,128]{2,1,0:T(4,128)(2,1)S(1)}, bf16[16,4,128]{2,1,0:T(4,128)(2,1)}, u32[]{:S(2)}) copy-start(bf16[16,4,128]{2,1,0:T(4,128)(2,1)} %param.14) | copy-start | bytes 49156
  0.7 25.3 %copy-start = (bf16[16,128,128]{2,1,0:T(8,128)(2,1)S(1)}, bf16[16,128,128]{2,1,0:T(8,128)(2,1)}, u32[]{:S(2)}) copy-start(bf16[16,128,128]{2,1,0:T(8,128)(2,1)} %cache_keys.1) | copy-start | bytes 1572868
  0.7 25.3 %copy-start.1 = (bf16[16,128,128]{2,1,0:T(8,128)(2,1)S(1)}, bf16[16,128,128]{2,1,0:T(8,128)(2,1)}, u32[]{:S(2)}) copy-start(bf16[16,128,128]{2,1,0:T(8,128)(2,1)} %cache_values.1) | copy-start | bytes 1572868
  0.7 25.3 %copy-start.4 = (s32[16]{0:T(128)S(1)}, s32[16]{0:T(128)}, u32[]{:S(2)}) copy-start(s32[16]{0:T(128)} %lengths.1) | copy-start | bytes 196
  0.7 52.9 %copy-start.2 = (bf16[256,128]{1,0:T(8,128)(2,1)S(1)}, bf16[256,128]{1,0:T(8,128)(2,1)}, u32[]{:S(2)}) copy-start(bf16[256,128]{1,0:T(8,128)(2,1)} %weight.1) | copy-start | bytes 196612
  0.7 7.7 %collective-permute-start = (bf16[16,4,1024]{2,1,0:T(4,128)(2,1)}, bf16[16,4,1024]{2,1,0:T(4,128)(2,1)S(1)}, u32[]{:S(2)}, u32[]{:S(2)}) collective-permute-start(bf16[16,4,1024]{2,1,0:T(4,128)(2,1)} %param.12), channel_id=1, source_target_pairs={{0,0},{1,33},{2,66},{3,99},{32,1},{33,34},{34,67},{35,96},{64,2},{... | collective-permute-start | bytes 393224 | tf_op jit(solution)/shard_map/ppermute | solution.py:36
  8.4 2.7 %collective-permute-start.1 = (bf16[4,4,256,128]{3,2,1,0:T(8,128)(2,1)S(1)}, bf16[4,4,256,128]{3,2,1,0:T(8,128)(2,1)S(1)}, u32[]{:S(2)}, u32[]{:S(2)}) collective-permute-start(bf16[4,4,256,128]{3,2,1,0:T(8,128)(2,1)S(1)} %get-tuple-element.36), channel_id=1, source_target_pairs={{0,128},{128,0},{1,129},{129,1},{2,130},{130,2},{3,131},{131,3},{4... | collective-permute-start | bytes 3145736 | tf_op jit(solution)/shard_map/ppermute | solution.py:27
  8.5 9.9 %collective-permute-start.11 = (bf16[16,4,1024]{2,1,0:T(4,128)(2,1)S(1)}, bf16[16,4,1024]{2,1,0:T(4,128)(2,1)S(1)}, u32[]{:S(2)}, u32[]{:S(2)}) collective-permute-start(bf16[16,4,1024]{2,1,0:T(4,128)(2,1)S(1)} %collective-permute-done.first), channel_id=1, source_target_pairs={{0,4},{4,0},{1,5},{5,1},{2,6},{6,2},{3,7},{7,3},{8,12},{12,8},{9,1... | collective-permute-start | bytes 393224 | tf_op jit(solution)/shard_map/ppermute | solution.py:27
  12.2 15.9 %collective-permute-start.2 = (bf16[4,256,128]{2,1,0:T(8,128)(2,1)}, bf16[4,256,128]{2,1,0:T(8,128)(2,1)S(1)}, u32[]{:S(2)}, u32[]{:S(2)}) collective-permute-start(bf16[4,256,128]{2,1,0:T(8,128)(2,1)} %get-tuple-element.38), channel_id=1, source_target_pairs={{0,16},{8,24},{16,0},{24,8},{1,17},{9,25},{17,1},{25,9},{2,18},{10... | collective-permute-start | bytes 786440 | tf_op jit(solution)/shard_map/ppermute | solution.py:27
  15.2 12.9 %collective-permute-start.3 = (bf16[4,256,128]{2,1,0:T(8,128)(2,1)}, bf16[4,256,128]{2,1,0:T(8,128)(2,1)S(1)}, u32[]{:S(2)}, u32[]{:S(2)}) collective-permute-start(bf16[4,256,128]{2,1,0:T(8,128)(2,1)} %get-tuple-element.39), channel_id=1, source_target_pairs={{0,8},{8,16},{16,24},{24,0},{1,9},{9,17},{17,25},{25,1},{2,10},{10... | collective-permute-start | bytes 786440 | tf_op jit(solution)/shard_map/ppermute | solution.py:27
  15.8 12.3 %collective-permute-start.4 = (bf16[4,256,128]{2,1,0:T(8,128)(2,1)S(1)}, bf16[4,256,128]{2,1,0:T(8,128)(2,1)S(1)}, u32[]{:S(2)}, u32[]{:S(2)}) collective-permute-start(bf16[4,256,128]{2,1,0:T(8,128)(2,1)S(1)} %get-tuple-element.40), channel_id=1, source_target_pairs={{0,24},{8,0},{16,8},{24,16},{1,25},{9,1},{17,9},{25,17},{2,26},{10... | collective-permute-start | bytes 786440 | tf_op jit(solution)/shard_map/ppermute | solution.py:27
  18.5 13.1 %collective-permute-start.12 = (bf16[2,64,1024]{2,1,0:T(8,128)(2,1)S(1)}, bf16[2,64,1024]{2,1,0:T(8,128)(2,1)S(1)}, u32[]{:S(2)}, u32[]{:S(2)}) collective-permute-start(bf16[2,64,1024]{2,1,0:T(8,128)(2,1)S(1)} %shard_map.118.first), channel_id=1, source_target_pairs={{0,1},{1,0},{2,3},{3,2},{4,5},{5,4},{6,7},{7,6},{8,9},{9,8},{10,11... | collective-permute-start | bytes 786440 | tf_op jit(solution)/shard_map/ppermute | solution.py:31
  31.7 31.6 %collective-permute-start.13 = (bf16[4,64,1024]{2,1,0:T(8,128)(2,1)S(1)}, bf16[4,64,1024]{2,1,0:T(8,128)(2,1)S(1)}, u32[]{:S(2)}, u32[]{:S(2)}) collective-permute-start(bf16[4,64,1024]{2,1,0:T(8,128)(2,1)S(1)} %shard_map.119.near), channel_id=1, source_target_pairs={{0,3},{1,2},{2,1},{3,0},{4,7},{5,6},{6,5},{7,4},{8,11},{9,10},{10,... | collective-permute-start | bytes 1572872 | tf_op jit(solution)/shard_map/ppermute | solution.py:31
  40.3 9.8 %collective-permute-start.5 = (bf16[256,128]{1,0:T(8,128)(2,1)S(1)}, bf16[256,128]{1,0:T(8,128)(2,1)S(1)}, u32[]{:S(2)}, u32[]{:S(2)}) collective-permute-start(bf16[256,128]{1,0:T(8,128)(2,1)S(1)} %get-tuple-element.49), channel_id=1, source_target_pairs={{0,64},{32,96},{64,0},{96,32},{1,65},{33,97},{65,1},{97,33},{2,66}... | collective-permute-start | bytes 196616 | tf_op jit(solution)/shard_map/ppermute | solution.py:27
  45.9 7.7 %collective-permute-start.6 = (bf16[256,128]{1,0:T(8,128)(2,1)S(1)}, bf16[256,128]{1,0:T(8,128)(2,1)S(1)}, u32[]{:S(2)}, u32[]{:S(2)}) collective-permute-start(bf16[256,128]{1,0:T(8,128)(2,1)S(1)} %get-tuple-element.50), channel_id=1, source_target_pairs={{0,32},{32,64},{64,96},{96,0},{1,33},{33,65},{65,97},{97,1},{2,34}... | collective-permute-start | bytes 196616 | tf_op jit(solution)/shard_map/ppermute | solution.py:27
  45.9 7.7 %collective-permute-start.7 = (bf16[256,128]{1,0:T(8,128)(2,1)S(1)}, bf16[256,128]{1,0:T(8,128)(2,1)S(1)}, u32[]{:S(2)}, u32[]{:S(2)}) collective-permute-start(bf16[256,128]{1,0:T(8,128)(2,1)S(1)} %get-tuple-element.51), channel_id=1, source_target_pairs={{0,96},{32,0},{64,32},{96,64},{1,97},{33,1},{65,33},{97,65},{2,98}... | collective-permute-start | bytes 196616 | tf_op jit(solution)/shard_map/ppermute | solution.py:27
  53.7 5.9 %collective-permute-start.8 = (bf16[256,128]{1,0:T(8,128)(2,1)S(1)}, bf16[256,128]{1,0:T(8,128)(2,1)S(1)}, u32[]{:S(2)}, u32[]{:S(2)}) collective-permute-start(bf16[256,128]{1,0:T(8,128)(2,1)S(1)} %shard_map.116), channel_id=1, source_target_pairs={{0,24},{8,0},{16,8},{24,16},{1,25},{9,1},{17,9},{25,17},{2,26},{10... | collective-permute-start | bytes 196616 | tf_op jit(solution)/shard_map/ppermute | solution.py:27
  56.7 5.9 %collective-permute-start.9 = (bf16[256,128]{1,0:T(8,128)(2,1)S(1)}, bf16[256,128]{1,0:T(8,128)(2,1)S(1)}, u32[]{:S(2)}, u32[]{:S(2)}) collective-permute-start(bf16[256,128]{1,0:T(8,128)(2,1)S(1)} %shard_map.116), channel_id=1, source_target_pairs={{0,16},{8,24},{16,0},{24,8},{1,17},{9,25},{17,1},{25,9},{2,18},{10... | collective-permute-start | bytes 196616 | tf_op jit(solution)/shard_map/ppermute | solution.py:27
  57.5 5.8 %collective-permute-start.10 = (bf16[256,128]{1,0:T(8,128)(2,1)S(1)}, bf16[256,128]{1,0:T(8,128)(2,1)S(1)}, u32[]{:S(2)}, u32[]{:S(2)}) collective-permute-start(bf16[256,128]{1,0:T(8,128)(2,1)S(1)} %shard_map.116), channel_id=1, source_target_pairs={{0,8},{8,16},{16,24},{24,0},{1,9},{9,17},{17,25},{25,1},{2,10},{10... | collective-permute-start | bytes 196616 | tf_op jit(solution)/shard_map/ppermute | solution.py:27
  63.3 1.6 %collective-permute-start.14 = (bf16[4,256,128]{2,1,0:T(8,128)(2,1)S(1)}, bf16[4,256,128]{2,1,0:T(8,128)(2,1)S(1)}, u32[]{:S(2)}, u32[]{:S(2)}) collective-permute-start(bf16[4,256,128]{2,1,0:T(8,128)(2,1)S(1)} %pad_maximum_fusion.u.u_own), channel_id=1, source_target_pairs={{0,128},{128,0},{1,129},{129,1},{2,130},{130,2},{3,131},{131,3},{4... | collective-permute-start | bytes 786440 | tf_op jit(solution)/shard_map/ppermute | solution.py:27

commit v10 on v5

--- a/solution.py
+++ b/solution.py
@@ -27,15 +27,13 @@
     return lax.ppermute(value, axis, [(i, (i + by) % n) for i in range(n)])
 
 
-def swap_places(value):
-    names = ("c", "zh", "zl", "y")
-    sizes = [SIZES[n] for n in names]
-    pairs = []
-    for c, zh, zl, y in np.ndindex(*sizes):
-        source = int(np.ravel_multi_index((c, zh, zl, y), sizes))
-        target = int(np.ravel_multi_index((zl, y, c, (zh + y) % 4), sizes))
-        pairs.append((source, target))
-    return lax.ppermute(value, names, pairs)
+def exchange(value, axis, bit):
+    return lax.ppermute(value, axis, [(i, i ^ bit) for i in range(SIZES[axis])])
+
+
+def swap_cores(value):
+    pairs = [(c * 2 + zl, zl * 2 + c) for c in range(2) for zl in range(2)]
+    return lax.ppermute(value, ("c", "zl"), pairs)
 
 
 def after(value, *others):
@@ -68,11 +66,13 @@
 
 def partial_gradient(place, normed_inputs, value_cotangent):
     tokens = normed_inputs.shape[0]
+    normed_inputs = pltpu.with_memory_space_constraint(normed_inputs, pltpu.HBM)
+    value_cotangent = pltpu.with_memory_space_constraint(value_cotangent, pltpu.HBM)
     return pl.pallas_call(
         partial_kernel,
         in_specs=[SMEM, HBM, HBM],
         out_specs=[VMEM, VMEM],
-        out_shape=[jax.ShapeDtypeStruct((4, 4, 256, HD), BF16)] * 2,
+        out_shape=[pltpu.VMEM((4, 4, 256, HD), BF16)] * 2,
         scratch_shapes=[
             pltpu.VMEM((8, tokens, 1024), BF16),
             pltpu.VMEM((tokens, HD), BF16),
@@ -85,12 +85,14 @@
     )(place, normed_inputs, value_cotangent)
 
 
-def small_call(kernel, outs, *args):
+def small_call(kernel, outs, *args, keep=True):
     return pl.pallas_call(
         kernel,
         in_specs=[VMEM] * len(args),
         out_specs=[VMEM] * len(outs),
-        out_shape=[jax.ShapeDtypeStruct(shape, dtype) for shape, dtype in outs],
+        out_shape=[
+            (pltpu.VMEM if keep else jax.ShapeDtypeStruct)(shape, dtype) for shape, dtype in outs
+        ],
         compiler_params=pltpu.CompilerParams(vmem_limit_bytes=16 * MIB),
         cost_estimate=pl.CostEstimate(flops=MIB, bytes_accessed=2 * MIB, transcendentals=0),
     )(*args)
@@ -109,6 +111,11 @@
             out[i, r * steps : (r + 1) * steps] = ref[r]
 
 
+def pair_kernel(first, second, out):
+    out[:2] = first[...]
+    out[2:] = second[...]
+
+
 def x_sum_kernel(own, r1, r2, r3, o0, o1, o2, o3):
     for e, out in enumerate((o0, o1, o2, o3)):
         total = own[e] + r1[e].astype(F32) + r2[e].astype(F32) + r3[e].astype(F32)
@@ -128,12 +135,16 @@
     gradient[...] = total_of(own, r1, r2, r3)
 
 
-def attend_kernel(lengths, queries, new_keys, cache_keys, cache_values, mixed_ref, weights_ref):
+def attend_kernel(
+    lengths, raw_queries, new_keys, cache_keys, cache_values, mixed_ref, weights_ref, queries
+):
     rows = cache_keys.shape[0]
     slots = cache_keys.shape[1]
-    steps = queries.shape[0] // rows
-    every = HEADS * queries.shape[0]
+    steps = raw_queries.shape[1]
+    every = HEADS * rows * steps
     factor = 1.0 / math.sqrt(HD)
+    for r in range(rows):
+        queries[r * steps : (r + 1) * steps] = raw_queries[r]
     heads = jnp.concatenate([queries[:, q * HD : (q + 1) * HD] for q in range(HEADS)], axis=0)
     place = lax.broadcasted_iota(jnp.int32, (every, slots), 0) % (rows * steps)
     lane = lax.broadcasted_iota(jnp.int32, (every, slots), 1)
@@ -163,7 +174,7 @@
 
 
 def attend_cache(lengths, queries, new_keys, cache_keys, cache_values):
-    places = queries.shape[0]
+    places = queries.shape[0] * queries.shape[1]
     return pl.pallas_call(
         attend_kernel,
         in_specs=[SMEM] + [VMEM] * 4,
@@ -172,6 +183,7 @@
             jax.ShapeDtypeStruct((HEADS * places, HD), F32),
             jax.ShapeDtypeStruct((HEADS * places, places), BF16),
         ],
+        scratch_shapes=[pltpu.VMEM((places, HEADS * HD), BF16)],
         compiler_params=pltpu.CompilerParams(vmem_limit_bytes=16 * MIB),
         cost_estimate=pl.CostEstimate(
             flops=MIB, bytes_accessed=MIB // 4, transcendentals=0
@@ -179,39 +191,45 @@
     )(lengths, queries, new_keys, cache_keys, cache_values)
 
 
-def project_kernel(place, d0, d1, d2, d3, u0, u1, u2, u3, out_ref, rows):
-    high, x, y, low = place[1], place[2], place[3], place[4]
+def project_kernel(place, near, far, u0, u1, u2, u3, own_ref, other_ref, rows):
+    core, high, x, y, low = (place[i] for i in range(5))
     for d, u in enumerate((u0, u1, u2, u3)):
-        rows[pl.ds(pl.multiple_of(lax.rem(x + d, 4) * 256, 256), 256), :] = u[...]
-    for d, piece in enumerate((d0, d1, d2, d3)):
-        zh = lax.rem(y + d + 4 - high, 4)
-        for j in range(2):
-            core = low if j == 0 else 1 - low
-            product = jnp.dot(piece[j], rows[...], preferred_element_type=F32)
-            out_ref[core * 4 + zh] = product.astype(out_ref.dtype)
-
-
-def project(place, pieces, updated):
-    places = pieces[0].shape[1]
+        for e in range(4):
+            block = lax.rem(high + e, 4) * 4 + lax.rem(x + d, 4)
+            rows[pl.ds(pl.multiple_of(block * 256, 256), 256), :] = u[e]
+    total = None
+    for bits, piece, first in ((0, near, 0), (1, near, 2), (3, far, 0), (2, far, 2)):
+        start = pl.multiple_of(jnp.bitwise_xor(y, bits) * 1024, 1024)
+        inputs = jnp.concatenate([piece[first], piece[first + 1]], axis=0)
+        product = jnp.dot(inputs, rows[pl.ds(start, 1024), :], preferred_element_type=F32)
+        total = product if total is None else total + product
+    size = total.shape[0] // 2
+    swap = core != low
+    own_ref[...] = jnp.where(swap, total[size:], total[:size])
+    other_ref[...] = jnp.where(swap, total[:size], total[size:]).astype(BF16)
+
+
+def project(place, near, far, updated):
+    places = near.shape[1]
     return pl.pallas_call(
         project_kernel,
-        in_specs=[SMEM] + [VMEM] * 8,
-        out_specs=VMEM,
-        out_shape=jax.ShapeDtypeStruct((8, places, HD), BF16),
-        scratch_shapes=[pltpu.VMEM((1024, HD), BF16)],
+        in_specs=[SMEM] + [VMEM] * 6,
+        out_specs=[VMEM, VMEM],
+        out_shape=[
+            jax.ShapeDtypeStruct((places, HD), F32),
+            jax.ShapeDtypeStruct((places, HD), BF16),
+        ],
+        scratch_shapes=[pltpu.VMEM((D // 2, HD), BF16)],
         compiler_params=pltpu.CompilerParams(vmem_limit_bytes=16 * MIB),
         cost_estimate=pl.CostEstimate(
-            flops=2 * 512 * 1024 * HD, bytes_accessed=3 * MIB // 2, transcendentals=0
-        ),
-    )(place, *pieces, *updated)
-
-
-def finish_kernel(parts, mixed, weights, values_ref, attended_ref):
+            flops=2 * 128 * 4096 * HD, bytes_accessed=2 * MIB, transcendentals=0
+        ),
+    )(place, near, far, *updated)
+
+
+def finish_kernel(own, received, mixed, weights, values_ref, attended_ref):
     steps = values_ref.shape[1]
-    total = parts[0].astype(F32)
-    for i in range(1, 8):
-        total += parts[i].astype(F32)
-    values = total.astype(BF16)
+    values = (own[...] + received[...].astype(F32)).astype(BF16)
     for r in range(values_ref.shape[0]):
         values_ref[r] = values[r * steps : (r + 1) * steps]
     places = values.shape[0]
@@ -223,17 +241,17 @@
             attended_ref[r, :, q * HD : (q + 1) * HD] = head[r * steps : (r + 1) * steps]
 
 
-def finish(parts, mixed, weights, rows, steps):
+def finish(own, received, mixed, weights, rows, steps):
     return pl.pallas_call(
         finish_kernel,
-        in_specs=[VMEM] * 3,
+        in_specs=[VMEM] * 4,
         out_specs=[VMEM, VMEM],
         out_shape=[
             jax.ShapeDtypeStruct((rows, steps, HD), BF16),
             jax.ShapeDtypeStruct((rows, steps, HEADS * HD), BF16),
         ],
         compiler_params=pltpu.CompilerParams(vmem_limit_bytes=16 * MIB),
-    )(parts, mixed, weights)
+    )(own, received, mixed, weights)
 
 
 def shards(
@@ -252,46 +270,45 @@
     places = row_count * step_count
     place = jnp.stack([core, high, x, y, low])
 
-    swapped = swap_places(decode_inputs)
+    swapped = swap_cores(decode_inputs)
     theirs, mine = partial_gradient(place, normed_inputs, value_cotangent)
     theirs, mine, swapped = lax.optimization_barrier((theirs, mine, swapped))
     received = shift(theirs, "c", 1)
     second = shift(swapped, "zl", 1)
 
-    mine, received, swapped = lax.optimization_barrier((mine, received, swapped))
     rows = (4, 256, HD)
     own, *sent = small_call(
         core_sum_kernel, [(rows, F32)] + [(rows, BF16)] * 3, mine, received
     )
     along_x = [shift(sent[d - 1], "x", d) for d in (2, 1, 3)]
-    swapped = after(swapped, own)
-    (both,) = small_call(join_kernel, [((2, places, D // 8), BF16)], swapped, second)
-    pieces = [both] + [shift(both, "y", -d) for d in (1, 3, 2)]
-    pieces = [pieces[0], pieces[1], pieces[3], pieces[2]]
+    (both,) = small_call(
+        join_kernel, [((2, places, D // 8), BF16)], after(swapped, own), second
+    )
+    near = exchange(both, "y", 1)
 
     rows = (256, HD)
     own, *sent = small_call(
         x_sum_kernel, [(rows, F32)] + [(rows, BF16)] * 3, own, *along_x
     )
-    sent[2], pieces[1] = lax.optimization_barrier((sent[2], pieces[1]))
     along_z = [shift(sent[e - 1], "zh", e) for e in (2, 1, 3)]
-    own, *along_z, pieces = lax.optimization_barrier((own, *along_z, pieces))
+    attended_cache, fresh_weights = attend_cache(
+        lengths, after(queries, own), new_keys.reshape(places, HD), cache_keys, cache_values
+    )
+    own, *along_z, near, attended_cache, fresh_weights = lax.optimization_barrier(
+        (own, *along_z, near, attended_cache, fresh_weights)
+    )
     (updated,) = small_call(update_kernel, [(rows, BF16)], value_weight, own, *along_z)
-    attended_cache, fresh_weights = attend_cache(
-        lengths,
-        after(queries.reshape(places, -1), updated),
-        new_keys.reshape(places, HD),
-        cache_keys,
-        cache_values,
-    )
     own = after(own, updated)
-    (gradient,) = small_call(gradient_kernel, [(rows, F32)], own, *along_z)
-
-    gathered = [updated] + [shift(updated, "x", -d) for d in (1, 2, 3)]
-    partial = project(place, pieces, gathered)
-    exchanged = lax.all_to_all(partial, ("c", "zh"), 0, 0, tiled=True)
+    (gradient,) = small_call(gradient_kernel, [(rows, F32)], own, *along_z, keep=False)
+
+    (near,) = small_call(pair_kernel, [((4, places, D // 8), BF16)], after(both, updated), near)
+    far = exchange(near, "y", 3)
+    gathered = jnp.stack([updated] + [shift(updated, "zh", -e) for e in (1, 2, 3)])
+    gathered, gradient = lax.optimization_barrier((gathered, gradient))
+    gathered = [gathered] + [shift(gathered, "x", -d) for d in (1, 2, 3)]
+    own, other = project(place, near, far, gathered)
     new_values, attended = finish(
-        exchanged, attended_cache, fresh_weights, row_count, step_count
+        own, shift(other, "c", 1), attended_cache, fresh_weights, row_count, step_count
     )
     return (gradient, new_values, attended)
 

time: 82.8 us -> 78.7 us (0.950)
  the two profiles are of different devices: /device:TPU:1 before, /device:TPU:32 now
where the time goes in v10:
time: 78.7 us; the launch traced here: 77.9 us
  starting transfers between devices  35.7 us (45%)
  waiting for transfers between devices  30.1 us (38%)
  Pallas kernels  11.1 us (14%)
  between operations  0.82 us (1%)
    ppermute x15, waiting for transfers between devices, shift(): return lax.ppermute(value, axis, [(i, (i + by) % n) for i in range(n)])  30.1 us
    ppermute x15, starting transfers between devices, shift(): return lax.ppermute(value, axis, [(i, (i + by) % n) for i in range(n)])  28.9 us
    pallas_call x1, Pallas kernels, partial_gradient(): pl.pallas_call(partial_kernel, in_specs=[SMEM, HBM, HBM], out_specs=[VMEM...  5.96 us
    ppermute x2, starting transfers between devices, exchange(): return lax.ppermute(value, axis, [(i, i ^ bit) for i in range(SIZES[axis])])  4.77 us
    pallas_call x1, Pallas kernels, attend_cache(): pl.pallas_call(attend_kernel, in_specs=[SMEM] + [VMEM] * 4, out_specs=[VM...  2.13 us
    ppermute x1, starting transfers between devices, swap_cores(): return lax.ppermute(value, ('c', 'zl'), pairs)  2.05 us
  transfers between devices with their start and end apart: 18, of which 11 were waited for; matrix products, arithmetic and copies ran while one was open for 0% of the time, Pallas kernels for 12%

profile of v10, /device:TPU:32, one launch (start us, length us, event | category | flops | bytes accessed | tf_op | source)
XLA Modules:
  0.0 77.9 jit_solution(8505953491981041189)
XLA Ops:
  0.7 2.1 %collective-permute-start = (bf16[16,4,1024]{2,1,0:T(4,128)(2,1)}, bf16[16,4,1024]{2,1,0:T(4,128)(2,1)S(1)}, u32[]{:S(2)}, u32[]{:S(2)}) collective-permute-start(bf16[16,4,1024]{2,1,0:T(4,128)(2,1)} %param.12), channel_id=1, source_target_pairs={{0,0},{4,128},{128,4},{132,132},{1,1},{5,129},{129,5},{133,133},{2... | collective-permute-start | bytes 393224 | tf_op jit(solution)/shard_map/ppermute | solution.py:36
  2.8 6.0 %shard_map.112 = (bf16[4,4,256,128]{3,2,1,0:T(8,128)(2,1)S(1)}, bf16[4,4,256,128]{3,2,1,0:T(8,128)(2,1)S(1)}) custom-call(s32[5]{0:T(128)S(1)} %stack.38.place, bf16[768,8192]{1,0:T(8,128)(2,1)} %x_hbm.1, bf16[768,128]{1,0:T(8,128)(2,1)} %v_hbm.1), custom_call_target="tpu_custom_call" | custom-call | flops 1610612736 | bytes 12582912 | tf_op jit(solution)/shard_map/pallas_call | solution.py:71
  8.9 2.1 %collective-permute-start.8 = (bf16[16,4,1024]{2,1,0:T(4,128)(2,1)S(1)}, bf16[16,4,1024]{2,1,0:T(4,128)(2,1)S(1)}, u32[]{:S(2)}, u32[]{:S(2)}) collective-permute-start(bf16[16,4,1024]{2,1,0:T(4,128)(2,1)S(1)} %collective-permute-done.first), channel_id=1, source_target_pairs={{0,4},{4,0},{1,5},{5,1},{2,6},{6,2},{3,7},{7,3},{8,12},{12,8},{9,1... | collective-permute-start | bytes 393224 | tf_op jit(solution)/shard_map/ppermute | solution.py:27
  11.8 3.1 %collective-permute-start.2 = (bf16[4,256,128]{2,1,0:T(8,128)(2,1)S(1)}, bf16[4,256,128]{2,1,0:T(8,128)(2,1)S(1)}, u32[]{:S(2)}, u32[]{:S(2)}) collective-permute-start(bf16[4,256,128]{2,1,0:T(8,128)(2,1)S(1)} %get-tuple-element.40), channel_id=1, source_target_pairs={{0,16},{8,24},{16,0},{24,8},{1,17},{9,25},{17,1},{25,9},{2,18},{10... | collective-permute-start | bytes 786440 | tf_op jit(solution)/shard_map/ppermute | solution.py:27
  15.5 2.6 %collective-permute-start.4 = (bf16[4,256,128]{2,1,0:T(8,128)(2,1)S(1)}, bf16[4,256,128]{2,1,0:T(8,128)(2,1)S(1)}, u32[]{:S(2)}, u32[]{:S(2)}) collective-permute-start(bf16[4,256,128]{2,1,0:T(8,128)(2,1)S(1)} %get-tuple-element.42), channel_id=1, source_target_pairs={{0,24},{8,0},{16,8},{24,16},{1,25},{9,1},{17,9},{25,17},{2,26},{10... | collective-permute-start | bytes 786440 | tf_op jit(solution)/shard_map/ppermute | solution.py:27
  18.2 1.7 %collective-permute-start.9 = (bf16[2,64,1024]{2,1,0:T(8,128)(2,1)S(1)}, bf16[2,64,1024]{2,1,0:T(8,128)(2,1)S(1)}, u32[]{:S(2)}, u32[]{:S(2)}) collective-permute-start(bf16[2,64,1024]{2,1,0:T(8,128)(2,1)S(1)} %shard_map.115.first), channel_id=1, source_target_pairs={{0,1},{1,0},{2,3},{3,2},{4,5},{5,4},{6,7},{7,6},{8,9},{9,8},{10,11... | collective-permute-start | bytes 786440 | tf_op jit(solution)/shard_map/ppermute | solution.py:31
  19.9 2.7 %collective-permute-done.2.r1 = bf16[4,256,128]{2,1,0:T(8,128)(2,1)S(1)} collective-permute-done((bf16[4,256,128]{2,1,0:T(8,128)(2,1)S(1)}, bf16[4,256,128]{2,1,0:T(8,128)(2,1)S(1)}, u32[]{:S(2)}, u32[]{:S(2)}) %collective-permute-start.2) | collective-permute-done | bytes 262176 | tf_op jit(solution)/shard_map/ppermute | solution.py:27
  22.6 4.8 %collective-permute-done.3.r2 = bf16[4,256,128]{2,1,0:T(8,128)(2,1)S(1)} collective-permute-done((bf16[4,256,128]{2,1,0:T(8,128)(2,1)S(1)}, bf16[4,256,128]{2,1,0:T(8,128)(2,1)S(1)}, u32[]{:S(2)}, u32[]{:S(2)}) %collective-permute-start.3) | collective-permute-done | bytes 262176 | tf_op jit(solution)/shard_map/ppermute | solution.py:27
  27.6 6.8 %collective-permute-start.5 = (bf16[256,128]{1,0:T(8,128)(2,1)S(1)}, bf16[256,128]{1,0:T(8,128)(2,1)S(1)}, u32[]{:S(2)}, u32[]{:S(2)}) collective-permute-start(bf16[256,128]{1,0:T(8,128)(2,1)S(1)} %get-tuple-element.44), channel_id=1, source_target_pairs={{0,64},{32,96},{64,0},{96,32},{1,65},{33,97},{65,1},{97,33},{2,66}... | collective-permute-start | bytes 196616 | tf_op jit(solution)/shard_map/ppermute | solution.py:27
  34.4 1.5 %collective-permute-start.6 = (bf16[256,128]{1,0:T(8,128)(2,1)S(1)}, bf16[256,128]{1,0:T(8,128)(2,1)S(1)}, u32[]{:S(2)}, u32[]{:S(2)}) collective-permute-start(bf16[256,128]{1,0:T(8,128)(2,1)S(1)} %get-tuple-element.45), channel_id=1, source_target_pairs={{0,32},{32,64},{64,96},{96,0},{1,33},{33,65},{65,97},{97,1},{2,34}... | collective-permute-start | bytes 196616 | tf_op jit(solution)/shard_map/ppermute | solution.py:27
  35.9 2.7 %collective-permute-start.7 = (bf16[256,128]{1,0:T(8,128)(2,1)S(1)}, bf16[256,128]{1,0:T(8,128)(2,1)S(1)}, u32[]{:S(2)}, u32[]{:S(2)}) collective-permute-start(bf16[256,128]{1,0:T(8,128)(2,1)S(1)} %get-tuple-element.46), channel_id=1, source_target_pairs={{0,96},{32,0},{64,32},{96,64},{1,97},{33,1},{65,33},{97,65},{2,98}... | collective-permute-start | bytes 196616 | tf_op jit(solution)/shard_map/ppermute | solution.py:27
  38.6 2.1 %shard_map.116 = (f32[512,128]{1,0:T(8,128)S(1)}, bf16[512,64]{1,0:T(8,128)(2,1)S(1)}) custom-call(s32[16]{0:T(128)S(1)} %copy-done.5, bf16[16,4,1024]{2,1,0:T(4,128)(2,1)S(1)} %copy-done.2, bf16[64,128]{1,0:T(8,128)(2,1)S(1)} %bitcast.11, bf16[16,128,128]{2,1,0:T(8,128)(2,1)S(1)} %copy-done, bf16[16,128,128]{2,1,0:T(8,128)(2,1)S(1)} %copy-done.1), custom_call_target="tpu_custom_call" | custom-call | flops 1048576 | bytes 262144 | tf_op jit(solution)/shard_map/pallas_call | solution.py:178
  40.7 1.9 %collective-permute-done.6.r2 = bf16[256,128]{1,0:T(8,128)(2,1)S(1)} collective-permute-done((bf16[256,128]{1,0:T(8,128)(2,1)S(1)}, bf16[256,128]{1,0:T(8,128)(2,1)S(1)}, u32[]{:S(2)}, u32[]{:S(2)}) %collective-permute-start.6) | collective-permute-done | bytes 65568 | tf_op jit(solution)/shard_map/ppermute | solution.py:27
  42.8 3.1 %collective-permute-start.13 = (bf16[4,64,1024]{2,1,0:T(8,128)(2,1)S(1)}, bf16[4,64,1024]{2,1,0:T(8,128)(2,1)S(1)}, u32[]{:S(2)}, u32[]{:S(2)}) collective-permute-start(bf16[4,64,1024]{2,1,0:T(8,128)(2,1)S(1)} %shard_map.119.near), channel_id=1, source_target_pairs={{0,3},{1,2},{2,1},{3,0},{4,7},{5,6},{6,5},{7,4},{8,11},{9,10},{10,... | collective-permute-start | bytes 1572872 | tf_op jit(solution)/shard_map/ppermute | solution.py:31
  45.9 2.8 %collective-permute-start.10 = (bf16[256,128]{1,0:T(8,128)(2,1)S(1)}, bf16[256,128]{1,0:T(8,128)(2,1)S(1)}, u32[]{:S(2)}, u32[]{:S(2)}) collective-permute-start(bf16[256,128]{1,0:T(8,128)(2,1)S(1)} %shard_map.117), channel_id=1, source_target_pairs={{0,96},{32,0},{64,32},{96,64},{1,97},{33,1},{65,33},{97,65},{2,98}... | collective-permute-start | bytes 196616 | tf_op jit(solution)/shard_map/ppermute | solution.py:27
  48.7 2.5 %collective-permute-start.11 = (bf16[256,128]{1,0:T(8,128)(2,1)S(1)}, bf16[256,128]{1,0:T(8,128)(2,1)S(1)}, u32[]{:S(2)}, u32[]{:S(2)}) collective-permute-start(bf16[256,128]{1,0:T(8,128)(2,1)S(1)} %shard_map.117), channel_id=1, source_target_pairs={{0,64},{32,96},{64,0},{96,32},{1,65},{33,97},{65,1},{97,33},{2,66}... | collective-permute-start | bytes 196616 | tf_op jit(solution)/shard_map/ppermute | solution.py:27
  52.0 5.1 %collective-permute-done.11 = bf16[256,128]{1,0:T(8,128)(2,1)S(1)} collective-permute-done((bf16[256,128]{1,0:T(8,128)(2,1)S(1)}, bf16[256,128]{1,0:T(8,128)(2,1)S(1)}, u32[]{:S(2)}, u32[]{:S(2)}) %collective-permute-start.11) | collective-permute-done | bytes 65568 | tf_op jit(solution)/shard_map/ppermute | solution.py:27
  57.1 1.8 %collective-permute-done.12 = bf16[256,128]{1,0:T(8,128)(2,1)S(1)} collective-permute-done((bf16[256,128]{1,0:T(8,128)(2,1)S(1)}, bf16[256,128]{1,0:T(8,128)(2,1)S(1)}, u32[]{:S(2)}, u32[]{:S(2)}) %collective-permute-start.12) | collective-permute-done | bytes 65568 | tf_op jit(solution)/shard_map/ppermute | solution.py:27
  59.0 2.8 %collective-permute-start.14 = (bf16[4,256,128]{2,1,0:T(8,128)(2,1)S(1)}, bf16[4,256,128]{2,1,0:T(8,128)(2,1)S(1)}, u32[]{:S(2)}, u32[]{:S(2)}) collective-permute-start(bf16[4,256,128]{2,1,0:T(8,128)(2,1)S(1)} %pad_maximum_fusion.u0), channel_id=1, source_target_pairs={{0,24},{8,0},{16,8},{24,16},{1,25},{9,1},{17,9},{25,17},{2,26},{10... | collective-permute-start | bytes 786440 | tf_op jit(solution)/shard_map/ppermute | solution.py:27
  62.7 8.3 %collective-permute-done.14.u1 = bf16[4,256,128]{2,1,0:T(8,128)(2,1)S(1)} collective-permute-done((bf16[4,256,128]{2,1,0:T(8,128)(2,1)S(1)}, bf16[4,256,128]{2,1,0:T(8,128)(2,1)S(1)}, u32[]{:S(2)}, u32[]{:S(2)}) %collective-permute-start.14) | collective-permute-done | bytes 262176 | tf_op jit(solution)/shard_map/ppermute | solution.py:27
  71.0 1.0 %collective-permute-done.15.u2 = bf16[4,256,128]{2,1,0:T(8,128)(2,1)S(1)} collective-permute-done((bf16[4,256,128]{2,1,0:T(8,128)(2,1)S(1)}, bf16[4,256,128]{2,1,0:T(8,128)(2,1)S(1)}, u32[]{:S(2)}, u32[]{:S(2)}) %collective-permute-start.15) | collective-permute-done | bytes 262176 | tf_op jit(solution)/shard_map/ppermute | solution.py:27
  72.0 2.7 %collective-permute-done.16.u3 = bf16[4,256,128]{2,1,0:T(8,128)(2,1)S(1)} collective-permute-done((bf16[4,256,128]{2,1,0:T(8,128)(2,1)S(1)}, bf16[4,256,128]{2,1,0:T(8,128)(2,1)S(1)}, u32[]{:S(2)}, u32[]{:S(2)}) %collective-permute-start.16) | collective-permute-done | bytes 262176 | tf_op jit(solution)/shard_map/ppermute | solution.py:27
  74.7 1.1 %shard_map.120 = (f32[64,128]{1,0:T(8,128)S(1)}, bf16[64,128]{1,0:T(8,128)(2,1)S(1)}) custom-call(s32[5]{0:T(128)S(1)} %stack.38.place, bf16[4,64,1024]{2,1,0:T(8,128)(2,1)S(1)} %shard_map.119.near, bf16[4,64,1024]{2,1,0:T(8,128)(2,1)S(1)} %collective-permute-done.13.far, bf16[4,256,128]{2,1,0:T(8,128)(2,1)S(1)} %pad_maximum_fusion.u0, ...), custom_call_target="tpu_custom_call" | custom-call | flops 134217728 | bytes 2097152 | tf_op jit(solution)/shard_map/pallas_call | solution.py:214
  75.9 1.2 %collective-permute-done.17.received = bf16[64,128]{1,0:T(8,128)(2,1)S(1)} collective-permute-done((bf16[64,128]{1,0:T(8,128)(2,1)S(1)}, bf16[64,128]{1,0:T(8,128)(2,1)S(1)}, u32[]{:S(2)}, u32[]{:S(2)}) %collective-permute-start.17) | collective-permute-done | bytes 16416 | tf_op jit(solution)/shard_map/ppermute | solution.py:27
  (36 shorter events, 4.7 us)
Async XLA Ops:
  0.6 37.9 %copy-start.2 = (bf16[16,4,1024]{2,1,0:T(4,128)(2,1)S(1)}, bf16[16,4,1024]{2,1,0:T(4,128)(2,1)}, u32[]{:S(2)}) copy-start(bf16[16,4,1024]{2,1,0:T(4,128)(2,1)} %raw_queries) | copy-start | bytes 393220
  0.6 37.9 %copy-start.4 = (bf16[16,4,128]{2,1,0:T(4,128)(2,1)S(1)}, bf16[16,4,128]{2,1,0:T(4,128)(2,1)}, u32[]{:S(2)}) copy-start(bf16[16,4,128]{2,1,0:T(4,128)(2,1)} %param.14) | copy-start | bytes 49156
  0.7 37.9 %copy-start = (bf16[16,128,128]{2,1,0:T(8,128)(2,1)S(1)}, bf16[16,128,128]{2,1,0:T(8,128)(2,1)}, u32[]{:S(2)}) copy-start(bf16[16,128,128]{2,1,0:T(8,128)(2,1)} %cache_keys.1) | copy-start | bytes 1572868
  0.7 37.9 %copy-start.1 = (bf16[16,128,128]{2,1,0:T(8,128)(2,1)S(1)}, bf16[16,128,128]{2,1,0:T(8,128)(2,1)}, u32[]{:S(2)}) copy-start(bf16[16,128,128]{2,1,0:T(8,128)(2,1)} %cache_values.1) | copy-start | bytes 1572868
  0.7 37.9 %copy-start.5 = (s32[16]{0:T(128)S(1)}, s32[16]{0:T(128)}, u32[]{:S(2)}) copy-start(s32[16]{0:T(128)} %lengths.1) | copy-start | bytes 196
  0.7 42.0 %copy-start.3 = (bf16[256,128]{1,0:T(8,128)(2,1)S(1)}, bf16[256,128]{1,0:T(8,128)(2,1)}, u32[]{:S(2)}) copy-start(bf16[256,128]{1,0:T(8,128)(2,1)} %weight.1) | copy-start | bytes 196612
  0.7 8.1 %collective-permute-start = (bf16[16,4,1024]{2,1,0:T(4,128)(2,1)}, bf16[16,4,1024]{2,1,0:T(4,128)(2,1)S(1)}, u32[]{:S(2)}, u32[]{:S(2)}) collective-permute-start(bf16[16,4,1024]{2,1,0:T(4,128)(2,1)} %param.12), channel_id=1, source_target_pairs={{0,0},{4,128},{128,4},{132,132},{1,1},{5,129},{129,5},{133,133},{2... | collective-permute-start | bytes 393224 | tf_op jit(solution)/shard_map/ppermute | solution.py:36
  8.8 2.7 %collective-permute-start.1 = (bf16[4,4,256,128]{3,2,1,0:T(8,128)(2,1)S(1)}, bf16[4,4,256,128]{3,2,1,0:T(8,128)(2,1)S(1)}, u32[]{:S(2)}, u32[]{:S(2)}) collective-permute-start(bf16[4,4,256,128]{3,2,1,0:T(8,128)(2,1)S(1)} %get-tuple-element.38), channel_id=1, source_target_pairs={{0,128},{128,0},{1,129},{129,1},{2,130},{130,2},{3,131},{131,3},{4... | collective-permute-start | bytes 3145736 | tf_op jit(solution)/shard_map/ppermute | solution.py:27
  8.9 9.2 %collective-permute-start.8 = (bf16[16,4,1024]{2,1,0:T(4,128)(2,1)S(1)}, bf16[16,4,1024]{2,1,0:T(4,128)(2,1)S(1)}, u32[]{:S(2)}, u32[]{:S(2)}) collective-permute-start(bf16[16,4,1024]{2,1,0:T(4,128)(2,1)S(1)} %collective-permute-done.first), channel_id=1, source_target_pairs={{0,4},{4,0},{1,5},{5,1},{2,6},{6,2},{3,7},{7,3},{8,12},{12,8},{9,1... | collective-permute-start | bytes 393224 | tf_op jit(solution)/shard_map/ppermute | solution.py:27
  11.8 10.8 %collective-permute-start.2 = (bf16[4,256,128]{2,1,0:T(8,128)(2,1)S(1)}, bf16[4,256,128]{2,1,0:T(8,128)(2,1)S(1)}, u32[]{:S(2)}, u32[]{:S(2)}) collective-permute-start(bf16[4,256,128]{2,1,0:T(8,128)(2,1)S(1)} %get-tuple-element.40), channel_id=1, source_target_pairs={{0,16},{8,24},{16,0},{24,8},{1,17},{9,25},{17,1},{25,9},{2,18},{10... | collective-permute-start | bytes 786440 | tf_op jit(solution)/shard_map/ppermute | solution.py:27
  14.9 12.4 %collective-permute-start.3 = (bf16[4,256,128]{2,1,0:T(8,128)(2,1)S(1)}, bf16[4,256,128]{2,1,0:T(8,128)(2,1)S(1)}, u32[]{:S(2)}, u32[]{:S(2)}) collective-permute-start(bf16[4,256,128]{2,1,0:T(8,128)(2,1)S(1)} %get-tuple-element.41), channel_id=1, source_target_pairs={{0,8},{8,16},{16,24},{24,0},{1,9},{9,17},{17,25},{25,1},{2,10},{10... | collective-permute-start | bytes 786440 | tf_op jit(solution)/shard_map/ppermute | solution.py:27
  15.5 12.0 %collective-permute-start.4 = (bf16[4,256,128]{2,1,0:T(8,128)(2,1)S(1)}, bf16[4,256,128]{2,1,0:T(8,128)(2,1)S(1)}, u32[]{:S(2)}, u32[]{:S(2)}) collective-permute-start(bf16[4,256,128]{2,1,0:T(8,128)(2,1)S(1)} %get-tuple-element.42), channel_id=1, source_target_pairs={{0,24},{8,0},{16,8},{24,16},{1,25},{9,1},{17,9},{25,17},{2,26},{10... | collective-permute-start | bytes 786440 | tf_op jit(solution)/shard_map/ppermute | solution.py:27
  18.2 22.5 %collective-permute-start.9 = (bf16[2,64,1024]{2,1,0:T(8,128)(2,1)S(1)}, bf16[2,64,1024]{2,1,0:T(8,128)(2,1)S(1)}, u32[]{:S(2)}, u32[]{:S(2)}) collective-permute-start(bf16[2,64,1024]{2,1,0:T(8,128)(2,1)S(1)} %shard_map.115.first), channel_id=1, source_target_pairs={{0,1},{1,0},{2,3},{3,2},{4,5},{5,4},{6,7},{7,6},{8,9},{9,8},{10,11... | collective-permute-start | bytes 786440 | tf_op jit(solution)/shard_map/ppermute | solution.py:31
  27.6 13.1 %collective-permute-start.5 = (bf16[256,128]{1,0:T(8,128)(2,1)S(1)}, bf16[256,128]{1,0:T(8,128)(2,1)S(1)}, u32[]{:S(2)}, u32[]{:S(2)}) collective-permute-start(bf16[256,128]{1,0:T(8,128)(2,1)S(1)} %get-tuple-element.44), channel_id=1, source_target_pairs={{0,64},{32,96},{64,0},{96,32},{1,65},{33,97},{65,1},{97,33},{2,66}... | collective-permute-start | bytes 196616 | tf_op jit(solution)/shard_map/ppermute | solution.py:27
  34.4 8.3 %collective-permute-start.6 = (bf16[256,128]{1,0:T(8,128)(2,1)S(1)}, bf16[256,128]{1,0:T(8,128)(2,1)S(1)}, u32[]{:S(2)}, u32[]{:S(2)}) collective-permute-start(bf16[256,128]{1,0:T(8,128)(2,1)S(1)} %get-tuple-element.45), channel_id=1, source_target_pairs={{0,32},{32,64},{64,96},{96,0},{1,33},{33,65},{65,97},{97,1},{2,34}... | collective-permute-start | bytes 196616 | tf_op jit(solution)/shard_map/ppermute | solution.py:27
  35.9 6.8 %collective-permute-start.7 = (bf16[256,128]{1,0:T(8,128)(2,1)S(1)}, bf16[256,128]{1,0:T(8,128)(2,1)S(1)}, u32[]{:S(2)}, u32[]{:S(2)}) collective-permute-start(bf16[256,128]{1,0:T(8,128)(2,1)S(1)} %get-tuple-element.46), channel_id=1, source_target_pairs={{0,96},{32,0},{64,32},{96,64},{1,97},{33,1},{65,33},{97,65},{2,98}... | collective-permute-start | bytes 196616 | tf_op jit(solution)/shard_map/ppermute | solution.py:27
  42.8 32.0 %collective-permute-start.13 = (bf16[4,64,1024]{2,1,0:T(8,128)(2,1)S(1)}, bf16[4,64,1024]{2,1,0:T(8,128)(2,1)S(1)}, u32[]{:S(2)}, u32[]{:S(2)}) collective-permute-start(bf16[4,64,1024]{2,1,0:T(8,128)(2,1)S(1)} %shard_map.119.near), channel_id=1, source_target_pairs={{0,3},{1,2},{2,1},{3,0},{4,7},{5,6},{6,5},{7,4},{8,11},{9,10},{10,... | collective-permute-start | bytes 1572872 | tf_op jit(solution)/shard_map/ppermute | solution.py:31
  45.9 6.2 %collective-permute-start.10 = (bf16[256,128]{1,0:T(8,128)(2,1)S(1)}, bf16[256,128]{1,0:T(8,128)(2,1)S(1)}, u32[]{:S(2)}, u32[]{:S(2)}) collective-permute-start(bf16[256,128]{1,0:T(8,128)(2,1)S(1)} %shard_map.117), channel_id=1, source_target_pairs={{0,96},{32,0},{64,32},{96,64},{1,97},{33,1},{65,33},{97,65},{2,98}... | collective-permute-start | bytes 196616 | tf_op jit(solution)/shard_map/ppermute | solution.py:27
  48.7 8.4 %collective-permute-start.11 = (bf16[256,128]{1,0:T(8,128)(2,1)S(1)}, bf16[256,128]{1,0:T(8,128)(2,1)S(1)}, u32[]{:S(2)}, u32[]{:S(2)}) collective-permute-start(bf16[256,128]{1,0:T(8,128)(2,1)S(1)} %shard_map.117), channel_id=1, source_target_pairs={{0,64},{32,96},{64,0},{96,32},{1,65},{33,97},{65,1},{97,33},{2,66}... | collective-permute-start | bytes 196616 | tf_op jit(solution)/shard_map/ppermute | solution.py:27
  51.2 7.7 %collective-permute-start.12 = (bf16[256,128]{1,0:T(8,128)(2,1)S(1)}, bf16[256,128]{1,0:T(8,128)(2,1)S(1)}, u32[]{:S(2)}, u32[]{:S(2)}) collective-permute-start(bf16[256,128]{1,0:T(8,128)(2,1)S(1)} %shard_map.117), channel_id=1, source_target_pairs={{0,32},{32,64},{64,96},{96,0},{1,33},{33,65},{65,97},{97,1},{2,34}... | collective-permute-start | bytes 196616 | tf_op jit(solution)/shard_map/ppermute | solution.py:27
  59.0 12.1 %collective-permute-start.14 = (bf16[4,256,128]{2,1,0:T(8,128)(2,1)S(1)}, bf16[4,256,128]{2,1,0:T(8,128)(2,1)S(1)}, u32[]{:S(2)}, u32[]{:S(2)}) collective-permute-start(bf16[4,256,128]{2,1,0:T(8,128)(2,1)S(1)} %pad_maximum_fusion.u0), channel_id=1, source_target_pairs={{0,24},{8,0},{16,8},{24,16},{1,25},{9,1},{17,9},{25,17},{2,26},{10... | collective-permute-start | bytes 786440 | tf_op jit(solution)/shard_map/ppermute | solution.py:27
  61.8 10.2 %collective-permute-start.15 = (bf16[4,256,128]{2,1,0:T(8,128)(2,1)S(1)}, bf16[4,256,128]{2,1,0:T(8,128)(2,1)S(1)}, u32[]{:S(2)}, u32[]{:S(2)}) collective-permute-start(bf16[4,256,128]{2,1,0:T(8,128)(2,1)S(1)} %pad_maximum_fusion.u0), channel_id=1, source_target_pairs={{0,16},{8,24},{16,0},{24,8},{1,17},{9,25},{17,1},{25,9},{2,18},{10... | collective-permute-start | bytes 786440 | tf_op jit(solution)/shard_map/ppermute | solution.py:27
  62.6 12.1 %collective-permute-start.16 = (bf16[4,256,128]{2,1,0:T(8,128)(2,1)S(1)}, bf16[4,256,128]{2,1,0:T(8,128)(2,1)S(1)}, u32[]{:S(2)}, u32[]{:S(2)}) collective-permute-start(bf16[4,256,128]{2,1,0:T(8,128)(2,1)S(1)} %pad_maximum_fusion.u0), channel_id=1, source_target_pairs={{0,8},{8,16},{16,24},{24,0},{1,9},{9,17},{17,25},{25,1},{2,10},{10... | collective-permute-start | bytes 786440 | tf_op jit(solution)/shard_map/ppermute | solution.py:27
  75.8 1.3 %collective-permute-start.17 = (bf16[64,128]{1,0:T(8,128)(2,1)S(1)}, bf16[64,128]{1,0:T(8,128)(2,1)S(1)}, u32[]{:S(2)}, u32[]{:S(2)}) collective-permute-start(bf16[64,128]{1,0:T(8,128)(2,1)S(1)} %get-tuple-element.62), channel_id=1, source_target_pairs={{0,128},{128,0},{1,129},{129,1},{2,130},{130,2},{3,131},{131,3},{4... | collective-permute-start | bytes 49160 | tf_op jit(solution)/shard_map/ppermute | solution.py:27

commit v11 on v10

--- a/solution.py
+++ b/solution.py
@@ -98,10 +98,28 @@
     )(*args)
 
 
-def core_sum_kernel(mine, received, o0, o1, o2, o3):
-    o0[...] = mine[0].astype(F32) + received[0].astype(F32)
-    for d, out in ((1, o1), (2, o2), (3, o3)):
-        out[...] = mine[d] + received[d]
+def core_sum_kernel(mine, received, own, to_next, to_far, to_last, kept):
+    own[...] = mine[0].astype(F32) + received[0].astype(F32)
+    to_next[...] = mine[1] + received[1]
+    to_far[...] = mine[2, :2] + received[2, :2]
+    to_last[:2] = mine[3, :2] + received[3, :2]
+    to_last[2:] = mine[2, 2:] + received[2, 2:]
+    kept[...] = mine[3, 2:] + received[3, 2:]
+
+
+def relay_kernel(kept, received, out):
+    out[...] = kept[...] + received[2:]
+
+
+def split_kernel(u0, u1, u2, u3, whole, half):
+    for e, u in enumerate((u0, u1, u2, u3)):
+        whole[e] = u[...]
+    half[0] = u0[...]
+    half[1] = u1[...]
+
+
+def second_half_kernel(whole, half):
+    half[...] = whole[2:]
 
 
 def join_kernel(first, second, out):
@@ -116,9 +134,13 @@
     out[2:] = second[...]
 
 
-def x_sum_kernel(own, r1, r2, r3, o0, o1, o2, o3):
+def x_sum_kernel(own, from_last, from_far, from_next, relayed, o0, o1, o2, o3):
     for e, out in enumerate((o0, o1, o2, o3)):
-        total = own[e] + r1[e].astype(F32) + r2[e].astype(F32) + r3[e].astype(F32)
+        total = own[e] + from_last[e].astype(F32)
+        if e < 2:
+            total += from_far[e].astype(F32) + from_next[e].astype(F32)
+        else:
+            total += relayed[e - 2].astype(F32)
         out[...] = total.astype(out.dtype)
 
 
@@ -191,12 +213,13 @@
     )(lengths, queries, new_keys, cache_keys, cache_values)
 
 
-def project_kernel(place, near, far, u0, u1, u2, u3, own_ref, other_ref, rows):
+def project_kernel(place, near, far, u0, u1, u2, u2_more, u3, own_ref, other_ref, rows):
     core, high, x, y, low = (place[i] for i in range(5))
     for d, u in enumerate((u0, u1, u2, u3)):
         for e in range(4):
             block = lax.rem(high + e, 4) * 4 + lax.rem(x + d, 4)
-            rows[pl.ds(pl.multiple_of(block * 256, 256), 256), :] = u[e]
+            part = u2_more[e - 2] if d == 2 and e >= 2 else u[e]
+            rows[pl.ds(pl.multiple_of(block * 256, 256), 256), :] = part
     total = None
     for bits, piece, first in ((0, near, 0), (1, near, 2), (3, far, 0), (2, far, 2)):
         start = pl.multiple_of(jnp.bitwise_xor(y, bits) * 1024, 1024)
@@ -213,7 +236,7 @@
     places = near.shape[1]
     return pl.pallas_call(
         project_kernel,
-        in_specs=[SMEM] + [VMEM] * 6,
+        in_specs=[SMEM] + [VMEM] * 7,
         out_specs=[VMEM, VMEM],
         out_shape=[
             jax.ShapeDtypeStruct((places, HD), F32),
@@ -276,19 +299,33 @@
     received = shift(theirs, "c", 1)
     second = shift(swapped, "zl", 1)
 
-    rows = (4, 256, HD)
-    own, *sent = small_call(
-        core_sum_kernel, [(rows, F32)] + [(rows, BF16)] * 3, mine, received
-    )
-    along_x = [shift(sent[d - 1], "x", d) for d in (2, 1, 3)]
+    rows, half = (4, 256, HD), (2, 256, HD)
+    own, to_next, to_far, to_last, kept = small_call(
+        core_sum_kernel,
+        [(rows, F32), (rows, BF16), (half, BF16), (rows, BF16), (half, BF16)],
+        mine,
+        received,
+    )
+    from_next = shift(to_last, "x", -1)
+    from_far = shift(to_far, "x", 2)
+    from_last = shift(to_next, "x", 1)
+    kept, from_next, from_far = lax.optimization_barrier((kept, from_next, from_far))
+    (passed,) = small_call(relay_kernel, [(half, BF16)], kept, from_next)
+    relayed = shift(passed, "x", -1)
     (both,) = small_call(
-        join_kernel, [((2, places, D // 8), BF16)], after(swapped, own), second
+        join_kernel, [((2, places, D // 8), BF16)], after(swapped, passed), second
     )
     near = exchange(both, "y", 1)
 
     rows = (256, HD)
     own, *sent = small_call(
-        x_sum_kernel, [(rows, F32)] + [(rows, BF16)] * 3, own, *along_x
+        x_sum_kernel,
+        [(rows, F32)] + [(rows, BF16)] * 3,
+        own,
+        from_last,
+        from_far,
+        from_next,
+        relayed,
     )
     along_z = [shift(sent[e - 1], "zh", e) for e in (2, 1, 3)]
     attended_cache, fresh_weights = attend_cache(
@@ -303,9 +340,16 @@
 
     (near,) = small_call(pair_kernel, [((4, places, D // 8), BF16)], after(both, updated), near)
     far = exchange(near, "y", 3)
-    gathered = jnp.stack([updated] + [shift(updated, "zh", -e) for e in (1, 2, 3)])
-    gathered, gradient = lax.optimization_barrier((gathered, gradient))
-    gathered = [gathered] + [shift(gathered, "x", -d) for d in (1, 2, 3)]
+    along_z = [updated] + [shift(updated, "zh", -e) for e in (1, 2, 3)]
+    along_z, gradient = lax.optimization_barrier((along_z, gradient))
+    rows = (4, 256, HD)
+    gathered, first = small_call(split_kernel, [(rows, BF16), (half, BF16)], *along_z)
+    from_next = shift(gathered, "x", -1)
+    from_far = shift(first, "x", 2)
+    from_last = shift(gathered, "x", 1)
+    (second,) = small_call(second_half_kernel, [(half, BF16)], from_next)
+    relayed = shift(second, "x", -1)
+    gathered = (gathered, from_next, from_far, relayed, from_last)
     own, other = project(place, near, far, gathered)
     new_values, attended = finish(
         own, shift(other, "c", 1), attended_cache, fresh_weights, row_count, step_count

time: 78.7 us -> 83.1 us (1.056)
  the two profiles are of different devices: /device:TPU:32 before, /device:TPU:7 now
where the time goes in v11:
time: 83.1 us; the launch traced here: 83 us
  starting transfers between devices  36.5 us (44%)
  waiting for transfers between devices  34.4 us (41%)
  Pallas kernels  11.2 us (13%)
  between operations  0.84 us (1%)
    ppermute x17, waiting for transfers between devices, shift(): return lax.ppermute(value, axis, [(i, (i + by) % n) for i in range(n)])  34.4 us
    ppermute x17, starting transfers between devices, shift(): return lax.ppermute(value, axis, [(i, (i + by) % n) for i in range(n)])  28.7 us
    pallas_call x1, Pallas kernels, partial_gradient(): pl.pallas_call(partial_kernel, in_specs=[SMEM, HBM, HBM], out_specs=[VMEM...  5.96 us
    ppermute x1, starting transfers between devices, swap_cores(): return lax.ppermute(value, ('c', 'zl'), pairs)  4.24 us
    ppermute x2, starting transfers between devices, exchange(): return lax.ppermute(value, axis, [(i, i ^ bit) for i in range(SIZES[axis])])  3.55 us
    pallas_call x1, Pallas kernels, attend_cache(): pl.pallas_call(attend_kernel, in_specs=[SMEM] + [VMEM] * 4, out_specs=[VM...  2.13 us
  transfers between devices with their start and end apart: 20, of which 12 were waited for; matrix products, arithmetic and copies ran while one was open for 0% of the time, Pallas kernels for 11%

profile of v11, /device:TPU:7, one launch (start us, length us, event | category | flops | bytes accessed | tf_op | source)
XLA Modules:
  0.0 83.0 jit_solution(1252584328119909488)
XLA Ops:
  0.7 4.2 %collective-permute-start = (bf16[16,4,1024]{2,1,0:T(4,128)(2,1)}, bf16[16,4,1024]{2,1,0:T(4,128)(2,1)S(1)}, u32[]{:S(2)}, u32[]{:S(2)}) collective-permute-start(bf16[16,4,1024]{2,1,0:T(4,128)(2,1)} %param.12), channel_id=1, source_target_pairs={{0,0},{4,128},{128,4},{132,132},{1,1},{5,129},{129,5},{133,133},{2... | collective-permute-start | bytes 393224 | tf_op jit(solution)/shard_map/ppermute | solution.py:36
  5.0 6.0 %shard_map.112 = (bf16[4,4,256,128]{3,2,1,0:T(8,128)(2,1)S(1)}, bf16[4,4,256,128]{3,2,1,0:T(8,128)(2,1)S(1)}) custom-call(s32[5]{0:T(128)S(1)} %stack.23.place, bf16[768,8192]{1,0:T(8,128)(2,1)} %x_hbm.1, bf16[768,128]{1,0:T(8,128)(2,1)} %v_hbm.1), custom_call_target="tpu_custom_call" | custom-call | flops 1610612736 | bytes 12582912 | tf_op jit(solution)/shard_map/pallas_call | solution.py:71
  11.1 2.6 %collective-permute-done.1.received = bf16[4,4,256,128]{3,2,1,0:T(8,128)(2,1)S(1)} collective-permute-done((bf16[4,4,256,128]{3,2,1,0:T(8,128)(2,1)S(1)}, bf16[4,4,256,128]{3,2,1,0:T(8,128)(2,1)S(1)}, u32[]{:S(2)}, u32[]{:S(2)}) %collective-permute-start.1) | collective-permute-done | bytes 1048608 | tf_op jit(solution)/shard_map/ppermute | solution.py:27
  15.4 1.8 %collective-permute-start.2 = (bf16[4,256,128]{2,1,0:T(8,128)(2,1)S(1)}, bf16[4,256,128]{2,1,0:T(8,128)(2,1)S(1)}, u32[]{:S(2)}, u32[]{:S(2)}) collective-permute-start(bf16[4,256,128]{2,1,0:T(8,128)(2,1)S(1)} %get-tuple-element.49), channel_id=1, source_target_pairs={{0,8},{8,16},{16,24},{24,0},{1,9},{9,17},{17,25},{25,1},{2,10},{10... | collective-permute-start | bytes 786440 | tf_op jit(solution)/shard_map/ppermute | solution.py:27
  17.2 7.3 %collective-permute-done.4.from_far = bf16[2,256,128]{2,1,0:T(8,128)(2,1)S(1)} collective-permute-done((bf16[2,256,128]{2,1,0:T(8,128)(2,1)S(1)}, bf16[2,256,128]{2,1,0:T(8,128)(2,1)S(1)}, u32[]{:S(2)}, u32[]{:S(2)}) %collective-permute-start.4) | collective-permute-done | bytes 131104 | tf_op jit(solution)/shard_map/ppermute | solution.py:27
  24.6 1.3 %collective-permute-done.3.received.from_next = bf16[4,256,128]{2,1,0:T(8,128)(2,1)S(1)} collective-permute-done((bf16[4,256,128]{2,1,0:T(8,128)(2,1)S(1)}, bf16[4,256,128]{2,1,0:T(8,128)(2,1)S(1)}, u32[]{:S(2)}, u32[]{:S(2)}) %collective-permute-start.3) | collective-permute-done | bytes 262176 | tf_op jit(solution)/shard_map/ppermute | solution.py:27
  26.0 1.4 %collective-permute-start.10 = (bf16[2,64,1024]{2,1,0:T(8,128)(2,1)S(1)}, bf16[2,64,1024]{2,1,0:T(8,128)(2,1)S(1)}, u32[]{:S(2)}, u32[]{:S(2)}) collective-permute-start(bf16[2,64,1024]{2,1,0:T(8,128)(2,1)S(1)} %shard_map.116.first), channel_id=1, source_target_pairs={{0,1},{1,0},{2,3},{3,2},{4,5},{5,4},{6,7},{7,6},{8,9},{9,8},{10,11... | collective-permute-start | bytes 786440 | tf_op jit(solution)/shard_map/ppermute | solution.py:31
  27.3 5.0 %collective-permute-done.5.relayed = bf16[2,256,128]{2,1,0:T(8,128)(2,1)S(1)} collective-permute-done((bf16[2,256,128]{2,1,0:T(8,128)(2,1)S(1)}, bf16[2,256,128]{2,1,0:T(8,128)(2,1)S(1)}, u32[]{:S(2)}, u32[]{:S(2)}) %collective-permute-start.5) | collective-permute-done | bytes 131104 | tf_op jit(solution)/shard_map/ppermute | solution.py:27
  32.5 6.1 %collective-permute-start.6 = (bf16[256,128]{1,0:T(8,128)(2,1)S(1)}, bf16[256,128]{1,0:T(8,128)(2,1)S(1)}, u32[]{:S(2)}, u32[]{:S(2)}) collective-permute-start(bf16[256,128]{1,0:T(8,128)(2,1)S(1)} %get-tuple-element.57), channel_id=1, source_target_pairs={{0,64},{32,96},{64,0},{96,32},{1,65},{33,97},{65,1},{97,33},{2,66}... | collective-permute-start | bytes 196616 | tf_op jit(solution)/shard_map/ppermute | solution.py:27
  38.6 1.2 %collective-permute-start.7 = (bf16[256,128]{1,0:T(8,128)(2,1)S(1)}, bf16[256,128]{1,0:T(8,128)(2,1)S(1)}, u32[]{:S(2)}, u32[]{:S(2)}) collective-permute-start(bf16[256,128]{1,0:T(8,128)(2,1)S(1)} %get-tuple-element.58), channel_id=1, source_target_pairs={{0,32},{32,64},{64,96},{96,0},{1,33},{33,65},{65,97},{97,1},{2,34}... | collective-permute-start | bytes 196616 | tf_op jit(solution)/shard_map/ppermute | solution.py:27
  39.8 2.4 %collective-permute-start.8 = (bf16[256,128]{1,0:T(8,128)(2,1)S(1)}, bf16[256,128]{1,0:T(8,128)(2,1)S(1)}, u32[]{:S(2)}, u32[]{:S(2)}) collective-permute-start(bf16[256,128]{1,0:T(8,128)(2,1)S(1)} %get-tuple-element.59), channel_id=1, source_target_pairs={{0,96},{32,0},{64,32},{96,64},{1,97},{33,1},{65,33},{97,65},{2,98}... | collective-permute-start | bytes 196616 | tf_op jit(solution)/shard_map/ppermute | solution.py:27
  42.2 2.1 %shard_map.117 = (f32[512,128]{1,0:T(8,128)S(1)}, bf16[512,64]{1,0:T(8,128)(2,1)S(1)}) custom-call(s32[16]{0:T(128)S(1)} %copy-done.5, bf16[16,4,1024]{2,1,0:T(4,128)(2,1)S(1)} %copy-done.2, bf16[64,128]{1,0:T(8,128)(2,1)S(1)} %bitcast.6, bf16[16,128,128]{2,1,0:T(8,128)(2,1)S(1)} %copy-done, bf16[16,128,128]{2,1,0:T(8,128)(2,1)S(1)} %copy-done.1), custom_call_target="tpu_custom_call" | custom-call | flops 1048576 | bytes 262144 | tf_op jit(solution)/shard_map/pallas_call | solution.py:200
  45.1 2.2 %collective-permute-start.14 = (bf16[4,64,1024]{2,1,0:T(8,128)(2,1)S(1)}, bf16[4,64,1024]{2,1,0:T(8,128)(2,1)S(1)}, u32[]{:S(2)}, u32[]{:S(2)}) collective-permute-start(bf16[4,64,1024]{2,1,0:T(8,128)(2,1)S(1)} %shard_map.120.near), channel_id=1, source_target_pairs={{0,3},{1,2},{2,1},{3,0},{4,7},{5,6},{6,5},{7,4},{8,11},{9,10},{10,... | collective-permute-start | bytes 1572872 | tf_op jit(solution)/shard_map/ppermute | solution.py:31
  47.2 3.7 %collective-permute-start.11 = (bf16[256,128]{1,0:T(8,128)(2,1)S(1)}, bf16[256,128]{1,0:T(8,128)(2,1)S(1)}, u32[]{:S(2)}, u32[]{:S(2)}) collective-permute-start(bf16[256,128]{1,0:T(8,128)(2,1)S(1)} %shard_map.118.u0), channel_id=1, source_target_pairs={{0,96},{32,0},{64,32},{96,64},{1,97},{33,1},{65,33},{97,65},{2,98}... | collective-permute-start | bytes 196616 | tf_op jit(solution)/shard_map/ppermute | solution.py:27
  50.9 0.9 %collective-permute-start.12 = (bf16[256,128]{1,0:T(8,128)(2,1)S(1)}, bf16[256,128]{1,0:T(8,128)(2,1)S(1)}, u32[]{:S(2)}, u32[]{:S(2)}) collective-permute-start(bf16[256,128]{1,0:T(8,128)(2,1)S(1)} %shard_map.118.u0), channel_id=1, source_target_pairs={{0,64},{32,96},{64,0},{96,32},{1,65},{33,97},{65,1},{97,33},{2,66}... | collective-permute-start | bytes 196616 | tf_op jit(solution)/shard_map/ppermute | solution.py:27
  51.9 1.1 %collective-permute-start.13 = (bf16[256,128]{1,0:T(8,128)(2,1)S(1)}, bf16[256,128]{1,0:T(8,128)(2,1)S(1)}, u32[]{:S(2)}, u32[]{:S(2)}) collective-permute-start(bf16[256,128]{1,0:T(8,128)(2,1)S(1)} %shard_map.118.u0), channel_id=1, source_target_pairs={{0,32},{32,64},{64,96},{96,0},{1,33},{33,65},{65,97},{97,1},{2,34}... | collective-permute-start | bytes 196616 | tf_op jit(solution)/shard_map/ppermute | solution.py:27
  53.9 4.5 %collective-permute-done.12.u2 = bf16[256,128]{1,0:T(8,128)(2,1)S(1)} collective-permute-done((bf16[256,128]{1,0:T(8,128)(2,1)S(1)}, bf16[256,128]{1,0:T(8,128)(2,1)S(1)}, u32[]{:S(2)}, u32[]{:S(2)}) %collective-permute-start.12) | collective-permute-done | bytes 65568 | tf_op jit(solution)/shard_map/ppermute | solution.py:27
  58.6 2.7 %collective-permute-start.18 = (bf16[4,256,128]{2,1,0:T(8,128)(2,1)S(1)}, bf16[4,256,128]{2,1,0:T(8,128)(2,1)S(1)}, u32[]{:S(2)}, u32[]{:S(2)}) collective-permute-start(bf16[4,256,128]{2,1,0:T(8,128)(2,1)S(1)} %get-tuple-element.77.u0), channel_id=1, source_target_pairs={{0,8},{8,16},{16,24},{24,0},{1,9},{9,17},{17,25},{25,1},{2,10},{10... | collective-permute-start | bytes 786440 | tf_op jit(solution)/shard_map/ppermute | solution.py:27
  61.3 3.8 %collective-permute-done.15.whole.u1 = bf16[4,256,128]{2,1,0:T(8,128)(2,1)S(1)} collective-permute-done((bf16[4,256,128]{2,1,0:T(8,128)(2,1)S(1)}, bf16[4,256,128]{2,1,0:T(8,128)(2,1)S(1)}, u32[]{:S(2)}, u32[]{:S(2)}) %collective-permute-start.15) | collective-permute-done | bytes 262176 | tf_op jit(solution)/shard_map/ppermute | solution.py:27
  65.1 2.6 %collective-permute-done.16.u2 = bf16[2,256,128]{2,1,0:T(8,128)(2,1)S(1)} collective-permute-done((bf16[2,256,128]{2,1,0:T(8,128)(2,1)S(1)}, bf16[2,256,128]{2,1,0:T(8,128)(2,1)S(1)}, u32[]{:S(2)}, u32[]{:S(2)}) %collective-permute-start.16) | collective-permute-done | bytes 131104 | tf_op jit(solution)/shard_map/ppermute | solution.py:27
  67.7 5.6 %collective-permute-done.17.u2_more = bf16[2,256,128]{2,1,0:T(8,128)(2,1)S(1)} collective-permute-done((bf16[2,256,128]{2,1,0:T(8,128)(2,1)S(1)}, bf16[2,256,128]{2,1,0:T(8,128)(2,1)S(1)}, u32[]{:S(2)}, u32[]{:S(2)}) %collective-permute-start.17) | collective-permute-done | bytes 131104 | tf_op jit(solution)/shard_map/ppermute | solution.py:27
  73.3 1.1 %shard_map.123 = (f32[64,128]{1,0:T(8,128)S(1)}, bf16[64,128]{1,0:T(8,128)(2,1)S(1)}) custom-call(s32[5]{0:T(128)S(1)} %stack.23.place, bf16[4,64,1024]{2,1,0:T(8,128)(2,1)S(1)} %shard_map.120.near, bf16[4,64,1024]{2,1,0:T(8,128)(2,1)S(1)} %collective-permute-done.14.far, bf16[4,256,128]{2,1,0:T(8,128)(2,1)S(1)} %get-tuple-element.77.u0, ...), custom_call_target="tpu_custom_call" | custom-call | flops 134217728 | bytes 2097152 | tf_op jit(solution)/shard_map/pallas_call | solution.py:237
  74.3 7.0 %collective-permute-start.19 = (bf16[64,128]{1,0:T(8,128)(2,1)S(1)}, bf16[64,128]{1,0:T(8,128)(2,1)S(1)}, u32[]{:S(2)}, u32[]{:S(2)}) collective-permute-start(bf16[64,128]{1,0:T(8,128)(2,1)S(1)} %get-tuple-element.80), channel_id=1, source_target_pairs={{0,128},{128,0},{1,129},{129,1},{2,130},{130,2},{3,131},{131,3},{4... | collective-permute-start | bytes 49160 | tf_op jit(solution)/shard_map/ppermute | solution.py:27
  81.3 0.8 %collective-permute-done.19.received = bf16[64,128]{1,0:T(8,128)(2,1)S(1)} collective-permute-done((bf16[64,128]{1,0:T(8,128)(2,1)S(1)}, bf16[64,128]{1,0:T(8,128)(2,1)S(1)}, u32[]{:S(2)}, u32[]{:S(2)}) %collective-permute-start.19) | collective-permute-done | bytes 16416 | tf_op jit(solution)/shard_map/ppermute | solution.py:27
  (42 shorter events, 4.8 us)
Async XLA Ops:
  0.6 41.5 %copy-start.2 = (bf16[16,4,1024]{2,1,0:T(4,128)(2,1)S(1)}, bf16[16,4,1024]{2,1,0:T(4,128)(2,1)}, u32[]{:S(2)}) copy-start(bf16[16,4,1024]{2,1,0:T(4,128)(2,1)} %raw_queries) | copy-start | bytes 393220
  0.6 41.5 %copy-start.4 = (bf16[16,4,128]{2,1,0:T(4,128)(2,1)S(1)}, bf16[16,4,128]{2,1,0:T(4,128)(2,1)}, u32[]{:S(2)}) copy-start(bf16[16,4,128]{2,1,0:T(4,128)(2,1)} %param.14) | copy-start | bytes 49156
  0.7 41.5 %copy-start = (bf16[16,128,128]{2,1,0:T(8,128)(2,1)S(1)}, bf16[16,128,128]{2,1,0:T(8,128)(2,1)}, u32[]{:S(2)}) copy-start(bf16[16,128,128]{2,1,0:T(8,128)(2,1)} %cache_keys.1) | copy-start | bytes 1572868
  0.7 44.3 %copy-start.3 = (bf16[256,128]{1,0:T(8,128)(2,1)S(1)}, bf16[256,128]{1,0:T(8,128)(2,1)}, u32[]{:S(2)}) copy-start(bf16[256,128]{1,0:T(8,128)(2,1)} %weight.1) | copy-start | bytes 196612
  0.7 10.3 %collective-permute-start = (bf16[16,4,1024]{2,1,0:T(4,128)(2,1)}, bf16[16,4,1024]{2,1,0:T(4,128)(2,1)S(1)}, u32[]{:S(2)}, u32[]{:S(2)}) collective-permute-start(bf16[16,4,1024]{2,1,0:T(4,128)(2,1)} %param.12), channel_id=1, source_target_pairs={{0,0},{4,128},{128,4},{132,132},{1,1},{5,129},{129,5},{133,133},{2... | collective-permute-start | bytes 393224 | tf_op jit(solution)/shard_map/ppermute | solution.py:36
  11.0 2.7 %collective-permute-start.1 = (bf16[4,4,256,128]{3,2,1,0:T(8,128)(2,1)S(1)}, bf16[4,4,256,128]{3,2,1,0:T(8,128)(2,1)S(1)}, u32[]{:S(2)}, u32[]{:S(2)}) collective-permute-start(bf16[4,4,256,128]{3,2,1,0:T(8,128)(2,1)S(1)} %get-tuple-element.47), channel_id=1, source_target_pairs={{0,128},{128,0},{1,129},{129,1},{2,130},{130,2},{3,131},{131,3},{4... | collective-permute-start | bytes 3145736 | tf_op jit(solution)/shard_map/ppermute | solution.py:27
  14.0 11.9 %collective-permute-start.3 = (bf16[4,256,128]{2,1,0:T(8,128)(2,1)S(1)}, bf16[4,256,128]{2,1,0:T(8,128)(2,1)S(1)}, u32[]{:S(2)}, u32[]{:S(2)}) collective-permute-start(bf16[4,256,128]{2,1,0:T(8,128)(2,1)S(1)} %get-tuple-element.51), channel_id=1, source_target_pairs={{0,24},{8,0},{16,8},{24,16},{1,25},{9,1},{17,9},{25,17},{2,26},{10... | collective-permute-start | bytes 786440 | tf_op jit(solution)/shard_map/ppermute | solution.py:27
  14.6 10.0 %collective-permute-start.4 = (bf16[2,256,128]{2,1,0:T(8,128)(2,1)S(1)}, bf16[2,256,128]{2,1,0:T(8,128)(2,1)S(1)}, u32[]{:S(2)}, u32[]{:S(2)}) collective-permute-start(bf16[2,256,128]{2,1,0:T(8,128)(2,1)S(1)} %get-tuple-element.52), channel_id=1, source_target_pairs={{0,16},{8,24},{16,0},{24,8},{1,17},{9,25},{17,1},{25,9},{2,18},{10... | collective-permute-start | bytes 393224 | tf_op jit(solution)/shard_map/ppermute | solution.py:27
  15.4 10.4 %collective-permute-start.9 = (bf16[16,4,1024]{2,1,0:T(4,128)(2,1)S(1)}, bf16[16,4,1024]{2,1,0:T(4,128)(2,1)S(1)}, u32[]{:S(2)}, u32[]{:S(2)}) collective-permute-start(bf16[16,4,1024]{2,1,0:T(4,128)(2,1)S(1)} %collective-permute-done.first), channel_id=1, source_target_pairs={{0,4},{4,0},{1,5},{5,1},{2,6},{6,2},{3,7},{7,3},{8,12},{12,8},{9,1... | collective-permute-start | bytes 393224 | tf_op jit(solution)/shard_map/ppermute | solution.py:27
  15.4 11.9 %collective-permute-start.2 = (bf16[4,256,128]{2,1,0:T(8,128)(2,1)S(1)}, bf16[4,256,128]{2,1,0:T(8,128)(2,1)S(1)}, u32[]{:S(2)}, u32[]{:S(2)}) collective-permute-start(bf16[4,256,128]{2,1,0:T(8,128)(2,1)S(1)} %get-tuple-element.49), channel_id=1, source_target_pairs={{0,8},{8,16},{16,24},{24,0},{1,9},{9,17},{17,25},{25,1},{2,10},{10... | collective-permute-start | bytes 786440 | tf_op jit(solution)/shard_map/ppermute | solution.py:27
  26.0 19.0 %collective-permute-start.10 = (bf16[2,64,1024]{2,1,0:T(8,128)(2,1)S(1)}, bf16[2,64,1024]{2,1,0:T(8,128)(2,1)S(1)}, u32[]{:S(2)}, u32[]{:S(2)}) collective-permute-start(bf16[2,64,1024]{2,1,0:T(8,128)(2,1)S(1)} %shard_map.116.first), channel_id=1, source_target_pairs={{0,1},{1,0},{2,3},{3,2},{4,5},{5,4},{6,7},{7,6},{8,9},{9,8},{10,11... | collective-permute-start | bytes 786440 | tf_op jit(solution)/shard_map/ppermute | solution.py:31
  27.3 5.0 %collective-permute-start.5 = (bf16[2,256,128]{2,1,0:T(8,128)(2,1)S(1)}, bf16[2,256,128]{2,1,0:T(8,128)(2,1)S(1)}, u32[]{:S(2)}, u32[]{:S(2)}) collective-permute-start(bf16[2,256,128]{2,1,0:T(8,128)(2,1)S(1)} %shard_map.114), channel_id=1, source_target_pairs={{0,24},{8,0},{16,8},{24,16},{1,25},{9,1},{17,9},{25,17},{2,26},{10... | collective-permute-start | bytes 393224 | tf_op jit(solution)/shard_map/ppermute | solution.py:27
  32.5 11.8 %collective-permute-start.6 = (bf16[256,128]{1,0:T(8,128)(2,1)S(1)}, bf16[256,128]{1,0:T(8,128)(2,1)S(1)}, u32[]{:S(2)}, u32[]{:S(2)}) collective-permute-start(bf16[256,128]{1,0:T(8,128)(2,1)S(1)} %get-tuple-element.57), channel_id=1, source_target_pairs={{0,64},{32,96},{64,0},{96,32},{1,65},{33,97},{65,1},{97,33},{2,66}... | collective-permute-start | bytes 196616 | tf_op jit(solution)/shard_map/ppermute | solution.py:27
  38.6 6.1 %collective-permute-start.7 = (bf16[256,128]{1,0:T(8,128)(2,1)S(1)}, bf16[256,128]{1,0:T(8,128)(2,1)S(1)}, u32[]{:S(2)}, u32[]{:S(2)}) collective-permute-start(bf16[256,128]{1,0:T(8,128)(2,1)S(1)} %get-tuple-element.58), channel_id=1, source_target_pairs={{0,32},{32,64},{64,96},{96,0},{1,33},{33,65},{65,97},{97,1},{2,34}... | collective-permute-start | bytes 196616 | tf_op jit(solution)/shard_map/ppermute | solution.py:27
  39.8 5.2 %collective-permute-start.8 = (bf16[256,128]{1,0:T(8,128)(2,1)S(1)}, bf16[256,128]{1,0:T(8,128)(2,1)S(1)}, u32[]{:S(2)}, u32[]{:S(2)}) collective-permute-start(bf16[256,128]{1,0:T(8,128)(2,1)S(1)} %get-tuple-element.59), channel_id=1, source_target_pairs={{0,96},{32,0},{64,32},{96,64},{1,97},{33,1},{65,33},{97,65},{2,98}... | collective-permute-start | bytes 196616 | tf_op jit(solution)/shard_map/ppermute | solution.py:27
  45.1 28.2 %collective-permute-start.14 = (bf16[4,64,1024]{2,1,0:T(8,128)(2,1)S(1)}, bf16[4,64,1024]{2,1,0:T(8,128)(2,1)S(1)}, u32[]{:S(2)}, u32[]{:S(2)}) collective-permute-start(bf16[4,64,1024]{2,1,0:T(8,128)(2,1)S(1)} %shard_map.120.near), channel_id=1, source_target_pairs={{0,3},{1,2},{2,1},{3,0},{4,7},{5,6},{6,5},{7,4},{8,11},{9,10},{10,... | collective-permute-start | bytes 1572872 | tf_op jit(solution)/shard_map/ppermute | solution.py:31
  47.2 6.7 %collective-permute-start.11 = (bf16[256,128]{1,0:T(8,128)(2,1)S(1)}, bf16[256,128]{1,0:T(8,128)(2,1)S(1)}, u32[]{:S(2)}, u32[]{:S(2)}) collective-permute-start(bf16[256,128]{1,0:T(8,128)(2,1)S(1)} %shard_map.118.u0), channel_id=1, source_target_pairs={{0,96},{32,0},{64,32},{96,64},{1,97},{33,1},{65,33},{97,65},{2,98}... | collective-permute-start | bytes 196616 | tf_op jit(solution)/shard_map/ppermute | solution.py:27
  50.9 7.5 %collective-permute-start.12 = (bf16[256,128]{1,0:T(8,128)(2,1)S(1)}, bf16[256,128]{1,0:T(8,128)(2,1)S(1)}, u32[]{:S(2)}, u32[]{:S(2)}) collective-permute-start(bf16[256,128]{1,0:T(8,128)(2,1)S(1)} %shard_map.118.u0), channel_id=1, source_target_pairs={{0,64},{32,96},{64,0},{96,32},{1,65},{33,97},{65,1},{97,33},{2,66}... | collective-permute-start | bytes 196616 | tf_op jit(solution)/shard_map/ppermute | solution.py:27
  51.9 6.6 %collective-permute-start.13 = (bf16[256,128]{1,0:T(8,128)(2,1)S(1)}, bf16[256,128]{1,0:T(8,128)(2,1)S(1)}, u32[]{:S(2)}, u32[]{:S(2)}) collective-permute-start(bf16[256,128]{1,0:T(8,128)(2,1)S(1)} %shard_map.118.u0), channel_id=1, source_target_pairs={{0,32},{32,64},{64,96},{96,0},{1,33},{33,65},{65,97},{97,1},{2,34}... | collective-permute-start | bytes 196616 | tf_op jit(solution)/shard_map/ppermute | solution.py:27
  58.5 6.5 %collective-permute-start.15 = (bf16[4,256,128]{2,1,0:T(8,128)(2,1)S(1)}, bf16[4,256,128]{2,1,0:T(8,128)(2,1)S(1)}, u32[]{:S(2)}, u32[]{:S(2)}) collective-permute-start(bf16[4,256,128]{2,1,0:T(8,128)(2,1)S(1)} %get-tuple-element.77.u0), channel_id=1, source_target_pairs={{0,24},{8,0},{16,8},{24,16},{1,25},{9,1},{17,9},{25,17},{2,26},{10... | collective-permute-start | bytes 786440 | tf_op jit(solution)/shard_map/ppermute | solution.py:27
  58.6 9.1 %collective-permute-start.18 = (bf16[4,256,128]{2,1,0:T(8,128)(2,1)S(1)}, bf16[4,256,128]{2,1,0:T(8,128)(2,1)S(1)}, u32[]{:S(2)}, u32[]{:S(2)}) collective-permute-start(bf16[4,256,128]{2,1,0:T(8,128)(2,1)S(1)} %get-tuple-element.77.u0), channel_id=1, source_target_pairs={{0,8},{8,16},{16,24},{24,0},{1,9},{9,17},{17,25},{25,1},{2,10},{10... | collective-permute-start | bytes 786440 | tf_op jit(solution)/shard_map/ppermute | solution.py:27
  61.3 6.4 %collective-permute-start.16 = (bf16[2,256,128]{2,1,0:T(8,128)(2,1)S(1)}, bf16[2,256,128]{2,1,0:T(8,128)(2,1)S(1)}, u32[]{:S(2)}, u32[]{:S(2)}) collective-permute-start(bf16[2,256,128]{2,1,0:T(8,128)(2,1)S(1)} %get-tuple-element.78), channel_id=1, source_target_pairs={{0,16},{8,24},{16,0},{24,8},{1,17},{9,25},{17,1},{25,9},{2,18},{10... | collective-permute-start | bytes 393224 | tf_op jit(solution)/shard_map/ppermute | solution.py:27
  65.0 8.2 %collective-permute-start.17 = (bf16[2,256,128]{2,1,0:T(8,128)(2,1)S(1)}, bf16[2,256,128]{2,1,0:T(8,128)(2,1)S(1)}, u32[]{:S(2)}, u32[]{:S(2)}) collective-permute-start(bf16[2,256,128]{2,1,0:T(8,128)(2,1)S(1)} %shard_map.122), channel_id=1, source_target_pairs={{0,24},{8,0},{16,8},{24,16},{1,25},{9,1},{17,9},{25,17},{2,26},{10... | collective-permute-start | bytes 393224 | tf_op jit(solution)/shard_map/ppermute | solution.py:27
  74.3 7.9 %collective-permute-start.19 = (bf16[64,128]{1,0:T(8,128)(2,1)S(1)}, bf16[64,128]{1,0:T(8,128)(2,1)S(1)}, u32[]{:S(2)}, u32[]{:S(2)}) collective-permute-start(bf16[64,128]{1,0:T(8,128)(2,1)S(1)} %get-tuple-element.80), channel_id=1, source_target_pairs={{0,128},{128,0},{1,129},{129,1},{2,130},{130,2},{3,131},{131,3},{4... | collective-permute-start | bytes 49160 | tf_op jit(solution)/shard_map/ppermute | solution.py:27
  (2 other events, 83.0 us)

commit v12 on v9

--- a/solution.py
+++ b/solution.py
@@ -135,12 +135,16 @@
     gradient[...] = total_of(own, r1, r2, r3)
 
 
-def attend_kernel(lengths, queries, new_keys, cache_keys, cache_values, mixed_ref, weights_ref):
+def attend_kernel(
+    lengths, raw_queries, new_keys, cache_keys, cache_values, mixed_ref, weights_ref, queries
+):
     rows = cache_keys.shape[0]
     slots = cache_keys.shape[1]
-    steps = queries.shape[0] // rows
-    every = HEADS * queries.shape[0]
+    steps = raw_queries.shape[1]
+    every = HEADS * rows * steps
     factor = 1.0 / math.sqrt(HD)
+    for r in range(rows):
+        queries[r * steps : (r + 1) * steps] = raw_queries[r]
     heads = jnp.concatenate([queries[:, q * HD : (q + 1) * HD] for q in range(HEADS)], axis=0)
     place = lax.broadcasted_iota(jnp.int32, (every, slots), 0) % (rows * steps)
     lane = lax.broadcasted_iota(jnp.int32, (every, slots), 1)
@@ -170,7 +174,7 @@
 
 
 def attend_cache(lengths, queries, new_keys, cache_keys, cache_values):
-    places = queries.shape[0]
+    places = queries.shape[0] * queries.shape[1]
     return pl.pallas_call(
         attend_kernel,
         in_specs=[SMEM] + [VMEM] * 4,
@@ -179,6 +183,7 @@
             jax.ShapeDtypeStruct((HEADS * places, HD), F32),
             jax.ShapeDtypeStruct((HEADS * places, places), BF16),
         ],
+        scratch_shapes=[pltpu.VMEM((places, HEADS * HD), BF16)],
         compiler_params=pltpu.CompilerParams(vmem_limit_bytes=16 * MIB),
         cost_estimate=pl.CostEstimate(
             flops=MIB, bytes_accessed=MIB // 4, transcendentals=0
@@ -279,11 +284,9 @@
     places = row_count * step_count
     place = jnp.stack([core, high, x, y, low])
 
-    swapped = swap_high(decode_inputs)
     theirs, mine = partial_gradient(place, normed_inputs, value_cotangent)
-    theirs, mine, swapped = lax.optimization_barrier((theirs, mine, swapped))
     received = shift(theirs, "c", 1)
-    second = shift(swapped, "zl", 1)
+    swapped = swap_high(after(decode_inputs, theirs))
 
     rows = (4, 256, HD)
     own, *sent = small_call(
@@ -291,33 +294,31 @@
     )
     along_x = [shift(sent[d - 1], "x", d) for d in (2, 1, 3)]
     attended_cache, fresh_weights = attend_cache(
-        lengths,
-        after(queries.reshape(places, -1), own),
-        new_keys.reshape(places, HD),
-        cache_keys,
-        cache_values,
-    )
+        lengths, after(queries, own), new_keys.reshape(places, HD), cache_keys, cache_values
+    )
+    swapped = after(swapped, own)
     (both,) = small_call(
-        join_kernel, [((2, places, D // 8), BF16)], after(swapped, own), second
-    )
-    near = exchange(both, "y", 1)
-
-    own, *along_x, attended_cache, fresh_weights = lax.optimization_barrier(
-        (own, *along_x, attended_cache, fresh_weights)
+        join_kernel, [((2, places, D // 8), BF16)], swapped, shift(swapped, "zl", 1)
+    )
+    own, *along_x, both, attended_cache, fresh_weights = lax.optimization_barrier(
+        (own, *along_x, both, attended_cache, fresh_weights)
     )
     rows = (256, HD)
     own, *sent = small_call(
         x_sum_kernel, [(rows, F32)] + [(rows, BF16)] * 3, own, *along_x
     )
-    (near,) = small_call(pair_kernel, [((4, places, D // 8), BF16)], after(both, own), near)
-    far = exchange(near, "y", 3)
     along_z = [shift(sent[e - 1], "zh", e) for e in (2, 1, 3)]
+    both = after(both, own)
+    near = exchange(both, "y", 1)
+    own, *along_z, near = lax.optimization_barrier((own, *along_z, near))
     (updated,) = small_call(update_kernel, [(rows, BF16)], value_weight, own, *along_z)
     own = after(own, updated)
     (gradient,) = small_call(gradient_kernel, [(rows, F32)], own, *along_z, keep=False)
 
+    (near,) = small_call(pair_kernel, [((4, places, D // 8), BF16)], after(both, updated), near)
+    far = exchange(near, "y", 3)
     gathered = jnp.stack([updated] + [shift(updated, "x", -d) for d in (1, 2, 3)])
-    gathered, gradient, far = lax.optimization_barrier((gathered, gradient, far))
+    gathered, gradient = lax.optimization_barrier((gathered, gradient))
     other = shift(gathered, "c", 1)
     partial = project(
         project_own_kernel, pltpu.VMEM((2 * places, HD), F32), 1, place, near, gathered

time: 78.7 us -> 73.3 us (0.931)
  starting transfers between devices: 39.8 us -> 28.3 us
  waiting for transfers between devices: 13.3 us -> 19 us
  Pallas kernels: 12.6 us -> 11.8 us
    ppermute x2, starting transfers between devices: 16 us -> 6.84 us  [exchange(): return lax.ppermute(value, axis, [(i, i ^ bit) for i in range(SIZES[axis])])]
    ppermute x12, waiting for transfers between devices: 9.94 us -> 17.1 us  [shift(): return lax.ppermute(value, axis, [(i, (i + by) % n) for i in range(n)])]
    ppermute x2, waiting for transfers between devices: 3.41 us -> 1.9 us  [exchange(): return lax.ppermute(value, axis, [(i, i ^ bit) for i in range(SIZES[axis])])]
    ppermute x12, starting transfers between devices: 22.1 us -> 20.8 us  [shift(): return lax.ppermute(value, axis, [(i, (i + by) % n) for i in range(n)])]
    ppermute x1, starting transfers between devices: 1.69 us -> 0.67 us  [swap_high(): return lax.ppermute(value, ('zh', 'y'), pairs)]
    pallas_call x6, Pallas kernels: 1.95 us -> 1.16 us  [small_call(): pl.pallas_call(kernel, in_specs=[VMEM] * len(args), out_specs=[VMEM] * le...]
  transfers between devices with their start and end apart: 15 -> 15, of which waited for: 7 -> 11; matrix products, arithmetic and copies ran while one was open for 0% -> 0% of each run, Pallas kernels for 14% -> 5%
where the time goes in v12:
time: 73.3 us; the launch traced here: 72.5 us
  starting transfers between devices  28.3 us (39%)
  waiting for transfers between devices  19 us (26%)
  blocking collectives  12.4 us (17%)
  Pallas kernels  11.8 us (16%)
  between operations  0.82 us (1%)
    ppermute x12, starting transfers between devices, shift(): return lax.ppermute(value, axis, [(i, (i + by) % n) for i in range(n)])  20.8 us
    ppermute x12, waiting for transfers between devices, shift(): return lax.ppermute(value, axis, [(i, (i + by) % n) for i in range(n)])  17.1 us
    all_to_all x1, blocking collectives, shards(): exchanged = lax.all_to_all(partial, 'zh', 0, 0, tiled=True)  12.4 us
    ppermute x2, starting transfers between devices, exchange(): return lax.ppermute(value, axis, [(i, i ^ bit) for i in range(SIZES[axis])])  6.84 us
    pallas_call x1, Pallas kernels, partial_gradient(): pl.pallas_call(partial_kernel, in_specs=[SMEM, HBM, HBM], out_specs=[VMEM...  5.95 us
    pallas_call x1, Pallas kernels, attend_cache(): pl.pallas_call(attend_kernel, in_specs=[SMEM] + [VMEM] * 4, out_specs=[VM...  2.14 us
    ppermute x2, waiting for transfers between devices, exchange(): return lax.ppermute(value, axis, [(i, i ^ bit) for i in range(SIZES[axis])])  1.9 us
    pallas_call x2, Pallas kernels, project(): pl.pallas_call(kernel, in_specs=[SMEM] + [VMEM] * len(args), out_specs=VM...  1.72 us
  transfers between devices with their start and end apart: 15, of which 11 were waited for; matrix products, arithmetic and copies ran while one was open for 0% of the time, Pallas kernels for 5%

profile of v12, /device:TPU:32, one launch (start us, length us, event | category | flops | bytes accessed | tf_op | source)
XLA Modules:
  0.0 72.5 jit_solution(12230559502462009477)
XLA Ops:
  0.8 6.0 %shard_map.112 = (bf16[4,4,256,128]{3,2,1,0:T(8,128)(2,1)S(1)}, bf16[4,4,256,128]{3,2,1,0:T(8,128)(2,1)S(1)}) custom-call(s32[5]{0:T(128)S(1)} %stack.38.place, bf16[768,8192]{1,0:T(8,128)(2,1)} %x_hbm.1, bf16[768,128]{1,0:T(8,128)(2,1)} %v_hbm.1), custom_call_target="tpu_custom_call" | custom-call | flops 1610612736 | bytes 12582912 | tf_op jit(solution)/shard_map/pallas_call | solution.py:71
  7.5 2.0 %collective-permute-done.received = bf16[4,4,256,128]{3,2,1,0:T(8,128)(2,1)S(1)} collective-permute-done((bf16[4,4,256,128]{3,2,1,0:T(8,128)(2,1)S(1)}, bf16[4,4,256,128]{3,2,1,0:T(8,128)(2,1)S(1)}, u32[]{:S(2)}, u32[]{:S(2)}) %collective-permute-start) | collective-permute-done | bytes 1048608 | tf_op jit(solution)/shard_map/ppermute | solution.py:27
  9.7 3.1 %collective-permute-start.1 = (bf16[4,256,128]{2,1,0:T(8,128)(2,1)S(1)}, bf16[4,256,128]{2,1,0:T(8,128)(2,1)S(1)}, u32[]{:S(2)}, u32[]{:S(2)}) collective-permute-start(bf16[4,256,128]{2,1,0:T(8,128)(2,1)S(1)} %get-tuple-element.40), channel_id=1, source_target_pairs={{0,16},{8,24},{16,0},{24,8},{1,17},{9,25},{17,1},{25,9},{2,18},{10... | collective-permute-start | bytes 786440 | tf_op jit(solution)/shard_map/ppermute | solution.py:27
  13.4 2.6 %collective-permute-start.3 = (bf16[4,256,128]{2,1,0:T(8,128)(2,1)S(1)}, bf16[4,256,128]{2,1,0:T(8,128)(2,1)S(1)}, u32[]{:S(2)}, u32[]{:S(2)}) collective-permute-start(bf16[4,256,128]{2,1,0:T(8,128)(2,1)S(1)} %get-tuple-element.42), channel_id=1, source_target_pairs={{0,24},{8,0},{16,8},{24,16},{1,25},{9,1},{17,9},{25,17},{2,26},{10... | collective-permute-start | bytes 786440 | tf_op jit(solution)/shard_map/ppermute | solution.py:27
  16.2 2.1 %shard_map.115 = (f32[512,128]{1,0:T(8,128)S(1)}, bf16[512,64]{1,0:T(8,128)(2,1)S(1)}) custom-call(s32[16]{0:T(128)S(1)} %copy-done.5, bf16[16,4,1024]{2,1,0:T(4,128)(2,1)S(1)} %copy-done.2, bf16[64,128]{1,0:T(8,128)(2,1)S(1)} %bitcast.11, bf16[16,128,128]{2,1,0:T(8,128)(2,1)S(1)} %copy-done, bf16[16,128,128]{2,1,0:T(8,128)(2,1)S(1)} %copy-done.1), custom_call_target="tpu_custom_call" | custom-call | flops 1048576 | bytes 262144 | tf_op jit(solution)/shard_map/pallas_call | solution.py:178
  18.3 3.2 %collective-permute-done.5.second = bf16[16,4,1024]{2,1,0:T(4,128)(2,1)S(1)} collective-permute-done((bf16[16,4,1024]{2,1,0:T(4,128)(2,1)S(1)}, bf16[16,4,1024]{2,1,0:T(4,128)(2,1)S(1)}, u32[]{:S(2)}, u32[]{:S(2)}) %collective-permute-start.5) | collective-permute-done | bytes 131104 | tf_op jit(solution)/shard_map/ppermute | solution.py:27
  21.6 3.7 %collective-permute-done.2.r2 = bf16[4,256,128]{2,1,0:T(8,128)(2,1)S(1)} collective-permute-done((bf16[4,256,128]{2,1,0:T(8,128)(2,1)S(1)}, bf16[4,256,128]{2,1,0:T(8,128)(2,1)S(1)}, u32[]{:S(2)}, u32[]{:S(2)}) %collective-permute-start.2) | collective-permute-done | bytes 262176 | tf_op jit(solution)/shard_map/ppermute | solution.py:27
  25.5 4.3 %collective-permute-start.9 = (bf16[2,64,1024]{2,1,0:T(8,128)(2,1)S(1)}, bf16[2,64,1024]{2,1,0:T(8,128)(2,1)S(1)}, u32[]{:S(2)}, u32[]{:S(2)}) collective-permute-start(bf16[2,64,1024]{2,1,0:T(8,128)(2,1)S(1)} %shard_map.114.first), channel_id=1, source_target_pairs={{0,1},{1,0},{2,3},{3,2},{4,5},{5,4},{6,7},{7,6},{8,9},{9,8},{10,11... | collective-permute-start | bytes 786440 | tf_op jit(solution)/shard_map/ppermute | solution.py:31
  29.8 5.3 %collective-permute-start.6 = (bf16[256,128]{1,0:T(8,128)(2,1)S(1)}, bf16[256,128]{1,0:T(8,128)(2,1)S(1)}, u32[]{:S(2)}, u32[]{:S(2)}) collective-permute-start(bf16[256,128]{1,0:T(8,128)(2,1)S(1)} %get-tuple-element.53), channel_id=1, source_target_pairs={{0,64},{32,96},{64,0},{96,32},{1,65},{33,97},{65,1},{97,33},{2,66}... | collective-permute-start | bytes 196616 | tf_op jit(solution)/shard_map/ppermute | solution.py:27
  35.1 3.2 %collective-permute-start.7 = (bf16[256,128]{1,0:T(8,128)(2,1)S(1)}, bf16[256,128]{1,0:T(8,128)(2,1)S(1)}, u32[]{:S(2)}, u32[]{:S(2)}) collective-permute-start(bf16[256,128]{1,0:T(8,128)(2,1)S(1)} %get-tuple-element.54), channel_id=1, source_target_pairs={{0,32},{32,64},{64,96},{96,0},{1,33},{33,65},{65,97},{97,1},{2,34}... | collective-permute-start | bytes 196616 | tf_op jit(solution)/shard_map/ppermute | solution.py:27
  38.3 0.9 %collective-permute-start.8 = (bf16[256,128]{1,0:T(8,128)(2,1)S(1)}, bf16[256,128]{1,0:T(8,128)(2,1)S(1)}, u32[]{:S(2)}, u32[]{:S(2)}) collective-permute-start(bf16[256,128]{1,0:T(8,128)(2,1)S(1)} %get-tuple-element.55), channel_id=1, source_target_pairs={{0,96},{32,0},{64,32},{96,64},{1,97},{33,1},{65,33},{97,65},{2,98}... | collective-permute-start | bytes 196616 | tf_op jit(solution)/shard_map/ppermute | solution.py:27
  39.3 2.2 %collective-permute-done.7.r2 = bf16[256,128]{1,0:T(8,128)(2,1)S(1)} collective-permute-done((bf16[256,128]{1,0:T(8,128)(2,1)S(1)}, bf16[256,128]{1,0:T(8,128)(2,1)S(1)}, u32[]{:S(2)}, u32[]{:S(2)}) %collective-permute-start.7) | collective-permute-done | bytes 65568 | tf_op jit(solution)/shard_map/ppermute | solution.py:27
  41.5 2.2 %collective-permute-done.8.r3 = bf16[256,128]{1,0:T(8,128)(2,1)S(1)} collective-permute-done((bf16[256,128]{1,0:T(8,128)(2,1)S(1)}, bf16[256,128]{1,0:T(8,128)(2,1)S(1)}, u32[]{:S(2)}, u32[]{:S(2)}) %collective-permute-start.8) | collective-permute-done | bytes 65568 | tf_op jit(solution)/shard_map/ppermute | solution.py:27
  43.8 2.5 %collective-permute-start.13 = (bf16[4,64,1024]{2,1,0:T(8,128)(2,1)S(1)}, bf16[4,64,1024]{2,1,0:T(8,128)(2,1)S(1)}, u32[]{:S(2)}, u32[]{:S(2)}) collective-permute-start(bf16[4,64,1024]{2,1,0:T(8,128)(2,1)S(1)} %shard_map.119.near), channel_id=1, source_target_pairs={{0,3},{1,2},{2,1},{3,0},{4,7},{5,6},{6,5},{7,4},{8,11},{9,10},{10,... | collective-permute-start | bytes 1572872 | tf_op jit(solution)/shard_map/ppermute | solution.py:31
  46.3 1.5 %collective-permute-start.12 = (bf16[256,128]{1,0:T(8,128)(2,1)S(1)}, bf16[256,128]{1,0:T(8,128)(2,1)S(1)}, u32[]{:S(2)}, u32[]{:S(2)}) collective-permute-start(bf16[256,128]{1,0:T(8,128)(2,1)S(1)} %shard_map.117), channel_id=1, source_target_pairs={{0,8},{8,16},{16,24},{24,0},{1,9},{9,17},{17,25},{25,1},{2,10},{10... | collective-permute-start | bytes 196616 | tf_op jit(solution)/shard_map/ppermute | solution.py:27
  47.8 2.7 %collective-permute-start.11 = (bf16[256,128]{1,0:T(8,128)(2,1)S(1)}, bf16[256,128]{1,0:T(8,128)(2,1)S(1)}, u32[]{:S(2)}, u32[]{:S(2)}) collective-permute-start(bf16[256,128]{1,0:T(8,128)(2,1)S(1)} %shard_map.117), channel_id=1, source_target_pairs={{0,16},{8,24},{16,0},{24,8},{1,17},{9,25},{17,1},{25,9},{2,18},{10... | collective-permute-start | bytes 196616 | tf_op jit(solution)/shard_map/ppermute | solution.py:27
  51.7 0.7 %collective-permute-done.12 = bf16[256,128]{1,0:T(8,128)(2,1)S(1)} collective-permute-done((bf16[256,128]{1,0:T(8,128)(2,1)S(1)}, bf16[256,128]{1,0:T(8,128)(2,1)S(1)}, u32[]{:S(2)}, u32[]{:S(2)}) %collective-permute-start.12) | collective-permute-done | bytes 65568 | tf_op jit(solution)/shard_map/ppermute | solution.py:27
  52.5 1.1 %collective-permute-done.11 = bf16[256,128]{1,0:T(8,128)(2,1)S(1)} collective-permute-done((bf16[256,128]{1,0:T(8,128)(2,1)S(1)}, bf16[256,128]{1,0:T(8,128)(2,1)S(1)}, u32[]{:S(2)}, u32[]{:S(2)}) %collective-permute-start.11) | collective-permute-done | bytes 65568 | tf_op jit(solution)/shard_map/ppermute | solution.py:27
  53.6 1.2 %collective-permute-done.10 = bf16[256,128]{1,0:T(8,128)(2,1)S(1)} collective-permute-done((bf16[256,128]{1,0:T(8,128)(2,1)S(1)}, bf16[256,128]{1,0:T(8,128)(2,1)S(1)}, u32[]{:S(2)}, u32[]{:S(2)}) %collective-permute-start.10) | collective-permute-done | bytes 65568 | tf_op jit(solution)/shard_map/ppermute | solution.py:27
  54.9 0.8 %shard_map.120.start = f32[128,128]{1,0:T(8,128)S(1)} custom-call(s32[5]{0:T(128)S(1)} %stack.38.place, bf16[4,64,1024]{2,1,0:T(8,128)(2,1)S(1)} %shard_map.119.near, bf16[4,256,128]{2,1,0:T(8,128)(2,1)S(1)} %pad_maximum_fusion.u.u_own), custom_call_target="tpu_custom_call" | custom-call | flops 67108864 | bytes 786432 | tf_op jit(solution)/shard_map/pallas_call | solution.py:228
  56.5 1.9 %collective-permute-done.13.far = bf16[4,64,1024]{2,1,0:T(8,128)(2,1)S(1)} collective-permute-done((bf16[4,64,1024]{2,1,0:T(8,128)(2,1)S(1)}, bf16[4,64,1024]{2,1,0:T(8,128)(2,1)S(1)}, u32[]{:S(2)}, u32[]{:S(2)}) %collective-permute-start.13) | collective-permute-done | bytes 524320 | tf_op jit(solution)/shard_map/ppermute | solution.py:31
  58.4 0.9 %shard_map.121 = bf16[4,64,128]{2,1,0:T(8,128)(2,1)S(1)} custom-call(s32[5]{0:T(128)S(1)} %stack.38.place, bf16[4,64,1024]{2,1,0:T(8,128)(2,1)S(1)} %shard_map.119.near, bf16[4,64,1024]{2,1,0:T(8,128)(2,1)S(1)} %collective-permute-done.13.far, bf16[4,256,128]{2,1,0:T(8,128)(2,1)S(1)} %pad_maximum_fusion.u.u_own, ...), custom_call_target="tpu_custom_call" | custom-call | flops 67108864 | bytes 786432 | tf_op jit(solution)/shard_map/pallas_call | solution.py:228
  59.3 12.4 %all_to_all.5.parts = bf16[4,64,128]{2,1,0:T(8,128)(2,1)S(1)} all-to-all(bf16[4,64,128]{2,1,0:T(8,128)(2,1)S(1)} %shard_map.121), channel_id=1, replica_groups=mesh['c'=2,'zh'=4,'x'=4,'zl'=2,'y'=4] {'zh'}, dimensions={0} | all-to-all | bytes 131072 | tf_op jit(solution)/shard_map/all_to_all | solution.py:337
  71.7 0.8 %shard_map.122 = (bf16[16,4,128]{2,1,0:T(4,128)(2,1)}, bf16[16,4,1024]{2,1,0:T(4,128)(2,1)}) custom-call(bf16[4,64,128]{2,1,0:T(8,128)(2,1)S(1)} %all_to_all.5.parts, f32[512,128]{1,0:T(8,128)S(1)} %get-tuple-element.67.mixed, bf16[512,64]{1,0:T(8,128)(2,1)S(1)} %get-tuple-element.68.weights), custom_call_target="tpu_custom_call" | custom-call | tf_op jit(solution)/shard_map/pallas_call | solution.py:259
  (34 shorter events, 4.3 us)
Async XLA Ops:
  0.6 6.2 %copy-start.6 = (bf16[16,4,1024]{2,1,0:T(4,128)(2,1)S(1)}, bf16[16,4,1024]{2,1,0:T(4,128)(2,1)}, u32[]{:S(2)}) copy-start(bf16[16,4,1024]{2,1,0:T(4,128)(2,1)} %param.12) | copy-start | bytes 393220
  0.6 15.5 %copy-start.2 = (bf16[16,4,1024]{2,1,0:T(4,128)(2,1)S(1)}, bf16[16,4,1024]{2,1,0:T(4,128)(2,1)}, u32[]{:S(2)}) copy-start(bf16[16,4,1024]{2,1,0:T(4,128)(2,1)} %raw_queries) | copy-start | bytes 393220
  0.7 15.5 %copy-start.5 = (s32[16]{0:T(128)S(1)}, s32[16]{0:T(128)}, u32[]{:S(2)}) copy-start(s32[16]{0:T(128)} %lengths.1) | copy-start | bytes 196
  0.7 15.5 %copy-start.1 = (bf16[16,128,128]{2,1,0:T(8,128)(2,1)S(1)}, bf16[16,128,128]{2,1,0:T(8,128)(2,1)}, u32[]{:S(2)}) copy-start(bf16[16,128,128]{2,1,0:T(8,128)(2,1)} %cache_values.1) | copy-start | bytes 1572868
  0.7 15.5 %copy-start = (bf16[16,128,128]{2,1,0:T(8,128)(2,1)S(1)}, bf16[16,128,128]{2,1,0:T(8,128)(2,1)}, u32[]{:S(2)}) copy-start(bf16[16,128,128]{2,1,0:T(8,128)(2,1)} %cache_keys.1) | copy-start | bytes 1572868
  0.7 15.5 %copy-start.4 = (bf16[16,4,128]{2,1,0:T(4,128)(2,1)S(1)}, bf16[16,4,128]{2,1,0:T(4,128)(2,1)}, u32[]{:S(2)}) copy-start(bf16[16,4,128]{2,1,0:T(4,128)(2,1)} %param.14) | copy-start | bytes 49156
  0.7 43.0 %copy-start.3 = (bf16[256,128]{1,0:T(8,128)(2,1)S(1)}, bf16[256,128]{1,0:T(8,128)(2,1)}, u32[]{:S(2)}) copy-start(bf16[256,128]{1,0:T(8,128)(2,1)} %weight.1) | copy-start | bytes 196612
  6.8 2.7 %collective-permute-start = (bf16[4,4,256,128]{3,2,1,0:T(8,128)(2,1)S(1)}, bf16[4,4,256,128]{3,2,1,0:T(8,128)(2,1)S(1)}, u32[]{:S(2)}, u32[]{:S(2)}) collective-permute-start(bf16[4,4,256,128]{3,2,1,0:T(8,128)(2,1)S(1)} %get-tuple-element.38), channel_id=1, source_target_pairs={{0,128},{128,0},{1,129},{129,1},{2,130},{130,2},{3,131},{131,3},{4... | collective-permute-start | bytes 3145736 | tf_op jit(solution)/shard_map/ppermute | solution.py:27
  6.9 9.2 %collective-permute-start.4 = (bf16[16,4,1024]{2,1,0:T(4,128)(2,1)S(1)}, bf16[16,4,1024]{2,1,0:T(4,128)(2,1)S(1)}, u32[]{:S(2)}, u32[]{:S(2)}) collective-permute-start(bf16[16,4,1024]{2,1,0:T(4,128)(2,1)S(1)} %copy-done.6), channel_id=1, source_target_pairs={{0,0},{1,33},{2,66},{3,99},{32,1},{33,34},{34,67},{35,96},{64,2},{... | collective-permute-start | bytes 393224 | tf_op jit(solution)/shard_map/ppermute | solution.py:36
  9.7 11.9 %collective-permute-start.1 = (bf16[4,256,128]{2,1,0:T(8,128)(2,1)S(1)}, bf16[4,256,128]{2,1,0:T(8,128)(2,1)S(1)}, u32[]{:S(2)}, u32[]{:S(2)}) collective-permute-start(bf16[4,256,128]{2,1,0:T(8,128)(2,1)S(1)} %get-tuple-element.40), channel_id=1, source_target_pairs={{0,16},{8,24},{16,0},{24,8},{1,17},{9,25},{17,1},{25,9},{2,18},{10... | collective-permute-start | bytes 786440 | tf_op jit(solution)/shard_map/ppermute | solution.py:27
  12.8 12.4 %collective-permute-start.2 = (bf16[4,256,128]{2,1,0:T(8,128)(2,1)S(1)}, bf16[4,256,128]{2,1,0:T(8,128)(2,1)S(1)}, u32[]{:S(2)}, u32[]{:S(2)}) collective-permute-start(bf16[4,256,128]{2,1,0:T(8,128)(2,1)S(1)} %get-tuple-element.41), channel_id=1, source_target_pairs={{0,8},{8,16},{16,24},{24,0},{1,9},{9,17},{17,25},{25,1},{2,10},{10... | collective-permute-start | bytes 786440 | tf_op jit(solution)/shard_map/ppermute | solution.py:27
  13.4 12.0 %collective-permute-start.3 = (bf16[4,256,128]{2,1,0:T(8,128)(2,1)S(1)}, bf16[4,256,128]{2,1,0:T(8,128)(2,1)S(1)}, u32[]{:S(2)}, u32[]{:S(2)}) collective-permute-start(bf16[4,256,128]{2,1,0:T(8,128)(2,1)S(1)} %get-tuple-element.42), channel_id=1, source_target_pairs={{0,24},{8,0},{16,8},{24,16},{1,25},{9,1},{17,9},{25,17},{2,26},{10... | collective-permute-start | bytes 786440 | tf_op jit(solution)/shard_map/ppermute | solution.py:27
  16.1 5.4 %collective-permute-start.5 = (bf16[16,4,1024]{2,1,0:T(4,128)(2,1)S(1)}, bf16[16,4,1024]{2,1,0:T(4,128)(2,1)S(1)}, u32[]{:S(2)}, u32[]{:S(2)}) collective-permute-start(bf16[16,4,1024]{2,1,0:T(4,128)(2,1)S(1)} %collective-permute-done.4.first), channel_id=1, source_target_pairs={{0,4},{4,0},{1,5},{5,1},{2,6},{6,2},{3,7},{7,3},{8,12},{12,8},{9,1... | collective-permute-start | bytes 393224 | tf_op jit(solution)/shard_map/ppermute | solution.py:27
  25.5 18.2 %collective-permute-start.9 = (bf16[2,64,1024]{2,1,0:T(8,128)(2,1)S(1)}, bf16[2,64,1024]{2,1,0:T(8,128)(2,1)S(1)}, u32[]{:S(2)}, u32[]{:S(2)}) collective-permute-start(bf16[2,64,1024]{2,1,0:T(8,128)(2,1)S(1)} %shard_map.114.first), channel_id=1, source_target_pairs={{0,1},{1,0},{2,3},{3,2},{4,5},{5,4},{6,7},{7,6},{8,9},{9,8},{10,11... | collective-permute-start | bytes 786440 | tf_op jit(solution)/shard_map/ppermute | solution.py:31
  29.8 9.4 %collective-permute-start.6 = (bf16[256,128]{1,0:T(8,128)(2,1)S(1)}, bf16[256,128]{1,0:T(8,128)(2,1)S(1)}, u32[]{:S(2)}, u32[]{:S(2)}) collective-permute-start(bf16[256,128]{1,0:T(8,128)(2,1)S(1)} %get-tuple-element.53), channel_id=1, source_target_pairs={{0,64},{32,96},{64,0},{96,32},{1,65},{33,97},{65,1},{97,33},{2,66}... | collective-permute-start | bytes 196616 | tf_op jit(solution)/shard_map/ppermute | solution.py:27
  35.1 6.4 %collective-permute-start.7 = (bf16[256,128]{1,0:T(8,128)(2,1)S(1)}, bf16[256,128]{1,0:T(8,128)(2,1)S(1)}, u32[]{:S(2)}, u32[]{:S(2)}) collective-permute-start(bf16[256,128]{1,0:T(8,128)(2,1)S(1)} %get-tuple-element.54), channel_id=1, source_target_pairs={{0,32},{32,64},{64,96},{96,0},{1,33},{33,65},{65,97},{97,1},{2,34}... | collective-permute-start | bytes 196616 | tf_op jit(solution)/shard_map/ppermute | solution.py:27
  38.3 5.3 %collective-permute-start.8 = (bf16[256,128]{1,0:T(8,128)(2,1)S(1)}, bf16[256,128]{1,0:T(8,128)(2,1)S(1)}, u32[]{:S(2)}, u32[]{:S(2)}) collective-permute-start(bf16[256,128]{1,0:T(8,128)(2,1)S(1)} %get-tuple-element.55), channel_id=1, source_target_pairs={{0,96},{32,0},{64,32},{96,64},{1,97},{33,1},{65,33},{97,65},{2,98}... | collective-permute-start | bytes 196616 | tf_op jit(solution)/shard_map/ppermute | solution.py:27
  43.8 14.6 %collective-permute-start.13 = (bf16[4,64,1024]{2,1,0:T(8,128)(2,1)S(1)}, bf16[4,64,1024]{2,1,0:T(8,128)(2,1)S(1)}, u32[]{:S(2)}, u32[]{:S(2)}) collective-permute-start(bf16[4,64,1024]{2,1,0:T(8,128)(2,1)S(1)} %shard_map.119.near), channel_id=1, source_target_pairs={{0,3},{1,2},{2,1},{3,0},{4,7},{5,6},{6,5},{7,4},{8,11},{9,10},{10,... | collective-permute-start | bytes 1572872 | tf_op jit(solution)/shard_map/ppermute | solution.py:31
  46.3 6.2 %collective-permute-start.12 = (bf16[256,128]{1,0:T(8,128)(2,1)S(1)}, bf16[256,128]{1,0:T(8,128)(2,1)S(1)}, u32[]{:S(2)}, u32[]{:S(2)}) collective-permute-start(bf16[256,128]{1,0:T(8,128)(2,1)S(1)} %shard_map.117), channel_id=1, source_target_pairs={{0,8},{8,16},{16,24},{24,0},{1,9},{9,17},{17,25},{25,1},{2,10},{10... | collective-permute-start | bytes 196616 | tf_op jit(solution)/shard_map/ppermute | solution.py:27
  47.8 5.8 %collective-permute-start.11 = (bf16[256,128]{1,0:T(8,128)(2,1)S(1)}, bf16[256,128]{1,0:T(8,128)(2,1)S(1)}, u32[]{:S(2)}, u32[]{:S(2)}) collective-permute-start(bf16[256,128]{1,0:T(8,128)(2,1)S(1)} %shard_map.117), channel_id=1, source_target_pairs={{0,16},{8,24},{16,0},{24,8},{1,17},{9,25},{17,1},{25,9},{2,18},{10... | collective-permute-start | bytes 196616 | tf_op jit(solution)/shard_map/ppermute | solution.py:27
  50.5 4.3 %collective-permute-start.10 = (bf16[256,128]{1,0:T(8,128)(2,1)S(1)}, bf16[256,128]{1,0:T(8,128)(2,1)S(1)}, u32[]{:S(2)}, u32[]{:S(2)}) collective-permute-start(bf16[256,128]{1,0:T(8,128)(2,1)S(1)} %shard_map.117), channel_id=1, source_target_pairs={{0,24},{8,0},{16,8},{24,16},{1,25},{9,1},{17,9},{25,17},{2,26},{10... | collective-permute-start | bytes 196616 | tf_op jit(solution)/shard_map/ppermute | solution.py:27
  54.8 1.6 %collective-permute-start.14 = (bf16[4,256,128]{2,1,0:T(8,128)(2,1)S(1)}, bf16[4,256,128]{2,1,0:T(8,128)(2,1)S(1)}, u32[]{:S(2)}, u32[]{:S(2)}) collective-permute-start(bf16[4,256,128]{2,1,0:T(8,128)(2,1)S(1)} %pad_maximum_fusion.u.u_own), channel_id=1, source_target_pairs={{0,128},{128,0},{1,129},{129,1},{2,130},{130,2},{3,131},{131,3},{4... | collective-permute-start | bytes 786440 | tf_op jit(solution)/shard_map/ppermute | solution.py:27

commit v13 on v12

--- a/solution.py
+++ b/solution.py
@@ -186,7 +186,7 @@
         scratch_shapes=[pltpu.VMEM((places, HEADS * HD), BF16)],
         compiler_params=pltpu.CompilerParams(vmem_limit_bytes=16 * MIB),
         cost_estimate=pl.CostEstimate(
-            flops=MIB, bytes_accessed=MIB // 4, transcendentals=0
+            flops=8000 * MIB, bytes_accessed=20 * MIB, transcendentals=0
         ),
     )(lengths, queries, new_keys, cache_keys, cache_values)
 
@@ -293,24 +293,24 @@
         core_sum_kernel, [(rows, F32)] + [(rows, BF16)] * 3, mine, received
     )
     along_x = [shift(sent[d - 1], "x", d) for d in (2, 1, 3)]
-    attended_cache, fresh_weights = attend_cache(
-        lengths, after(queries, own), new_keys.reshape(places, HD), cache_keys, cache_values
-    )
     swapped = after(swapped, own)
     (both,) = small_call(
         join_kernel, [((2, places, D // 8), BF16)], swapped, shift(swapped, "zl", 1)
     )
-    own, *along_x, both, attended_cache, fresh_weights = lax.optimization_barrier(
-        (own, *along_x, both, attended_cache, fresh_weights)
-    )
+    near = exchange(both, "y", 1)
+
+    own, *along_x, both = lax.optimization_barrier((own, *along_x, both))
     rows = (256, HD)
     own, *sent = small_call(
         x_sum_kernel, [(rows, F32)] + [(rows, BF16)] * 3, own, *along_x
     )
     along_z = [shift(sent[e - 1], "zh", e) for e in (2, 1, 3)]
-    both = after(both, own)
-    near = exchange(both, "y", 1)
-    own, *along_z, near = lax.optimization_barrier((own, *along_z, near))
+    attended_cache, fresh_weights = attend_cache(
+        lengths, after(queries, own), new_keys.reshape(places, HD), cache_keys, cache_values
+    )
+    own, *along_z, near, attended_cache, fresh_weights = lax.optimization_barrier(
+        (own, *along_z, near, attended_cache, fresh_weights)
+    )
     (updated,) = small_call(update_kernel, [(rows, BF16)], value_weight, own, *along_z)
     own = after(own, updated)
     (gradient,) = small_call(gradient_kernel, [(rows, F32)], own, *along_z, keep=False)

time: 73.3 us -> 72.6 us (level)
  waiting for transfers between devices: 19 us -> 15.1 us
  starting transfers between devices: 28.3 us -> 31.6 us
    ppermute x12, waiting for transfers between devices: 17.1 us -> 13.2 us  [shift(): return lax.ppermute(value, axis, [(i, (i + by) % n) for i in range(n)])]
    ppermute x12, starting transfers between devices: 20.8 us -> 22.8 us  [shift(): return lax.ppermute(value, axis, [(i, (i + by) % n) for i in range(n)])]
    ppermute x2, starting transfers between devices: 6.84 us -> 8.09 us  [exchange(): return lax.ppermute(value, axis, [(i, i ^ bit) for i in range(SIZES[axis])])]
  transfers between devices with their start and end apart: 15 -> 15, of which waited for: 11 -> 8; matrix products, arithmetic and copies ran while one was open for 0% -> 0% of each run, Pallas kernels for 5% -> 6%
where the time goes in v13:
time: 72.6 us; the launch traced here: 72.5 us
  starting transfers between devices  31.6 us (44%)
  waiting for transfers between devices  15.1 us (21%)
  blocking collectives  13 us (18%)
  Pallas kernels  11.8 us (16%)
  between operations  0.82 us (1%)
    ppermute x12, starting transfers between devices, shift(): return lax.ppermute(value, axis, [(i, (i + by) % n) for i in range(n)])  22.8 us
    ppermute x12, waiting for transfers between devices, shift(): return lax.ppermute(value, axis, [(i, (i + by) % n) for i in range(n)])  13.2 us
    all_to_all x1, blocking collectives, shards(): exchanged = lax.all_to_all(partial, 'zh', 0, 0, tiled=True)  13 us
    ppermute x2, starting transfers between devices, exchange(): return lax.ppermute(value, axis, [(i, i ^ bit) for i in range(SIZES[axis])])  8.09 us
    pallas_call x1, Pallas kernels, partial_gradient(): pl.pallas_call(partial_kernel, in_specs=[SMEM, HBM, HBM], out_specs=[VMEM...  5.96 us
    pallas_call x1, Pallas kernels, attend_cache(): pl.pallas_call(attend_kernel, in_specs=[SMEM] + [VMEM] * 4, out_specs=[VM...  2.14 us
    ppermute x2, waiting for transfers between devices, exchange(): return lax.ppermute(value, axis, [(i, i ^ bit) for i in range(SIZES[axis])])  1.86 us
    pallas_call x2, Pallas kernels, project(): pl.pallas_call(kernel, in_specs=[SMEM] + [VMEM] * len(args), out_specs=VM...  1.72 us
  transfers between devices with their start and end apart: 15, of which 8 were waited for; matrix products, arithmetic and copies ran while one was open for 0% of the time, Pallas kernels for 6%

profile of v13, /device:TPU:32, one launch (start us, length us, event | category | flops | bytes accessed | tf_op | source)
XLA Modules:
  0.0 72.5 jit_solution(16560914128769718969)
XLA Ops:
  0.8 6.0 %shard_map.112 = (bf16[4,4,256,128]{3,2,1,0:T(8,128)(2,1)S(1)}, bf16[4,4,256,128]{3,2,1,0:T(8,128)(2,1)S(1)}) custom-call(s32[5]{0:T(128)S(1)} %stack.38.place, bf16[768,8192]{1,0:T(8,128)(2,1)} %x_hbm.1, bf16[768,128]{1,0:T(8,128)(2,1)} %v_hbm.1), custom_call_target="tpu_custom_call" | custom-call | flops 1610612736 | bytes 12582912 | tf_op jit(solution)/shard_map/pallas_call | solution.py:71
  6.9 0.7 collective-permute-start.4
  7.5 2.0 %collective-permute-done.received = bf16[4,4,256,128]{3,2,1,0:T(8,128)(2,1)S(1)} collective-permute-done((bf16[4,4,256,128]{3,2,1,0:T(8,128)(2,1)S(1)}, bf16[4,4,256,128]{3,2,1,0:T(8,128)(2,1)S(1)}, u32[]{:S(2)}, u32[]{:S(2)}) %collective-permute-start) | collective-permute-done | bytes 1048608 | tf_op jit(solution)/shard_map/ppermute | solution.py:27
  9.7 3.1 %collective-permute-start.1 = (bf16[4,256,128]{2,1,0:T(8,128)(2,1)S(1)}, bf16[4,256,128]{2,1,0:T(8,128)(2,1)S(1)}, u32[]{:S(2)}, u32[]{:S(2)}) collective-permute-start(bf16[4,256,128]{2,1,0:T(8,128)(2,1)S(1)} %get-tuple-element.39), channel_id=1, source_target_pairs={{0,16},{8,24},{16,0},{24,8},{1,17},{9,25},{17,1},{25,9},{2,18},{10... | collective-permute-start | bytes 786440 | tf_op jit(solution)/shard_map/ppermute | solution.py:27
  13.4 2.6 %collective-permute-start.3 = (bf16[4,256,128]{2,1,0:T(8,128)(2,1)S(1)}, bf16[4,256,128]{2,1,0:T(8,128)(2,1)S(1)}, u32[]{:S(2)}, u32[]{:S(2)}) collective-permute-start(bf16[4,256,128]{2,1,0:T(8,128)(2,1)S(1)} %get-tuple-element.41), channel_id=1, source_target_pairs={{0,24},{8,0},{16,8},{24,16},{1,25},{9,1},{17,9},{25,17},{2,26},{10... | collective-permute-start | bytes 786440 | tf_op jit(solution)/shard_map/ppermute | solution.py:27
  16.2 5.3 %collective-permute-done.5.second = bf16[16,4,1024]{2,1,0:T(4,128)(2,1)S(1)} collective-permute-done((bf16[16,4,1024]{2,1,0:T(4,128)(2,1)S(1)}, bf16[16,4,1024]{2,1,0:T(4,128)(2,1)S(1)}, u32[]{:S(2)}, u32[]{:S(2)}) %collective-permute-start.5) | collective-permute-done | bytes 131104 | tf_op jit(solution)/shard_map/ppermute | solution.py:27
  21.6 6.2 %collective-permute-start.9 = (bf16[2,64,1024]{2,1,0:T(8,128)(2,1)S(1)}, bf16[2,64,1024]{2,1,0:T(8,128)(2,1)S(1)}, u32[]{:S(2)}, u32[]{:S(2)}) collective-permute-start(bf16[2,64,1024]{2,1,0:T(8,128)(2,1)S(1)} %shard_map.114.first), channel_id=1, source_target_pairs={{0,1},{1,0},{2,3},{3,2},{4,5},{5,4},{6,7},{7,6},{8,9},{9,8},{10,11... | collective-permute-start | bytes 786440 | tf_op jit(solution)/shard_map/ppermute | solution.py:31
  27.9 6.7 %collective-permute-start.6 = (bf16[256,128]{1,0:T(8,128)(2,1)S(1)}, bf16[256,128]{1,0:T(8,128)(2,1)S(1)}, u32[]{:S(2)}, u32[]{:S(2)}) collective-permute-start(bf16[256,128]{1,0:T(8,128)(2,1)S(1)} %get-tuple-element.49), channel_id=1, source_target_pairs={{0,64},{32,96},{64,0},{96,32},{1,65},{33,97},{65,1},{97,33},{2,66}... | collective-permute-start | bytes 196616 | tf_op jit(solution)/shard_map/ppermute | solution.py:27
  34.7 3.7 %collective-permute-start.7 = (bf16[256,128]{1,0:T(8,128)(2,1)S(1)}, bf16[256,128]{1,0:T(8,128)(2,1)S(1)}, u32[]{:S(2)}, u32[]{:S(2)}) collective-permute-start(bf16[256,128]{1,0:T(8,128)(2,1)S(1)} %get-tuple-element.50), channel_id=1, source_target_pairs={{0,32},{32,64},{64,96},{96,0},{1,33},{33,65},{65,97},{97,1},{2,34}... | collective-permute-start | bytes 196616 | tf_op jit(solution)/shard_map/ppermute | solution.py:27
  38.8 2.1 %shard_map.116 = (f32[512,128]{1,0:T(8,128)S(1)}, bf16[512,64]{1,0:T(8,128)(2,1)S(1)}) custom-call(s32[16]{0:T(128)S(1)} %copy-done.5, bf16[16,4,1024]{2,1,0:T(4,128)(2,1)S(1)} %copy-done.3, bf16[64,128]{1,0:T(8,128)(2,1)S(1)} %bitcast.11, bf16[16,128,128]{2,1,0:T(8,128)(2,1)S(1)} %copy-done.1, bf16[16,128,128]{2,1,0:T(8,128)(2,1)S(1)} %copy-done.2), custom_call_target="tpu_custom_call" | custom-call | flops 8388608000 | bytes 20971520 | tf_op jit(solution)/shard_map/pallas_call | solution.py:178
  41.1 2.7 %collective-permute-done.8.r3 = bf16[256,128]{1,0:T(8,128)(2,1)S(1)} collective-permute-done((bf16[256,128]{1,0:T(8,128)(2,1)S(1)}, bf16[256,128]{1,0:T(8,128)(2,1)S(1)}, u32[]{:S(2)}, u32[]{:S(2)}) %collective-permute-start.8) | collective-permute-done | bytes 65568 | tf_op jit(solution)/shard_map/ppermute | solution.py:27
  43.8 1.9 %collective-permute-start.13 = (bf16[4,64,1024]{2,1,0:T(8,128)(2,1)S(1)}, bf16[4,64,1024]{2,1,0:T(8,128)(2,1)S(1)}, u32[]{:S(2)}, u32[]{:S(2)}) collective-permute-start(bf16[4,64,1024]{2,1,0:T(8,128)(2,1)S(1)} %shard_map.119.near), channel_id=1, source_target_pairs={{0,3},{1,2},{2,1},{3,0},{4,7},{5,6},{6,5},{7,4},{8,11},{9,10},{10,... | collective-permute-start | bytes 1572872 | tf_op jit(solution)/shard_map/ppermute | solution.py:31
  45.7 1.5 %collective-permute-start.12 = (bf16[256,128]{1,0:T(8,128)(2,1)S(1)}, bf16[256,128]{1,0:T(8,128)(2,1)S(1)}, u32[]{:S(2)}, u32[]{:S(2)}) collective-permute-start(bf16[256,128]{1,0:T(8,128)(2,1)S(1)} %shard_map.117), channel_id=1, source_target_pairs={{0,8},{8,16},{16,24},{24,0},{1,9},{9,17},{17,25},{25,1},{2,10},{10... | collective-permute-start | bytes 196616 | tf_op jit(solution)/shard_map/ppermute | solution.py:27
  47.2 2.7 %collective-permute-start.11 = (bf16[256,128]{1,0:T(8,128)(2,1)S(1)}, bf16[256,128]{1,0:T(8,128)(2,1)S(1)}, u32[]{:S(2)}, u32[]{:S(2)}) collective-permute-start(bf16[256,128]{1,0:T(8,128)(2,1)S(1)} %shard_map.117), channel_id=1, source_target_pairs={{0,16},{8,24},{16,0},{24,8},{1,17},{9,25},{17,1},{25,9},{2,18},{10... | collective-permute-start | bytes 196616 | tf_op jit(solution)/shard_map/ppermute | solution.py:27
  49.9 1.1 %collective-permute-start.10 = (bf16[256,128]{1,0:T(8,128)(2,1)S(1)}, bf16[256,128]{1,0:T(8,128)(2,1)S(1)}, u32[]{:S(2)}, u32[]{:S(2)}) collective-permute-start(bf16[256,128]{1,0:T(8,128)(2,1)S(1)} %shard_map.117), channel_id=1, source_target_pairs={{0,24},{8,0},{16,8},{24,16},{1,25},{9,1},{17,9},{25,17},{2,26},{10... | collective-permute-start | bytes 196616 | tf_op jit(solution)/shard_map/ppermute | solution.py:27
  51.0 0.7 shard_map.118
  51.9 1.1 %collective-permute-done.11 = bf16[256,128]{1,0:T(8,128)(2,1)S(1)} collective-permute-done((bf16[256,128]{1,0:T(8,128)(2,1)S(1)}, bf16[256,128]{1,0:T(8,128)(2,1)S(1)}, u32[]{:S(2)}, u32[]{:S(2)}) %collective-permute-start.11) | collective-permute-done | bytes 65568 | tf_op jit(solution)/shard_map/ppermute | solution.py:27
  52.9 1.2 %collective-permute-done.10 = bf16[256,128]{1,0:T(8,128)(2,1)S(1)} collective-permute-done((bf16[256,128]{1,0:T(8,128)(2,1)S(1)}, bf16[256,128]{1,0:T(8,128)(2,1)S(1)}, u32[]{:S(2)}, u32[]{:S(2)}) %collective-permute-start.10) | collective-permute-done | bytes 65568 | tf_op jit(solution)/shard_map/ppermute | solution.py:27
  54.3 0.8 %shard_map.120.start = f32[128,128]{1,0:T(8,128)S(1)} custom-call(s32[5]{0:T(128)S(1)} %stack.38.place, bf16[4,64,1024]{2,1,0:T(8,128)(2,1)S(1)} %shard_map.119.near, bf16[4,256,128]{2,1,0:T(8,128)(2,1)S(1)} %pad_maximum_fusion.u.u_own), custom_call_target="tpu_custom_call" | custom-call | flops 67108864 | bytes 786432 | tf_op jit(solution)/shard_map/pallas_call | solution.py:228
  55.1 0.7 %collective-permute-done.14.u_other = bf16[4,256,128]{2,1,0:T(8,128)(2,1)S(1)} collective-permute-done((bf16[4,256,128]{2,1,0:T(8,128)(2,1)S(1)}, bf16[4,256,128]{2,1,0:T(8,128)(2,1)S(1)}, u32[]{:S(2)}, u32[]{:S(2)}) %collective-permute-start.14) | collective-permute-done | bytes 262176 | tf_op jit(solution)/shard_map/ppermute | solution.py:27
  55.8 1.9 %collective-permute-done.13.far = bf16[4,64,1024]{2,1,0:T(8,128)(2,1)S(1)} collective-permute-done((bf16[4,64,1024]{2,1,0:T(8,128)(2,1)S(1)}, bf16[4,64,1024]{2,1,0:T(8,128)(2,1)S(1)}, u32[]{:S(2)}, u32[]{:S(2)}) %collective-permute-start.13) | collective-permute-done | bytes 524320 | tf_op jit(solution)/shard_map/ppermute | solution.py:31
  57.7 0.9 %shard_map.121 = bf16[4,64,128]{2,1,0:T(8,128)(2,1)S(1)} custom-call(s32[5]{0:T(128)S(1)} %stack.38.place, bf16[4,64,1024]{2,1,0:T(8,128)(2,1)S(1)} %shard_map.119.near, bf16[4,64,1024]{2,1,0:T(8,128)(2,1)S(1)} %collective-permute-done.13.far, bf16[4,256,128]{2,1,0:T(8,128)(2,1)S(1)} %pad_maximum_fusion.u.u_own, ...), custom_call_target="tpu_custom_call" | custom-call | flops 67108864 | bytes 786432 | tf_op jit(solution)/shard_map/pallas_call | solution.py:228
  58.6 13.0 %all_to_all.5.parts = bf16[4,64,128]{2,1,0:T(8,128)(2,1)S(1)} all-to-all(bf16[4,64,128]{2,1,0:T(8,128)(2,1)S(1)} %shard_map.121), channel_id=1, replica_groups=mesh['c'=2,'zh'=4,'x'=4,'zl'=2,'y'=4] {'zh'}, dimensions={0} | all-to-all | bytes 131072 | tf_op jit(solution)/shard_map/all_to_all | solution.py:337
  71.6 0.8 %shard_map.122 = (bf16[16,4,128]{2,1,0:T(4,128)(2,1)}, bf16[16,4,1024]{2,1,0:T(4,128)(2,1)}) custom-call(bf16[4,64,128]{2,1,0:T(8,128)(2,1)S(1)} %all_to_all.5.parts, f32[512,128]{1,0:T(8,128)S(1)} %get-tuple-element.65.mixed, bf16[512,64]{1,0:T(8,128)(2,1)S(1)} %get-tuple-element.66.weights), custom_call_target="tpu_custom_call" | custom-call | tf_op jit(solution)/shard_map/pallas_call | solution.py:259
  (34 shorter events, 2.2 us)
Async XLA Ops:
  0.6 6.2 %copy-start.6 = (bf16[16,4,1024]{2,1,0:T(4,128)(2,1)S(1)}, bf16[16,4,1024]{2,1,0:T(4,128)(2,1)}, u32[]{:S(2)}) copy-start(bf16[16,4,1024]{2,1,0:T(4,128)(2,1)} %param.12) | copy-start | bytes 393220
  0.6 38.2 %copy-start.3 = (bf16[16,4,1024]{2,1,0:T(4,128)(2,1)S(1)}, bf16[16,4,1024]{2,1,0:T(4,128)(2,1)}, u32[]{:S(2)}) copy-start(bf16[16,4,1024]{2,1,0:T(4,128)(2,1)} %raw_queries) | copy-start | bytes 393220
  0.7 38.2 %copy-start.5 = (s32[16]{0:T(128)S(1)}, s32[16]{0:T(128)}, u32[]{:S(2)}) copy-start(s32[16]{0:T(128)} %lengths.1) | copy-start | bytes 196
  0.7 38.2 %copy-start.2 = (bf16[16,128,128]{2,1,0:T(8,128)(2,1)S(1)}, bf16[16,128,128]{2,1,0:T(8,128)(2,1)}, u32[]{:S(2)}) copy-start(bf16[16,128,128]{2,1,0:T(8,128)(2,1)} %cache_values.1) | copy-start | bytes 1572868
  0.7 38.1 %copy-start.1 = (bf16[16,128,128]{2,1,0:T(8,128)(2,1)S(1)}, bf16[16,128,128]{2,1,0:T(8,128)(2,1)}, u32[]{:S(2)}) copy-start(bf16[16,128,128]{2,1,0:T(8,128)(2,1)} %cache_keys.1) | copy-start | bytes 1572868
  0.7 38.1 %copy-start.4 = (bf16[16,4,128]{2,1,0:T(4,128)(2,1)S(1)}, bf16[16,4,128]{2,1,0:T(4,128)(2,1)}, u32[]{:S(2)}) copy-start(bf16[16,4,128]{2,1,0:T(4,128)(2,1)} %param.14) | copy-start | bytes 49156
  6.8 2.7 %collective-permute-start = (bf16[4,4,256,128]{3,2,1,0:T(8,128)(2,1)S(1)}, bf16[4,4,256,128]{3,2,1,0:T(8,128)(2,1)S(1)}, u32[]{:S(2)}, u32[]{:S(2)}) collective-permute-start(bf16[4,4,256,128]{3,2,1,0:T(8,128)(2,1)S(1)} %get-tuple-element.37), channel_id=1, source_target_pairs={{0,128},{128,0},{1,129},{129,1},{2,130},{130,2},{3,131},{131,3},{4... | collective-permute-start | bytes 3145736 | tf_op jit(solution)/shard_map/ppermute | solution.py:27
  6.9 9.2 %collective-permute-start.4 = (bf16[16,4,1024]{2,1,0:T(4,128)(2,1)S(1)}, bf16[16,4,1024]{2,1,0:T(4,128)(2,1)S(1)}, u32[]{:S(2)}, u32[]{:S(2)}) collective-permute-start(bf16[16,4,1024]{2,1,0:T(4,128)(2,1)S(1)} %copy-done.6), channel_id=1, source_target_pairs={{0,0},{1,33},{2,66},{3,99},{32,1},{33,34},{34,67},{35,96},{64,2},{... | collective-permute-start | bytes 393224 | tf_op jit(solution)/shard_map/ppermute | solution.py:36
  9.7 18.1 %collective-permute-start.1 = (bf16[4,256,128]{2,1,0:T(8,128)(2,1)S(1)}, bf16[4,256,128]{2,1,0:T(8,128)(2,1)S(1)}, u32[]{:S(2)}, u32[]{:S(2)}) collective-permute-start(bf16[4,256,128]{2,1,0:T(8,128)(2,1)S(1)} %get-tuple-element.39), channel_id=1, source_target_pairs={{0,16},{8,24},{16,0},{24,8},{1,17},{9,25},{17,1},{25,9},{2,18},{10... | collective-permute-start | bytes 786440 | tf_op jit(solution)/shard_map/ppermute | solution.py:27
  12.8 15.0 %collective-permute-start.2 = (bf16[4,256,128]{2,1,0:T(8,128)(2,1)S(1)}, bf16[4,256,128]{2,1,0:T(8,128)(2,1)S(1)}, u32[]{:S(2)}, u32[]{:S(2)}) collective-permute-start(bf16[4,256,128]{2,1,0:T(8,128)(2,1)S(1)} %get-tuple-element.40), channel_id=1, source_target_pairs={{0,8},{8,16},{16,24},{24,0},{1,9},{9,17},{17,25},{25,1},{2,10},{10... | collective-permute-start | bytes 786440 | tf_op jit(solution)/shard_map/ppermute | solution.py:27
  13.4 14.4 %collective-permute-start.3 = (bf16[4,256,128]{2,1,0:T(8,128)(2,1)S(1)}, bf16[4,256,128]{2,1,0:T(8,128)(2,1)S(1)}, u32[]{:S(2)}, u32[]{:S(2)}) collective-permute-start(bf16[4,256,128]{2,1,0:T(8,128)(2,1)S(1)} %get-tuple-element.41), channel_id=1, source_target_pairs={{0,24},{8,0},{16,8},{24,16},{1,25},{9,1},{17,9},{25,17},{2,26},{10... | collective-permute-start | bytes 786440 | tf_op jit(solution)/shard_map/ppermute | solution.py:27
  16.1 5.4 %collective-permute-start.5 = (bf16[16,4,1024]{2,1,0:T(4,128)(2,1)S(1)}, bf16[16,4,1024]{2,1,0:T(4,128)(2,1)S(1)}, u32[]{:S(2)}, u32[]{:S(2)}) collective-permute-start(bf16[16,4,1024]{2,1,0:T(4,128)(2,1)S(1)} %collective-permute-done.4.first), channel_id=1, source_target_pairs={{0,4},{4,0},{1,5},{5,1},{2,6},{6,2},{3,7},{7,3},{8,12},{12,8},{9,1... | collective-permute-start | bytes 393224 | tf_op jit(solution)/shard_map/ppermute | solution.py:27
  21.6 22.2 %collective-permute-start.9 = (bf16[2,64,1024]{2,1,0:T(8,128)(2,1)S(1)}, bf16[2,64,1024]{2,1,0:T(8,128)(2,1)S(1)}, u32[]{:S(2)}, u32[]{:S(2)}) collective-permute-start(bf16[2,64,1024]{2,1,0:T(8,128)(2,1)S(1)} %shard_map.114.first), channel_id=1, source_target_pairs={{0,1},{1,0},{2,3},{3,2},{4,5},{5,4},{6,7},{7,6},{8,9},{9,8},{10,11... | collective-permute-start | bytes 786440 | tf_op jit(solution)/shard_map/ppermute | solution.py:31
  27.9 13.1 %collective-permute-start.6 = (bf16[256,128]{1,0:T(8,128)(2,1)S(1)}, bf16[256,128]{1,0:T(8,128)(2,1)S(1)}, u32[]{:S(2)}, u32[]{:S(2)}) collective-permute-start(bf16[256,128]{1,0:T(8,128)(2,1)S(1)} %get-tuple-element.49), channel_id=1, source_target_pairs={{0,64},{32,96},{64,0},{96,32},{1,65},{33,97},{65,1},{97,33},{2,66}... | collective-permute-start | bytes 196616 | tf_op jit(solution)/shard_map/ppermute | solution.py:27
  34.7 6.4 %collective-permute-start.7 = (bf16[256,128]{1,0:T(8,128)(2,1)S(1)}, bf16[256,128]{1,0:T(8,128)(2,1)S(1)}, u32[]{:S(2)}, u32[]{:S(2)}) collective-permute-start(bf16[256,128]{1,0:T(8,128)(2,1)S(1)} %get-tuple-element.50), channel_id=1, source_target_pairs={{0,32},{32,64},{64,96},{96,0},{1,33},{33,65},{65,97},{97,1},{2,34}... | collective-permute-start | bytes 196616 | tf_op jit(solution)/shard_map/ppermute | solution.py:27
  38.4 5.3 %collective-permute-start.8 = (bf16[256,128]{1,0:T(8,128)(2,1)S(1)}, bf16[256,128]{1,0:T(8,128)(2,1)S(1)}, u32[]{:S(2)}, u32[]{:S(2)}) collective-permute-start(bf16[256,128]{1,0:T(8,128)(2,1)S(1)} %get-tuple-element.51), channel_id=1, source_target_pairs={{0,96},{32,0},{64,32},{96,64},{1,97},{33,1},{65,33},{97,65},{2,98}... | collective-permute-start | bytes 196616 | tf_op jit(solution)/shard_map/ppermute | solution.py:27
  38.8 4.9 %copy-start = (bf16[256,128]{1,0:T(8,128)(2,1)S(1)}, bf16[256,128]{1,0:T(8,128)(2,1)}, u32[]{:S(2)}) copy-start(bf16[256,128]{1,0:T(8,128)(2,1)} %weight.1) | copy-start | bytes 196612
  43.8 13.9 %collective-permute-start.13 = (bf16[4,64,1024]{2,1,0:T(8,128)(2,1)S(1)}, bf16[4,64,1024]{2,1,0:T(8,128)(2,1)S(1)}, u32[]{:S(2)}, u32[]{:S(2)}) collective-permute-start(bf16[4,64,1024]{2,1,0:T(8,128)(2,1)S(1)} %shard_map.119.near), channel_id=1, source_target_pairs={{0,3},{1,2},{2,1},{3,0},{4,7},{5,6},{6,5},{7,4},{8,11},{9,10},{10,... | collective-permute-start | bytes 1572872 | tf_op jit(solution)/shard_map/ppermute | solution.py:31
  45.7 6.2 %collective-permute-start.12 = (bf16[256,128]{1,0:T(8,128)(2,1)S(1)}, bf16[256,128]{1,0:T(8,128)(2,1)S(1)}, u32[]{:S(2)}, u32[]{:S(2)}) collective-permute-start(bf16[256,128]{1,0:T(8,128)(2,1)S(1)} %shard_map.117), channel_id=1, source_target_pairs={{0,8},{8,16},{16,24},{24,0},{1,9},{9,17},{17,25},{25,1},{2,10},{10... | collective-permute-start | bytes 196616 | tf_op jit(solution)/shard_map/ppermute | solution.py:27
  47.2 5.8 %collective-permute-start.11 = (bf16[256,128]{1,0:T(8,128)(2,1)S(1)}, bf16[256,128]{1,0:T(8,128)(2,1)S(1)}, u32[]{:S(2)}, u32[]{:S(2)}) collective-permute-start(bf16[256,128]{1,0:T(8,128)(2,1)S(1)} %shard_map.117), channel_id=1, source_target_pairs={{0,16},{8,24},{16,0},{24,8},{1,17},{9,25},{17,1},{25,9},{2,18},{10... | collective-permute-start | bytes 196616 | tf_op jit(solution)/shard_map/ppermute | solution.py:27
  49.9 4.3 %collective-permute-start.10 = (bf16[256,128]{1,0:T(8,128)(2,1)S(1)}, bf16[256,128]{1,0:T(8,128)(2,1)S(1)}, u32[]{:S(2)}, u32[]{:S(2)}) collective-permute-start(bf16[256,128]{1,0:T(8,128)(2,1)S(1)} %shard_map.117), channel_id=1, source_target_pairs={{0,24},{8,0},{16,8},{24,16},{1,25},{9,1},{17,9},{25,17},{2,26},{10... | collective-permute-start | bytes 196616 | tf_op jit(solution)/shard_map/ppermute | solution.py:27
  54.2 1.6 %collective-permute-start.14 = (bf16[4,256,128]{2,1,0:T(8,128)(2,1)S(1)}, bf16[4,256,128]{2,1,0:T(8,128)(2,1)S(1)}, u32[]{:S(2)}, u32[]{:S(2)}) collective-permute-start(bf16[4,256,128]{2,1,0:T(8,128)(2,1)S(1)} %pad_maximum_fusion.u.u_own), channel_id=1, source_target_pairs={{0,128},{128,0},{1,129},{129,1},{2,130},{130,2},{3,131},{131,3},{4... | collective-permute-start | bytes 786440 | tf_op jit(solution)/shard_map/ppermute | solution.py:27

commit v14 on v13

--- a/solution.py
+++ b/solution.py
@@ -85,7 +85,7 @@
     )(place, normed_inputs, value_cotangent)
 
 
-def small_call(kernel, outs, *args, keep=True):
+def small_call(kernel, outs, *args, keep=True, flops=MIB):
     return pl.pallas_call(
         kernel,
         in_specs=[VMEM] * len(args),
@@ -94,7 +94,7 @@
             (pltpu.VMEM if keep else jax.ShapeDtypeStruct)(shape, dtype) for shape, dtype in outs
         ],
         compiler_params=pltpu.CompilerParams(vmem_limit_bytes=16 * MIB),
-        cost_estimate=pl.CostEstimate(flops=MIB, bytes_accessed=2 * MIB, transcendentals=0),
+        cost_estimate=pl.CostEstimate(flops=flops, bytes_accessed=2 * MIB, transcendentals=0),
     )(*args)
 
 
@@ -302,21 +302,21 @@
     own, *along_x, both = lax.optimization_barrier((own, *along_x, both))
     rows = (256, HD)
     own, *sent = small_call(
-        x_sum_kernel, [(rows, F32)] + [(rows, BF16)] * 3, own, *along_x
+        x_sum_kernel, [(rows, F32)] + [(rows, BF16)] * 3, own, *along_x, flops=8000 * MIB
     )
     along_z = [shift(sent[e - 1], "zh", e) for e in (2, 1, 3)]
+    (near,) = small_call(pair_kernel, [((4, places, D // 8), BF16)], after(both, own), near)
+    far = exchange(near, "y", 3)
     attended_cache, fresh_weights = attend_cache(
-        lengths, after(queries, own), new_keys.reshape(places, HD), cache_keys, cache_values
-    )
-    own, *along_z, near, attended_cache, fresh_weights = lax.optimization_barrier(
-        (own, *along_z, near, attended_cache, fresh_weights)
+        lengths, after(queries, near), new_keys.reshape(places, HD), cache_keys, cache_values
+    )
+    own, *along_z, attended_cache, fresh_weights = lax.optimization_barrier(
+        (own, *along_z, attended_cache, fresh_weights)
     )
     (updated,) = small_call(update_kernel, [(rows, BF16)], value_weight, own, *along_z)
     own = after(own, updated)
     (gradient,) = small_call(gradient_kernel, [(rows, F32)], own, *along_z, keep=False)
 
-    (near,) = small_call(pair_kernel, [((4, places, D // 8), BF16)], after(both, updated), near)
-    far = exchange(near, "y", 3)
     gathered = jnp.stack([updated] + [shift(updated, "x", -d) for d in (1, 2, 3)])
     gathered, gradient = lax.optimization_barrier((gathered, gradient))
     other = shift(gathered, "c", 1)

time: 72.6 us -> 69.2 us (0.953)
  waiting for transfers between devices: 15.1 us -> 10.2 us
  starting transfers between devices: 31.6 us -> 33.8 us
  blocking collectives: 13 us -> 11.6 us
    ppermute x12, waiting for transfers between devices: 13.2 us -> 10.2 us  [shift(): return lax.ppermute(value, axis, [(i, (i + by) % n) for i in range(n)])]
    ppermute x2, waiting for transfers between devices: 1.86 us -> 0.01 us  [exchange(): return lax.ppermute(value, axis, [(i, i ^ bit) for i in range(SIZES[axis])])]
    ppermute x2, starting transfers between devices: 8.09 us -> 9.73 us  [exchange(): return lax.ppermute(value, axis, [(i, i ^ bit) for i in range(SIZES[axis])])]
    all_to_all x1, blocking collectives: 13 us -> 11.6 us  [shards(): exchanged = lax.all_to_all(partial, 'zh', 0, 0, tiled=True)]
  transfers between devices with their start and end apart: 15 -> 15, of which waited for: 8 -> 5; matrix products, arithmetic and copies ran while one was open for 0% -> 0% of each run, Pallas kernels for 6% -> 6%
where the time goes in v14:
time: 69.2 us; the launch traced here: 68.4 us
  starting transfers between devices  33.8 us (49%)
  Pallas kernels  11.8 us (17%)
  blocking collectives  11.6 us (17%)
  waiting for transfers between devices  10.2 us (15%)
  between operations  0.84 us (1%)
    ppermute x12, starting transfers between devices, shift(): return lax.ppermute(value, axis, [(i, (i + by) % n) for i in range(n)])  23.4 us
    all_to_all x1, blocking collectives, shards(): exchanged = lax.all_to_all(partial, 'zh', 0, 0, tiled=True)  11.6 us
    ppermute x12, waiting for transfers between devices, shift(): return lax.ppermute(value, axis, [(i, (i + by) % n) for i in range(n)])  10.2 us
    ppermute x2, starting transfers between devices, exchange(): return lax.ppermute(value, axis, [(i, i ^ bit) for i in range(SIZES[axis])])  9.73 us
    pallas_call x1, Pallas kernels, partial_gradient(): pl.pallas_call(partial_kernel, in_specs=[SMEM, HBM, HBM], out_specs=[VMEM...  5.96 us
    pallas_call x1, Pallas kernels, attend_cache(): pl.pallas_call(attend_kernel, in_specs=[SMEM] + [VMEM] * 4, out_specs=[VM...  2.15 us
    pallas_call x2, Pallas kernels, project(): pl.pallas_call(kernel, in_specs=[SMEM] + [VMEM] * len(args), out_specs=VM...  1.72 us
  transfers between devices with their start and end apart: 15, of which 5 were waited for; matrix products, arithmetic and copies ran while one was open for 0% of the time, Pallas kernels for 6%

profile of v14, /device:TPU:32, one launch (start us, length us, event | category | flops | bytes accessed | tf_op | source)
XLA Modules:
  0.0 68.4 jit_solution(17587021890659718464)
XLA Ops:
  0.7 6.0 %shard_map.112 = (bf16[4,4,256,128]{3,2,1,0:T(8,128)(2,1)S(1)}, bf16[4,4,256,128]{3,2,1,0:T(8,128)(2,1)S(1)}) custom-call(s32[5]{0:T(128)S(1)} %stack.38.place, bf16[768,8192]{1,0:T(8,128)(2,1)} %x_hbm.1, bf16[768,128]{1,0:T(8,128)(2,1)} %v_hbm.1), custom_call_target="tpu_custom_call" | custom-call | flops 1610612736 | bytes 12582912 | tf_op jit(solution)/shard_map/pallas_call | solution.py:71
  6.8 0.7 collective-permute-start.4
  7.5 2.0 %collective-permute-done.received = bf16[4,4,256,128]{3,2,1,0:T(8,128)(2,1)S(1)} collective-permute-done((bf16[4,4,256,128]{3,2,1,0:T(8,128)(2,1)S(1)}, bf16[4,4,256,128]{3,2,1,0:T(8,128)(2,1)S(1)}, u32[]{:S(2)}, u32[]{:S(2)}) %collective-permute-start) | collective-permute-done | bytes 1048608 | tf_op jit(solution)/shard_map/ppermute | solution.py:27
  9.7 3.1 %collective-permute-start.1 = (bf16[4,256,128]{2,1,0:T(8,128)(2,1)S(1)}, bf16[4,256,128]{2,1,0:T(8,128)(2,1)S(1)}, u32[]{:S(2)}, u32[]{:S(2)}) collective-permute-start(bf16[4,256,128]{2,1,0:T(8,128)(2,1)S(1)} %get-tuple-element.38), channel_id=1, source_target_pairs={{0,16},{8,24},{16,0},{24,8},{1,17},{9,25},{17,1},{25,9},{2,18},{10... | collective-permute-start | bytes 786440 | tf_op jit(solution)/shard_map/ppermute | solution.py:27
  12.8 0.6 collective-permute-start.2
  13.4 2.6 %collective-permute-start.3 = (bf16[4,256,128]{2,1,0:T(8,128)(2,1)S(1)}, bf16[4,256,128]{2,1,0:T(8,128)(2,1)S(1)}, u32[]{:S(2)}, u32[]{:S(2)}) collective-permute-start(bf16[4,256,128]{2,1,0:T(8,128)(2,1)S(1)} %get-tuple-element.40), channel_id=1, source_target_pairs={{0,24},{8,0},{16,8},{24,16},{1,25},{9,1},{17,9},{25,17},{2,26},{10... | collective-permute-start | bytes 786440 | tf_op jit(solution)/shard_map/ppermute | solution.py:27
  16.1 5.3 %collective-permute-done.5.second = bf16[16,4,1024]{2,1,0:T(4,128)(2,1)S(1)} collective-permute-done((bf16[16,4,1024]{2,1,0:T(4,128)(2,1)S(1)}, bf16[16,4,1024]{2,1,0:T(4,128)(2,1)S(1)}, u32[]{:S(2)}, u32[]{:S(2)}) %collective-permute-start.5) | collective-permute-done | bytes 131104 | tf_op jit(solution)/shard_map/ppermute | solution.py:27
  21.6 6.2 %collective-permute-start.9 = (bf16[2,64,1024]{2,1,0:T(8,128)(2,1)S(1)}, bf16[2,64,1024]{2,1,0:T(8,128)(2,1)S(1)}, u32[]{:S(2)}, u32[]{:S(2)}) collective-permute-start(bf16[2,64,1024]{2,1,0:T(8,128)(2,1)S(1)} %shard_map.114.first), channel_id=1, source_target_pairs={{0,1},{1,0},{2,3},{3,2},{4,5},{5,4},{6,7},{7,6},{8,9},{9,8},{10,11... | collective-permute-start | bytes 786440 | tf_op jit(solution)/shard_map/ppermute | solution.py:31
  27.9 6.7 %collective-permute-start.6 = (bf16[256,128]{1,0:T(8,128)(2,1)S(1)}, bf16[256,128]{1,0:T(8,128)(2,1)S(1)}, u32[]{:S(2)}, u32[]{:S(2)}) collective-permute-start(bf16[256,128]{1,0:T(8,128)(2,1)S(1)} %get-tuple-element.48), channel_id=1, source_target_pairs={{0,64},{32,96},{64,0},{96,32},{1,65},{33,97},{65,1},{97,33},{2,66}... | collective-permute-start | bytes 196616 | tf_op jit(solution)/shard_map/ppermute | solution.py:27
  34.7 3.7 %collective-permute-start.7 = (bf16[256,128]{1,0:T(8,128)(2,1)S(1)}, bf16[256,128]{1,0:T(8,128)(2,1)S(1)}, u32[]{:S(2)}, u32[]{:S(2)}) collective-permute-start(bf16[256,128]{1,0:T(8,128)(2,1)S(1)} %get-tuple-element.49), channel_id=1, source_target_pairs={{0,32},{32,64},{64,96},{96,0},{1,33},{33,65},{65,97},{97,1},{2,34}... | collective-permute-start | bytes 196616 | tf_op jit(solution)/shard_map/ppermute | solution.py:27
  38.4 0.4 collective-permute-start.8
  38.9 3.5 %collective-permute-start.13 = (bf16[4,64,1024]{2,1,0:T(8,128)(2,1)S(1)}, bf16[4,64,1024]{2,1,0:T(8,128)(2,1)S(1)}, u32[]{:S(2)}, u32[]{:S(2)}) collective-permute-start(bf16[4,64,1024]{2,1,0:T(8,128)(2,1)S(1)} %shard_map.116.near), channel_id=1, source_target_pairs={{0,3},{1,2},{2,1},{3,0},{4,7},{5,6},{6,5},{7,4},{8,11},{9,10},{10,... | collective-permute-start | bytes 1572872 | tf_op jit(solution)/shard_map/ppermute | solution.py:31
  42.4 2.1 %shard_map.117 = (f32[512,128]{1,0:T(8,128)S(1)}, bf16[512,64]{1,0:T(8,128)(2,1)S(1)}) custom-call(s32[16]{0:T(128)S(1)} %copy-done.5, bf16[16,4,1024]{2,1,0:T(4,128)(2,1)S(1)} %copy-done.3, bf16[64,128]{1,0:T(8,128)(2,1)S(1)} %bitcast.11, bf16[16,128,128]{2,1,0:T(8,128)(2,1)S(1)} %copy-done.1, bf16[16,128,128]{2,1,0:T(8,128)(2,1)S(1)} %copy-done.2), custom_call_target="tpu_custom_call" | custom-call | flops 8388608000 | bytes 20971520 | tf_op jit(solution)/shard_map/pallas_call | solution.py:178
  44.6 1.7 %collective-permute-start.12 = (bf16[256,128]{1,0:T(8,128)(2,1)S(1)}, bf16[256,128]{1,0:T(8,128)(2,1)S(1)}, u32[]{:S(2)}, u32[]{:S(2)}) collective-permute-start(bf16[256,128]{1,0:T(8,128)(2,1)S(1)} %shard_map.118), channel_id=1, source_target_pairs={{0,8},{8,16},{16,24},{24,0},{1,9},{9,17},{17,25},{25,1},{2,10},{10... | collective-permute-start | bytes 196616 | tf_op jit(solution)/shard_map/ppermute | solution.py:27
  46.4 2.7 %collective-permute-start.11 = (bf16[256,128]{1,0:T(8,128)(2,1)S(1)}, bf16[256,128]{1,0:T(8,128)(2,1)S(1)}, u32[]{:S(2)}, u32[]{:S(2)}) collective-permute-start(bf16[256,128]{1,0:T(8,128)(2,1)S(1)} %shard_map.118), channel_id=1, source_target_pairs={{0,16},{8,24},{16,0},{24,8},{1,17},{9,25},{17,1},{25,9},{2,18},{10... | collective-permute-start | bytes 196616 | tf_op jit(solution)/shard_map/ppermute | solution.py:27
  49.1 1.4 %collective-permute-start.10 = (bf16[256,128]{1,0:T(8,128)(2,1)S(1)}, bf16[256,128]{1,0:T(8,128)(2,1)S(1)}, u32[]{:S(2)}, u32[]{:S(2)}) collective-permute-start(bf16[256,128]{1,0:T(8,128)(2,1)S(1)} %shard_map.118), channel_id=1, source_target_pairs={{0,24},{8,0},{16,8},{24,16},{1,25},{9,1},{17,9},{25,17},{2,26},{10... | collective-permute-start | bytes 196616 | tf_op jit(solution)/shard_map/ppermute | solution.py:27
  50.6 0.7 shard_map.119
  51.2 0.9 %collective-permute-done.11 = bf16[256,128]{1,0:T(8,128)(2,1)S(1)} collective-permute-done((bf16[256,128]{1,0:T(8,128)(2,1)S(1)}, bf16[256,128]{1,0:T(8,128)(2,1)S(1)}, u32[]{:S(2)}, u32[]{:S(2)}) %collective-permute-start.11) | collective-permute-done | bytes 65568 | tf_op jit(solution)/shard_map/ppermute | solution.py:27
  52.2 1.2 %collective-permute-done.10 = bf16[256,128]{1,0:T(8,128)(2,1)S(1)} collective-permute-done((bf16[256,128]{1,0:T(8,128)(2,1)S(1)}, bf16[256,128]{1,0:T(8,128)(2,1)S(1)}, u32[]{:S(2)}, u32[]{:S(2)}) %collective-permute-start.10) | collective-permute-done | bytes 65568 | tf_op jit(solution)/shard_map/ppermute | solution.py:27
  53.5 0.8 %shard_map.120.start = f32[128,128]{1,0:T(8,128)S(1)} custom-call(s32[5]{0:T(128)S(1)} %stack.38.place, bf16[4,64,1024]{2,1,0:T(8,128)(2,1)S(1)} %shard_map.116.near, bf16[4,256,128]{2,1,0:T(8,128)(2,1)S(1)} %pad_maximum_fusion.u.u_own), custom_call_target="tpu_custom_call" | custom-call | flops 67108864 | bytes 786432 | tf_op jit(solution)/shard_map/pallas_call | solution.py:228
  54.3 0.7 %collective-permute-done.14.u_other = bf16[4,256,128]{2,1,0:T(8,128)(2,1)S(1)} collective-permute-done((bf16[4,256,128]{2,1,0:T(8,128)(2,1)S(1)}, bf16[4,256,128]{2,1,0:T(8,128)(2,1)S(1)}, u32[]{:S(2)}, u32[]{:S(2)}) %collective-permute-start.14) | collective-permute-done | bytes 262176 | tf_op jit(solution)/shard_map/ppermute | solution.py:27
  55.1 0.9 %shard_map.121 = bf16[4,64,128]{2,1,0:T(8,128)(2,1)S(1)} custom-call(s32[5]{0:T(128)S(1)} %stack.38.place, bf16[4,64,1024]{2,1,0:T(8,128)(2,1)S(1)} %shard_map.116.near, bf16[4,64,1024]{2,1,0:T(8,128)(2,1)S(1)} %collective-permute-done.13.far, bf16[4,256,128]{2,1,0:T(8,128)(2,1)S(1)} %pad_maximum_fusion.u.u_own, ...), custom_call_target="tpu_custom_call" | custom-call | flops 67108864 | bytes 786432 | tf_op jit(solution)/shard_map/pallas_call | solution.py:228
  56.0 11.6 %all_to_all.5.parts = bf16[4,64,128]{2,1,0:T(8,128)(2,1)S(1)} all-to-all(bf16[4,64,128]{2,1,0:T(8,128)(2,1)S(1)} %shard_map.121), channel_id=1, replica_groups=mesh['c'=2,'zh'=4,'x'=4,'zl'=2,'y'=4] {'zh'}, dimensions={0} | all-to-all | bytes 131072 | tf_op jit(solution)/shard_map/all_to_all | solution.py:337
  67.6 0.8 %shard_map.122 = (bf16[16,4,128]{2,1,0:T(4,128)(2,1)}, bf16[16,4,1024]{2,1,0:T(4,128)(2,1)}) custom-call(bf16[4,64,128]{2,1,0:T(8,128)(2,1)S(1)} %all_to_all.5.parts, f32[512,128]{1,0:T(8,128)S(1)} %get-tuple-element.63.mixed, bf16[512,64]{1,0:T(8,128)(2,1)S(1)} %get-tuple-element.64.weights), custom_call_target="tpu_custom_call" | custom-call | tf_op jit(solution)/shard_map/pallas_call | solution.py:259
  (34 shorter events, 1.0 us)
Async XLA Ops:
  0.6 6.2 %copy-start.6 = (bf16[16,4,1024]{2,1,0:T(4,128)(2,1)S(1)}, bf16[16,4,1024]{2,1,0:T(4,128)(2,1)}, u32[]{:S(2)}) copy-start(bf16[16,4,1024]{2,1,0:T(4,128)(2,1)} %param.12) | copy-start | bytes 393220
  6.7 2.7 %collective-permute-start = (bf16[4,4,256,128]{3,2,1,0:T(8,128)(2,1)S(1)}, bf16[4,4,256,128]{3,2,1,0:T(8,128)(2,1)S(1)}, u32[]{:S(2)}, u32[]{:S(2)}) collective-permute-start(bf16[4,4,256,128]{3,2,1,0:T(8,128)(2,1)S(1)} %get-tuple-element.36), channel_id=1, source_target_pairs={{0,128},{128,0},{1,129},{129,1},{2,130},{130,2},{3,131},{131,3},{4... | collective-permute-start | bytes 3145736 | tf_op jit(solution)/shard_map/ppermute | solution.py:27
  6.8 9.2 %collective-permute-start.4 = (bf16[16,4,1024]{2,1,0:T(4,128)(2,1)S(1)}, bf16[16,4,1024]{2,1,0:T(4,128)(2,1)S(1)}, u32[]{:S(2)}, u32[]{:S(2)}) collective-permute-start(bf16[16,4,1024]{2,1,0:T(4,128)(2,1)S(1)} %copy-done.6), channel_id=1, source_target_pairs={{0,0},{1,33},{2,66},{3,99},{32,1},{33,34},{34,67},{35,96},{64,2},{... | collective-permute-start | bytes 393224 | tf_op jit(solution)/shard_map/ppermute | solution.py:36
  9.7 18.1 %collective-permute-start.1 = (bf16[4,256,128]{2,1,0:T(8,128)(2,1)S(1)}, bf16[4,256,128]{2,1,0:T(8,128)(2,1)S(1)}, u32[]{:S(2)}, u32[]{:S(2)}) collective-permute-start(bf16[4,256,128]{2,1,0:T(8,128)(2,1)S(1)} %get-tuple-element.38), channel_id=1, source_target_pairs={{0,16},{8,24},{16,0},{24,8},{1,17},{9,25},{17,1},{25,9},{2,18},{10... | collective-permute-start | bytes 786440 | tf_op jit(solution)/shard_map/ppermute | solution.py:27
  12.8 15.0 %collective-permute-start.2 = (bf16[4,256,128]{2,1,0:T(8,128)(2,1)S(1)}, bf16[4,256,128]{2,1,0:T(8,128)(2,1)S(1)}, u32[]{:S(2)}, u32[]{:S(2)}) collective-permute-start(bf16[4,256,128]{2,1,0:T(8,128)(2,1)S(1)} %get-tuple-element.39), channel_id=1, source_target_pairs={{0,8},{8,16},{16,24},{24,0},{1,9},{9,17},{17,25},{25,1},{2,10},{10... | collective-permute-start | bytes 786440 | tf_op jit(solution)/shard_map/ppermute | solution.py:27
  13.4 14.5 %collective-permute-start.3 = (bf16[4,256,128]{2,1,0:T(8,128)(2,1)S(1)}, bf16[4,256,128]{2,1,0:T(8,128)(2,1)S(1)}, u32[]{:S(2)}, u32[]{:S(2)}) collective-permute-start(bf16[4,256,128]{2,1,0:T(8,128)(2,1)S(1)} %get-tuple-element.40), channel_id=1, source_target_pairs={{0,24},{8,0},{16,8},{24,16},{1,25},{9,1},{17,9},{25,17},{2,26},{10... | collective-permute-start | bytes 786440 | tf_op jit(solution)/shard_map/ppermute | solution.py:27
  16.0 5.4 %collective-permute-start.5 = (bf16[16,4,1024]{2,1,0:T(4,128)(2,1)S(1)}, bf16[16,4,1024]{2,1,0:T(4,128)(2,1)S(1)}, u32[]{:S(2)}, u32[]{:S(2)}) collective-permute-start(bf16[16,4,1024]{2,1,0:T(4,128)(2,1)S(1)} %collective-permute-done.4.first), channel_id=1, source_target_pairs={{0,4},{4,0},{1,5},{5,1},{2,6},{6,2},{3,7},{7,3},{8,12},{12,8},{9,1... | collective-permute-start | bytes 393224 | tf_op jit(solution)/shard_map/ppermute | solution.py:27
  21.5 20.8 %copy-start.1 = (bf16[16,128,128]{2,1,0:T(8,128)(2,1)S(1)}, bf16[16,128,128]{2,1,0:T(8,128)(2,1)}, u32[]{:S(2)}) copy-start(bf16[16,128,128]{2,1,0:T(8,128)(2,1)} %cache_keys.1) | copy-start | bytes 1572868
  21.5 20.8 %copy-start.2 = (bf16[16,128,128]{2,1,0:T(8,128)(2,1)S(1)}, bf16[16,128,128]{2,1,0:T(8,128)(2,1)}, u32[]{:S(2)}) copy-start(bf16[16,128,128]{2,1,0:T(8,128)(2,1)} %cache_values.1) | copy-start | bytes 1572868
  21.5 20.8 %copy-start.3 = (bf16[16,4,1024]{2,1,0:T(4,128)(2,1)S(1)}, bf16[16,4,1024]{2,1,0:T(4,128)(2,1)}, u32[]{:S(2)}) copy-start(bf16[16,4,1024]{2,1,0:T(4,128)(2,1)} %raw_queries) | copy-start | bytes 393220
  21.6 20.8 %copy-start.4 = (bf16[16,4,128]{2,1,0:T(4,128)(2,1)S(1)}, bf16[16,4,128]{2,1,0:T(4,128)(2,1)}, u32[]{:S(2)}) copy-start(bf16[16,4,128]{2,1,0:T(4,128)(2,1)} %param.14) | copy-start | bytes 49156
  21.6 20.8 %copy-start.5 = (s32[16]{0:T(128)S(1)}, s32[16]{0:T(128)}, u32[]{:S(2)}) copy-start(s32[16]{0:T(128)} %lengths.1) | copy-start | bytes 196
  21.6 17.2 %collective-permute-start.9 = (bf16[2,64,1024]{2,1,0:T(8,128)(2,1)S(1)}, bf16[2,64,1024]{2,1,0:T(8,128)(2,1)S(1)}, u32[]{:S(2)}, u32[]{:S(2)}) collective-permute-start(bf16[2,64,1024]{2,1,0:T(8,128)(2,1)S(1)} %shard_map.114.first), channel_id=1, source_target_pairs={{0,1},{1,0},{2,3},{3,2},{4,5},{5,4},{6,7},{7,6},{8,9},{9,8},{10,11... | collective-permute-start | bytes 786440 | tf_op jit(solution)/shard_map/ppermute | solution.py:31
  27.9 16.6 %collective-permute-start.6 = (bf16[256,128]{1,0:T(8,128)(2,1)S(1)}, bf16[256,128]{1,0:T(8,128)(2,1)S(1)}, u32[]{:S(2)}, u32[]{:S(2)}) collective-permute-start(bf16[256,128]{1,0:T(8,128)(2,1)S(1)} %get-tuple-element.48), channel_id=1, source_target_pairs={{0,64},{32,96},{64,0},{96,32},{1,65},{33,97},{65,1},{97,33},{2,66}... | collective-permute-start | bytes 196616 | tf_op jit(solution)/shard_map/ppermute | solution.py:27
  34.7 9.9 %collective-permute-start.7 = (bf16[256,128]{1,0:T(8,128)(2,1)S(1)}, bf16[256,128]{1,0:T(8,128)(2,1)S(1)}, u32[]{:S(2)}, u32[]{:S(2)}) collective-permute-start(bf16[256,128]{1,0:T(8,128)(2,1)S(1)} %get-tuple-element.49), channel_id=1, source_target_pairs={{0,32},{32,64},{64,96},{96,0},{1,33},{33,65},{65,97},{97,1},{2,34}... | collective-permute-start | bytes 196616 | tf_op jit(solution)/shard_map/ppermute | solution.py:27
  38.4 6.2 %collective-permute-start.8 = (bf16[256,128]{1,0:T(8,128)(2,1)S(1)}, bf16[256,128]{1,0:T(8,128)(2,1)S(1)}, u32[]{:S(2)}, u32[]{:S(2)}) collective-permute-start(bf16[256,128]{1,0:T(8,128)(2,1)S(1)} %get-tuple-element.50), channel_id=1, source_target_pairs={{0,96},{32,0},{64,32},{96,64},{1,97},{33,1},{65,33},{97,65},{2,98}... | collective-permute-start | bytes 196616 | tf_op jit(solution)/shard_map/ppermute | solution.py:27
  38.9 16.2 %collective-permute-start.13 = (bf16[4,64,1024]{2,1,0:T(8,128)(2,1)S(1)}, bf16[4,64,1024]{2,1,0:T(8,128)(2,1)S(1)}, u32[]{:S(2)}, u32[]{:S(2)}) collective-permute-start(bf16[4,64,1024]{2,1,0:T(8,128)(2,1)S(1)} %shard_map.116.near), channel_id=1, source_target_pairs={{0,3},{1,2},{2,1},{3,0},{4,7},{5,6},{6,5},{7,4},{8,11},{9,10},{10,... | collective-permute-start | bytes 1572872 | tf_op jit(solution)/shard_map/ppermute | solution.py:31
  42.4 2.2 %copy-start = (bf16[256,128]{1,0:T(8,128)(2,1)S(1)}, bf16[256,128]{1,0:T(8,128)(2,1)}, u32[]{:S(2)}) copy-start(bf16[256,128]{1,0:T(8,128)(2,1)} %weight.1) | copy-start | bytes 196612
  44.6 6.6 %collective-permute-start.12 = (bf16[256,128]{1,0:T(8,128)(2,1)S(1)}, bf16[256,128]{1,0:T(8,128)(2,1)S(1)}, u32[]{:S(2)}, u32[]{:S(2)}) collective-permute-start(bf16[256,128]{1,0:T(8,128)(2,1)S(1)} %shard_map.118), channel_id=1, source_target_pairs={{0,8},{8,16},{16,24},{24,0},{1,9},{9,17},{17,25},{25,1},{2,10},{10... | collective-permute-start | bytes 196616 | tf_op jit(solution)/shard_map/ppermute | solution.py:27
  46.4 5.8 %collective-permute-start.11 = (bf16[256,128]{1,0:T(8,128)(2,1)S(1)}, bf16[256,128]{1,0:T(8,128)(2,1)S(1)}, u32[]{:S(2)}, u32[]{:S(2)}) collective-permute-start(bf16[256,128]{1,0:T(8,128)(2,1)S(1)} %shard_map.118), channel_id=1, source_target_pairs={{0,16},{8,24},{16,0},{24,8},{1,17},{9,25},{17,1},{25,9},{2,18},{10... | collective-permute-start | bytes 196616 | tf_op jit(solution)/shard_map/ppermute | solution.py:27
  49.1 4.3 %collective-permute-start.10 = (bf16[256,128]{1,0:T(8,128)(2,1)S(1)}, bf16[256,128]{1,0:T(8,128)(2,1)S(1)}, u32[]{:S(2)}, u32[]{:S(2)}) collective-permute-start(bf16[256,128]{1,0:T(8,128)(2,1)S(1)} %shard_map.118), channel_id=1, source_target_pairs={{0,24},{8,0},{16,8},{24,16},{1,25},{9,1},{17,9},{25,17},{2,26},{10... | collective-permute-start | bytes 196616 | tf_op jit(solution)/shard_map/ppermute | solution.py:27
  53.4 1.6 %collective-permute-start.14 = (bf16[4,256,128]{2,1,0:T(8,128)(2,1)S(1)}, bf16[4,256,128]{2,1,0:T(8,128)(2,1)S(1)}, u32[]{:S(2)}, u32[]{:S(2)}) collective-permute-start(bf16[4,256,128]{2,1,0:T(8,128)(2,1)S(1)} %pad_maximum_fusion.u.u_own), channel_id=1, source_target_pairs={{0,128},{128,0},{1,129},{129,1},{2,130},{130,2},{3,131},{131,3},{4... | collective-permute-start | bytes 786440 | tf_op jit(solution)/shard_map/ppermute | solution.py:27

commit v15 on v14

--- a/solution.py
+++ b/solution.py
@@ -186,7 +186,7 @@
         scratch_shapes=[pltpu.VMEM((places, HEADS * HD), BF16)],
         compiler_params=pltpu.CompilerParams(vmem_limit_bytes=16 * MIB),
         cost_estimate=pl.CostEstimate(
-            flops=8000 * MIB, bytes_accessed=20 * MIB, transcendentals=0
+            flops=1 * MIB, bytes_accessed=MIB // 4, transcendentals=0
         ),
     )(lengths, queries, new_keys, cache_keys, cache_values)
 
@@ -200,21 +200,39 @@
     return lax.rem(jnp.bitwise_xor(place[3], bits) + 4 - place[1], 4)
 
 
-def project_own_kernel(place, near, u, out_ref, rows):
+def arrange_kernel(place, near, own_ref, rest_ref):
     own = jnp.where(place[0] == place[4], 0, 1)
+    size = near.shape[1]
+    for i in range(2):
+        own_ref[i * size : (i + 1) * size] = near[2 * i + own]
+        rest_ref[i * size : (i + 1) * size] = near[2 * i + 1 - own]
+
+
+def arrange(place, near):
+    shape = jax.ShapeDtypeStruct((2 * near.shape[1], near.shape[2]), BF16)
+    return pl.pallas_call(
+        arrange_kernel,
+        in_specs=[SMEM, VMEM],
+        out_specs=[VMEM, VMEM],
+        out_shape=[shape, shape],
+        compiler_params=pltpu.CompilerParams(vmem_limit_bytes=16 * MIB),
+        cost_estimate=pl.CostEstimate(
+            flops=8000 * MIB, bytes_accessed=2 * MIB, transcendentals=0
+        ),
+    )(place, near)
+
+
+def project_own_kernel(place, inputs, u, out_ref, rows):
     fill_rows(rows, place[2], u)
-    inputs = jnp.concatenate([near[own], near[2 + own]], axis=0)
-    out_ref[...] = jnp.dot(inputs, rows[...], preferred_element_type=F32)
+    out_ref[...] = jnp.dot(inputs[...], rows[...], preferred_element_type=F32)
 
 
 def project_rest_kernel(place, near, far, u_own, u_other, start, out_ref, rows, last):
     own = jnp.where(place[0] == place[4], 0, 1)
     fill_rows(last, place[2], u_own)
     fill_rows(rows, place[2], u_other)
-    inputs = [near[1 - own], near[3 - own], far[1 - own], far[3 - own]]
-    product = jnp.dot(
-        jnp.concatenate(inputs, axis=0), rows[...], preferred_element_type=F32
-    )
+    inputs = jnp.concatenate([near[...], far[1 - own], far[3 - own]], axis=0)
+    product = jnp.dot(inputs, rows[...], preferred_element_type=F32)
     inputs = jnp.concatenate([far[own], far[2 + own]], axis=0)
     more = jnp.dot(inputs, last[...], preferred_element_type=F32)
     size = far.shape[1]
@@ -299,7 +317,12 @@
     )
     near = exchange(both, "y", 1)
 
-    own, *along_x, both = lax.optimization_barrier((own, *along_x, both))
+    attended_cache, fresh_weights = attend_cache(
+        lengths, after(queries, own), new_keys.reshape(places, HD), cache_keys, cache_values
+    )
+    own, *along_x, both, attended_cache, fresh_weights = lax.optimization_barrier(
+        (own, *along_x, both, attended_cache, fresh_weights)
+    )
     rows = (256, HD)
     own, *sent = small_call(
         x_sum_kernel, [(rows, F32)] + [(rows, BF16)] * 3, own, *along_x, flops=8000 * MIB
@@ -307,11 +330,9 @@
     along_z = [shift(sent[e - 1], "zh", e) for e in (2, 1, 3)]
     (near,) = small_call(pair_kernel, [((4, places, D // 8), BF16)], after(both, own), near)
     far = exchange(near, "y", 3)
-    attended_cache, fresh_weights = attend_cache(
-        lengths, after(queries, near), new_keys.reshape(places, HD), cache_keys, cache_values
-    )
-    own, *along_z, attended_cache, fresh_weights = lax.optimization_barrier(
-        (own, *along_z, attended_cache, fresh_weights)
+    near_own, near_rest = arrange(place, near)
+    own, *along_z, near_own, near_rest = lax.optimization_barrier(
+        (own, *along_z, near_own, near_rest)
     )
     (updated,) = small_call(update_kernel, [(rows, BF16)], value_weight, own, *along_z)
     own = after(own, updated)
@@ -321,14 +342,14 @@
     gathered, gradient = lax.optimization_barrier((gathered, gradient))
     other = shift(gathered, "c", 1)
     partial = project(
-        project_own_kernel, pltpu.VMEM((2 * places, HD), F32), 1, place, near, gathered
+        project_own_kernel, pltpu.VMEM((2 * places, HD), F32), 1, place, near_own, gathered
     )
     partial = project(
         project_rest_kernel,
         pltpu.VMEM((4, places, HD), BF16),
         2,
         place,
-        near,
+        near_rest,
         far,
         gathered,
         other,

time: 69.2 us -> 69.2 us (level)
  waiting for transfers between devices: 10.2 us -> 8.77 us
    ppermute x12, waiting for transfers between devices: 10.2 us -> 8.76 us  [shift(): return lax.ppermute(value, axis, [(i, (i + by) % n) for i in range(n)])]
  transfers between devices with their start and end apart: 15 -> 15, of which waited for: 5 -> 6; matrix products, arithmetic and copies ran while one was open for 0% -> 0% of each run, Pallas kernels for 6% -> 7%
where the time goes in v15:
time: 69.2 us; the launch traced here: 68 us
  starting transfers between devices  33.8 us (49%)
  Pallas kernels  12.4 us (18%)
  blocking collectives  12 us (17%)
  waiting for transfers between devices  8.77 us (13%)
  between operations  0.83 us (1%)
    ppermute x12, starting transfers between devices, shift(): return lax.ppermute(value, axis, [(i, (i + by) % n) for i in range(n)])  23.4 us
    all_to_all x1, blocking collectives, shards(): exchanged = lax.all_to_all(partial, 'zh', 0, 0, tiled=True)  12 us
    ppermute x2, starting transfers between devices, exchange(): return lax.ppermute(value, axis, [(i, i ^ bit) for i in range(SIZES[axis])])  9.73 us
    ppermute x12, waiting for transfers between devices, shift(): return lax.ppermute(value, axis, [(i, (i + by) % n) for i in range(n)])  8.76 us
    pallas_call x1, Pallas kernels, partial_gradient(): pl.pallas_call(partial_kernel, in_specs=[SMEM, HBM, HBM], out_specs=[VMEM...  5.96 us
    pallas_call x1, Pallas kernels, attend_cache(): pl.pallas_call(attend_kernel, in_specs=[SMEM] + [VMEM] * 4, out_specs=[VM...  2.14 us
    pallas_call x2, Pallas kernels, project(): pl.pallas_call(kernel, in_specs=[SMEM] + [VMEM] * len(args), out_specs=VM...  1.72 us
  transfers between devices with their start and end apart: 15, of which 6 were waited for; matrix products, arithmetic and copies ran while one was open for 0% of the time, Pallas kernels for 7%

profile of v15, /device:TPU:32, one launch (start us, length us, event | category | flops | bytes accessed | tf_op | source)
XLA Modules:
  0.0 68.0 jit_solution(5385681509595507422)
XLA Ops:
  0.8 6.0 %shard_map.112 = (bf16[4,4,256,128]{3,2,1,0:T(8,128)(2,1)S(1)}, bf16[4,4,256,128]{3,2,1,0:T(8,128)(2,1)S(1)}) custom-call(s32[5]{0:T(128)S(1)} %stack.38.place, bf16[768,8192]{1,0:T(8,128)(2,1)} %x_hbm.1, bf16[768,128]{1,0:T(8,128)(2,1)} %v_hbm.1), custom_call_target="tpu_custom_call" | custom-call | flops 1610612736 | bytes 12582912 | tf_op jit(solution)/shard_map/pallas_call | solution.py:71
  6.9 0.7 collective-permute-start.4
  7.5 2.0 %collective-permute-done.received = bf16[4,4,256,128]{3,2,1,0:T(8,128)(2,1)S(1)} collective-permute-done((bf16[4,4,256,128]{3,2,1,0:T(8,128)(2,1)S(1)}, bf16[4,4,256,128]{3,2,1,0:T(8,128)(2,1)S(1)}, u32[]{:S(2)}, u32[]{:S(2)}) %collective-permute-start) | collective-permute-done | bytes 1048608 | tf_op jit(solution)/shard_map/ppermute | solution.py:27
  9.7 3.1 %collective-permute-start.1 = (bf16[4,256,128]{2,1,0:T(8,128)(2,1)S(1)}, bf16[4,256,128]{2,1,0:T(8,128)(2,1)S(1)}, u32[]{:S(2)}, u32[]{:S(2)}) collective-permute-start(bf16[4,256,128]{2,1,0:T(8,128)(2,1)S(1)} %get-tuple-element.42), channel_id=1, source_target_pairs={{0,16},{8,24},{16,0},{24,8},{1,17},{9,25},{17,1},{25,9},{2,18},{10... | collective-permute-start | bytes 786440 | tf_op jit(solution)/shard_map/ppermute | solution.py:27
  12.8 0.6 collective-permute-start.2
  13.4 2.6 %collective-permute-start.3 = (bf16[4,256,128]{2,1,0:T(8,128)(2,1)S(1)}, bf16[4,256,128]{2,1,0:T(8,128)(2,1)S(1)}, u32[]{:S(2)}, u32[]{:S(2)}) collective-permute-start(bf16[4,256,128]{2,1,0:T(8,128)(2,1)S(1)} %get-tuple-element.44), channel_id=1, source_target_pairs={{0,24},{8,0},{16,8},{24,16},{1,25},{9,1},{17,9},{25,17},{2,26},{10... | collective-permute-start | bytes 786440 | tf_op jit(solution)/shard_map/ppermute | solution.py:27
  16.2 2.1 %shard_map.115 = (f32[512,128]{1,0:T(8,128)S(1)}, bf16[512,64]{1,0:T(8,128)(2,1)S(1)}) custom-call(s32[16]{0:T(128)S(1)} %copy-done.5, bf16[16,4,1024]{2,1,0:T(4,128)(2,1)S(1)} %copy-done.2, bf16[64,128]{1,0:T(8,128)(2,1)S(1)} %bitcast.11, bf16[16,128,128]{2,1,0:T(8,128)(2,1)S(1)} %copy-done, bf16[16,128,128]{2,1,0:T(8,128)(2,1)S(1)} %copy-done.1), custom_call_target="tpu_custom_call" | custom-call | flops 1048576 | bytes 262144 | tf_op jit(solution)/shard_map/pallas_call | solution.py:178
  18.3 3.2 %collective-permute-done.5.second = bf16[16,4,1024]{2,1,0:T(4,128)(2,1)S(1)} collective-permute-done((bf16[16,4,1024]{2,1,0:T(4,128)(2,1)S(1)}, bf16[16,4,1024]{2,1,0:T(4,128)(2,1)S(1)}, u32[]{:S(2)}, u32[]{:S(2)}) %collective-permute-start.5) | collective-permute-done | bytes 131104 | tf_op jit(solution)/shard_map/ppermute | solution.py:27
  21.6 6.2 %collective-permute-start.9 = (bf16[2,64,1024]{2,1,0:T(8,128)(2,1)S(1)}, bf16[2,64,1024]{2,1,0:T(8,128)(2,1)S(1)}, u32[]{:S(2)}, u32[]{:S(2)}) collective-permute-start(bf16[2,64,1024]{2,1,0:T(8,128)(2,1)S(1)} %shard_map.114.first), channel_id=1, source_target_pairs={{0,1},{1,0},{2,3},{3,2},{4,5},{5,4},{6,7},{7,6},{8,9},{9,8},{10,11... | collective-permute-start | bytes 786440 | tf_op jit(solution)/shard_map/ppermute | solution.py:31
  28.0 6.7 %collective-permute-start.6 = (bf16[256,128]{1,0:T(8,128)(2,1)S(1)}, bf16[256,128]{1,0:T(8,128)(2,1)S(1)}, u32[]{:S(2)}, u32[]{:S(2)}) collective-permute-start(bf16[256,128]{1,0:T(8,128)(2,1)S(1)} %get-tuple-element.55), channel_id=1, source_target_pairs={{0,64},{32,96},{64,0},{96,32},{1,65},{33,97},{65,1},{97,33},{2,66}... | collective-permute-start | bytes 196616 | tf_op jit(solution)/shard_map/ppermute | solution.py:27
  34.7 3.7 %collective-permute-start.7 = (bf16[256,128]{1,0:T(8,128)(2,1)S(1)}, bf16[256,128]{1,0:T(8,128)(2,1)S(1)}, u32[]{:S(2)}, u32[]{:S(2)}) collective-permute-start(bf16[256,128]{1,0:T(8,128)(2,1)S(1)} %get-tuple-element.56), channel_id=1, source_target_pairs={{0,32},{32,64},{64,96},{96,0},{1,33},{33,65},{65,97},{97,1},{2,34}... | collective-permute-start | bytes 196616 | tf_op jit(solution)/shard_map/ppermute | solution.py:27
  38.9 3.5 %collective-permute-start.13 = (bf16[4,64,1024]{2,1,0:T(8,128)(2,1)S(1)}, bf16[4,64,1024]{2,1,0:T(8,128)(2,1)S(1)}, u32[]{:S(2)}, u32[]{:S(2)}) collective-permute-start(bf16[4,64,1024]{2,1,0:T(8,128)(2,1)S(1)} %shard_map.117.near), channel_id=1, source_target_pairs={{0,3},{1,2},{2,1},{3,0},{4,7},{5,6},{6,5},{7,4},{8,11},{9,10},{10,... | collective-permute-start | bytes 1572872 | tf_op jit(solution)/shard_map/ppermute | solution.py:31
  43.0 0.8 %collective-permute-done.8.r3 = bf16[256,128]{1,0:T(8,128)(2,1)S(1)} collective-permute-done((bf16[256,128]{1,0:T(8,128)(2,1)S(1)}, bf16[256,128]{1,0:T(8,128)(2,1)S(1)}, u32[]{:S(2)}, u32[]{:S(2)}) %collective-permute-start.8) | collective-permute-done | bytes 65568 | tf_op jit(solution)/shard_map/ppermute | solution.py:27
  43.8 1.8 %collective-permute-start.12 = (bf16[256,128]{1,0:T(8,128)(2,1)S(1)}, bf16[256,128]{1,0:T(8,128)(2,1)S(1)}, u32[]{:S(2)}, u32[]{:S(2)}) collective-permute-start(bf16[256,128]{1,0:T(8,128)(2,1)S(1)} %shard_map.119), channel_id=1, source_target_pairs={{0,8},{8,16},{16,24},{24,0},{1,9},{9,17},{17,25},{25,1},{2,10},{10... | collective-permute-start | bytes 196616 | tf_op jit(solution)/shard_map/ppermute | solution.py:27
  45.5 2.7 %collective-permute-start.11 = (bf16[256,128]{1,0:T(8,128)(2,1)S(1)}, bf16[256,128]{1,0:T(8,128)(2,1)S(1)}, u32[]{:S(2)}, u32[]{:S(2)}) collective-permute-start(bf16[256,128]{1,0:T(8,128)(2,1)S(1)} %shard_map.119), channel_id=1, source_target_pairs={{0,16},{8,24},{16,0},{24,8},{1,17},{9,25},{17,1},{25,9},{2,18},{10... | collective-permute-start | bytes 196616 | tf_op jit(solution)/shard_map/ppermute | solution.py:27
  48.3 1.4 %collective-permute-start.10 = (bf16[256,128]{1,0:T(8,128)(2,1)S(1)}, bf16[256,128]{1,0:T(8,128)(2,1)S(1)}, u32[]{:S(2)}, u32[]{:S(2)}) collective-permute-start(bf16[256,128]{1,0:T(8,128)(2,1)S(1)} %shard_map.119), channel_id=1, source_target_pairs={{0,24},{8,0},{16,8},{24,16},{1,25},{9,1},{17,9},{25,17},{2,26},{10... | collective-permute-start | bytes 196616 | tf_op jit(solution)/shard_map/ppermute | solution.py:27
  49.7 0.7 %shard_map.120 = f32[256,128]{1,0:T(8,128)} custom-call(f32[256,128]{1,0:T(8,128)S(1)} %get-tuple-element.66.own, bf16[256,128]{1,0:T(8,128)(2,1)S(1)} %collective-permute-done.6.r1, bf16[256,128]{1,0:T(8,128)(2,1)S(1)} %collective-permute-done.7.r2, bf16[256,128]{1,0:T(8,128)(2,1)S(1)} %collective-permute-done.8.r3), custom_call_target="tpu_custom_call" | custom-call | flops 1048576 | bytes 2097152 | tf_op jit(solution)/shard_map/pallas_call | solution.py:89
  50.4 0.9 %collective-permute-done.11 = bf16[256,128]{1,0:T(8,128)(2,1)S(1)} collective-permute-done((bf16[256,128]{1,0:T(8,128)(2,1)S(1)}, bf16[256,128]{1,0:T(8,128)(2,1)S(1)}, u32[]{:S(2)}, u32[]{:S(2)}) %collective-permute-start.11) | collective-permute-done | bytes 65568 | tf_op jit(solution)/shard_map/ppermute | solution.py:27
  51.3 1.2 %collective-permute-done.10 = bf16[256,128]{1,0:T(8,128)(2,1)S(1)} collective-permute-done((bf16[256,128]{1,0:T(8,128)(2,1)S(1)}, bf16[256,128]{1,0:T(8,128)(2,1)S(1)}, u32[]{:S(2)}, u32[]{:S(2)}) %collective-permute-start.10) | collective-permute-done | bytes 65568 | tf_op jit(solution)/shard_map/ppermute | solution.py:27
  52.7 0.8 %shard_map.121.start = f32[128,128]{1,0:T(8,128)S(1)} custom-call(s32[5]{0:T(128)S(1)} %stack.38.place, bf16[128,1024]{1,0:T(8,128)(2,1)S(1)} %get-tuple-element.70.inputs, bf16[4,256,128]{2,1,0:T(8,128)(2,1)S(1)} %pad_maximum_fusion.u.u_own), custom_call_target="tpu_custom_call" | custom-call | flops 67108864 | bytes 786432 | tf_op jit(solution)/shard_map/pallas_call | solution.py:246
  53.5 0.7 %collective-permute-done.14.u_other = bf16[4,256,128]{2,1,0:T(8,128)(2,1)S(1)} collective-permute-done((bf16[4,256,128]{2,1,0:T(8,128)(2,1)S(1)}, bf16[4,256,128]{2,1,0:T(8,128)(2,1)S(1)}, u32[]{:S(2)}, u32[]{:S(2)}) %collective-permute-start.14) | collective-permute-done | bytes 262176 | tf_op jit(solution)/shard_map/ppermute | solution.py:27
  54.2 0.9 %shard_map.122 = bf16[4,64,128]{2,1,0:T(8,128)(2,1)S(1)} custom-call(s32[5]{0:T(128)S(1)} %stack.38.place, bf16[128,1024]{1,0:T(8,128)(2,1)S(1)} %get-tuple-element.68.near, bf16[4,64,1024]{2,1,0:T(8,128)(2,1)S(1)} %collective-permute-done.13.far, bf16[4,256,128]{2,1,0:T(8,128)(2,1)S(1)} %pad_maximum_fusion.u.u_own, ...), custom_call_target="tpu_custom_call" | custom-call | flops 67108864 | bytes 786432 | tf_op jit(solution)/shard_map/pallas_call | solution.py:246
  55.2 12.0 %all_to_all.5.parts = bf16[4,64,128]{2,1,0:T(8,128)(2,1)S(1)} all-to-all(bf16[4,64,128]{2,1,0:T(8,128)(2,1)S(1)} %shard_map.122), channel_id=1, replica_groups=mesh['c'=2,'zh'=4,'x'=4,'zl'=2,'y'=4] {'zh'}, dimensions={0} | all-to-all | bytes 131072 | tf_op jit(solution)/shard_map/all_to_all | solution.py:358
  67.1 0.8 %shard_map.123 = (bf16[16,4,128]{2,1,0:T(4,128)(2,1)}, bf16[16,4,1024]{2,1,0:T(4,128)(2,1)}) custom-call(bf16[4,64,128]{2,1,0:T(8,128)(2,1)S(1)} %all_to_all.5.parts, f32[512,128]{1,0:T(8,128)S(1)} %get-tuple-element.71.mixed, bf16[512,64]{1,0:T(8,128)(2,1)S(1)} %get-tuple-element.72.weights), custom_call_target="tpu_custom_call" | custom-call | tf_op jit(solution)/shard_map/pallas_call | solution.py:277
  (35 shorter events, 2.0 us)
Async XLA Ops:
  0.6 6.2 %copy-start.6 = (bf16[16,4,1024]{2,1,0:T(4,128)(2,1)S(1)}, bf16[16,4,1024]{2,1,0:T(4,128)(2,1)}, u32[]{:S(2)}) copy-start(bf16[16,4,1024]{2,1,0:T(4,128)(2,1)} %param.12) | copy-start | bytes 393220
  0.6 15.5 %copy-start.2 = (bf16[16,4,1024]{2,1,0:T(4,128)(2,1)S(1)}, bf16[16,4,1024]{2,1,0:T(4,128)(2,1)}, u32[]{:S(2)}) copy-start(bf16[16,4,1024]{2,1,0:T(4,128)(2,1)} %raw_queries) | copy-start | bytes 393220
  0.7 15.5 %copy-start.5 = (s32[16]{0:T(128)S(1)}, s32[16]{0:T(128)}, u32[]{:S(2)}) copy-start(s32[16]{0:T(128)} %lengths.1) | copy-start | bytes 196
  0.7 15.5 %copy-start.1 = (bf16[16,128,128]{2,1,0:T(8,128)(2,1)S(1)}, bf16[16,128,128]{2,1,0:T(8,128)(2,1)}, u32[]{:S(2)}) copy-start(bf16[16,128,128]{2,1,0:T(8,128)(2,1)} %cache_values.1) | copy-start | bytes 1572868
  0.7 15.5 %copy-start = (bf16[16,128,128]{2,1,0:T(8,128)(2,1)S(1)}, bf16[16,128,128]{2,1,0:T(8,128)(2,1)}, u32[]{:S(2)}) copy-start(bf16[16,128,128]{2,1,0:T(8,128)(2,1)} %cache_keys.1) | copy-start | bytes 1572868
  0.7 15.5 %copy-start.4 = (bf16[16,4,128]{2,1,0:T(4,128)(2,1)S(1)}, bf16[16,4,128]{2,1,0:T(4,128)(2,1)}, u32[]{:S(2)}) copy-start(bf16[16,4,128]{2,1,0:T(4,128)(2,1)} %param.14) | copy-start | bytes 49156
  6.8 2.7 %collective-permute-start = (bf16[4,4,256,128]{3,2,1,0:T(8,128)(2,1)S(1)}, bf16[4,4,256,128]{3,2,1,0:T(8,128)(2,1)S(1)}, u32[]{:S(2)}, u32[]{:S(2)}) collective-permute-start(bf16[4,4,256,128]{3,2,1,0:T(8,128)(2,1)S(1)} %get-tuple-element.40), channel_id=1, source_target_pairs={{0,128},{128,0},{1,129},{129,1},{2,130},{130,2},{3,131},{131,3},{4... | collective-permute-start | bytes 3145736 | tf_op jit(solution)/shard_map/ppermute | solution.py:27
  6.9 9.2 %collective-permute-start.4 = (bf16[16,4,1024]{2,1,0:T(4,128)(2,1)S(1)}, bf16[16,4,1024]{2,1,0:T(4,128)(2,1)S(1)}, u32[]{:S(2)}, u32[]{:S(2)}) collective-permute-start(bf16[16,4,1024]{2,1,0:T(4,128)(2,1)S(1)} %copy-done.6), channel_id=1, source_target_pairs={{0,0},{1,33},{2,66},{3,99},{32,1},{33,34},{34,67},{35,96},{64,2},{... | collective-permute-start | bytes 393224 | tf_op jit(solution)/shard_map/ppermute | solution.py:36
  9.7 18.1 %collective-permute-start.1 = (bf16[4,256,128]{2,1,0:T(8,128)(2,1)S(1)}, bf16[4,256,128]{2,1,0:T(8,128)(2,1)S(1)}, u32[]{:S(2)}, u32[]{:S(2)}) collective-permute-start(bf16[4,256,128]{2,1,0:T(8,128)(2,1)S(1)} %get-tuple-element.42), channel_id=1, source_target_pairs={{0,16},{8,24},{16,0},{24,8},{1,17},{9,25},{17,1},{25,9},{2,18},{10... | collective-permute-start | bytes 786440 | tf_op jit(solution)/shard_map/ppermute | solution.py:27
  12.8 15.0 %collective-permute-start.2 = (bf16[4,256,128]{2,1,0:T(8,128)(2,1)S(1)}, bf16[4,256,128]{2,1,0:T(8,128)(2,1)S(1)}, u32[]{:S(2)}, u32[]{:S(2)}) collective-permute-start(bf16[4,256,128]{2,1,0:T(8,128)(2,1)S(1)} %get-tuple-element.43), channel_id=1, source_target_pairs={{0,8},{8,16},{16,24},{24,0},{1,9},{9,17},{17,25},{25,1},{2,10},{10... | collective-permute-start | bytes 786440 | tf_op jit(solution)/shard_map/ppermute | solution.py:27
  13.4 14.4 %collective-permute-start.3 = (bf16[4,256,128]{2,1,0:T(8,128)(2,1)S(1)}, bf16[4,256,128]{2,1,0:T(8,128)(2,1)S(1)}, u32[]{:S(2)}, u32[]{:S(2)}) collective-permute-start(bf16[4,256,128]{2,1,0:T(8,128)(2,1)S(1)} %get-tuple-element.44), channel_id=1, source_target_pairs={{0,24},{8,0},{16,8},{24,16},{1,25},{9,1},{17,9},{25,17},{2,26},{10... | collective-permute-start | bytes 786440 | tf_op jit(solution)/shard_map/ppermute | solution.py:27
  16.1 5.4 %collective-permute-start.5 = (bf16[16,4,1024]{2,1,0:T(4,128)(2,1)S(1)}, bf16[16,4,1024]{2,1,0:T(4,128)(2,1)S(1)}, u32[]{:S(2)}, u32[]{:S(2)}) collective-permute-start(bf16[16,4,1024]{2,1,0:T(4,128)(2,1)S(1)} %collective-permute-done.4.first), channel_id=1, source_target_pairs={{0,4},{4,0},{1,5},{5,1},{2,6},{6,2},{3,7},{7,3},{8,12},{12,8},{9,1... | collective-permute-start | bytes 393224 | tf_op jit(solution)/shard_map/ppermute | solution.py:27
  21.6 17.3 %collective-permute-start.9 = (bf16[2,64,1024]{2,1,0:T(8,128)(2,1)S(1)}, bf16[2,64,1024]{2,1,0:T(8,128)(2,1)S(1)}, u32[]{:S(2)}, u32[]{:S(2)}) collective-permute-start(bf16[2,64,1024]{2,1,0:T(8,128)(2,1)S(1)} %shard_map.114.first), channel_id=1, source_target_pairs={{0,1},{1,0},{2,3},{3,2},{4,5},{5,4},{6,7},{7,6},{8,9},{9,8},{10,11... | collective-permute-start | bytes 786440 | tf_op jit(solution)/shard_map/ppermute | solution.py:31
  28.0 15.0 %collective-permute-start.6 = (bf16[256,128]{1,0:T(8,128)(2,1)S(1)}, bf16[256,128]{1,0:T(8,128)(2,1)S(1)}, u32[]{:S(2)}, u32[]{:S(2)}) collective-permute-start(bf16[256,128]{1,0:T(8,128)(2,1)S(1)} %get-tuple-element.55), channel_id=1, source_target_pairs={{0,64},{32,96},{64,0},{96,32},{1,65},{33,97},{65,1},{97,33},{2,66}... | collective-permute-start | bytes 196616 | tf_op jit(solution)/shard_map/ppermute | solution.py:27
  34.7 8.3 %collective-permute-start.7 = (bf16[256,128]{1,0:T(8,128)(2,1)S(1)}, bf16[256,128]{1,0:T(8,128)(2,1)S(1)}, u32[]{:S(2)}, u32[]{:S(2)}) collective-permute-start(bf16[256,128]{1,0:T(8,128)(2,1)S(1)} %get-tuple-element.56), channel_id=1, source_target_pairs={{0,32},{32,64},{64,96},{96,0},{1,33},{33,65},{65,97},{97,1},{2,34}... | collective-permute-start | bytes 196616 | tf_op jit(solution)/shard_map/ppermute | solution.py:27
  38.4 5.3 %collective-permute-start.8 = (bf16[256,128]{1,0:T(8,128)(2,1)S(1)}, bf16[256,128]{1,0:T(8,128)(2,1)S(1)}, u32[]{:S(2)}, u32[]{:S(2)}) collective-permute-start(bf16[256,128]{1,0:T(8,128)(2,1)S(1)} %get-tuple-element.57), channel_id=1, source_target_pairs={{0,96},{32,0},{64,32},{96,64},{1,97},{33,1},{65,33},{97,65},{2,98}... | collective-permute-start | bytes 196616 | tf_op jit(solution)/shard_map/ppermute | solution.py:27
  38.9 4.9 %copy-start.3 = (bf16[256,128]{1,0:T(8,128)(2,1)S(1)}, bf16[256,128]{1,0:T(8,128)(2,1)}, u32[]{:S(2)}) copy-start(bf16[256,128]{1,0:T(8,128)(2,1)} %weight.1) | copy-start | bytes 196612
  38.9 15.3 %collective-permute-start.13 = (bf16[4,64,1024]{2,1,0:T(8,128)(2,1)S(1)}, bf16[4,64,1024]{2,1,0:T(8,128)(2,1)S(1)}, u32[]{:S(2)}, u32[]{:S(2)}) collective-permute-start(bf16[4,64,1024]{2,1,0:T(8,128)(2,1)S(1)} %shard_map.117.near), channel_id=1, source_target_pairs={{0,3},{1,2},{2,1},{3,0},{4,7},{5,6},{6,5},{7,4},{8,11},{9,10},{10,... | collective-permute-start | bytes 1572872 | tf_op jit(solution)/shard_map/ppermute | solution.py:31
  43.8 6.6 %collective-permute-start.12 = (bf16[256,128]{1,0:T(8,128)(2,1)S(1)}, bf16[256,128]{1,0:T(8,128)(2,1)S(1)}, u32[]{:S(2)}, u32[]{:S(2)}) collective-permute-start(bf16[256,128]{1,0:T(8,128)(2,1)S(1)} %shard_map.119), channel_id=1, source_target_pairs={{0,8},{8,16},{16,24},{24,0},{1,9},{9,17},{17,25},{25,1},{2,10},{10... | collective-permute-start | bytes 196616 | tf_op jit(solution)/shard_map/ppermute | solution.py:27
  45.5 5.8 %collective-permute-start.11 = (bf16[256,128]{1,0:T(8,128)(2,1)S(1)}, bf16[256,128]{1,0:T(8,128)(2,1)S(1)}, u32[]{:S(2)}, u32[]{:S(2)}) collective-permute-start(bf16[256,128]{1,0:T(8,128)(2,1)S(1)} %shard_map.119), channel_id=1, source_target_pairs={{0,16},{8,24},{16,0},{24,8},{1,17},{9,25},{17,1},{25,9},{2,18},{10... | collective-permute-start | bytes 196616 | tf_op jit(solution)/shard_map/ppermute | solution.py:27
  48.3 4.3 %collective-permute-start.10 = (bf16[256,128]{1,0:T(8,128)(2,1)S(1)}, bf16[256,128]{1,0:T(8,128)(2,1)S(1)}, u32[]{:S(2)}, u32[]{:S(2)}) collective-permute-start(bf16[256,128]{1,0:T(8,128)(2,1)S(1)} %shard_map.119), channel_id=1, source_target_pairs={{0,24},{8,0},{16,8},{24,16},{1,25},{9,1},{17,9},{25,17},{2,26},{10... | collective-permute-start | bytes 196616 | tf_op jit(solution)/shard_map/ppermute | solution.py:27
  52.6 1.6 %collective-permute-start.14 = (bf16[4,256,128]{2,1,0:T(8,128)(2,1)S(1)}, bf16[4,256,128]{2,1,0:T(8,128)(2,1)S(1)}, u32[]{:S(2)}, u32[]{:S(2)}) collective-permute-start(bf16[4,256,128]{2,1,0:T(8,128)(2,1)S(1)} %pad_maximum_fusion.u.u_own), channel_id=1, source_target_pairs={{0,128},{128,0},{1,129},{129,1},{2,130},{130,2},{3,131},{131,3},{4... | collective-permute-start | bytes 786440 | tf_op jit(solution)/shard_map/ppermute | solution.py:27

commit v16 on v14

--- a/solution.py
+++ b/solution.py
@@ -207,7 +207,7 @@
     out_ref[...] = jnp.dot(inputs, rows[...], preferred_element_type=F32)
 
 
-def project_rest_kernel(place, near, far, u_own, u_other, start, out_ref, rows, last):
+def project_rest_kernel(place, near, far, u_own, u_other, start, o0, o1, o2, o3, rows, last, sums):
     own = jnp.where(place[0] == place[4], 0, 1)
     fill_rows(last, place[2], u_own)
     fill_rows(rows, place[2], u_other)
@@ -221,16 +221,18 @@
     for i, bits in enumerate((0, 1, 3, 2)):
         rest = start[i * size : (i + 1) * size] if i < 2 else more[(i - 2) * size : (i - 1) * size]
         total = product[i * size : (i + 1) * size] + rest
-        out_ref[tokens_of(place, bits)] = total.astype(out_ref.dtype)
-
-
-def project(kernel, out_shape, scratches, place, *args):
+        sums[lax.rem(tokens_of(place, bits) + 4 - place[1], 4)] = total
+    for e, out in enumerate((o0, o1, o2, o3)):
+        out[...] = sums[e].astype(out.dtype)
+
+
+def project(kernel, outs, scratches, place, *args):
     return pl.pallas_call(
         kernel,
         in_specs=[SMEM] + [VMEM] * len(args),
-        out_specs=VMEM,
-        out_shape=out_shape,
-        scratch_shapes=[pltpu.VMEM((1024, HD), BF16)] * scratches,
+        out_specs=[VMEM] * len(outs),
+        out_shape=[jax.ShapeDtypeStruct(shape, dtype) for shape, dtype in outs],
+        scratch_shapes=[pltpu.VMEM(shape, dtype) for shape, dtype in scratches],
         compiler_params=pltpu.CompilerParams(vmem_limit_bytes=16 * MIB),
         cost_estimate=pl.CostEstimate(
             flops=2 * 256 * 1024 * HD, bytes_accessed=3 * MIB // 4, transcendentals=0
@@ -238,12 +240,9 @@
     )(place, *args)
 
 
-def finish_kernel(parts, mixed, weights, values_ref, attended_ref):
+def finish_kernel(own, r1, r2, r3, mixed, weights, values_ref, attended_ref):
     steps = values_ref.shape[1]
-    total = parts[0].astype(F32)
-    for i in range(1, 4):
-        total += parts[i].astype(F32)
-    values = total.astype(BF16)
+    values = total_of(own, r1, r2, r3).astype(BF16)
     for r in range(values_ref.shape[0]):
         values_ref[r] = values[r * steps : (r + 1) * steps]
     places = values.shape[0]
@@ -258,14 +257,14 @@
 def finish(parts, mixed, weights, rows, steps):
     return pl.pallas_call(
         finish_kernel,
-        in_specs=[VMEM] * 3,
+        in_specs=[VMEM] * 6,
         out_specs=[VMEM, VMEM],
         out_shape=[
             jax.ShapeDtypeStruct((rows, steps, HD), BF16),
             jax.ShapeDtypeStruct((rows, steps, HEADS * HD), BF16),
         ],
         compiler_params=pltpu.CompilerParams(vmem_limit_bytes=16 * MIB),
-    )(parts, mixed, weights)
+    )(*parts, mixed, weights)
 
 
 def shards(
@@ -320,13 +319,14 @@
     gathered = jnp.stack([updated] + [shift(updated, "x", -d) for d in (1, 2, 3)])
     gathered, gradient = lax.optimization_barrier((gathered, gradient))
     other = shift(gathered, "c", 1)
-    partial = project(
-        project_own_kernel, pltpu.VMEM((2 * places, HD), F32), 1, place, near, gathered
-    )
-    partial = project(
+    scratch, tokens = ((1024, HD), BF16), (places, HD)
+    (partial,) = project(
+        project_own_kernel, [((2 * places, HD), F32)], [scratch], place, near, gathered
+    )
+    own, *sent = project(
         project_rest_kernel,
-        pltpu.VMEM((4, places, HD), BF16),
-        2,
+        [(tokens, F32)] + [(tokens, BF16)] * 3,
+        [scratch, scratch, ((4, places, HD), F32)],
         place,
         near,
         far,
@@ -334,7 +334,7 @@
         other,
         partial,
     )
-    exchanged = lax.all_to_all(partial, "zh", 0, 0, tiled=True)
+    exchanged = [own] + [shift(sent[e - 1], "zh", e) for e in (2, 1, 3)]
     new_values, attended = finish(
         exchanged, attended_cache, fresh_weights, row_count, step_count
     )

time: 69.2 us -> 67.1 us (0.970)
  blocking collectives: 11.6 us -> 0 us
  starting transfers between devices: 33.8 us -> 40.4 us
  waiting for transfers between devices: 10.2 us -> 12.6 us
    all_to_all x1 -> x0, blocking collectives: 11.6 us -> none  [shards(): exchanged = lax.all_to_all(partial, 'zh', 0, 0, tiled=True)]
    ppermute x12 -> x15, starting transfers between devices: 23.4 us -> 30 us  [shift(): return lax.ppermute(value, axis, [(i, (i + by) % n) for i in range(n)])]
    ppermute x12 -> x15, waiting for transfers between devices: 10.2 us -> 12.6 us  [shift(): return lax.ppermute(value, axis, [(i, (i + by) % n) for i in range(n)])]
  transfers between devices with their start and end apart: 15 -> 18, of which waited for: 5 -> 8; matrix products, arithmetic and copies ran while one was open for 0% -> 0% of each run, Pallas kernels for 6% -> 6%
where the time goes in v16:
time: 67.1 us; the launch traced here: 65.8 us
  starting transfers between devices  40.4 us (60%)
  waiting for transfers between devices  12.6 us (19%)
  Pallas kernels  11.8 us (18%)
  between operations  0.85 us (1%)
    ppermute x15, starting transfers between devices, shift(): return lax.ppermute(value, axis, [(i, (i + by) % n) for i in range(n)])  30 us
    ppermute x15, waiting for transfers between devices, shift(): return lax.ppermute(value, axis, [(i, (i + by) % n) for i in range(n)])  12.6 us
    ppermute x2, starting transfers between devices, exchange(): return lax.ppermute(value, axis, [(i, i ^ bit) for i in range(SIZES[axis])])  9.73 us
    pallas_call x1, Pallas kernels, partial_gradient(): pl.pallas_call(partial_kernel, in_specs=[SMEM, HBM, HBM], out_specs=[VMEM...  5.96 us
    pallas_call x1, Pallas kernels, attend_cache(): pl.pallas_call(attend_kernel, in_specs=[SMEM] + [VMEM] * 4, out_specs=[VM...  2.15 us
    pallas_call x2, Pallas kernels, project(): pl.pallas_call(kernel, in_specs=[SMEM] + [VMEM] * len(args), out_specs=[V...  1.74 us
  transfers between devices with their start and end apart: 18, of which 8 were waited for; matrix products, arithmetic and copies ran while one was open for 0% of the time, Pallas kernels for 6%

profile of v16, /device:TPU:32, one launch (start us, length us, event | category | flops | bytes accessed | tf_op | source)
XLA Modules:
  0.0 65.8 jit_solution(1479827305570166317)
XLA Ops:
  0.7 6.0 %shard_map.112 = (bf16[4,4,256,128]{3,2,1,0:T(8,128)(2,1)S(1)}, bf16[4,4,256,128]{3,2,1,0:T(8,128)(2,1)S(1)}) custom-call(s32[5]{0:T(128)S(1)} %stack.38.place, bf16[768,8192]{1,0:T(8,128)(2,1)} %x_hbm.1, bf16[768,128]{1,0:T(8,128)(2,1)} %v_hbm.1), custom_call_target="tpu_custom_call" | custom-call | flops 1610612736 | bytes 12582912 | tf_op jit(solution)/shard_map/pallas_call | solution.py:71
  7.5 2.0 %collective-permute-done.received = bf16[4,4,256,128]{3,2,1,0:T(8,128)(2,1)S(1)} collective-permute-done((bf16[4,4,256,128]{3,2,1,0:T(8,128)(2,1)S(1)}, bf16[4,4,256,128]{3,2,1,0:T(8,128)(2,1)S(1)}, u32[]{:S(2)}, u32[]{:S(2)}) %collective-permute-start) | collective-permute-done | bytes 1048608 | tf_op jit(solution)/shard_map/ppermute | solution.py:27
  9.7 3.1 %collective-permute-start.1 = (bf16[4,256,128]{2,1,0:T(8,128)(2,1)S(1)}, bf16[4,256,128]{2,1,0:T(8,128)(2,1)S(1)}, u32[]{:S(2)}, u32[]{:S(2)}) collective-permute-start(bf16[4,256,128]{2,1,0:T(8,128)(2,1)S(1)} %get-tuple-element.42), channel_id=1, source_target_pairs={{0,16},{8,24},{16,0},{24,8},{1,17},{9,25},{17,1},{25,9},{2,18},{10... | collective-permute-start | bytes 786440 | tf_op jit(solution)/shard_map/ppermute | solution.py:27
  13.4 2.6 %collective-permute-start.3 = (bf16[4,256,128]{2,1,0:T(8,128)(2,1)S(1)}, bf16[4,256,128]{2,1,0:T(8,128)(2,1)S(1)}, u32[]{:S(2)}, u32[]{:S(2)}) collective-permute-start(bf16[4,256,128]{2,1,0:T(8,128)(2,1)S(1)} %get-tuple-element.44), channel_id=1, source_target_pairs={{0,24},{8,0},{16,8},{24,16},{1,25},{9,1},{17,9},{25,17},{2,26},{10... | collective-permute-start | bytes 786440 | tf_op jit(solution)/shard_map/ppermute | solution.py:27
  16.1 5.3 %collective-permute-done.5.second = bf16[16,4,1024]{2,1,0:T(4,128)(2,1)S(1)} collective-permute-done((bf16[16,4,1024]{2,1,0:T(4,128)(2,1)S(1)}, bf16[16,4,1024]{2,1,0:T(4,128)(2,1)S(1)}, u32[]{:S(2)}, u32[]{:S(2)}) %collective-permute-start.5) | collective-permute-done | bytes 131104 | tf_op jit(solution)/shard_map/ppermute | solution.py:27
  21.6 6.2 %collective-permute-start.9 = (bf16[2,64,1024]{2,1,0:T(8,128)(2,1)S(1)}, bf16[2,64,1024]{2,1,0:T(8,128)(2,1)S(1)}, u32[]{:S(2)}, u32[]{:S(2)}) collective-permute-start(bf16[2,64,1024]{2,1,0:T(8,128)(2,1)S(1)} %shard_map.114.first), channel_id=1, source_target_pairs={{0,1},{1,0},{2,3},{3,2},{4,5},{5,4},{6,7},{7,6},{8,9},{9,8},{10,11... | collective-permute-start | bytes 786440 | tf_op jit(solution)/shard_map/ppermute | solution.py:31
  27.9 6.7 %collective-permute-start.6 = (bf16[256,128]{1,0:T(8,128)(2,1)S(1)}, bf16[256,128]{1,0:T(8,128)(2,1)S(1)}, u32[]{:S(2)}, u32[]{:S(2)}) collective-permute-start(bf16[256,128]{1,0:T(8,128)(2,1)S(1)} %get-tuple-element.52), channel_id=1, source_target_pairs={{0,64},{32,96},{64,0},{96,32},{1,65},{33,97},{65,1},{97,33},{2,66}... | collective-permute-start | bytes 196616 | tf_op jit(solution)/shard_map/ppermute | solution.py:27
  34.7 3.7 %collective-permute-start.7 = (bf16[256,128]{1,0:T(8,128)(2,1)S(1)}, bf16[256,128]{1,0:T(8,128)(2,1)S(1)}, u32[]{:S(2)}, u32[]{:S(2)}) collective-permute-start(bf16[256,128]{1,0:T(8,128)(2,1)S(1)} %get-tuple-element.53), channel_id=1, source_target_pairs={{0,32},{32,64},{64,96},{96,0},{1,33},{33,65},{65,97},{97,1},{2,34}... | collective-permute-start | bytes 196616 | tf_op jit(solution)/shard_map/ppermute | solution.py:27
  38.9 3.5 %collective-permute-start.13 = (bf16[4,64,1024]{2,1,0:T(8,128)(2,1)S(1)}, bf16[4,64,1024]{2,1,0:T(8,128)(2,1)S(1)}, u32[]{:S(2)}, u32[]{:S(2)}) collective-permute-start(bf16[4,64,1024]{2,1,0:T(8,128)(2,1)S(1)} %shard_map.116.near), channel_id=1, source_target_pairs={{0,3},{1,2},{2,1},{3,0},{4,7},{5,6},{6,5},{7,4},{8,11},{9,10},{10,... | collective-permute-start | bytes 1572872 | tf_op jit(solution)/shard_map/ppermute | solution.py:31
  42.4 2.1 %shard_map.117 = (f32[512,128]{1,0:T(8,128)S(1)}, bf16[512,64]{1,0:T(8,128)(2,1)S(1)}) custom-call(s32[16]{0:T(128)S(1)} %copy-done.5, bf16[16,4,1024]{2,1,0:T(4,128)(2,1)S(1)} %copy-done.3, bf16[64,128]{1,0:T(8,128)(2,1)S(1)} %bitcast.11, bf16[16,128,128]{2,1,0:T(8,128)(2,1)S(1)} %copy-done.1, bf16[16,128,128]{2,1,0:T(8,128)(2,1)S(1)} %copy-done.2), custom_call_target="tpu_custom_call" | custom-call | flops 8388608000 | bytes 20971520 | tf_op jit(solution)/shard_map/pallas_call | solution.py:178
  44.6 1.7 %collective-permute-start.12 = (bf16[256,128]{1,0:T(8,128)(2,1)S(1)}, bf16[256,128]{1,0:T(8,128)(2,1)S(1)}, u32[]{:S(2)}, u32[]{:S(2)}) collective-permute-start(bf16[256,128]{1,0:T(8,128)(2,1)S(1)} %shard_map.118), channel_id=1, source_target_pairs={{0,8},{8,16},{16,24},{24,0},{1,9},{9,17},{17,25},{25,1},{2,10},{10... | collective-permute-start | bytes 196616 | tf_op jit(solution)/shard_map/ppermute | solution.py:27
  46.4 2.7 %collective-permute-start.11 = (bf16[256,128]{1,0:T(8,128)(2,1)S(1)}, bf16[256,128]{1,0:T(8,128)(2,1)S(1)}, u32[]{:S(2)}, u32[]{:S(2)}) collective-permute-start(bf16[256,128]{1,0:T(8,128)(2,1)S(1)} %shard_map.118), channel_id=1, source_target_pairs={{0,16},{8,24},{16,0},{24,8},{1,17},{9,25},{17,1},{25,9},{2,18},{10... | collective-permute-start | bytes 196616 | tf_op jit(solution)/shard_map/ppermute | solution.py:27
  49.1 1.4 %collective-permute-start.10 = (bf16[256,128]{1,0:T(8,128)(2,1)S(1)}, bf16[256,128]{1,0:T(8,128)(2,1)S(1)}, u32[]{:S(2)}, u32[]{:S(2)}) collective-permute-start(bf16[256,128]{1,0:T(8,128)(2,1)S(1)} %shard_map.118), channel_id=1, source_target_pairs={{0,24},{8,0},{16,8},{24,16},{1,25},{9,1},{17,9},{25,17},{2,26},{10... | collective-permute-start | bytes 196616 | tf_op jit(solution)/shard_map/ppermute | solution.py:27
  50.6 0.7 %shard_map.119 = f32[256,128]{1,0:T(8,128)} custom-call(f32[256,128]{1,0:T(8,128)S(1)} %get-tuple-element.64.own, bf16[256,128]{1,0:T(8,128)(2,1)S(1)} %collective-permute-done.6.r1, bf16[256,128]{1,0:T(8,128)(2,1)S(1)} %collective-permute-done.7.r2, bf16[256,128]{1,0:T(8,128)(2,1)S(1)} %collective-permute-done.8.r3), custom_call_target="tpu_custom_call" | custom-call | flops 1048576 | bytes 2097152 | tf_op jit(solution)/shard_map/pallas_call | solution.py:89
  51.2 0.9 %collective-permute-done.11 = bf16[256,128]{1,0:T(8,128)(2,1)S(1)} collective-permute-done((bf16[256,128]{1,0:T(8,128)(2,1)S(1)}, bf16[256,128]{1,0:T(8,128)(2,1)S(1)}, u32[]{:S(2)}, u32[]{:S(2)}) %collective-permute-start.11) | collective-permute-done | bytes 65568 | tf_op jit(solution)/shard_map/ppermute | solution.py:27
  52.2 1.2 %collective-permute-done.10 = bf16[256,128]{1,0:T(8,128)(2,1)S(1)} collective-permute-done((bf16[256,128]{1,0:T(8,128)(2,1)S(1)}, bf16[256,128]{1,0:T(8,128)(2,1)S(1)}, u32[]{:S(2)}, u32[]{:S(2)}) %collective-permute-start.10) | collective-permute-done | bytes 65568 | tf_op jit(solution)/shard_map/ppermute | solution.py:27
  53.5 0.8 %shard_map.120.start = f32[128,128]{1,0:T(8,128)S(1)} custom-call(s32[5]{0:T(128)S(1)} %stack.38.place, bf16[4,64,1024]{2,1,0:T(8,128)(2,1)S(1)} %shard_map.116.near, bf16[4,256,128]{2,1,0:T(8,128)(2,1)S(1)} %pad_maximum_fusion.u.u_own), custom_call_target="tpu_custom_call" | custom-call | flops 67108864 | bytes 786432 | tf_op jit(solution)/shard_map/pallas_call | solution.py:230
  54.3 0.7 %collective-permute-done.14.u_other = bf16[4,256,128]{2,1,0:T(8,128)(2,1)S(1)} collective-permute-done((bf16[4,256,128]{2,1,0:T(8,128)(2,1)S(1)}, bf16[4,256,128]{2,1,0:T(8,128)(2,1)S(1)}, u32[]{:S(2)}, u32[]{:S(2)}) %collective-permute-start.14) | collective-permute-done | bytes 262176 | tf_op jit(solution)/shard_map/ppermute | solution.py:27
  55.1 1.0 %shard_map.121 = (f32[64,128]{1,0:T(8,128)S(1)}, bf16[64,128]{1,0:T(8,128)(2,1)S(1)}, bf16[64,128]{1,0:T(8,128)(2,1)S(1)}, bf16[64,128]{1,0:T(8,128)(2,1)S(1)}) custom-call(s32[5]{0:T(128)S(1)} %stack.38.place, bf16[4,64,1024]{2,1,0:T(8,128)(2,1)S(1)} %shard_map.116.near, bf16[4,64,1024]{2,1,0:T(8,128)(2,1)S(1)} %collective-permute-done.13.far, ...), custom_call_target="tpu_custom_call" | custom-call | flops 67108864 | bytes 786432 | tf_op jit(solution)/shard_map/pallas_call | solution.py:230
  56.0 2.4 %collective-permute-start.15 = (bf16[64,128]{1,0:T(8,128)(2,1)S(1)}, bf16[64,128]{1,0:T(8,128)(2,1)S(1)}, u32[]{:S(2)}, u32[]{:S(2)}) collective-permute-start(bf16[64,128]{1,0:T(8,128)(2,1)S(1)} %get-tuple-element.68), channel_id=1, source_target_pairs={{0,64},{32,96},{64,0},{96,32},{1,65},{33,97},{65,1},{97,33},{2,66}... | collective-permute-start | bytes 49160 | tf_op jit(solution)/shard_map/ppermute | solution.py:27
  58.4 1.9 %collective-permute-start.16 = (bf16[64,128]{1,0:T(8,128)(2,1)S(1)}, bf16[64,128]{1,0:T(8,128)(2,1)S(1)}, u32[]{:S(2)}, u32[]{:S(2)}) collective-permute-start(bf16[64,128]{1,0:T(8,128)(2,1)S(1)} %get-tuple-element.69), channel_id=1, source_target_pairs={{0,32},{32,64},{64,96},{96,0},{1,33},{33,65},{65,97},{97,1},{2,34}... | collective-permute-start | bytes 49160 | tf_op jit(solution)/shard_map/ppermute | solution.py:27
  60.3 2.2 %collective-permute-start.17 = (bf16[64,128]{1,0:T(8,128)(2,1)S(1)}, bf16[64,128]{1,0:T(8,128)(2,1)S(1)}, u32[]{:S(2)}, u32[]{:S(2)}) collective-permute-start(bf16[64,128]{1,0:T(8,128)(2,1)S(1)} %get-tuple-element.70), channel_id=1, source_target_pairs={{0,96},{32,0},{64,32},{96,64},{1,97},{33,1},{65,33},{97,65},{2,98}... | collective-permute-start | bytes 49160 | tf_op jit(solution)/shard_map/ppermute | solution.py:27
  62.6 1.2 %collective-permute-done.15.r1 = bf16[64,128]{1,0:T(8,128)(2,1)S(1)} collective-permute-done((bf16[64,128]{1,0:T(8,128)(2,1)S(1)}, bf16[64,128]{1,0:T(8,128)(2,1)S(1)}, u32[]{:S(2)}, u32[]{:S(2)}) %collective-permute-start.15) | collective-permute-done | bytes 16416 | tf_op jit(solution)/shard_map/ppermute | solution.py:27
  65.0 0.8 %shard_map.122 = (bf16[16,4,128]{2,1,0:T(4,128)(2,1)}, bf16[16,4,1024]{2,1,0:T(4,128)(2,1)}) custom-call(f32[64,128]{1,0:T(8,128)S(1)} %get-tuple-element.67.own, bf16[64,128]{1,0:T(8,128)(2,1)S(1)} %collective-permute-done.15.r1, bf16[64,128]{1,0:T(8,128)(2,1)S(1)} %collective-permute-done.16.r2, bf16[64,128]{1,0:T(8,128)(2,1)S(1)} %collective-permute-done.17.r3, ...), custom_call_target="tpu_custom_call" | custom-call | tf_op jit(solution)/shard_map/pallas_call | solution.py:258
  (39 shorter events, 3.9 us)
Async XLA Ops:
  0.6 6.2 %copy-start.6 = (bf16[16,4,1024]{2,1,0:T(4,128)(2,1)S(1)}, bf16[16,4,1024]{2,1,0:T(4,128)(2,1)}, u32[]{:S(2)}) copy-start(bf16[16,4,1024]{2,1,0:T(4,128)(2,1)} %param.12) | copy-start | bytes 393220
  6.7 2.7 %collective-permute-start = (bf16[4,4,256,128]{3,2,1,0:T(8,128)(2,1)S(1)}, bf16[4,4,256,128]{3,2,1,0:T(8,128)(2,1)S(1)}, u32[]{:S(2)}, u32[]{:S(2)}) collective-permute-start(bf16[4,4,256,128]{3,2,1,0:T(8,128)(2,1)S(1)} %get-tuple-element.40), channel_id=1, source_target_pairs={{0,128},{128,0},{1,129},{129,1},{2,130},{130,2},{3,131},{131,3},{4... | collective-permute-start | bytes 3145736 | tf_op jit(solution)/shard_map/ppermute | solution.py:27
  6.8 9.2 %collective-permute-start.4 = (bf16[16,4,1024]{2,1,0:T(4,128)(2,1)S(1)}, bf16[16,4,1024]{2,1,0:T(4,128)(2,1)S(1)}, u32[]{:S(2)}, u32[]{:S(2)}) collective-permute-start(bf16[16,4,1024]{2,1,0:T(4,128)(2,1)S(1)} %copy-done.6), channel_id=1, source_target_pairs={{0,0},{1,33},{2,66},{3,99},{32,1},{33,34},{34,67},{35,96},{64,2},{... | collective-permute-start | bytes 393224 | tf_op jit(solution)/shard_map/ppermute | solution.py:36
  9.7 18.1 %collective-permute-start.1 = (bf16[4,256,128]{2,1,0:T(8,128)(2,1)S(1)}, bf16[4,256,128]{2,1,0:T(8,128)(2,1)S(1)}, u32[]{:S(2)}, u32[]{:S(2)}) collective-permute-start(bf16[4,256,128]{2,1,0:T(8,128)(2,1)S(1)} %get-tuple-element.42), channel_id=1, source_target_pairs={{0,16},{8,24},{16,0},{24,8},{1,17},{9,25},{17,1},{25,9},{2,18},{10... | collective-permute-start | bytes 786440 | tf_op jit(solution)/shard_map/ppermute | solution.py:27
  12.8 15.0 %collective-permute-start.2 = (bf16[4,256,128]{2,1,0:T(8,128)(2,1)S(1)}, bf16[4,256,128]{2,1,0:T(8,128)(2,1)S(1)}, u32[]{:S(2)}, u32[]{:S(2)}) collective-permute-start(bf16[4,256,128]{2,1,0:T(8,128)(2,1)S(1)} %get-tuple-element.43), channel_id=1, source_target_pairs={{0,8},{8,16},{16,24},{24,0},{1,9},{9,17},{17,25},{25,1},{2,10},{10... | collective-permute-start | bytes 786440 | tf_op jit(solution)/shard_map/ppermute | solution.py:27
  13.4 14.5 %collective-permute-start.3 = (bf16[4,256,128]{2,1,0:T(8,128)(2,1)S(1)}, bf16[4,256,128]{2,1,0:T(8,128)(2,1)S(1)}, u32[]{:S(2)}, u32[]{:S(2)}) collective-permute-start(bf16[4,256,128]{2,1,0:T(8,128)(2,1)S(1)} %get-tuple-element.44), channel_id=1, source_target_pairs={{0,24},{8,0},{16,8},{24,16},{1,25},{9,1},{17,9},{25,17},{2,26},{10... | collective-permute-start | bytes 786440 | tf_op jit(solution)/shard_map/ppermute | solution.py:27
  16.0 5.4 %collective-permute-start.5 = (bf16[16,4,1024]{2,1,0:T(4,128)(2,1)S(1)}, bf16[16,4,1024]{2,1,0:T(4,128)(2,1)S(1)}, u32[]{:S(2)}, u32[]{:S(2)}) collective-permute-start(bf16[16,4,1024]{2,1,0:T(4,128)(2,1)S(1)} %collective-permute-done.4.first), channel_id=1, source_target_pairs={{0,4},{4,0},{1,5},{5,1},{2,6},{6,2},{3,7},{7,3},{8,12},{12,8},{9,1... | collective-permute-start | bytes 393224 | tf_op jit(solution)/shard_map/ppermute | solution.py:27
  21.5 20.8 %copy-start.1 = (bf16[16,128,128]{2,1,0:T(8,128)(2,1)S(1)}, bf16[16,128,128]{2,1,0:T(8,128)(2,1)}, u32[]{:S(2)}) copy-start(bf16[16,128,128]{2,1,0:T(8,128)(2,1)} %cache_keys.1) | copy-start | bytes 1572868
  21.5 20.8 %copy-start.2 = (bf16[16,128,128]{2,1,0:T(8,128)(2,1)S(1)}, bf16[16,128,128]{2,1,0:T(8,128)(2,1)}, u32[]{:S(2)}) copy-start(bf16[16,128,128]{2,1,0:T(8,128)(2,1)} %cache_values.1) | copy-start | bytes 1572868
  21.5 20.8 %copy-start.3 = (bf16[16,4,1024]{2,1,0:T(4,128)(2,1)S(1)}, bf16[16,4,1024]{2,1,0:T(4,128)(2,1)}, u32[]{:S(2)}) copy-start(bf16[16,4,1024]{2,1,0:T(4,128)(2,1)} %raw_queries) | copy-start | bytes 393220
  21.6 20.8 %copy-start.4 = (bf16[16,4,128]{2,1,0:T(4,128)(2,1)S(1)}, bf16[16,4,128]{2,1,0:T(4,128)(2,1)}, u32[]{:S(2)}) copy-start(bf16[16,4,128]{2,1,0:T(4,128)(2,1)} %param.14) | copy-start | bytes 49156
  21.6 20.8 %copy-start.5 = (s32[16]{0:T(128)S(1)}, s32[16]{0:T(128)}, u32[]{:S(2)}) copy-start(s32[16]{0:T(128)} %lengths.1) | copy-start | bytes 196
  21.6 17.2 %collective-permute-start.9 = (bf16[2,64,1024]{2,1,0:T(8,128)(2,1)S(1)}, bf16[2,64,1024]{2,1,0:T(8,128)(2,1)S(1)}, u32[]{:S(2)}, u32[]{:S(2)}) collective-permute-start(bf16[2,64,1024]{2,1,0:T(8,128)(2,1)S(1)} %shard_map.114.first), channel_id=1, source_target_pairs={{0,1},{1,0},{2,3},{3,2},{4,5},{5,4},{6,7},{7,6},{8,9},{9,8},{10,11... | collective-permute-start | bytes 786440 | tf_op jit(solution)/shard_map/ppermute | solution.py:31
  27.9 16.6 %collective-permute-start.6 = (bf16[256,128]{1,0:T(8,128)(2,1)S(1)}, bf16[256,128]{1,0:T(8,128)(2,1)S(1)}, u32[]{:S(2)}, u32[]{:S(2)}) collective-permute-start(bf16[256,128]{1,0:T(8,128)(2,1)S(1)} %get-tuple-element.52), channel_id=1, source_target_pairs={{0,64},{32,96},{64,0},{96,32},{1,65},{33,97},{65,1},{97,33},{2,66}... | collective-permute-start | bytes 196616 | tf_op jit(solution)/shard_map/ppermute | solution.py:27
  34.7 9.9 %collective-permute-start.7 = (bf16[256,128]{1,0:T(8,128)(2,1)S(1)}, bf16[256,128]{1,0:T(8,128)(2,1)S(1)}, u32[]{:S(2)}, u32[]{:S(2)}) collective-permute-start(bf16[256,128]{1,0:T(8,128)(2,1)S(1)} %get-tuple-element.53), channel_id=1, source_target_pairs={{0,32},{32,64},{64,96},{96,0},{1,33},{33,65},{65,97},{97,1},{2,34}... | collective-permute-start | bytes 196616 | tf_op jit(solution)/shard_map/ppermute | solution.py:27
  38.4 6.2 %collective-permute-start.8 = (bf16[256,128]{1,0:T(8,128)(2,1)S(1)}, bf16[256,128]{1,0:T(8,128)(2,1)S(1)}, u32[]{:S(2)}, u32[]{:S(2)}) collective-permute-start(bf16[256,128]{1,0:T(8,128)(2,1)S(1)} %get-tuple-element.54), channel_id=1, source_target_pairs={{0,96},{32,0},{64,32},{96,64},{1,97},{33,1},{65,33},{97,65},{2,98}... | collective-permute-start | bytes 196616 | tf_op jit(solution)/shard_map/ppermute | solution.py:27
  38.9 16.2 %collective-permute-start.13 = (bf16[4,64,1024]{2,1,0:T(8,128)(2,1)S(1)}, bf16[4,64,1024]{2,1,0:T(8,128)(2,1)S(1)}, u32[]{:S(2)}, u32[]{:S(2)}) collective-permute-start(bf16[4,64,1024]{2,1,0:T(8,128)(2,1)S(1)} %shard_map.116.near), channel_id=1, source_target_pairs={{0,3},{1,2},{2,1},{3,0},{4,7},{5,6},{6,5},{7,4},{8,11},{9,10},{10,... | collective-permute-start | bytes 1572872 | tf_op jit(solution)/shard_map/ppermute | solution.py:31
  44.6 6.6 %collective-permute-start.12 = (bf16[256,128]{1,0:T(8,128)(2,1)S(1)}, bf16[256,128]{1,0:T(8,128)(2,1)S(1)}, u32[]{:S(2)}, u32[]{:S(2)}) collective-permute-start(bf16[256,128]{1,0:T(8,128)(2,1)S(1)} %shard_map.118), channel_id=1, source_target_pairs={{0,8},{8,16},{16,24},{24,0},{1,9},{9,17},{17,25},{25,1},{2,10},{10... | collective-permute-start | bytes 196616 | tf_op jit(solution)/shard_map/ppermute | solution.py:27
  46.4 5.8 %collective-permute-start.11 = (bf16[256,128]{1,0:T(8,128)(2,1)S(1)}, bf16[256,128]{1,0:T(8,128)(2,1)S(1)}, u32[]{:S(2)}, u32[]{:S(2)}) collective-permute-start(bf16[256,128]{1,0:T(8,128)(2,1)S(1)} %shard_map.118), channel_id=1, source_target_pairs={{0,16},{8,24},{16,0},{24,8},{1,17},{9,25},{17,1},{25,9},{2,18},{10... | collective-permute-start | bytes 196616 | tf_op jit(solution)/shard_map/ppermute | solution.py:27
  49.1 4.3 %collective-permute-start.10 = (bf16[256,128]{1,0:T(8,128)(2,1)S(1)}, bf16[256,128]{1,0:T(8,128)(2,1)S(1)}, u32[]{:S(2)}, u32[]{:S(2)}) collective-permute-start(bf16[256,128]{1,0:T(8,128)(2,1)S(1)} %shard_map.118), channel_id=1, source_target_pairs={{0,24},{8,0},{16,8},{24,16},{1,25},{9,1},{17,9},{25,17},{2,26},{10... | collective-permute-start | bytes 196616 | tf_op jit(solution)/shard_map/ppermute | solution.py:27
  53.4 1.6 %collective-permute-start.14 = (bf16[4,256,128]{2,1,0:T(8,128)(2,1)S(1)}, bf16[4,256,128]{2,1,0:T(8,128)(2,1)S(1)}, u32[]{:S(2)}, u32[]{:S(2)}) collective-permute-start(bf16[4,256,128]{2,1,0:T(8,128)(2,1)S(1)} %pad_maximum_fusion.u.u_own), channel_id=1, source_target_pairs={{0,128},{128,0},{1,129},{129,1},{2,130},{130,2},{3,131},{131,3},{4... | collective-permute-start | bytes 786440 | tf_op jit(solution)/shard_map/ppermute | solution.py:27
  56.0 7.7 %collective-permute-start.15 = (bf16[64,128]{1,0:T(8,128)(2,1)S(1)}, bf16[64,128]{1,0:T(8,128)(2,1)S(1)}, u32[]{:S(2)}, u32[]{:S(2)}) collective-permute-start(bf16[64,128]{1,0:T(8,128)(2,1)S(1)} %get-tuple-element.68), channel_id=1, source_target_pairs={{0,64},{32,96},{64,0},{96,32},{1,65},{33,97},{65,1},{97,33},{2,66}... | collective-permute-start | bytes 49160 | tf_op jit(solution)/shard_map/ppermute | solution.py:27
  58.4 5.8 %collective-permute-start.16 = (bf16[64,128]{1,0:T(8,128)(2,1)S(1)}, bf16[64,128]{1,0:T(8,128)(2,1)S(1)}, u32[]{:S(2)}, u32[]{:S(2)}) collective-permute-start(bf16[64,128]{1,0:T(8,128)(2,1)S(1)} %get-tuple-element.69), channel_id=1, source_target_pairs={{0,32},{32,64},{64,96},{96,0},{1,33},{33,65},{65,97},{97,1},{2,34}... | collective-permute-start | bytes 49160 | tf_op jit(solution)/shard_map/ppermute | solution.py:27
  60.3 4.6 %collective-permute-start.17 = (bf16[64,128]{1,0:T(8,128)(2,1)S(1)}, bf16[64,128]{1,0:T(8,128)(2,1)S(1)}, u32[]{:S(2)}, u32[]{:S(2)}) collective-permute-start(bf16[64,128]{1,0:T(8,128)(2,1)S(1)} %get-tuple-element.70), channel_id=1, source_target_pairs={{0,96},{32,0},{64,32},{96,64},{1,97},{33,1},{65,33},{97,65},{2,98}... | collective-permute-start | bytes 49160 | tf_op jit(solution)/shard_map/ppermute | solution.py:27
  (1 other events, 2.2 us)

commit v17 on v16

--- a/solution.py
+++ b/solution.py
@@ -191,36 +191,30 @@
     )(lengths, queries, new_keys, cache_keys, cache_values)
 
 
-def fill_rows(rows, x, updated):
-    for d in range(4):
-        rows[pl.ds(pl.multiple_of(lax.rem(x + d, 4) * 256, 256), 256), :] = updated[d]
+def fill_rows(rows, x, updated, core):
+    for d, u in enumerate(updated):
+        rows[pl.ds(pl.multiple_of(lax.rem(x + d, 4) * 256, 256), 256), :] = u[core]
 
 
 def tokens_of(place, bits):
     return lax.rem(jnp.bitwise_xor(place[3], bits) + 4 - place[1], 4)
 
 
-def project_own_kernel(place, near, u, out_ref, rows):
+def project_kernel(place, near, far, u0, u1, u2, u3, o0, o1, o2, o3, rows, last, sums):
     own = jnp.where(place[0] == place[4], 0, 1)
-    fill_rows(rows, place[2], u)
-    inputs = jnp.concatenate([near[own], near[2 + own]], axis=0)
-    out_ref[...] = jnp.dot(inputs, rows[...], preferred_element_type=F32)
-
-
-def project_rest_kernel(place, near, far, u_own, u_other, start, o0, o1, o2, o3, rows, last, sums):
-    own = jnp.where(place[0] == place[4], 0, 1)
-    fill_rows(last, place[2], u_own)
-    fill_rows(rows, place[2], u_other)
+    fill_rows(last, place[2], (u0, u1, u2, u3), 0)
+    fill_rows(rows, place[2], (u0, u1, u2, u3), 1)
     inputs = [near[1 - own], near[3 - own], far[1 - own], far[3 - own]]
     product = jnp.dot(
         jnp.concatenate(inputs, axis=0), rows[...], preferred_element_type=F32
     )
-    inputs = jnp.concatenate([far[own], far[2 + own]], axis=0)
-    more = jnp.dot(inputs, last[...], preferred_element_type=F32)
+    inputs = [near[own], near[2 + own], far[own], far[2 + own]]
+    product += jnp.dot(
+        jnp.concatenate(inputs, axis=0), last[...], preferred_element_type=F32
+    )
     size = far.shape[1]
     for i, bits in enumerate((0, 1, 3, 2)):
-        rest = start[i * size : (i + 1) * size] if i < 2 else more[(i - 2) * size : (i - 1) * size]
-        total = product[i * size : (i + 1) * size] + rest
+        total = product[i * size : (i + 1) * size]
         sums[lax.rem(tokens_of(place, bits) + 4 - place[1], 4)] = total
     for e, out in enumerate((o0, o1, o2, o3)):
         out[...] = sums[e].astype(out.dtype)
@@ -316,23 +310,18 @@
     own = after(own, updated)
     (gradient,) = small_call(gradient_kernel, [(rows, F32)], own, *along_z, keep=False)
 
-    gathered = jnp.stack([updated] + [shift(updated, "x", -d) for d in (1, 2, 3)])
+    pair = jnp.stack([updated, shift(updated, "c", 1)])
+    gathered = [pair] + [shift(pair, "x", -d) for d in (1, 2, 3)]
     gathered, gradient = lax.optimization_barrier((gathered, gradient))
-    other = shift(gathered, "c", 1)
     scratch, tokens = ((1024, HD), BF16), (places, HD)
-    (partial,) = project(
-        project_own_kernel, [((2 * places, HD), F32)], [scratch], place, near, gathered
-    )
     own, *sent = project(
-        project_rest_kernel,
+        project_kernel,
         [(tokens, F32)] + [(tokens, BF16)] * 3,
         [scratch, scratch, ((4, places, HD), F32)],
         place,
         near,
         far,
-        gathered,
-        other,
-        partial,
+        *gathered,
     )
     exchanged = [own] + [shift(sent[e - 1], "zh", e) for e in (2, 1, 3)]
     new_values, attended = finish(

time: 67.1 us -> 68.8 us (1.025)
  waiting for transfers between devices: 12.6 us -> 15.2 us
  Pallas kernels: 11.8 us -> 11.1 us
    ppermute x15, waiting for transfers between devices: 12.6 us -> 15.2 us  [shift(): return lax.ppermute(value, axis, [(i, (i + by) % n) for i in range(n)])]
    pallas_call x2 -> x1, Pallas kernels: 1.74 us -> 1.02 us  [project(): pl.pallas_call(kernel, in_specs=[SMEM] + [VMEM] * len(args), out_specs=[V...]
  transfers between devices with their start and end apart: 18 -> 18, of which waited for: 8 -> 8; matrix products, arithmetic and copies ran while one was open for 0% -> 0% of each run, Pallas kernels for 6% -> 5%
where the time goes in v17:
time: 68.8 us; the launch traced here: 67.7 us
  starting transfers between devices  40.4 us (59%)
  waiting for transfers between devices  15.2 us (22%)
  Pallas kernels  11.1 us (16%)
  between operations  0.84 us (1%)
    ppermute x15, starting transfers between devices, shift(): return lax.ppermute(value, axis, [(i, (i + by) % n) for i in range(n)])  30 us
    ppermute x15, waiting for transfers between devices, shift(): return lax.ppermute(value, axis, [(i, (i + by) % n) for i in range(n)])  15.2 us
    ppermute x2, starting transfers between devices, exchange(): return lax.ppermute(value, axis, [(i, i ^ bit) for i in range(SIZES[axis])])  9.73 us
    pallas_call x1, Pallas kernels, partial_gradient(): pl.pallas_call(partial_kernel, in_specs=[SMEM, HBM, HBM], out_specs=[VMEM...  5.96 us
    pallas_call x1, Pallas kernels, attend_cache(): pl.pallas_call(attend_kernel, in_specs=[SMEM] + [VMEM] * 4, out_specs=[VM...  2.15 us
  transfers between devices with their start and end apart: 18, of which 8 were waited for; matrix products, arithmetic and copies ran while one was open for 0% of the time, Pallas kernels for 5%

profile of v17, /device:TPU:32, one launch (start us, length us, event | category | flops | bytes accessed | tf_op | source)
XLA Modules:
  0.0 67.7 jit_solution(13925458060326960752)
XLA Ops:
  0.7 6.0 %shard_map.112 = (bf16[4,4,256,128]{3,2,1,0:T(8,128)(2,1)S(1)}, bf16[4,4,256,128]{3,2,1,0:T(8,128)(2,1)S(1)}) custom-call(s32[5]{0:T(128)S(1)} %stack.32.place, bf16[768,8192]{1,0:T(8,128)(2,1)} %x_hbm.1, bf16[768,128]{1,0:T(8,128)(2,1)} %v_hbm.1), custom_call_target="tpu_custom_call" | custom-call | flops 1610612736 | bytes 12582912 | tf_op jit(solution)/shard_map/pallas_call | solution.py:71
  6.8 0.7 collective-permute-start.4
  7.5 2.0 %collective-permute-done.received = bf16[4,4,256,128]{3,2,1,0:T(8,128)(2,1)S(1)} collective-permute-done((bf16[4,4,256,128]{3,2,1,0:T(8,128)(2,1)S(1)}, bf16[4,4,256,128]{3,2,1,0:T(8,128)(2,1)S(1)}, u32[]{:S(2)}, u32[]{:S(2)}) %collective-permute-start) | collective-permute-done | bytes 1048608 | tf_op jit(solution)/shard_map/ppermute | solution.py:27
  9.7 3.1 %collective-permute-start.1 = (bf16[4,256,128]{2,1,0:T(8,128)(2,1)S(1)}, bf16[4,256,128]{2,1,0:T(8,128)(2,1)S(1)}, u32[]{:S(2)}, u32[]{:S(2)}) collective-permute-start(bf16[4,256,128]{2,1,0:T(8,128)(2,1)S(1)} %get-tuple-element.45), channel_id=1, source_target_pairs={{0,16},{8,24},{16,0},{24,8},{1,17},{9,25},{17,1},{25,9},{2,18},{10... | collective-permute-start | bytes 786440 | tf_op jit(solution)/shard_map/ppermute | solution.py:27
  13.4 2.6 %collective-permute-start.3 = (bf16[4,256,128]{2,1,0:T(8,128)(2,1)S(1)}, bf16[4,256,128]{2,1,0:T(8,128)(2,1)S(1)}, u32[]{:S(2)}, u32[]{:S(2)}) collective-permute-start(bf16[4,256,128]{2,1,0:T(8,128)(2,1)S(1)} %get-tuple-element.47), channel_id=1, source_target_pairs={{0,24},{8,0},{16,8},{24,16},{1,25},{9,1},{17,9},{25,17},{2,26},{10... | collective-permute-start | bytes 786440 | tf_op jit(solution)/shard_map/ppermute | solution.py:27
  16.1 5.3 %collective-permute-done.5.second = bf16[16,4,1024]{2,1,0:T(4,128)(2,1)S(1)} collective-permute-done((bf16[16,4,1024]{2,1,0:T(4,128)(2,1)S(1)}, bf16[16,4,1024]{2,1,0:T(4,128)(2,1)S(1)}, u32[]{:S(2)}, u32[]{:S(2)}) %collective-permute-start.5) | collective-permute-done | bytes 131104 | tf_op jit(solution)/shard_map/ppermute | solution.py:27
  21.6 6.2 %collective-permute-start.9 = (bf16[2,64,1024]{2,1,0:T(8,128)(2,1)S(1)}, bf16[2,64,1024]{2,1,0:T(8,128)(2,1)S(1)}, u32[]{:S(2)}, u32[]{:S(2)}) collective-permute-start(bf16[2,64,1024]{2,1,0:T(8,128)(2,1)S(1)} %shard_map.114.first), channel_id=1, source_target_pairs={{0,1},{1,0},{2,3},{3,2},{4,5},{5,4},{6,7},{7,6},{8,9},{9,8},{10,11... | collective-permute-start | bytes 786440 | tf_op jit(solution)/shard_map/ppermute | solution.py:31
  27.9 6.7 %collective-permute-start.6 = (bf16[256,128]{1,0:T(8,128)(2,1)S(1)}, bf16[256,128]{1,0:T(8,128)(2,1)S(1)}, u32[]{:S(2)}, u32[]{:S(2)}) collective-permute-start(bf16[256,128]{1,0:T(8,128)(2,1)S(1)} %get-tuple-element.55), channel_id=1, source_target_pairs={{0,64},{32,96},{64,0},{96,32},{1,65},{33,97},{65,1},{97,33},{2,66}... | collective-permute-start | bytes 196616 | tf_op jit(solution)/shard_map/ppermute | solution.py:27
  34.7 3.7 %collective-permute-start.7 = (bf16[256,128]{1,0:T(8,128)(2,1)S(1)}, bf16[256,128]{1,0:T(8,128)(2,1)S(1)}, u32[]{:S(2)}, u32[]{:S(2)}) collective-permute-start(bf16[256,128]{1,0:T(8,128)(2,1)S(1)} %get-tuple-element.56), channel_id=1, source_target_pairs={{0,32},{32,64},{64,96},{96,0},{1,33},{33,65},{65,97},{97,1},{2,34}... | collective-permute-start | bytes 196616 | tf_op jit(solution)/shard_map/ppermute | solution.py:27
  38.9 3.5 %collective-permute-start.14 = (bf16[4,64,1024]{2,1,0:T(8,128)(2,1)S(1)}, bf16[4,64,1024]{2,1,0:T(8,128)(2,1)S(1)}, u32[]{:S(2)}, u32[]{:S(2)}) collective-permute-start(bf16[4,64,1024]{2,1,0:T(8,128)(2,1)S(1)} %shard_map.116.near), channel_id=1, source_target_pairs={{0,3},{1,2},{2,1},{3,0},{4,7},{5,6},{6,5},{7,4},{8,11},{9,10},{10,... | collective-permute-start | bytes 1572872 | tf_op jit(solution)/shard_map/ppermute | solution.py:31
  42.4 2.1 %shard_map.117 = (f32[512,128]{1,0:T(8,128)S(1)}, bf16[512,64]{1,0:T(8,128)(2,1)S(1)}) custom-call(s32[16]{0:T(128)S(1)} %copy-done.5, bf16[16,4,1024]{2,1,0:T(4,128)(2,1)S(1)} %copy-done.3, bf16[64,128]{1,0:T(8,128)(2,1)S(1)} %bitcast.9, bf16[16,128,128]{2,1,0:T(8,128)(2,1)S(1)} %copy-done.1, bf16[16,128,128]{2,1,0:T(8,128)(2,1)S(1)} %copy-done.2), custom_call_target="tpu_custom_call" | custom-call | flops 8388608000 | bytes 20971520 | tf_op jit(solution)/shard_map/pallas_call | solution.py:178
  44.7 1.2 %collective-permute-done.10 = bf16[256,128]{1,0:T(8,128)(2,1)S(1)} collective-permute-done((bf16[256,128]{1,0:T(8,128)(2,1)S(1)}, bf16[256,128]{1,0:T(8,128)(2,1)S(1)}, u32[]{:S(2)}, u32[]{:S(2)}) %collective-permute-start.10) | collective-permute-done | bytes 65568 | tf_op jit(solution)/shard_map/ppermute | solution.py:27
  46.0 1.7 %collective-permute-start.13 = (bf16[2,256,128]{2,1,0:T(8,128)(2,1)S(1)}, bf16[2,256,128]{2,1,0:T(8,128)(2,1)S(1)}, u32[]{:S(2)}, u32[]{:S(2)}) collective-permute-start(bf16[2,256,128]{2,1,0:T(8,128)(2,1)S(1)} %pad_maximum_fusion.u0), channel_id=1, source_target_pairs={{0,8},{8,16},{16,24},{24,0},{1,9},{9,17},{17,25},{25,1},{2,10},{10... | collective-permute-start | bytes 393224 | tf_op jit(solution)/shard_map/ppermute | solution.py:27
  47.7 2.7 %collective-permute-start.12 = (bf16[2,256,128]{2,1,0:T(8,128)(2,1)S(1)}, bf16[2,256,128]{2,1,0:T(8,128)(2,1)S(1)}, u32[]{:S(2)}, u32[]{:S(2)}) collective-permute-start(bf16[2,256,128]{2,1,0:T(8,128)(2,1)S(1)} %pad_maximum_fusion.u0), channel_id=1, source_target_pairs={{0,16},{8,24},{16,0},{24,8},{1,17},{9,25},{17,1},{25,9},{2,18},{10... | collective-permute-start | bytes 393224 | tf_op jit(solution)/shard_map/ppermute | solution.py:27
  50.5 1.4 %collective-permute-start.11 = (bf16[2,256,128]{2,1,0:T(8,128)(2,1)S(1)}, bf16[2,256,128]{2,1,0:T(8,128)(2,1)S(1)}, u32[]{:S(2)}, u32[]{:S(2)}) collective-permute-start(bf16[2,256,128]{2,1,0:T(8,128)(2,1)S(1)} %pad_maximum_fusion.u0), channel_id=1, source_target_pairs={{0,24},{8,0},{16,8},{24,16},{1,25},{9,1},{17,9},{25,17},{2,26},{10... | collective-permute-start | bytes 393224 | tf_op jit(solution)/shard_map/ppermute | solution.py:27
  51.9 0.7 %shard_map.119 = f32[256,128]{1,0:T(8,128)} custom-call(f32[256,128]{1,0:T(8,128)S(1)} %get-tuple-element.67.own, bf16[256,128]{1,0:T(8,128)(2,1)S(1)} %collective-permute-done.6.r1, bf16[256,128]{1,0:T(8,128)(2,1)S(1)} %collective-permute-done.7.r2, bf16[256,128]{1,0:T(8,128)(2,1)S(1)} %collective-permute-done.8.r3), custom_call_target="tpu_custom_call" | custom-call | flops 1048576 | bytes 2097152 | tf_op jit(solution)/shard_map/pallas_call | solution.py:89
  53.0 3.8 %collective-permute-done.12.u2 = bf16[2,256,128]{2,1,0:T(8,128)(2,1)S(1)} collective-permute-done((bf16[2,256,128]{2,1,0:T(8,128)(2,1)S(1)}, bf16[2,256,128]{2,1,0:T(8,128)(2,1)S(1)}, u32[]{:S(2)}, u32[]{:S(2)}) %collective-permute-start.12) | collective-permute-done | bytes 131104 | tf_op jit(solution)/shard_map/ppermute | solution.py:27
  56.8 1.0 %shard_map.120 = (f32[64,128]{1,0:T(8,128)S(1)}, bf16[64,128]{1,0:T(8,128)(2,1)S(1)}, bf16[64,128]{1,0:T(8,128)(2,1)S(1)}, bf16[64,128]{1,0:T(8,128)(2,1)S(1)}) custom-call(s32[5]{0:T(128)S(1)} %stack.32.place, bf16[4,64,1024]{2,1,0:T(8,128)(2,1)S(1)} %shard_map.116.near, bf16[4,64,1024]{2,1,0:T(8,128)(2,1)S(1)} %collective-permute-done.14.far, ...), custom_call_target="tpu_custom_call" | custom-call | flops 67108864 | bytes 786432 | tf_op jit(solution)/shard_map/pallas_call | solution.py:224
  57.9 2.4 %collective-permute-start.15 = (bf16[64,128]{1,0:T(8,128)(2,1)S(1)}, bf16[64,128]{1,0:T(8,128)(2,1)S(1)}, u32[]{:S(2)}, u32[]{:S(2)}) collective-permute-start(bf16[64,128]{1,0:T(8,128)(2,1)S(1)} %get-tuple-element.74), channel_id=1, source_target_pairs={{0,64},{32,96},{64,0},{96,32},{1,65},{33,97},{65,1},{97,33},{2,66}... | collective-permute-start | bytes 49160 | tf_op jit(solution)/shard_map/ppermute | solution.py:27
  60.3 1.9 %collective-permute-start.16 = (bf16[64,128]{1,0:T(8,128)(2,1)S(1)}, bf16[64,128]{1,0:T(8,128)(2,1)S(1)}, u32[]{:S(2)}, u32[]{:S(2)}) collective-permute-start(bf16[64,128]{1,0:T(8,128)(2,1)S(1)} %get-tuple-element.75), channel_id=1, source_target_pairs={{0,32},{32,64},{64,96},{96,0},{1,33},{33,65},{65,97},{97,1},{2,34}... | collective-permute-start | bytes 49160 | tf_op jit(solution)/shard_map/ppermute | solution.py:27
  62.2 2.2 %collective-permute-start.17 = (bf16[64,128]{1,0:T(8,128)(2,1)S(1)}, bf16[64,128]{1,0:T(8,128)(2,1)S(1)}, u32[]{:S(2)}, u32[]{:S(2)}) collective-permute-start(bf16[64,128]{1,0:T(8,128)(2,1)S(1)} %get-tuple-element.76), channel_id=1, source_target_pairs={{0,96},{32,0},{64,32},{96,64},{1,97},{33,1},{65,33},{97,65},{2,98}... | collective-permute-start | bytes 49160 | tf_op jit(solution)/shard_map/ppermute | solution.py:27
  64.4 1.2 %collective-permute-done.15.r1 = bf16[64,128]{1,0:T(8,128)(2,1)S(1)} collective-permute-done((bf16[64,128]{1,0:T(8,128)(2,1)S(1)}, bf16[64,128]{1,0:T(8,128)(2,1)S(1)}, u32[]{:S(2)}, u32[]{:S(2)}) %collective-permute-start.15) | collective-permute-done | bytes 16416 | tf_op jit(solution)/shard_map/ppermute | solution.py:27
  66.1 0.7 %collective-permute-done.17.r3 = bf16[64,128]{1,0:T(8,128)(2,1)S(1)} collective-permute-done((bf16[64,128]{1,0:T(8,128)(2,1)S(1)}, bf16[64,128]{1,0:T(8,128)(2,1)S(1)}, u32[]{:S(2)}, u32[]{:S(2)}) %collective-permute-start.17) | collective-permute-done | bytes 16416 | tf_op jit(solution)/shard_map/ppermute | solution.py:27
  66.8 0.8 %shard_map.121 = (bf16[16,4,128]{2,1,0:T(4,128)(2,1)}, bf16[16,4,1024]{2,1,0:T(4,128)(2,1)}) custom-call(f32[64,128]{1,0:T(8,128)S(1)} %get-tuple-element.73.own, bf16[64,128]{1,0:T(8,128)(2,1)S(1)} %collective-permute-done.15.r1, bf16[64,128]{1,0:T(8,128)(2,1)S(1)} %collective-permute-done.16.r2, bf16[64,128]{1,0:T(8,128)(2,1)S(1)} %collective-permute-done.17.r3, ...), custom_call_target="tpu_custom_call" | custom-call | tf_op jit(solution)/shard_map/pallas_call | solution.py:252
  (38 shorter events, 2.9 us)
Async XLA Ops:
  0.6 6.2 %copy-start.6 = (bf16[16,4,1024]{2,1,0:T(4,128)(2,1)S(1)}, bf16[16,4,1024]{2,1,0:T(4,128)(2,1)}, u32[]{:S(2)}) copy-start(bf16[16,4,1024]{2,1,0:T(4,128)(2,1)} %param.12) | copy-start | bytes 393220
  6.7 2.7 %collective-permute-start = (bf16[4,4,256,128]{3,2,1,0:T(8,128)(2,1)S(1)}, bf16[4,4,256,128]{3,2,1,0:T(8,128)(2,1)S(1)}, u32[]{:S(2)}, u32[]{:S(2)}) collective-permute-start(bf16[4,4,256,128]{3,2,1,0:T(8,128)(2,1)S(1)} %get-tuple-element.43), channel_id=1, source_target_pairs={{0,128},{128,0},{1,129},{129,1},{2,130},{130,2},{3,131},{131,3},{4... | collective-permute-start | bytes 3145736 | tf_op jit(solution)/shard_map/ppermute | solution.py:27
  6.8 9.2 %collective-permute-start.4 = (bf16[16,4,1024]{2,1,0:T(4,128)(2,1)S(1)}, bf16[16,4,1024]{2,1,0:T(4,128)(2,1)S(1)}, u32[]{:S(2)}, u32[]{:S(2)}) collective-permute-start(bf16[16,4,1024]{2,1,0:T(4,128)(2,1)S(1)} %copy-done.6), channel_id=1, source_target_pairs={{0,0},{1,33},{2,66},{3,99},{32,1},{33,34},{34,67},{35,96},{64,2},{... | collective-permute-start | bytes 393224 | tf_op jit(solution)/shard_map/ppermute | solution.py:36
  9.7 18.1 %collective-permute-start.1 = (bf16[4,256,128]{2,1,0:T(8,128)(2,1)S(1)}, bf16[4,256,128]{2,1,0:T(8,128)(2,1)S(1)}, u32[]{:S(2)}, u32[]{:S(2)}) collective-permute-start(bf16[4,256,128]{2,1,0:T(8,128)(2,1)S(1)} %get-tuple-element.45), channel_id=1, source_target_pairs={{0,16},{8,24},{16,0},{24,8},{1,17},{9,25},{17,1},{25,9},{2,18},{10... | collective-permute-start | bytes 786440 | tf_op jit(solution)/shard_map/ppermute | solution.py:27
  12.8 15.0 %collective-permute-start.2 = (bf16[4,256,128]{2,1,0:T(8,128)(2,1)S(1)}, bf16[4,256,128]{2,1,0:T(8,128)(2,1)S(1)}, u32[]{:S(2)}, u32[]{:S(2)}) collective-permute-start(bf16[4,256,128]{2,1,0:T(8,128)(2,1)S(1)} %get-tuple-element.46), channel_id=1, source_target_pairs={{0,8},{8,16},{16,24},{24,0},{1,9},{9,17},{17,25},{25,1},{2,10},{10... | collective-permute-start | bytes 786440 | tf_op jit(solution)/shard_map/ppermute | solution.py:27
  13.4 14.5 %collective-permute-start.3 = (bf16[4,256,128]{2,1,0:T(8,128)(2,1)S(1)}, bf16[4,256,128]{2,1,0:T(8,128)(2,1)S(1)}, u32[]{:S(2)}, u32[]{:S(2)}) collective-permute-start(bf16[4,256,128]{2,1,0:T(8,128)(2,1)S(1)} %get-tuple-element.47), channel_id=1, source_target_pairs={{0,24},{8,0},{16,8},{24,16},{1,25},{9,1},{17,9},{25,17},{2,26},{10... | collective-permute-start | bytes 786440 | tf_op jit(solution)/shard_map/ppermute | solution.py:27
  16.0 5.4 %collective-permute-start.5 = (bf16[16,4,1024]{2,1,0:T(4,128)(2,1)S(1)}, bf16[16,4,1024]{2,1,0:T(4,128)(2,1)S(1)}, u32[]{:S(2)}, u32[]{:S(2)}) collective-permute-start(bf16[16,4,1024]{2,1,0:T(4,128)(2,1)S(1)} %collective-permute-done.4.first), channel_id=1, source_target_pairs={{0,4},{4,0},{1,5},{5,1},{2,6},{6,2},{3,7},{7,3},{8,12},{12,8},{9,1... | collective-permute-start | bytes 393224 | tf_op jit(solution)/shard_map/ppermute | solution.py:27
  21.5 20.8 %copy-start.1 = (bf16[16,128,128]{2,1,0:T(8,128)(2,1)S(1)}, bf16[16,128,128]{2,1,0:T(8,128)(2,1)}, u32[]{:S(2)}) copy-start(bf16[16,128,128]{2,1,0:T(8,128)(2,1)} %cache_keys.1) | copy-start | bytes 1572868
  21.5 20.8 %copy-start.2 = (bf16[16,128,128]{2,1,0:T(8,128)(2,1)S(1)}, bf16[16,128,128]{2,1,0:T(8,128)(2,1)}, u32[]{:S(2)}) copy-start(bf16[16,128,128]{2,1,0:T(8,128)(2,1)} %cache_values.1) | copy-start | bytes 1572868
  21.5 20.8 %copy-start.3 = (bf16[16,4,1024]{2,1,0:T(4,128)(2,1)S(1)}, bf16[16,4,1024]{2,1,0:T(4,128)(2,1)}, u32[]{:S(2)}) copy-start(bf16[16,4,1024]{2,1,0:T(4,128)(2,1)} %raw_queries) | copy-start | bytes 393220
  21.6 20.8 %copy-start.4 = (bf16[16,4,128]{2,1,0:T(4,128)(2,1)S(1)}, bf16[16,4,128]{2,1,0:T(4,128)(2,1)}, u32[]{:S(2)}) copy-start(bf16[16,4,128]{2,1,0:T(4,128)(2,1)} %param.14) | copy-start | bytes 49156
  21.6 20.8 %copy-start.5 = (s32[16]{0:T(128)S(1)}, s32[16]{0:T(128)}, u32[]{:S(2)}) copy-start(s32[16]{0:T(128)} %lengths.1) | copy-start | bytes 196
  21.6 17.2 %collective-permute-start.9 = (bf16[2,64,1024]{2,1,0:T(8,128)(2,1)S(1)}, bf16[2,64,1024]{2,1,0:T(8,128)(2,1)S(1)}, u32[]{:S(2)}, u32[]{:S(2)}) collective-permute-start(bf16[2,64,1024]{2,1,0:T(8,128)(2,1)S(1)} %shard_map.114.first), channel_id=1, source_target_pairs={{0,1},{1,0},{2,3},{3,2},{4,5},{5,4},{6,7},{7,6},{8,9},{9,8},{10,11... | collective-permute-start | bytes 786440 | tf_op jit(solution)/shard_map/ppermute | solution.py:31
  27.9 16.6 %collective-permute-start.6 = (bf16[256,128]{1,0:T(8,128)(2,1)S(1)}, bf16[256,128]{1,0:T(8,128)(2,1)S(1)}, u32[]{:S(2)}, u32[]{:S(2)}) collective-permute-start(bf16[256,128]{1,0:T(8,128)(2,1)S(1)} %get-tuple-element.55), channel_id=1, source_target_pairs={{0,64},{32,96},{64,0},{96,32},{1,65},{33,97},{65,1},{97,33},{2,66}... | collective-permute-start | bytes 196616 | tf_op jit(solution)/shard_map/ppermute | solution.py:27
  34.7 9.9 %collective-permute-start.7 = (bf16[256,128]{1,0:T(8,128)(2,1)S(1)}, bf16[256,128]{1,0:T(8,128)(2,1)S(1)}, u32[]{:S(2)}, u32[]{:S(2)}) collective-permute-start(bf16[256,128]{1,0:T(8,128)(2,1)S(1)} %get-tuple-element.56), channel_id=1, source_target_pairs={{0,32},{32,64},{64,96},{96,0},{1,33},{33,65},{65,97},{97,1},{2,34}... | collective-permute-start | bytes 196616 | tf_op jit(solution)/shard_map/ppermute | solution.py:27
  38.4 6.2 %collective-permute-start.8 = (bf16[256,128]{1,0:T(8,128)(2,1)S(1)}, bf16[256,128]{1,0:T(8,128)(2,1)S(1)}, u32[]{:S(2)}, u32[]{:S(2)}) collective-permute-start(bf16[256,128]{1,0:T(8,128)(2,1)S(1)} %get-tuple-element.57), channel_id=1, source_target_pairs={{0,96},{32,0},{64,32},{96,64},{1,97},{33,1},{65,33},{97,65},{2,98}... | collective-permute-start | bytes 196616 | tf_op jit(solution)/shard_map/ppermute | solution.py:27
  38.9 18.0 %collective-permute-start.14 = (bf16[4,64,1024]{2,1,0:T(8,128)(2,1)S(1)}, bf16[4,64,1024]{2,1,0:T(8,128)(2,1)S(1)}, u32[]{:S(2)}, u32[]{:S(2)}) collective-permute-start(bf16[4,64,1024]{2,1,0:T(8,128)(2,1)S(1)} %shard_map.116.near), channel_id=1, source_target_pairs={{0,3},{1,2},{2,1},{3,0},{4,7},{5,6},{6,5},{7,4},{8,11},{9,10},{10,... | collective-permute-start | bytes 1572872 | tf_op jit(solution)/shard_map/ppermute | solution.py:31
  44.6 1.3 %collective-permute-start.10 = (bf16[256,128]{1,0:T(8,128)(2,1)S(1)}, bf16[256,128]{1,0:T(8,128)(2,1)S(1)}, u32[]{:S(2)}, u32[]{:S(2)}) collective-permute-start(bf16[256,128]{1,0:T(8,128)(2,1)S(1)} %shard_map.118), channel_id=1, source_target_pairs={{0,128},{128,0},{1,129},{129,1},{2,130},{130,2},{3,131},{131,3},{4... | collective-permute-start | bytes 196616 | tf_op jit(solution)/shard_map/ppermute | solution.py:27
  46.0 7.0 %collective-permute-start.13 = (bf16[2,256,128]{2,1,0:T(8,128)(2,1)S(1)}, bf16[2,256,128]{2,1,0:T(8,128)(2,1)S(1)}, u32[]{:S(2)}, u32[]{:S(2)}) collective-permute-start(bf16[2,256,128]{2,1,0:T(8,128)(2,1)S(1)} %pad_maximum_fusion.u0), channel_id=1, source_target_pairs={{0,8},{8,16},{16,24},{24,0},{1,9},{9,17},{17,25},{25,1},{2,10},{10... | collective-permute-start | bytes 393224 | tf_op jit(solution)/shard_map/ppermute | solution.py:27
  47.7 9.1 %collective-permute-start.12 = (bf16[2,256,128]{2,1,0:T(8,128)(2,1)S(1)}, bf16[2,256,128]{2,1,0:T(8,128)(2,1)S(1)}, u32[]{:S(2)}, u32[]{:S(2)}) collective-permute-start(bf16[2,256,128]{2,1,0:T(8,128)(2,1)S(1)} %pad_maximum_fusion.u0), channel_id=1, source_target_pairs={{0,16},{8,24},{16,0},{24,8},{1,17},{9,25},{17,1},{25,9},{2,18},{10... | collective-permute-start | bytes 393224 | tf_op jit(solution)/shard_map/ppermute | solution.py:27
  50.5 6.3 %collective-permute-start.11 = (bf16[2,256,128]{2,1,0:T(8,128)(2,1)S(1)}, bf16[2,256,128]{2,1,0:T(8,128)(2,1)S(1)}, u32[]{:S(2)}, u32[]{:S(2)}) collective-permute-start(bf16[2,256,128]{2,1,0:T(8,128)(2,1)S(1)} %pad_maximum_fusion.u0), channel_id=1, source_target_pairs={{0,24},{8,0},{16,8},{24,16},{1,25},{9,1},{17,9},{25,17},{2,26},{10... | collective-permute-start | bytes 393224 | tf_op jit(solution)/shard_map/ppermute | solution.py:27
  57.9 7.7 %collective-permute-start.15 = (bf16[64,128]{1,0:T(8,128)(2,1)S(1)}, bf16[64,128]{1,0:T(8,128)(2,1)S(1)}, u32[]{:S(2)}, u32[]{:S(2)}) collective-permute-start(bf16[64,128]{1,0:T(8,128)(2,1)S(1)} %get-tuple-element.74), channel_id=1, source_target_pairs={{0,64},{32,96},{64,0},{96,32},{1,65},{33,97},{65,1},{97,33},{2,66}... | collective-permute-start | bytes 49160 | tf_op jit(solution)/shard_map/ppermute | solution.py:27
  60.3 5.8 %collective-permute-start.16 = (bf16[64,128]{1,0:T(8,128)(2,1)S(1)}, bf16[64,128]{1,0:T(8,128)(2,1)S(1)}, u32[]{:S(2)}, u32[]{:S(2)}) collective-permute-start(bf16[64,128]{1,0:T(8,128)(2,1)S(1)} %get-tuple-element.75), channel_id=1, source_target_pairs={{0,32},{32,64},{64,96},{96,0},{1,33},{33,65},{65,97},{97,1},{2,34}... | collective-permute-start | bytes 49160 | tf_op jit(solution)/shard_map/ppermute | solution.py:27
  62.2 4.6 %collective-permute-start.17 = (bf16[64,128]{1,0:T(8,128)(2,1)S(1)}, bf16[64,128]{1,0:T(8,128)(2,1)S(1)}, u32[]{:S(2)}, u32[]{:S(2)}) collective-permute-start(bf16[64,128]{1,0:T(8,128)(2,1)S(1)} %get-tuple-element.76), channel_id=1, source_target_pairs={{0,96},{32,0},{64,32},{96,64},{1,97},{33,1},{65,33},{97,65},{2,98}... | collective-permute-start | bytes 49160 | tf_op jit(solution)/shard_map/ppermute | solution.py:27
  (1 other events, 2.2 us)
